TPU v7x, 32 devices: a whole 2x2x4 slice. The times are simulated.
32 devices in a mesh: group: 2 (over x), branch: 8 (over z, y), expert: 2 (over core).
Axes of the slice: x: 2, y: 2, z: 4, core: 2. Of those that a mesh axis runs over, the one named last changes fastest.
Arguments:
- latent_cache: bfloat16 [16, 2048, 512], P(('group', 'branch'), 'expert'), parts along dimension 0, may hold values from -4 to 4
- rope_cache: bfloat16 [16, 256, 512], P(('group', 'branch'), 'expert'), parts along dimension 0, may hold values from -4 to 4
- q_latent: bfloat16 [256, 2, 128, 512], P(('group', 'branch', 'expert')), parts along dimension 0, may hold values from -4.8 to 4.8
- q_rope: bfloat16 [256, 2, 8192], P(('group', 'branch', 'expert')), parts along dimension 0, may hold values from -192 to 192
- new_latent: bfloat16 [256, 2, 512], P(('group', 'branch', 'expert')), parts along dimension 0, may hold values from -4 to 4
- new_rope: bfloat16 [256, 2, 64], P(('group', 'branch', 'expert')), parts along dimension 0, may hold values from -4.2 to 4.2
- branch_slot: int32 [256], P(('group', 'branch', 'expert')), parts along dimension 0, may hold values from 0 to 7, as said below
- moe_input: bfloat16 [256, 2, 7168], P(('group', 'branch', 'expert')), parts along dimension 0, may hold values from -6 to 6
- routes: int32 [256, 2, 8], P(('group', 'branch', 'expert')), parts along dimension 0, may hold values from 0 to 255, as said below
- route_gate: float32 [256, 2, 8], P(('group', 'branch', 'expert')), parts along dimension 0, may hold values from 0.05 to 0.6
- w_gate: bfloat16 [16, 7168, 128], P(('branch', 'expert')), may hold values from -0.0625 to 0.0625
- w_up: bfloat16 [16, 7168, 128], P(('branch', 'expert')), may hold values from -0.0625 to 0.0625
- w_down: bfloat16 [16, 128, 7168], P(('branch', 'expert')), may hold values from -0.1875 to 0.1875
Outputs:
- attended: bfloat16 [256, 2, 128, 512], P(('group', 'branch', 'expert')), parts along dimension 0
- moe_out: bfloat16 [256, 2, 7168], P(('group', 'branch', 'expert')), parts along dimension 0
There are 2 independent parts, one for each index of `group`. A program takes and returns all parts, laid end to end along the dimension named above; an argument that names none is the same for every part. Nothing has to cross between parts.
Inputs may be any that keep to these rules, and one draw needn't show every extreme that they name: `branch_slot`: among the 8 tokens of one device every number from 0 to 7 stands exactly once. `routes`: each row (a token at a step) names 8 different experts, at most one of them below 2; within the 16 rows of one device no expert below 2 is named more than 2 times, and some one exactly 2 times.
All inputs are finite; a program needn't handle non-finite values.
Results may differ from a plain program's by a relative error of at most 0.0057.
Values may be sent and summed in bfloat16 or wider, within the bound.
No kernel may reach another device: no remote copies, remote signals or barrier semaphores. Data moves between devices by JAX's collectives and lax.ppermute only.
A program may use at most 192 MiB of HBM per device.

v0:
```python
import jax
import jax.numpy as jnp
from jax import lax
from jax.sharding import PartitionSpec as P

SHARDS = 8
CAP = 2


softmax_scale = 192.0 ** (-0.5)


def swapped(x, axis, bit):
    return lax.ppermute(x, axis, [(i, i ^ 1 << bit) for i in range(lax.axis_size(axis))])


def partial_softmax(query_lat, query_rope, keys_lat, keys_rope):
    scores = jnp.einsum("omshc,opc->omshp", query_lat, keys_lat, preferred_element_type=jnp.float32)
    scores = scores + jnp.einsum(
        "omshr,opr->omshp", query_rope, keys_rope, preferred_element_type=jnp.float32
    )
    scores = scores * softmax_scale
    cache_peak = jnp.max(scores, axis=-1)
    exponent = jnp.exp(scores - cache_peak[..., None])
    totals = jnp.sum(exponent, axis=-1)
    weights = exponent.astype(jnp.bfloat16)
    summed = jnp.einsum("omshp,opc->omshc", weights, keys_lat, preferred_element_type=jnp.float32)
    cache_out = (summed / totals[..., None]).astype(jnp.bfloat16)
    cache_lse = cache_peak + jnp.log(totals)
    return (cache_out, cache_lse)


def split_half(source, stride):
    pieces = source.reshape((source.shape[0] // (2 * stride), 2, stride) + source.shape[1:])
    return (pieces[:, 0], pieces[:, 1])


def join_half(staying, arrived):
    return jnp.stack([staying, arrived], axis=1).reshape((-1,) + staying.shape[2:])


def on_device(
    latent_cache,
    rope_cache,
    q_latent,
    q_rope,
    new_latent,
    new_rope,
    branch_slot,
    moe_input,
    routes,
    route_gate,
    w_gate,
    w_up,
    w_down,
):
    tok_rows = q_latent.shape[0]
    step_count = q_latent.shape[1]
    head_count = q_latent.shape[2]
    rope_width = new_rope.shape[-1]
    rounds = tok_rows.bit_length() - 1
    lowest = lax.axis_index("expert") == 0
    rope_query = q_rope.reshape(tok_rows, step_count, head_count, rope_width)
    counting = jnp.arange(tok_rows, dtype=jnp.int32)
    other_lat, other_rope = swapped((latent_cache[0], rope_cache[0]), "expert", 0)
    full_lat = jnp.where(
        lowest,
        jnp.concatenate([latent_cache[0], other_lat]),
        jnp.concatenate([other_lat, latent_cache[0]]),
    )[None]
    full_rope = jnp.where(
        lowest,
        jnp.concatenate([rope_cache[0], other_rope]),
        jnp.concatenate([other_rope, rope_cache[0]]),
    )
    full_rope = full_rope.reshape(1, -1, rope_width)
    own_index = lax.axis_index("branch") % tok_rows
    target = jnp.bitwise_xor(own_index, branch_slot)
    chooser = (target[None, :] == counting[:, None]).astype(jnp.int32)
    ordering = jnp.sum(chooser * counting[None, :], axis=1)
    query_lat = jnp.take(q_latent, ordering, axis=0)
    query_rope = jnp.take(q_rope, ordering, axis=0)
    for bit_number in range(rounds):
        stride = 1 << bit_number
        staying_lat, leaving_lat = split_half(query_lat, stride)
        staying_rope, leaving_rope = split_half(query_rope, stride)
        arrived_lat, arrived_rope = swapped((leaving_lat, leaving_rope), "branch", bit_number)
        query_lat = join_half(staying_lat, arrived_lat)
        query_rope = join_half(staying_rope, arrived_rope)
    query_rope = query_rope.reshape(tok_rows, step_count, head_count, rope_width)
    cache_out, cache_lse = partial_softmax(query_lat[None], query_rope[None], full_lat, full_rope)
    cache_out, cache_lse = (cache_out[0], cache_lse[0])
    for bit_number in range(rounds):
        stride = 1 << bit_number
        staying_out, leaving_out = split_half(cache_out, stride)
        staying_lse, leaving_lse = split_half(cache_lse, stride)
        arrived_out, arrived_lse = (
            swapped(leaving_out.astype(jnp.float32), "branch", bit_number).astype(
                leaving_out.dtype
            ),
            swapped(leaving_lse, "branch", bit_number),
        )
        cache_out = join_half(staying_out, arrived_out)
        cache_lse = join_half(staying_lse, arrived_lse)
    cache_out = jnp.take(cache_out, target, axis=0)
    cache_lse = jnp.take(cache_lse, target, axis=0)
    own_scores = jnp.einsum(
        "rshc,rjc->rshj", q_latent, new_latent, preferred_element_type=jnp.float32
    )
    own_scores = own_scores + jnp.einsum(
        "rshp,rjp->rshj", rope_query, new_rope, preferred_element_type=jnp.float32
    )
    own_scores = own_scores * softmax_scale
    causal = (jnp.arange(step_count)[None, :] <= jnp.arange(step_count)[:, None])[None, :, None, :]
    own_peak = jnp.max(jnp.where(causal, own_scores, -1e30), axis=-1)
    own_weight = jnp.where(causal, jnp.exp(own_scores - own_peak[..., None]), 0.0)
    own_total = jnp.sum(own_weight, axis=-1)
    own_sum = jnp.einsum(
        "rshj,rjc->rshc",
        own_weight,
        new_latent.astype(jnp.float32),
        precision=lax.Precision.HIGHEST,
    )
    top_value = jnp.maximum(cache_lse, own_peak)
    factor = jnp.exp(cache_lse - top_value)
    own_factor = jnp.exp(own_peak - top_value)
    numerator = factor[..., None] * cache_out.astype(jnp.float32) + own_factor[..., None] * own_sum
    denominator = factor + own_factor * own_total
    attended = (numerator / denominator[..., None]).astype(jnp.bfloat16)
    model_width = moe_input.shape[-1]
    top_count = routes.shape[-1]
    tok_total = tok_rows * step_count
    expert_count = lax.axis_size("branch") * lax.axis_size("expert") // SHARDS
    capacity = CAP
    flat_routes = routes.reshape(-1)
    inside = flat_routes < expert_count
    onehot = (flat_routes[:, None] == jnp.arange(expert_count, dtype=jnp.int32)[None, :]).astype(
        jnp.int32
    )
    before = jnp.cumsum(onehot, axis=0) - onehot
    position = jnp.sum(before * onehot, axis=1)
    slot_index = jnp.where(inside, flat_routes * capacity + position, -1)
    placing = (
        slot_index[None, :] == jnp.arange(expert_count * capacity, dtype=jnp.int32)[:, None]
    ).astype(jnp.float32)
    placing = jnp.sum(
        placing.reshape(expert_count * capacity, tok_total, top_count), axis=-1
    ).astype(jnp.bfloat16)
    tokens_flat = moe_input.reshape(tok_total, model_width)
    outgoing = jnp.dot(placing, tokens_flat, preferred_element_type=jnp.float32).astype(
        jnp.bfloat16
    )
    outgoing = outgoing.reshape(expert_count, 1, capacity, model_width)
    copies = jnp.broadcast_to(outgoing, (expert_count, SHARDS, capacity, model_width))
    copies = copies.reshape(expert_count * SHARDS, capacity, model_width)
    arrived = lax.all_to_all(copies, ("branch", "expert"), split_axis=0, concat_axis=0, tiled=True)
    flattened = arrived.reshape(-1, model_width)
    gate_value = jnp.dot(flattened, w_gate[0], preferred_element_type=jnp.float32)
    lifted = jnp.dot(flattened, w_up[0], preferred_element_type=jnp.float32)
    hidden = (jax.nn.silu(gate_value) * lifted).astype(jnp.bfloat16)
    returned = lax.all_to_all(
        jnp.dot(hidden, w_down[0], preferred_element_type=jnp.float32)
        .astype(jnp.bfloat16)
        .reshape(arrived.shape),
        ("branch", "expert"),
        split_axis=0,
        concat_axis=0,
        tiled=True,
    )
    expert_sums = jnp.sum(
        returned.reshape(expert_count, SHARDS, capacity, model_width).astype(jnp.float32), axis=1
    )
    expert_sums = expert_sums.reshape(expert_count * capacity, model_width)
    safe_index = jnp.maximum(slot_index, 0)
    picked = jnp.take(expert_sums, safe_index, axis=0).reshape(tok_total, top_count, model_width)
    gate_used = jnp.where(inside, route_gate.reshape(-1), 0.0).reshape(tok_total, top_count, 1)
    combined = jnp.sum(gate_used * picked, axis=1)
    moe_out = combined.astype(jnp.bfloat16).reshape(tok_rows, step_count, model_width)
    return (attended, moe_out)


def solution(mesh):
    return jax.shard_map(
        on_device,
        mesh=mesh,
        in_specs=(
            P(("group", "branch"), "expert", None),
            P(("group", "branch"), "expert", None),
            P(("group", "branch", "expert"), None, None, None),
            P(("group", "branch", "expert"), None, None),
            P(("group", "branch", "expert"), None, None),
            P(("group", "branch", "expert"), None, None),
            P(("group", "branch", "expert")),
            P(("group", "branch", "expert"), None, None),
            P(("group", "branch", "expert"), None, None),
            P(("group", "branch", "expert"), None, None),
            P(("branch", "expert"), None, None),
            P(("branch", "expert"), None, None),
            P(("branch", "expert"), None, None),
        ),
        out_specs=(
            P(("group", "branch", "expert"), None, None, None),
            P(("group", "branch", "expert"), None, None),
        ),
        check_vma=False,
    )
```

profile of v0, /device:TPU:0, one launch (start us, length us, event | category | flops | bytes accessed | tf_op | source)
XLA Modules:
  0.0 288.2 jit_solution(16954718998658454671)
XLA Ops:
  0.7 1.3 compare_and_fusion.2
  2.5 2.0 gather_fusion.3
  4.5 1.9 broadcast_select_fusion
  7.5 3.0 %collective-permute-start = (bf16[4,1,2,128,512]{4,3,2,0,1:T(8,128)(2,1)}, bf16[4,1,2,128,512]{4,3,2,0,1:T(8,128)(2,1)}, u32[]{:S(2)}, u32[]{:S(2)}) collective-permute-start(bf16[4,1,2,128,512]{4,3,2,0,1:T(8,128)(2,1)} %get-tuple-element.21), channel_id=1, source_target_pairs={{0,2},{2,0},{4,6},{6,4},{8,10},{10,8},{12,14},{14,12},{1,3},{3,1},... | collective-permute-start | bytes 3145736 | tf_op jit(solution)/shard_map/ppermute | solution.py:14
  10.6 1.8 gather_fusion
  16.2 1.4 fusion.36
  17.6 1.6 reduce_window_sum.11
  19.2 1.6 select_reduce_fusion
  21.6 1.3 lt.65
  25.5 1.7 reshape.359
  27.2 1.7 convolution_convert_fusion.1
  28.9 1.5 broadcast_in_dim.105
  30.4 1.8 broadcast_in_dim.106
  32.2 6.5 %all-to-all-start = ((bf16[16,2,7168]{2,1,0:T(2,128)(2,1)}), bf16[16,2,7168]{2,1,0:T(2,128)(2,1)}, u32[]{:S(2)}, u32[]{:S(2)}) async-start(bf16[16,2,7168]{2,1,0:T(2,128)(2,1)} %bitcast.168), calls=%async_computation | async-start | bytes 917504 | tf_op jit(solution)/shard_map/all_to_all | solution.py:156
  39.9 1.9 fusion.50
  43.8 1.9 collective-permute-start.5
  48.0 4.3 %collective-permute-done.5 = bf16[2,2,2,8192]{3,2,1,0:T(2,128)(2,1)} collective-permute-done((bf16[2,2,2,8192]{3,2,1,0:T(2,128)(2,1)}, bf16[2,2,2,8192]{3,2,1,0:T(2,128)(2,1)}, u32[]{:S(2)}, u32[]{:S(2)}) %collective-permute-start.5) | collective-permute-done | bytes 131104 | tf_op jit(solution)/shard_map/ppermute | solution.py:14
  53.6 1.4 fusion.28
  55.5 4.0 %collective-permute-start.6 = (bf16[1,4,2,8192]{3,2,1,0:T(2,128)(2,1)S(1)}, bf16[1,4,2,8192]{3,2,1,0:T(2,128)(2,1)S(1)}, u32[]{:S(2)}, u32[]{:S(2)}) collective-permute-start(bf16[1,4,2,8192]{3,2,1,0:T(2,128)(2,1)S(1)} %get-tuple-element.23), channel_id=1, source_target_pairs={{0,8},{2,10},{4,12},{6,14},{8,0},{10,2},{12,4},{14,6},{1,9},{3,11}... | collective-permute-start | bytes 393224 | tf_op jit(solution)/shard_map/ppermute | solution.py:14
  59.6 23.2 %collective-permute-done.1 = bf16[2,2,2,128,512]{4,3,2,1,0:T(8,128)(2,1)S(1)} collective-permute-done((bf16[2,2,2,128,512]{4,3,2,1,0:T(8,128)(2,1)S(1)}, bf16[2,2,2,128,512]{4,3,2,1,0:T(8,128)(2,1)S(1)}, u32[]{:S(2)}, u32[]{:S(2)}) %collective-permute-start.1) | collective-permute-done | bytes 1048608 | tf_op jit(solution)/shard_map/ppermute | solution.py:14
  84.2 1.9 collective-permute-start.2
  87.6 9.3 %fusion.33 = f32[8,2,128,2048]{3,2,1,0:T(8,128)} fusion(bf16[8,2,128,64]{3,2,1,0:T(8,128)(2,1)} %reshape.353, bf16[2048,64]{1,0:T(8,128)(2,1)} %select_n.141), kind=kOutput, calls=%fused_computation.57 | convolution fusion | flops 536870912 | bytes 17301504 | tf_op jit(solution)/shard_map/omshr,opr->omshp/dot_general | solution.py:19
  96.8 35.1 %collective-permute-done.2 = bf16[1,4,2,128,512]{4,3,2,1,0:T(8,128)(2,1)} collective-permute-done((bf16[1,4,2,128,512]{4,3,2,1,0:T(8,128)(2,1)}, bf16[1,4,2,128,512]{4,3,2,1,0:T(8,128)(2,1)}, u32[]{:S(2)}, u32[]{:S(2)}) %collective-permute-start.2) | collective-permute-done | bytes 1048608 | tf_op jit(solution)/shard_map/ppermute | solution.py:14
  131.9 1.5 pad_maximum_fusion.1
  133.4 14.6 %fusion.70 = (f32[8,2,128]{2,1,0:T(2,128)S(1)}, f32[8,2,128,2048]{3,2,1,0:T(8,128)}) fusion(f32[8,2,128,2048]{3,2,1,0:T(8,128)} %fusion.33, bf16[8,2,128,512]{3,2,1,0:T(8,128)(2,1)S(1)} %bitcast.159, bf16[1024,512]{1,0:T(8,128)(2,1)} %collective-permute-done.3, bf16[1024,512]{1,0:T(8,128)(2,1)S(1)} %bitcast.170, pred[]{:T(512)S(6)} %eq.48), kind=kOutput, calls=%fused_computation.143 | convolution fusion | flops 4316985344 | bytes 37756928 | tf_op jit(solution)/shard_map/omshc,opc->omshp/dot_general | solution.py:18
  148.0 8.2 %fusion.1 = f32[8,2,128]{2,1,0:T(2,128)S(1)} fusion(f32[8,2,128,2048]{3,2,1,0:T(8,128)} %get-tuple-element.35, f32[8,2,128]{2,1,0:T(2,128)S(1)} %get-tuple-element.34), kind=kLoop, calls=%fused_computation.8 | loop fusion | flops 8386560 | bytes 16793600 | tf_op jit(solution)/shard_map/reduce_sum | solution.py:25
  156.3 11.3 %divide_convert_fusion.1 = bf16[8,2,128,512]{3,2,1,0:T(8,128)(2,1)S(1)} fusion(f32[8,2,128,2048]{3,2,1,0:T(8,128)} %get-tuple-element.35, f32[8,2,128]{2,1,0:T(2,128)S(1)} %get-tuple-element.34, f32[8,2,128]{2,1,0:T(2,128)S(1)} %fusion.1, bf16[1024,512]{1,0:T(8,128)(2,1)} %collective-permute-done.3, bf16[1024,512]{1,0:T(8,128)(2,1)S(1)} %bitcast.171, ...), kind=kOutput, calls=%fused_computation.14 | convolution fusion | flops 4314890240 | bytes 20987904 | tf_op jit(solution)/shard_map/omshp,opc->omshc/dot_general | solution.py:27
  167.7 1.5 fusion.64
  169.2 1.8 collective-permute-start.11
  172.0 2.0 reshape.361
  174.0 20.5 %collective-permute-done.11 = bf16[4,1,2,128,512]{4,3,2,0,1:T(8,128)(2,1)S(1)} collective-permute-done((bf16[4,1,2,128,512]{4,3,2,0,1:T(8,128)(2,1)}, bf16[4,1,2,128,512]{4,3,2,0,1:T(8,128)(2,1)S(1)}, u32[]{:S(2)}, u32[]{:S(2)}) %collective-permute-start.11) | collective-permute-done | bytes 1048608 | tf_op jit(solution)/shard_map/ppermute | solution.py:14
  195.4 2.9 fusion.27
  198.8 3.7 %convolution_convert_fusion = bf16[32,7168]{1,0:T(8,128)(2,1)} fusion(bf16[1,128,7168]{2,1,0:T(8,128)(2,1)} %param.27, bf16[32,7168]{1,0:T(8,128)(2,1)} %reshape.361, bf16[1,7168,128]{2,1,0:T(8,128)(2,1)} %param.26, f32[32,128]{1,0:T(8,128)S(1)} %fusion.13), kind=kOutput, calls=%fused_computation.11 | convolution fusion | flops 117694464 | bytes 4603904 | tf_op jit(solution)/shard_map/dot_general | solution.py:162
  202.6 2.0 reshape.362
  204.5 4.8 %all-to-all-start.1 = ((bf16[16,2,7168]{2,1,0:T(2,128)(2,1)}), bf16[16,2,7168]{2,1,0:T(2,128)(2,1)}, u32[]{:S(2)}, u32[]{:S(2)}) async-start(bf16[16,2,7168]{2,1,0:T(2,128)(2,1)} %reshape.362), calls=%async_computation.1 | async-start | bytes 917504 | tf_op jit(solution)/shard_map/all_to_all | solution.py:161
  209.4 1.9 collective-permute-start.8
  211.3 2.4 collective-permute-done.8
  213.7 1.5 collective-permute-start.9
  215.2 13.2 %collective-permute-done.12 = bf16[2,2,2,128,512]{4,3,2,0,1:T(8,128)(2,1)} collective-permute-done((bf16[2,2,2,128,512]{4,3,2,0,1:T(8,128)(2,1)}, bf16[2,2,2,128,512]{4,3,2,0,1:T(8,128)(2,1)}, u32[]{:S(2)}, u32[]{:S(2)}) %collective-permute-start.12) | collective-permute-done | bytes 1048608 | tf_op jit(solution)/shard_map/ppermute | solution.py:14
  228.4 1.4 pad_maximum_fusion.2
  232.5 1.5 convert_reduce_fusion
  234.1 3.3 %gather_fusion.2 = f32[128,7168]{1,0:T(8,128)} fusion(f32[4,7168]{1,0:T(4,128)S(1)} %reshape.363, s32[1024]{0:T(1024)S(1)} %pad_clamp_fusion), kind=kCustom, calls=%fused_computation.4 | custom fusion | bytes 7340544 | tf_op jit(solution)/shard_map/jit(_take)/gather | solution.py:175
  237.4 1.5 collective-permute-start.10
  238.9 3.3 %fusion.6 = bf16[16,7168]{1,0:T(8,128)(2,1)S(1)} fusion(f32[128,7168]{1,0:T(8,128)} %gather_fusion.2, f32[16,8]{1,0:T(8,128)S(1)} %broadcast_select_fusion.3, pred[16,8]{1,0:T(8,128)(4,1)S(1)} %copy-done.13), kind=kLoop, calls=%fused_computation.17 | loop fusion | flops 2637824 | bytes 3900032 | tf_op jit(solution)/shard_map/reduce_sum | solution.py:177
  243.0 32.9 %collective-permute-done.10 = f32[1,4,2,128]{3,2,1,0:T(2,128)S(1)} collective-permute-done((f32[1,4,2,128]{3,2,1,0:T(2,128)S(1)}, f32[1,4,2,128]{3,2,1,0:T(2,128)S(1)}, u32[]{:S(2)}, u32[]{:S(2)}) %collective-permute-start.10) | collective-permute-done | bytes 4128 | tf_op jit(solution)/shard_map/ppermute | solution.py:14
  276.6 2.7 pad_maximum_fusion.3
  279.3 3.6 %gather_fusion.4 = bf16[8,2,128,512]{3,2,1,0:T(8,128)(2,1)} fusion(bf16[8,2,128,512]{3,2,1,0:T(8,128)(2,1)} %bitcast.163, s32[1024]{0:T(1024)S(1)} %pad_clamp_fusion.1), kind=kCustom, calls=%fused_computation.1.clone | custom fusion | bytes 4194336 | tf_op jit(solution)/shard_map/jit(_take)/gather | solution.py:105
  282.9 5.3 %divide_convert_fusion = bf16[8,2,128,512]{3,2,1,0:T(8,128)(2,1)} fusion(bf16[8,2,128,512]{3,2,1,0:T(8,128)(2,1)} %gather_fusion.4, f32[8,2,128]{2,1,0:T(2,128)S(1)} %get-tuple-element.5, f32[8,2,128]{2,1,0:T(2,128)S(1)} %get-tuple-element.6, f32[8,2,128]{2,1,0:T(2,128)S(1)} %get-tuple-element.7, pred[8]{0:T(512)(128)(4,1)S(1)} %copy-done.17, ...), kind=kOutput, calls=%fused_computation.13 | convolution fusion | flops 32514048 | bytes 4259852 | tf_op jit(solution)/shard_map/rshj,rjc->rshc/dot_general | solution.py:118
  (109 shorter events, 26.2 us)
Async XLA Ops:
  0.6 1.8 copy-start
  1.9 0.5 copy-start.18
  6.3 4.3 %copy-start.5 = (bf16[8,2,8192]{2,1,0:T(2,128)(2,1)S(1)}, bf16[8,2,8192]{2,1,0:T(2,128)(2,1)}, u32[]{:S(2)}) copy-start(bf16[8,2,8192]{2,1,0:T(2,128)(2,1)} %param.18) | copy-start | bytes 786436
  6.4 8.6 %copy-start.7 = (s32[8,2,8]{2,1,0:T(2,128)S(1)}, s32[8,2,8]{2,1,0:T(2,128)}, u32[]{:S(2)}) copy-start(s32[8,2,8]{2,1,0:T(2,128)} %param.23) | copy-start | bytes 1540
  7.5 46.0 %collective-permute-start = (bf16[4,1,2,128,512]{4,3,2,0,1:T(8,128)(2,1)}, bf16[4,1,2,128,512]{4,3,2,0,1:T(8,128)(2,1)}, u32[]{:S(2)}, u32[]{:S(2)}) collective-permute-start(bf16[4,1,2,128,512]{4,3,2,0,1:T(8,128)(2,1)} %get-tuple-element.21), channel_id=1, source_target_pairs={{0,2},{2,0},{4,6},{6,4},{8,10},{10,8},{12,14},{14,12},{1,3},{3,1},... | collective-permute-start | bytes 3145736 | tf_op jit(solution)/shard_map/ppermute | solution.py:14
  14.4 27.3 %collective-permute-start.4 = (bf16[4,1,2,8192]{3,2,0,1:T(2,128)(2,1)}, bf16[4,1,2,8192]{3,2,0,1:T(2,128)(2,1)}, u32[]{:S(2)}, u32[]{:S(2)}) collective-permute-start(bf16[4,1,2,8192]{3,2,0,1:T(2,128)(2,1)} %get-tuple-element.27), channel_id=1, source_target_pairs={{0,2},{2,0},{4,6},{6,4},{8,10},{10,8},{12,14},{14,12},{1,3},{3,1},... | collective-permute-start | bytes 393224 | tf_op jit(solution)/shard_map/ppermute | solution.py:14
  14.5 31.3 %collective-permute-start.7 = (bf16[128,512]{1,0:T(8,128)(2,1)}, bf16[128,512]{1,0:T(8,128)(2,1)}, u32[]{:S(2)}, u32[]{:S(2)}) collective-permute-start(bf16[128,512]{1,0:T(8,128)(2,1)} %bitcast.179), channel_id=1, source_target_pairs={{0,1},{1,0},{2,3},{3,2},{4,5},{5,4},{6,7},{7,6},{8,9},{9,8},{10,11... | collective-permute-start | bytes 393224 | tf_op jit(solution)/shard_map/ppermute | solution.py:14
  14.5 119.0 %collective-permute-start.3 = (bf16[1024,512]{1,0:T(8,128)(2,1)}, bf16[1024,512]{1,0:T(8,128)(2,1)}, u32[]{:S(2)}, u32[]{:S(2)}) collective-permute-start(bf16[1024,512]{1,0:T(8,128)(2,1)} %bitcast.169), channel_id=1, source_target_pairs={{0,1},{1,0},{2,3},{3,2},{4,5},{5,4},{6,7},{7,6},{8,9},{9,8},{10,11... | collective-permute-start | bytes 3145736 | tf_op jit(solution)/shard_map/ppermute | solution.py:14
  24.1 15.8 %copy-start.16 = (bf16[8,2,64]{2,1,0:T(2,128)(2,1)S(1)}, bf16[8,2,64]{2,1,0:T(2,128)(2,1)}, u32[]{:S(2)}) copy-start(bf16[8,2,64]{2,1,0:T(2,128)(2,1)} %param.20) | copy-start | bytes 6148
  27.2 18.5 %copy-start.19 = (s32[8]{0:T(128)S(1)}, s32[8]{0:T(128)}, u32[]{:S(2)}) copy-start(s32[8]{0:T(128)} %copy-done.18) | copy-start | bytes 100
  32.2 139.8 %all-to-all-start = ((bf16[16,2,7168]{2,1,0:T(2,128)(2,1)}), bf16[16,2,7168]{2,1,0:T(2,128)(2,1)}, u32[]{:S(2)}, u32[]{:S(2)}) async-start(bf16[16,2,7168]{2,1,0:T(2,128)(2,1)} %bitcast.168), calls=%async_computation | async-start | bytes 917504 | tf_op jit(solution)/shard_map/all_to_all | solution.py:156
  43.8 8.5 %collective-permute-start.5 = (bf16[2,2,2,8192]{3,2,1,0:T(2,128)(2,1)}, bf16[2,2,2,8192]{3,2,1,0:T(2,128)(2,1)}, u32[]{:S(2)}, u32[]{:S(2)}) collective-permute-start(bf16[2,2,2,8192]{3,2,1,0:T(2,128)(2,1)} %bitcast.154), channel_id=1, source_target_pairs={{0,4},{2,6},{4,0},{6,2},{8,12},{10,14},{12,8},{14,10},{1,5},{3,7},... | collective-permute-start | bytes 393224 | tf_op jit(solution)/shard_map/ppermute | solution.py:14
  55.0 27.8 %collective-permute-start.1 = (bf16[2,2,2,128,512]{4,3,2,1,0:T(8,128)(2,1)S(1)}, bf16[2,2,2,128,512]{4,3,2,1,0:T(8,128)(2,1)S(1)}, u32[]{:S(2)}, u32[]{:S(2)}) collective-permute-start(bf16[2,2,2,128,512]{4,3,2,1,0:T(8,128)(2,1)S(1)} %bitcast.173), channel_id=1, source_target_pairs={{0,4},{2,6},{4,0},{6,2},{8,12},{10,14},{12,8},{14,10},{1,5},{3,7},... | collective-permute-start | bytes 3145736 | tf_op jit(solution)/shard_map/ppermute | solution.py:14
  55.5 30.5 %collective-permute-start.6 = (bf16[1,4,2,8192]{3,2,1,0:T(2,128)(2,1)S(1)}, bf16[1,4,2,8192]{3,2,1,0:T(2,128)(2,1)S(1)}, u32[]{:S(2)}, u32[]{:S(2)}) collective-permute-start(bf16[1,4,2,8192]{3,2,1,0:T(2,128)(2,1)S(1)} %get-tuple-element.23), channel_id=1, source_target_pairs={{0,8},{2,10},{4,12},{6,14},{8,0},{10,2},{12,4},{14,6},{1,9},{3,11}... | collective-permute-start | bytes 393224 | tf_op jit(solution)/shard_map/ppermute | solution.py:14
  84.2 47.7 %collective-permute-start.2 = (bf16[1,4,2,128,512]{4,3,2,1,0:T(8,128)(2,1)}, bf16[1,4,2,128,512]{4,3,2,1,0:T(8,128)(2,1)}, u32[]{:S(2)}, u32[]{:S(2)}) collective-permute-start(bf16[1,4,2,128,512]{4,3,2,1,0:T(8,128)(2,1)} %get-tuple-element.17), channel_id=1, source_target_pairs={{0,8},{2,10},{4,12},{6,14},{8,0},{10,2},{12,4},{14,6},{1,9},{3,11}... | collective-permute-start | bytes 3145736 | tf_op jit(solution)/shard_map/ppermute | solution.py:14
  131.9 1.5 copy-start.3
  148.0 8.2 %copy-start.4 = (bf16[1,1024,512]{2,1,0:T(8,128)(2,1)S(1)}, bf16[1,1024,512]{2,1,0:T(8,128)(2,1)}, u32[]{:S(2)}) copy-start(bf16[1,1024,512]{2,1,0:T(8,128)(2,1)} %param.15) | copy-start | bytes 3145732
  167.6 3.4 %copy-start.9 = (pred[8,2,8]{2,1,0:T(4,128)(4,1)S(1)}, pred[8,2,8]{2,1,0:T(4,128)(4,1)}, u32[]{:S(2)}) copy-start(pred[8,2,8]{2,1,0:T(4,128)(4,1)} %broadcast_compare_fusion) | copy-start | bytes 388
  167.6 3.5 %copy-start.8 = (f32[8,2,128,2]{2,3,1,0:T(2,128)S(1)}, f32[8,2,128,2]{2,3,1,0:T(2,128)}, u32[]{:S(2)}) copy-start(f32[8,2,128,2]{2,3,1,0:T(2,128)} %fusion.50) | copy-start | bytes 49156
  167.6 3.5 %copy-start.11 = (bf16[8,2,512]{2,1,0:T(2,128)(2,1)S(1)}, bf16[8,2,512]{2,1,0:T(2,128)(2,1)}, u32[]{:S(2)}) copy-start(bf16[8,2,512]{2,1,0:T(2,128)(2,1)} %param.19) | copy-start | bytes 49156
  169.1 2.8 copy-start.15
  169.1 2.8 copy-start.10
  169.1 2.9 copy-start.14
  169.2 25.3 %collective-permute-start.11 = (bf16[4,1,2,128,512]{4,3,2,0,1:T(8,128)(2,1)}, bf16[4,1,2,128,512]{4,3,2,0,1:T(8,128)(2,1)S(1)}, u32[]{:S(2)}, u32[]{:S(2)}) collective-permute-start(bf16[4,1,2,128,512]{4,3,2,0,1:T(8,128)(2,1)} %get-tuple-element.15), channel_id=1, source_target_pairs={{0,2},{2,0},{4,6},{6,4},{8,10},{10,8},{12,14},{14,12},{1,3},{3,1},... | collective-permute-start | bytes 3145736 | tf_op jit(solution)/shard_map/ppermute | solution.py:14
  194.5 1.0 copy-start.6
  195.4 3.0 %copy-start.1 = (bf16[32,7168]{1,0:T(8,128)(2,1)S(1)}, bf16[32,7168]{1,0:T(8,128)(2,1)}, u32[]{:S(2)}) copy-start(bf16[32,7168]{1,0:T(8,128)(2,1)} %reshape.361) | copy-start | bytes 1376260
  195.4 3.0 %copy-start.2 = (bf16[1,7168,128]{2,1,0:T(8,128)(2,1)S(1)}, bf16[1,7168,128]{2,1,0:T(8,128)(2,1)}, u32[]{:S(2)}) copy-start(bf16[1,7168,128]{2,1,0:T(8,128)(2,1)} %param.25) | copy-start | bytes 5505028
  198.3 30.1 %collective-permute-start.12 = (bf16[2,2,2,128,512]{4,3,2,0,1:T(8,128)(2,1)}, bf16[2,2,2,128,512]{4,3,2,0,1:T(8,128)(2,1)}, u32[]{:S(2)}, u32[]{:S(2)}) collective-permute-start(bf16[2,2,2,128,512]{4,3,2,0,1:T(8,128)(2,1)} %get-tuple-element.13), channel_id=1, source_target_pairs={{0,4},{2,6},{4,0},{6,2},{8,12},{10,14},{12,8},{14,10},{1,5},{3,7},... | collective-permute-start | bytes 3145736 | tf_op jit(solution)/shard_map/ppermute | solution.py:14
  204.5 28.0 %all-to-all-start.1 = ((bf16[16,2,7168]{2,1,0:T(2,128)(2,1)}), bf16[16,2,7168]{2,1,0:T(2,128)(2,1)}, u32[]{:S(2)}, u32[]{:S(2)}) async-start(bf16[16,2,7168]{2,1,0:T(2,128)(2,1)} %reshape.362), calls=%async_computation.1 | async-start | bytes 917504 | tf_op jit(solution)/shard_map/all_to_all | solution.py:161
  209.4 4.4 %collective-permute-start.8 = (f32[4,1,2,128]{3,2,0,1:T(2,128)S(1)}, f32[4,1,2,128]{3,2,0,1:T(2,128)S(1)}, u32[]{:S(2)}, u32[]{:S(2)}) collective-permute-start(f32[4,1,2,128]{3,2,0,1:T(2,128)S(1)} %get-tuple-element.33), channel_id=1, source_target_pairs={{0,2},{2,0},{4,6},{6,4},{8,10},{10,8},{12,14},{14,12},{1,3},{3,1},... | collective-permute-start | bytes 12296 | tf_op jit(solution)/shard_map/ppermute | solution.py:14
  213.7 23.7 %collective-permute-start.9 = (f32[2,2,2,128]{3,2,0,1:T(2,128)S(1)}, f32[2,2,2,128]{3,2,0,1:T(2,128)S(1)}, u32[]{:S(2)}, u32[]{:S(2)}) collective-permute-start(f32[2,2,2,128]{3,2,0,1:T(2,128)S(1)} %get-tuple-element.31), channel_id=1, source_target_pairs={{0,4},{2,6},{4,0},{6,2},{8,12},{10,14},{12,8},{14,10},{1,5},{3,7},... | collective-permute-start | bytes 12296 | tf_op jit(solution)/shard_map/ppermute | solution.py:14
  231.0 45.6 %collective-permute-start.13 = (bf16[1,4,2,128,512]{4,3,2,1,0:T(8,128)(2,1)}, bf16[1,4,2,128,512]{4,3,2,1,0:T(8,128)(2,1)}, u32[]{:S(2)}, u32[]{:S(2)}) collective-permute-start(bf16[1,4,2,128,512]{4,3,2,1,0:T(8,128)(2,1)} %get-tuple-element.11), channel_id=1, source_target_pairs={{0,8},{2,10},{4,12},{6,14},{8,0},{10,2},{12,4},{14,6},{1,9},{3,11}... | collective-permute-start | bytes 3145736 | tf_op jit(solution)/shard_map/ppermute | solution.py:14
  234.1 4.8 %copy-start.13 = (pred[16,8]{1,0:T(8,128)(4,1)S(1)}, pred[16,8]{1,0:T(8,128)(4,1)}, u32[]{:S(2)}) copy-start(pred[16,8]{1,0:T(8,128)(4,1)} %get-tuple-element.3) | copy-start | bytes 388
  237.4 38.5 %collective-permute-start.10 = (f32[1,4,2,128]{3,2,1,0:T(2,128)S(1)}, f32[1,4,2,128]{3,2,1,0:T(2,128)S(1)}, u32[]{:S(2)}, u32[]{:S(2)}) collective-permute-start(f32[1,4,2,128]{3,2,1,0:T(2,128)S(1)} %get-tuple-element.29), channel_id=1, source_target_pairs={{0,8},{2,10},{4,12},{6,14},{8,0},{10,2},{12,4},{14,6},{1,9},{3,11}... | collective-permute-start | bytes 12296 | tf_op jit(solution)/shard_map/ppermute | solution.py:14
  238.9 37.6 %copy-start.17 = (pred[8]{0:T(512)(128)(4,1)S(1)}, pred[8]{0:T(512)(128)(4,1)}, u32[]{:S(2)}) copy-start(pred[8]{0:T(512)(128)(4,1)} %get-tuple-element.8) | copy-start | bytes 28
  279.3 3.6 %copy-start.12 = (bf16[8,2,512]{2,1,0:T(2,128)(2,1)S(1)}, bf16[8,2,512]{2,1,0:T(2,128)(2,1)}, u32[]{:S(2)}) copy-start(bf16[8,2,512]{2,1,0:T(2,128)(2,1)} %param.19) | copy-start | bytes 49156
where the time goes:
time: 289 us; the launch traced here: 288 us
  waiting for transfers between devices  132 us (46%)
  matrix products  48.9 us (17%)
  other arithmetic  39 us (13%)
  local copies, waits for them, and re-layouts  36.6 us (13%)
  starting transfers between devices  30.6 us (11%)
    ppermute x14, waiting for transfers between devices, swapped(): lax.ppermute(x, axis, [(i, i ^ 1 << bit) for i in range(lax.axis_size(axi...  132 us
    ppermute x14, starting transfers between devices, swapped(): lax.ppermute(x, axis, [(i, i ^ 1 << bit) for i in range(lax.axis_size(axi...  19.3 us
    dot_general x1, matrix products, partial_softmax(): jnp.einsum('omshc,opc->omshp', query_lat, keys_lat, preferred_element_typ...  14.6 us
    dot_general x1, matrix products, partial_softmax(): jnp.einsum('omshp,opc->omshc', weights, keys_lat, preferred_element_type=...  11.3 us
    another operation x10, other arithmetic, join_half(): jnp.stack([staying, arrived], axis=1).reshape((-1,) + staying.shape[2:])  10.2 us
    dot_general x1, matrix products, partial_softmax(): jnp.einsum('omshr,opr->omshp', query_rope, keys_rope, preferred_element_t...  9.26 us
    reduce_sum x1, other arithmetic, partial_softmax(): totals = jnp.sum(exponent, axis=-1)  8.23 us
    all_to_all x1, starting transfers between devices, on_device(): lax.all_to_all(copies, ('branch', 'expert'), split_axis=0, concat_axis=0,...  6.5 us
  transfers between devices with their start and end apart: 16, of which 8 were waited for; matrix products, arithmetic and copies ran while one was open for 35% of the time, Pallas kernels for 0%

commit v1 on v0

v1 whole, which is shorter than its diff:
```python
import functools

import jax
import jax.numpy as jnp
from jax import lax
from jax.experimental import pallas as pl
from jax.experimental.pallas import tpu as pltpu
from jax.sharding import PartitionSpec as P

SHARDS = 8
CAP = 2
LANES = 128
PAD = 16

softmax_scale = 192.0 ** (-0.5)
log2e = 1.4426950408889634


def swapped(x, axis, bit):
    return lax.ppermute(x, axis, [(i, i ^ 1 << bit) for i in range(lax.axis_size(axis))])


def line_hop(x, block, moves):
    pairs = []
    for base in range(0, lax.axis_size("branch"), block):
        for low in range(2):
            pairs += [(base + 2 * i + low, base + 2 * j + low) for i, j in moves]
    return lax.ppermute(x, "branch", pairs)


def pack_cache_kernel(lat_ref, rope_ref, out_ref, sems):
    rows = lat_ref.shape[0]
    first = pltpu.make_async_copy(lat_ref, out_ref.at[pl.ds(0, rows)], sems.at[0])
    second = pltpu.make_async_copy(
        rope_ref, out_ref.at[pl.ds(rows, rope_ref.shape[0])], sems.at[1]
    )
    first.start()
    second.start()
    first.wait()
    second.wait()


def pack_cache(lat, rope):
    return pl.pallas_call(
        pack_cache_kernel,
        out_shape=jax.ShapeDtypeStruct((lat.shape[0] + rope.shape[0], lat.shape[1]), lat.dtype),
        in_specs=[pl.BlockSpec(memory_space=pl.ANY)] * 2,
        out_specs=pl.BlockSpec(memory_space=pl.ANY),
        scratch_shapes=[pltpu.SemaphoreType.DMA((2,))],
        cost_estimate=pl.CostEstimate(flops=0, bytes_accessed=2 * 2 * lat.size, transcendentals=0),
        name="pack_cache",
    )(lat, rope)


def pack_queries_kernel(stay_row, leave_row, q_ref, rope_ref, new_ref, stay_ref, leave_ref, sems):
    slots = stay_ref.shape[0]
    copies = []
    for out, rows, group in ((leave_ref, leave_row, 0), (stay_ref, stay_row, 1)):
        for slot in range(slots):
            start = 0
            for part, source in enumerate((q_ref, rope_ref, new_ref)):
                count = source.shape[1]
                copies.append(
                    pltpu.make_async_copy(
                        source.at[rows[slot]],
                        out.at[slot, pl.ds(start, count)],
                        sems.at[group, slot, part],
                    )
                )
                start += count
    for copy in copies:
        copy.start()
    for copy in copies:
        copy.wait()


def pack_queries(stay_row, leave_row, q_lat, q_rope, new):
    slots = stay_row.shape[0]
    rows = q_lat.shape[1] + q_rope.shape[1] + new.shape[1]
    shape = jax.ShapeDtypeStruct((slots, rows, q_lat.shape[2]), q_lat.dtype)
    return pl.pallas_call(
        pack_queries_kernel,
        out_shape=(shape, shape),
        in_specs=[pl.BlockSpec(memory_space=pltpu.SMEM)] * 2
        + [pl.BlockSpec(memory_space=pl.ANY)] * 3,
        out_specs=(pl.BlockSpec(memory_space=pl.ANY),) * 2,
        scratch_shapes=[pltpu.SemaphoreType.DMA((2, slots, 3))],
        cost_estimate=pl.CostEstimate(flops=0, bytes_accessed=4 * q_lat.size, transcendentals=0),
        name="pack_queries",
    )(stay_row, leave_row, q_lat, q_rope, new)


def spread_matrix(raw_rows, width):
    per_row = width // (LANES // 2)
    blocks = width // LANES
    shape = (raw_rows * per_row, raw_rows * blocks)
    row = lax.broadcasted_iota(jnp.int32, shape, 0)
    column = lax.broadcasted_iota(jnp.int32, shape, 1)
    wanted = ((row % per_row) // 2) * raw_rows + row // per_row
    return (column == wanted).astype(jnp.bfloat16)


def spread(matrix, raw):
    blocks = raw.shape[1] // LANES
    stacked = jnp.concatenate(
        [raw[:, b * LANES : (b + 1) * LANES] for b in range(blocks)], axis=0
    )
    rows = jnp.dot(matrix, stacked, preferred_element_type=jnp.float32)
    row = lax.broadcasted_iota(jnp.int32, rows.shape, 0)
    lane = lax.broadcasted_iota(jnp.int32, rows.shape, 1)
    return jnp.where(row % 2 == lane // (LANES // 2), rows, 0.0)


def build_attend(heads, steps, width, half, rope_rows, raw_group):
    q_rows = heads * steps
    token_rope = q_rows // 8

    def one_token(q_ref, keys):
        lat = q_ref[0:q_rows, :]
        matrix = spread_matrix(raw_group, width)
        pieces = []
        for start in range(0, token_rope, raw_group):
            part = spread(matrix, q_ref[q_rows + start : q_rows + start + raw_group, :])
            pieces.append(part + pltpu.roll(part, LANES // 2, 1))
        rope = pieces[0] if len(pieces) == 1 else jnp.concatenate(pieces, axis=0)
        rope = rope.astype(jnp.bfloat16)
        query = jnp.concatenate([lat, rope], axis=1)
        contract = (((1,), (1,)), ((), ()))
        scores = lax.dot_general(query, keys[...], contract, preferred_element_type=jnp.float32)
        peak = jnp.max(scores, axis=1, keepdims=True)
        base = q_rows + token_rope
        fresh = q_ref[base : base + PAD, :]
        fresh_rope = q_ref[base + PAD : base + 2 * PAD, 0:LANES]
        own = lax.dot_general(lat, fresh, contract, preferred_element_type=jnp.float32)
        own = own + lax.dot_general(rope, fresh_rope, contract, preferred_element_type=jnp.float32)
        factor = softmax_scale * log2e
        weights = jnp.exp2(scores * factor - peak * factor)
        total = jnp.sum(weights, axis=1, keepdims=True)
        summed = jnp.dot(
            weights.astype(jnp.bfloat16), keys[:, 0:width], preferred_element_type=jnp.float32
        )
        row_step = lax.broadcasted_iota(jnp.int32, (q_rows, 1), 0) // heads
        columns = [
            jnp.where(row_step >= j, own[:, j : j + 1], -1e30) for j in range(steps)
        ]
        top = peak
        for column in columns:
            top = jnp.maximum(top, column)
        share = jnp.exp2((peak - top) * factor)
        numerator = summed * share
        denominator = total * share
        fresh32 = fresh.astype(jnp.float32)
        for j, column in enumerate(columns):
            weight = jnp.where(row_step >= j, jnp.exp2((column - top) * factor), 0.0)
            numerator = numerator + weight * fresh32[j : j + 1, :]
            denominator = denominator + weight
        return (numerator / denominator).astype(jnp.bfloat16)

    def load_keys(caches, keys, sems):
        copies = []
        for i, cache in enumerate(caches):
            copies.append(
                pltpu.make_async_copy(
                    cache.at[pl.ds(0, half)],
                    keys.at[pl.ds(i * half, half), pl.ds(0, width)],
                    sems.at[i],
                )
            )
        for copy in copies:
            copy.start()
        return copies

    def spread_keys(rope_scratch, keys):
        matrix = spread_matrix(raw_group, width)
        grown = raw_group * width // (LANES // 2)
        for i in range(2):
            for start in range(0, rope_rows, raw_group):
                part = spread(matrix, rope_scratch[i, start : start + raw_group, :])
                first = i * half + start * (width // (LANES // 2))
                keys[first : first + grown, width : width + LANES] = part.astype(jnp.bfloat16)

    def kernel(kinds, n_arrived, has_placed, *refs):
        refs = list(refs)
        index = refs.pop(0)
        queries = [refs.pop(0) for _ in kinds]
        caches = [refs.pop(0) for _ in range(2)]
        arrived = [refs.pop(0) for _ in range(n_arrived)]
        if has_placed:
            refs.pop(0)
        gives = [refs.pop(0) for kind in kinds if kind == "give"]
        placed = refs.pop(0) if ("keep" in kinds or n_arrived) else None
        keys, rope_scratch, result, sems, place_sems = refs
        copies = load_keys(caches, keys, sems)
        rope_copies = []
        for i in range(2):
            copy = pltpu.make_async_copy(
                caches[i].at[pl.ds(half, rope_rows)], rope_scratch.at[i], sems.at[2 + i]
            )
            copy.start()
            rope_copies.append(copy)
        placing = []
        for i, source in enumerate(arrived):
            copy = pltpu.make_async_copy(source, placed.at[index[1 + i]], place_sems.at[1 + i])
            copy.start()
            placing.append(copy)
        for copy in rope_copies:
            copy.wait()
        spread_keys(rope_scratch, keys)
        for copy in copies:
            copy.wait()
        for kind, query in zip(kinds, queries):
            value = one_token(query.at[0], keys)
            if kind == "give":
                gives.pop(0)[...] = value
            else:
                result[...] = value
                copy = pltpu.make_async_copy(result, placed.at[index[0]], place_sems.at[0])
                copy.start()
                placing.append(copy)
        for copy in placing:
            copy.wait()

    def call(index, kinds, slot, packed, caches, arrived, placed, count):
        n_tok = len(kinds)
        rows = packed[0].shape[1]
        any_spec = pl.BlockSpec(memory_space=pl.ANY)
        in_specs = [pl.BlockSpec(memory_space=pltpu.SMEM)]
        in_specs += [
            pl.BlockSpec((1, rows, width), lambda i: (slot, 0, 0)) for _ in range(n_tok)
        ]
        in_specs += [any_spec] * (2 + len(arrived))
        operands = [index, *packed, *caches, *arrived]
        has_placed = placed is not None
        out_shape, out_specs, alias = [], [], {}
        for kind in kinds:
            if kind == "give":
                out_shape.append(jax.ShapeDtypeStruct((q_rows, width), jnp.bfloat16))
                out_specs.append(pl.BlockSpec((q_rows, width), lambda i: (0, 0)))
        if "keep" in kinds or arrived:
            out_shape.append(jax.ShapeDtypeStruct((count, q_rows, width), jnp.bfloat16))
            out_specs.append(any_spec)
            if has_placed:
                alias = {len(operands): len(out_shape) - 1}
        if has_placed:
            in_specs.append(any_spec)
            operands.append(placed)
        all_rows = 2 * half
        return pl.pallas_call(
            functools.partial(kernel, kinds, len(arrived), has_placed),
            grid=(1,),
            out_shape=tuple(out_shape),
            in_specs=in_specs,
            out_specs=tuple(out_specs),
            scratch_shapes=[
                pltpu.VMEM((all_rows, width + LANES), jnp.bfloat16),
                pltpu.VMEM((2, rope_rows, width), jnp.bfloat16),
                pltpu.VMEM((q_rows, width), jnp.bfloat16),
                pltpu.SemaphoreType.DMA((4,)),
                pltpu.SemaphoreType.DMA((1 + max(1, len(arrived)),)),
            ],
            input_output_aliases=alias,
            cost_estimate=pl.CostEstimate(
                flops=2 * n_tok * q_rows * all_rows * (2 * width + LANES),
                bytes_accessed=2 * all_rows * (width + LANES) + 4 * n_tok * q_rows * width,
                transcendentals=n_tok * q_rows * all_rows,
            ),
            compiler_params=pltpu.CompilerParams(vmem_limit_bytes=32 * 1024 * 1024),
            name="attend_" + "_".join(kinds),
        )(*operands)

    return call


def place_kernel(index, source, before, placed, sem):
    copy = pltpu.make_async_copy(source, placed.at[index[0]], sem)
    copy.start()
    copy.wait()


def place(index, source, placed):
    return pl.pallas_call(
        place_kernel,
        out_shape=jax.ShapeDtypeStruct(placed.shape, placed.dtype),
        in_specs=[pl.BlockSpec(memory_space=pltpu.SMEM)]
        + [pl.BlockSpec(memory_space=pl.ANY)] * 2,
        out_specs=pl.BlockSpec(memory_space=pl.ANY),
        scratch_shapes=[pltpu.SemaphoreType.DMA],
        input_output_aliases={2: 0},
        name="place",
    )(index, source, placed)


def dispatch_kernel(experts, block_ref, routes_ref, gate_ref, tokens_ref, out_ref, share_ref):
    block = block_ref[0]
    routes = routes_ref[...]
    gates = gate_ref[...]
    rows = routes.shape[0]
    down = lax.broadcasted_iota(jnp.int32, (rows, rows), 0)
    across = lax.broadcasted_iota(jnp.int32, (rows, rows), 1)
    same = (down == across).astype(jnp.float32)
    slots = experts * CAP
    slot_row = lax.broadcasted_iota(jnp.int32, (slots, rows), 0)
    slot_column = lax.broadcasted_iota(jnp.int32, (rows, slots), 1)
    placing = jnp.zeros((slots, rows), jnp.float32)
    share = jnp.zeros((rows, slots), jnp.float32)
    for k in range(experts):
        expert = lax.rem(block + k, experts)
        hit = routes == expert
        has = jnp.sum(hit.astype(jnp.float32), axis=1, keepdims=True)
        weight = jnp.sum(jnp.where(hit, gates, 0.0), axis=1, keepdims=True)
        has_row = jnp.sum(has * same, axis=0, keepdims=True)
        before_row = jnp.sum(jnp.where(down < across, has, 0.0), axis=0, keepdims=True)
        before = jnp.sum(jnp.where(across < down, has_row, 0.0), axis=1, keepdims=True)
        for c in range(CAP):
            slot = k * CAP + c
            placing += jnp.where((slot_row == slot) & (before_row == c), has_row, 0.0)
            share += jnp.where((slot_column == slot) & (before == c), weight, 0.0)
    out_ref[...] = jnp.dot(
        placing.astype(jnp.bfloat16), tokens_ref[...], preferred_element_type=jnp.float32
    ).astype(jnp.bfloat16)
    share_ref[...] = share


def dispatch(block, routes, gates, tokens, experts):
    slots = experts * CAP
    return pl.pallas_call(
        functools.partial(dispatch_kernel, experts),
        out_shape=(
            jax.ShapeDtypeStruct((slots, tokens.shape[1]), tokens.dtype),
            jax.ShapeDtypeStruct((tokens.shape[0], slots), jnp.float32),
        ),
        in_specs=[pl.BlockSpec(memory_space=pltpu.SMEM)]
        + [pl.BlockSpec(memory_space=pltpu.VMEM)] * 3,
        out_specs=(pl.BlockSpec(memory_space=pltpu.VMEM),) * 2,
        cost_estimate=pl.CostEstimate(
            flops=2 * slots * tokens.size, bytes_accessed=3 * tokens.size, transcendentals=0
        ),
        name="dispatch",
    )(block, routes, gates, tokens)


def on_device(
    latent_cache,
    rope_cache,
    q_latent,
    q_rope,
    new_latent,
    new_rope,
    branch_slot,
    moe_input,
    routes,
    route_gate,
    w_gate,
    w_up,
    w_down,
):
    tok_rows, step_count, head_count, width = q_latent.shape
    rope_width = new_rope.shape[-1]
    line = tok_rows // 2
    q_rows = step_count * head_count
    half = latent_cache.shape[1]
    rope_rows = rope_cache.shape[1]
    branch = lax.axis_index("branch")
    own = branch % tok_rows
    low = own % 2
    high = own // 2
    middle = jnp.logical_and(high > 0, high < line - 1)

    outer = [(i, i ^ 1) for i in range(line)]
    inner = [(i, i + 1) for i in range(1, line - 1, 2)]
    inner = inner + [(j, i) for i, j in inner]
    outward = [(i, i ^ 1) for i in range(1, line - 1)]
    own_cache = pack_cache(latent_cache[0], rope_cache[0])
    cache_a = line_hop(own_cache, tok_rows, outer)
    first_b = line_hop(own_cache, tok_rows, inner)
    second_b = line_hop(first_b, tok_rows, outward)
    first_c = line_hop(cache_a, tok_rows, inner)
    second_c = line_hop(first_c, tok_rows, outward)
    cache_b = jnp.where(middle, first_b, second_b)
    cache_c = jnp.where(middle, first_c, second_c)
    caches = [own_cache, cache_a, cache_b, cache_c]
    caches = [(cache, swapped(cache, "expert", 0)) for cache in caches]

    nearer = jnp.where(high < line // 2, line // 2, line // 2 - 1)
    farther = jnp.where(high < line // 2, line - 1, 0)
    order = jnp.stack([high, high ^ 1, nearer, farther])
    row_of = jnp.sum(
        jnp.where(
            branch_slot[None, :] == jnp.arange(tok_rows, dtype=jnp.int32)[:, None],
            jnp.arange(tok_rows, dtype=jnp.int32)[None, :],
            0,
        ),
        axis=1,
    )
    stay_row = row_of[2 * order + low]
    leave_row = row_of[2 * order + 1 - low]

    q_lat = q_latent.reshape(tok_rows, q_rows, width)
    rope_raw = q_rope.reshape(tok_rows, q_rows * rope_width // width, width)
    fresh = jnp.concatenate(
        [
            jnp.pad(new_latent, ((0, 0), (0, PAD - step_count), (0, 0))),
            jnp.pad(new_rope, ((0, 0), (0, PAD - step_count), (0, width - rope_width))),
        ],
        axis=1,
    )
    stay, leave = pack_queries(stay_row, leave_row, q_lat, rope_raw, fresh)
    guest = swapped(leave, "branch", 0)

    attend = build_attend(head_count, step_count, width, half, rope_rows, 32)
    placed = None
    waiting = []
    for slot in range(line):
        index = jnp.stack([stay_row[slot]] + [leave_row[s] for s, _ in waiting])
        arrived = [value for _, value in waiting]
        if slot < line - 1:
            given, placed = attend(
                index,
                ("give", "keep"),
                slot,
                (guest, stay),
                caches[slot],
                arrived,
                placed,
                tok_rows,
            )
        else:
            (given,) = attend(index, ("give",), slot, (guest,), caches[slot], [], None, tok_rows)
            (placed,) = attend(
                index, ("keep",), slot, (stay,), caches[slot], arrived, placed, tok_rows
            )
        waiting = [(slot, swapped(given, "branch", 0))]
    placed = place(leave_row[line - 1 :], waiting[0][1], placed)
    attended = placed.reshape(tok_rows, step_count, head_count, width)

    model_width = moe_input.shape[-1]
    tok_total = tok_rows * step_count
    device = branch * lax.axis_size("expert") + lax.axis_index("expert")
    experts = lax.axis_size("branch") * lax.axis_size("expert") // SHARDS
    cores = lax.axis_size("expert")
    shard_branches = SHARDS // cores
    block = device // SHARDS
    outgoing, share = dispatch(
        block[None],
        routes.reshape(tok_total, -1),
        route_gate.reshape(tok_total, -1),
        moe_input.reshape(tok_total, model_width),
        experts,
    )

    def to_block(x, shift):
        count = lax.axis_size("branch")
        return lax.ppermute(
            x, "branch", [(i, (i + shift * shard_branches) % count) for i in range(count)]
        )

    rows = [outgoing[:CAP]]
    for k in range(1, experts):
        rows.append(to_block(outgoing[k * CAP : (k + 1) * CAP], k))
    rows = jnp.concatenate(rows, axis=0)
    bits = [("branch", b) for b in reversed(range(shard_branches.bit_length() - 1))]
    bits += [("expert", b) for b in reversed(range(cores.bit_length() - 1))]
    for axis, bit in bits:
        rows = jnp.concatenate([rows, swapped(rows, axis, bit)], axis=0)
    gate_value = jnp.dot(rows, w_gate[0], preferred_element_type=jnp.float32)
    lifted = jnp.dot(rows, w_up[0], preferred_element_type=jnp.float32)
    hidden = (jax.nn.silu(gate_value) * lifted).astype(jnp.bfloat16)
    parts = jnp.dot(hidden, w_down[0], preferred_element_type=jnp.float32)
    for axis, bit in reversed(bits):
        count = parts.shape[0] // 2
        parts = parts[:count] + swapped(
            parts[count:].astype(jnp.bfloat16), axis, bit
        ).astype(jnp.float32)
    sums = [parts[:CAP]]
    for k in range(1, experts):
        sums.append(to_block(parts[k * CAP : (k + 1) * CAP], -k))
    sums = jnp.concatenate(sums, axis=0)
    combined = jnp.sum(share[:, :, None] * sums[None, :, :], axis=1)
    moe_out = combined.astype(jnp.bfloat16).reshape(tok_rows, step_count, model_width)
    return (attended, moe_out)


def solution(mesh):
    return jax.shard_map(
        on_device,
        mesh=mesh,
        in_specs=(
            P(("group", "branch"), "expert", None),
            P(("group", "branch"), "expert", None),
            P(("group", "branch", "expert"), None, None, None),
            P(("group", "branch", "expert"), None, None),
            P(("group", "branch", "expert"), None, None),
            P(("group", "branch", "expert"), None, None),
            P(("group", "branch", "expert")),
            P(("group", "branch", "expert"), None, None),
            P(("group", "branch", "expert"), None, None),
            P(("group", "branch", "expert"), None, None),
            P(("branch", "expert"), None, None),
            P(("branch", "expert"), None, None),
            P(("branch", "expert"), None, None),
        ),
        out_specs=(
            P(("group", "branch", "expert"), None, None, None),
            P(("group", "branch", "expert"), None, None),
        ),
        check_vma=False,
    )
```

time: 289 us -> 292 us (1.010)
  Pallas kernels: 0 us -> 160 us
  waiting for transfers between devices: 132 us -> 80.6 us
  matrix products: 48.9 us -> 5.21 us
  other arithmetic: 39 us -> 8.35 us
  local copies, waits for them, and re-layouts: 36.6 us -> 13.6 us
  starting transfers between devices: 30.6 us -> 21.8 us
    pallas_call x0 -> x9, Pallas kernels: none -> 160 us  [the longest x1 81.4 us: pack_queries(): pl.pallas_call(pack_queries_kernel, out_shape=(shape, shape), in_specs=[p...]
    ppermute x14 -> x15, waiting for transfers between devices: 132 us -> 29.4 us  [swapped(): lax.ppermute(x, axis, [(i, i ^ 1 << bit) for i in range(lax.axis_size(axi...]
    ppermute x0 -> x7, waiting for transfers between devices: none -> 51.2 us  [the longest x5 27.3 us: line_hop(): return lax.ppermute(x, 'branch', pairs)]
    dot_general x9 -> x2, matrix products: 48.9 us -> 5.21 us  [the longest x1 3.31 us: on_device(): parts = jnp.dot(hidden, w_down[0], preferred_element_type=jnp.float32)]
    reduce_sum x7 -> x2, other arithmetic: 15.4 us -> 1 us  [the longest x1 0.88 us: on_device(): combined = jnp.sum(share[:, :, None] * sums[None, :, :], axis=1)]
    ppermute x0 -> x7, starting transfers between devices: none -> 11.5 us  [the longest x5 7.83 us: line_hop(): return lax.ppermute(x, 'branch', pairs)]
    all_to_all x2 -> x0, starting transfers between devices: 11.3 us -> none  [the longest x1 6.5 us: on_device(): lax.all_to_all(copies, ('branch', 'expert'), split_axis=0, concat_axis=0,...]
    ppermute x14 -> x15, starting transfers between devices: 19.3 us -> 10.3 us  [swapped(): lax.ppermute(x, axis, [(i, i ^ 1 << bit) for i in range(lax.axis_size(axi...]
  transfers between devices with their start and end apart: 16 -> 22, of which waited for: 8 -> 7; matrix products, arithmetic and copies ran while one was open for 35% -> 8% of each run, Pallas kernels for 0% -> 39%
where the time goes in v1:
time: 292 us; the launch traced here: 291 us
  Pallas kernels  160 us (55%)
  waiting for transfers between devices  80.6 us (28%)
  starting transfers between devices  21.8 us (7%)
  local copies, waits for them, and re-layouts  13.6 us (5%)
  other arithmetic  8.35 us (3%)
  matrix products  5.21 us (2%)
    pallas_call x1, Pallas kernels, pack_queries(): pl.pallas_call(pack_queries_kernel, out_shape=(shape, shape), in_specs=[p...  81.4 us
    pallas_call x1, Pallas kernels, pack_cache(): pl.pallas_call(pack_cache_kernel, out_shape=jax.ShapeDtypeStruct((lat.sha...  36.9 us
    pallas_call x5, Pallas kernels, call(): pl.pallas_call(functools.partial(kernel, kinds, len(arrived), has_placed)...  30.6 us
    ppermute x15, waiting for transfers between devices, swapped(): lax.ppermute(x, axis, [(i, i ^ 1 << bit) for i in range(lax.axis_size(axi...  29.4 us
    ppermute x5, waiting for transfers between devices, line_hop(): return lax.ppermute(x, 'branch', pairs)  27.3 us
    ppermute x2, waiting for transfers between devices, to_block(): lax.ppermute(x, 'branch', [(i, (i + shift * shard_branches) % count) for...  23.9 us
    ppermute x15, starting transfers between devices, swapped(): lax.ppermute(x, axis, [(i, i ^ 1 << bit) for i in range(lax.axis_size(axi...  10.3 us
    pallas_call x1, Pallas kernels, place(): pl.pallas_call(place_kernel, out_shape=jax.ShapeDtypeStruct(placed.shape,...  9.68 us
  transfers between devices with their start and end apart: 22, of which 7 were waited for; matrix products, arithmetic and copies ran while one was open for 8% of the time, Pallas kernels for 39%

profile of v1, /device:TPU:0, one launch (start us, length us, event | category | flops | bytes accessed | tf_op | source)
XLA Modules:
  0.0 291.2 jit_solution(12133044025678967008)
XLA Ops:
  0.7 36.9 %pack_cache.1.refs_3_ = bf16[1152,512]{1,0:T(8,128)(2,1)} custom-call(bf16[1024,512]{1,0:T(8,128)(2,1)} %bitcast.32, bf16[128,512]{1,0:T(8,128)(2,1)} %bitcast.33), custom_call_target="tpu_custom_call" | custom-call | bytes 2097152 | tf_op jit(solution)/shard_map/pack_cache/pallas_call | solution.py:44
  38.1 2.7 collective-permute-start.1
  40.7 1.7 collective-permute-start.6
  42.4 0.8 reshape.151.tokens_ref
  43.2 1.9 dispatch.1
  45.1 0.9 fusion.18
  46.0 2.9 collective-permute-start.14
  49.0 23.9 %collective-permute-done.14 = bf16[2,7168]{1,0:T(2,128)(2,1)S(1)} collective-permute-done((bf16[2,7168]{1,0:T(2,128)(2,1)S(1)}, bf16[2,7168]{1,0:T(2,128)(2,1)S(1)}, u32[]{:S(2)}, u32[]{:S(2)}) %collective-permute-start.14) | collective-permute-done | bytes 28704 | tf_op jit(solution)/shard_map/ppermute | solution.py:453
  73.1 4.2 %collective-permute-done.15 = bf16[4,7168]{1,0:T(4,128)(2,1)S(1)} collective-permute-done((bf16[4,7168]{1,0:T(4,128)(2,1)S(1)}, bf16[4,7168]{1,0:T(4,128)(2,1)S(1)}, u32[]{:S(2)}, u32[]{:S(2)}) %collective-permute-start.15) | collective-permute-done | bytes 57376 | tf_op jit(solution)/shard_map/ppermute | solution.py:20
  77.4 1.6 collective-permute-start.16
  79.1 1.2 gather_fusion
  80.2 2.0 collective-permute-done.16
  82.5 1.1 gather_fusion.1
  83.6 0.9 reshape.147.rope_ref
  84.5 0.7 fusion.8.new_ref
  85.2 81.4 %pack_queries.1 = (bf16[4,320,512]{2,1,0:T(8,128)(2,1)}, bf16[4,320,512]{2,1,0:T(8,128)(2,1)}) custom-call(s32[4]{0:T(128)} %gather_fusion.1, s32[4]{0:T(128)} %gather_fusion, bf16[8,256,512]{2,1,0:T(8,128)(2,1)} %bitcast.31, bf16[8,32,512]{2,1,0:T(8,128)(2,1)} %reshape.147.rope_ref, bf16[8,32,512]{2,1,0:T(8,128)(2,1)} %fusion.8.new_ref), custom_call_target="tpu_custom_call" | custom-call | bytes 4194304 | tf_op jit(solution)/shard_map/pack_queries/pallas_call | solution.py:81
  166.6 1.6 collective-permute-start
  168.4 1.9 fusion.2
  170.4 3.3 %fusion = f32[32,7168]{1,0:T(8,128)} fusion(bf16[1,128,7168]{2,1,0:T(8,128)(2,1)S(1)} %copy-done, f32[32,128]{1,0:T(8,128)S(1)} %fusion.2, bf16[32,7168]{1,0:T(8,128)(2,1)S(1)} %concatenate.36, bf16[1,7168,128]{2,1,0:T(8,128)(2,1)} %param.23), kind=kOutput, calls=%fused_computation.2 | convolution fusion | flops 117465088 | bytes 5062656 | tf_op jit(solution)/shard_map/dot_general | solution.py:468
  173.7 1.1 slice.93
  175.7 0.7 fusion.20
  176.4 1.3 pad_add_fusion.2.refs_0_
  177.7 1.1 slice_add_fusion
  179.6 1.2 pad_add_fusion.1.refs_0_
  180.9 1.3 pad_add_fusion.refs_0_
  182.2 0.7 collective-permute-start.2
  182.9 17.6 %collective-permute-done.19 = bf16[8,7168]{1,0:T(8,128)(2,1)S(1)} collective-permute-done((bf16[8,7168]{1,0:T(8,128)(2,1)S(1)}, bf16[8,7168]{1,0:T(8,128)(2,1)S(1)}, u32[]{:S(2)}, u32[]{:S(2)}) %collective-permute-start.19) | collective-permute-done | bytes 114720 | tf_op jit(solution)/shard_map/ppermute | solution.py:20
  200.5 1.0 slice_add_fusion.1
  201.7 1.3 collective-permute-start.7
  203.0 1.3 copy-done.4
  204.3 7.9 %attend_give_keep.3 = (bf16[256,512]{1,0:T(8,128)(2,1)S(1)}, bf16[8,256,512]{2,1,0:T(8,128)(2,1)}) custom-call(s32[1]{0:T(128)} %get-tuple-element.28.refs_0_, bf16[4,320,512]{2,1,0:T(8,128)(2,1)} %collective-permute-done.refs_1_, bf16[4,320,512]{2,1,0:T(8,128)(2,1)S(1)} %copy-done.1, bf16[1152,512]{1,0:T(8,128)(2,1)S(1)} %copy-done.4, ...), custom_call_target="tpu_custom_call" | custom-call | flops 2415919104 | bytes 3670016 | tf_op jit(solution)/shard_map/attend_give_keep/pallas_call | solution.py:248
  212.2 1.6 collective-permute-start.11
  213.8 1.5 collective-permute-start.3
  215.3 5.6 %collective-permute-done.11.refs_5_ = bf16[256,512]{1,0:T(8,128)(2,1)S(1)} collective-permute-done((bf16[256,512]{1,0:T(8,128)(2,1)S(1)}, bf16[256,512]{1,0:T(8,128)(2,1)S(1)}, u32[]{:S(2)}, u32[]{:S(2)}) %collective-permute-start.11) | collective-permute-done | bytes 262176 | tf_op jit(solution)/shard_map/ppermute | solution.py:20
  221.0 7.4 %attend_give_keep.4 = (bf16[256,512]{1,0:T(8,128)(2,1)S(1)}, bf16[8,256,512]{2,1,0:T(8,128)(2,1)}) custom-call(s32[2]{0:T(128)S(1)} %pad_add_fusion.2.refs_0_, bf16[4,320,512]{2,1,0:T(8,128)(2,1)} %collective-permute-done.refs_1_, bf16[4,320,512]{2,1,0:T(8,128)(2,1)S(1)} %copy-done.1, ...), custom_call_target="tpu_custom_call", output_to_operand_aliasing={{1}: (6, {})} | custom-call | flops 2415919104 | bytes 3670016 | tf_op jit(solution)/shard_map/attend_give_keep/pallas_call | solution.py:248
  228.3 1.6 collective-permute-start.12
  229.9 2.7 collective-permute-done.7
  232.8 24.6 %collective-permute-done.3 = bf16[1152,512]{1,0:T(8,128)(2,1)S(1)} collective-permute-done((bf16[1152,512]{1,0:T(8,128)(2,1)S(1)}, bf16[1152,512]{1,0:T(8,128)(2,1)S(1)}, u32[]{:S(2)}, u32[]{:S(2)}) %collective-permute-start.3) | collective-permute-done | bytes 1179680 | tf_op jit(solution)/shard_map/ppermute | solution.py:28
  257.7 0.8 collective-permute-start.21
  258.5 6.5 %attend_give_keep.5 = (bf16[256,512]{1,0:T(8,128)(2,1)S(1)}, bf16[8,256,512]{2,1,0:T(8,128)(2,1)}) custom-call(s32[2]{0:T(128)S(1)} %pad_add_fusion.1.refs_0_, bf16[4,320,512]{2,1,0:T(8,128)(2,1)} %collective-permute-done.refs_1_, bf16[4,320,512]{2,1,0:T(8,128)(2,1)S(1)} %copy-done.2, ...), custom_call_target="tpu_custom_call", output_to_operand_aliasing={{1}: (6, {})} | custom-call | flops 2415919104 | bytes 3670016 | tf_op jit(solution)/shard_map/attend_give_keep/pallas_call | solution.py:248
  265.0 1.6 collective-permute-start.13
  266.6 4.7 %attend_give.1 = bf16[256,512]{1,0:T(8,128)(2,1)} custom-call(s32[2]{0:T(128)S(1)} %pad_add_fusion.refs_0_, bf16[4,320,512]{2,1,0:T(8,128)(2,1)} %collective-permute-done.refs_1_, bf16[1152,512]{1,0:T(8,128)(2,1)S(1)} %broadcast_select_fusion.1.refs_2_, bf16[1152,512]{1,0:T(8,128)(2,1)S(1)} %collective-permute-done.4.refs_3_), custom_call_target="tpu_custom_call" | custom-call | flops 1207959552 | bytes 3145728 | tf_op jit(solution)/shard_map/attend_give/pallas_call | solution.py:248
  272.0 0.9 multiply_reduce_fusion
  272.9 1.7 convert_element_type.31
  274.6 1.3 copy-done.3
  275.9 1.3 copy-done.6
  277.2 4.1 %attend_keep.1.before = bf16[8,256,512]{2,1,0:T(8,128)(2,1)} custom-call(s32[2]{0:T(128)S(1)} %pad_add_fusion.refs_0_, bf16[4,320,512]{2,1,0:T(8,128)(2,1)S(1)} %copy-done.3, bf16[1152,512]{1,0:T(8,128)(2,1)S(1)} %broadcast_select_fusion.1.refs_2_, bf16[1152,512]{1,0:T(8,128)(2,1)S(1)} %copy-done.6, ...), custom_call_target="tpu_custom_call", output_to_operand_aliasing={{}: (5, {})} | custom-call | flops 1207959552 | bytes 3145728 | tf_op jit(solution)/shard_map/attend_keep/pallas_call | solution.py:248
  281.3 9.7 %place.1 = bf16[8,256,512]{2,1,0:T(8,128)(2,1)} custom-call(s32[1]{0:T(128)} %get-tuple-element.35.index, bf16[256,512]{1,0:T(8,128)(2,1)} %collective-permute-done.5.source, bf16[8,256,512]{2,1,0:T(8,128)(2,1)} %attend_keep.1.before), custom_call_target="tpu_custom_call", output_to_operand_aliasing={{}: (2, {})} | custom-call | tf_op jit(solution)/shard_map/place/pallas_call | solution.py:281
  (72 shorter events, 4.6 us)
Async XLA Ops:
  0.6 169.7 %copy-start = (bf16[1,128,7168]{2,1,0:T(8,128)(2,1)S(1)}, bf16[1,128,7168]{2,1,0:T(8,128)(2,1)}, u32[]{:S(2)}) copy-start(bf16[1,128,7168]{2,1,0:T(8,128)(2,1)} %param.25) | copy-start | bytes 5505028
  0.6 41.8 %copy-start.9 = (bf16[8,2,7168]{2,1,0:T(2,128)(2,1)S(1)}, bf16[8,2,7168]{2,1,0:T(2,128)(2,1)}, u32[]{:S(2)}) copy-start(bf16[8,2,7168]{2,1,0:T(2,128)(2,1)} %param.20) | copy-start | bytes 688132
  0.7 78.3 %copy-start.15 = (s32[8]{0:T(128)S(1)}, s32[8]{0:T(128)}, u32[]{:S(2)}) copy-start(s32[8]{0:T(128)} %param.19) | copy-start | bytes 100
  37.5 46.1 %copy-start.8 = (bf16[8,2,8192]{2,1,0:T(2,128)(2,1)S(1)}, bf16[8,2,8192]{2,1,0:T(2,128)(2,1)}, u32[]{:S(2)}) copy-start(bf16[8,2,8192]{2,1,0:T(2,128)(2,1)} %param.16) | copy-start | bytes 786436
  37.5 46.9 %copy-start.12 = (bf16[8,2,512]{2,1,0:T(2,128)(2,1)S(1)}, bf16[8,2,512]{2,1,0:T(2,128)(2,1)}, u32[]{:S(2)}) copy-start(bf16[8,2,512]{2,1,0:T(2,128)(2,1)} %param.17) | copy-start | bytes 49156
  37.6 46.9 %copy-start.14 = (bf16[8,2,64]{2,1,0:T(2,128)(2,1)S(1)}, bf16[8,2,64]{2,1,0:T(2,128)(2,1)}, u32[]{:S(2)}) copy-start(bf16[8,2,64]{2,1,0:T(2,128)(2,1)} %param.18) | copy-start | bytes 6148
  37.6 164.0 %collective-permute-start.10 = (bf16[1152,512]{1,0:T(8,128)(2,1)}, bf16[1152,512]{1,0:T(8,128)(2,1)}, u32[]{:S(2)}, u32[]{:S(2)}) collective-permute-start(bf16[1152,512]{1,0:T(8,128)(2,1)} %pack_cache.1.refs_3_), channel_id=1, source_target_pairs={{0,1},{1,0},{2,3},{3,2},{4,5},{5,4},{6,7},{7,6},{8,9},{9,8},{10,11... | collective-permute-start | bytes 3538952 | tf_op jit(solution)/shard_map/ppermute | solution.py:20
  38.1 144.1 %collective-permute-start.1 = (bf16[1152,512]{1,0:T(8,128)(2,1)}, bf16[1152,512]{1,0:T(8,128)(2,1)}, u32[]{:S(2)}, u32[]{:S(2)}) collective-permute-start(bf16[1152,512]{1,0:T(8,128)(2,1)} %pack_cache.1.refs_3_), channel_id=1, source_target_pairs={{0,4},{4,0},{8,12},{12,8},{2,6},{6,2},{10,14},{14,10},{1,5},{5,1},... | collective-permute-start | bytes 3538952 | tf_op jit(solution)/shard_map/ppermute | solution.py:28
  40.7 161.0 %collective-permute-start.6 = (bf16[1152,512]{1,0:T(8,128)(2,1)}, bf16[1152,512]{1,0:T(8,128)(2,1)}, u32[]{:S(2)}, u32[]{:S(2)}) collective-permute-start(bf16[1152,512]{1,0:T(8,128)(2,1)} %pack_cache.1.refs_3_), channel_id=1, source_target_pairs={{4,8},{8,4},{6,10},{10,6},{5,9},{9,5},{7,11},{11,7},{20,24},{24,20... | collective-permute-start | bytes 3538952 | tf_op jit(solution)/shard_map/ppermute | solution.py:28
  46.0 26.9 %collective-permute-start.14 = (bf16[2,7168]{1,0:T(2,128)(2,1)S(1)}, bf16[2,7168]{1,0:T(2,128)(2,1)S(1)}, u32[]{:S(2)}, u32[]{:S(2)}) collective-permute-start(bf16[2,7168]{1,0:T(2,128)(2,1)S(1)} %get-tuple-element.26), channel_id=1, source_target_pairs={{0,8},{2,10},{4,12},{6,14},{8,0},{10,2},{12,4},{14,6},{1,9},{3,11}... | collective-permute-start | bytes 86024 | tf_op jit(solution)/shard_map/ppermute | solution.py:453
  73.0 4.2 %collective-permute-start.15 = (bf16[4,7168]{1,0:T(4,128)(2,1)S(1)}, bf16[4,7168]{1,0:T(4,128)(2,1)S(1)}, u32[]{:S(2)}, u32[]{:S(2)}) collective-permute-start(bf16[4,7168]{1,0:T(4,128)(2,1)S(1)} %pad_maximum_fusion.3), channel_id=1, source_target_pairs={{0,4},{2,6},{4,0},{6,2},{8,12},{10,14},{12,8},{14,10},{1,5},{3,7},... | collective-permute-start | bytes 172040 | tf_op jit(solution)/shard_map/ppermute | solution.py:20
  77.4 4.9 %collective-permute-start.16 = (bf16[8,7168]{1,0:T(8,128)(2,1)S(1)}, bf16[8,7168]{1,0:T(8,128)(2,1)S(1)}, u32[]{:S(2)}, u32[]{:S(2)}) collective-permute-start(bf16[8,7168]{1,0:T(8,128)(2,1)S(1)} %pad_maximum_fusion.1), channel_id=1, source_target_pairs={{0,2},{2,0},{4,6},{6,4},{8,10},{10,8},{12,14},{14,12},{1,3},{3,1},... | collective-permute-start | bytes 344072 | tf_op jit(solution)/shard_map/ppermute | solution.py:20
  82.4 85.8 %collective-permute-start.17 = (bf16[16,7168]{1,0:T(8,128)(2,1)S(1)}, bf16[16,7168]{1,0:T(8,128)(2,1)S(1)}, u32[]{:S(2)}, u32[]{:S(2)}) collective-permute-start(bf16[16,7168]{1,0:T(8,128)(2,1)S(1)} %pad_maximum_fusion), channel_id=1, source_target_pairs={{0,1},{1,0},{2,3},{3,2},{4,5},{5,4},{6,7},{7,6},{8,9},{9,8},{10,11... | collective-permute-start | bytes 688136 | tf_op jit(solution)/shard_map/ppermute | solution.py:20
  166.6 36.4 %collective-permute-start = (bf16[4,320,512]{2,1,0:T(8,128)(2,1)}, bf16[4,320,512]{2,1,0:T(8,128)(2,1)}, u32[]{:S(2)}, u32[]{:S(2)}) collective-permute-start(bf16[4,320,512]{2,1,0:T(8,128)(2,1)} %get-tuple-element.12), channel_id=1, source_target_pairs={{0,2},{2,0},{4,6},{6,4},{8,10},{10,8},{12,14},{14,12},{1,3},{3,1},... | collective-permute-start | bytes 3932168 | tf_op jit(solution)/shard_map/ppermute | solution.py:20
  170.4 4.8 %copy-start.11 = (s32[4]{0:T(128)S(1)}, s32[4]{0:T(128)}, u32[]{:S(2)}) copy-start(s32[4]{0:T(128)} %gather_fusion.1) | copy-start | bytes 52
  170.4 5.4 %copy-start.10 = (s32[4]{0:T(128)S(1)}, s32[4]{0:T(128)}, u32[]{:S(2)}) copy-start(s32[4]{0:T(128)} %gather_fusion) | copy-start | bytes 52
  173.7 7.1 %copy-start.13 = (f32[16,4]{1,0:T(8,128)S(1)}, f32[16,4]{1,0:T(8,128)}, u32[]{:S(2)}) copy-start(f32[16,4]{1,0:T(8,128)} %get-tuple-element.20) | copy-start | bytes 772
  173.7 29.3 %copy-start.1 = (bf16[4,320,512]{2,1,0:T(8,128)(2,1)S(1)}, bf16[4,320,512]{2,1,0:T(8,128)(2,1)}, u32[]{:S(2)}) copy-start(bf16[4,320,512]{2,1,0:T(8,128)(2,1)} %get-tuple-element.13.refs_2_.refs_1_) | copy-start | bytes 3932164
  174.8 2.8 collective-permute-start.18
  178.7 0.8 copy-start.7
  178.8 21.8 %collective-permute-start.19 = (bf16[8,7168]{1,0:T(8,128)(2,1)S(1)}, bf16[8,7168]{1,0:T(8,128)(2,1)S(1)}, u32[]{:S(2)}, u32[]{:S(2)}) collective-permute-start(bf16[8,7168]{1,0:T(8,128)(2,1)S(1)} %slice.94), channel_id=1, source_target_pairs={{0,2},{2,0},{4,6},{6,4},{8,10},{10,8},{12,14},{14,12},{1,3},{3,1},... | collective-permute-start | bytes 344072 | tf_op jit(solution)/shard_map/ppermute | solution.py:20
  182.2 31.6 %collective-permute-start.2 = (bf16[1152,512]{1,0:T(8,128)(2,1)}, bf16[1152,512]{1,0:T(8,128)(2,1)S(1)}, u32[]{:S(2)}, u32[]{:S(2)}) collective-permute-start(bf16[1152,512]{1,0:T(8,128)(2,1)} %collective-permute-done.1.refs_3_), channel_id=1, source_target_pairs={{4,8},{8,4},{6,10},{10,6},{5,9},{9,5},{7,11},{11,7},{20,24},{24,20... | collective-permute-start | bytes 3538952 | tf_op jit(solution)/shard_map/ppermute | solution.py:28
  201.5 13.7 %collective-permute-start.20 = (bf16[4,7168]{1,0:T(4,128)(2,1)S(1)}, bf16[4,7168]{1,0:T(4,128)(2,1)S(1)}, u32[]{:S(2)}, u32[]{:S(2)}) collective-permute-start(bf16[4,7168]{1,0:T(4,128)(2,1)S(1)} %slice.95), channel_id=1, source_target_pairs={{0,4},{2,6},{4,0},{6,2},{8,12},{10,14},{12,8},{14,10},{1,5},{3,7},... | collective-permute-start | bytes 172040 | tf_op jit(solution)/shard_map/ppermute | solution.py:20
  201.6 19.3 %collective-permute-start.9 = (bf16[1152,512]{1,0:T(8,128)(2,1)}, bf16[1152,512]{1,0:T(8,128)(2,1)S(1)}, u32[]{:S(2)}, u32[]{:S(2)}) collective-permute-start(bf16[1152,512]{1,0:T(8,128)(2,1)} %collective-permute-done.1.refs_3_), channel_id=1, source_target_pairs={{0,1},{1,0},{2,3},{3,2},{4,5},{5,4},{6,7},{7,6},{8,9},{9,8},{10,11... | collective-permute-start | bytes 3538952 | tf_op jit(solution)/shard_map/ppermute | solution.py:20
  201.7 30.9 %collective-permute-start.7 = (bf16[1152,512]{1,0:T(8,128)(2,1)}, bf16[1152,512]{1,0:T(8,128)(2,1)S(1)}, u32[]{:S(2)}, u32[]{:S(2)}) collective-permute-start(bf16[1152,512]{1,0:T(8,128)(2,1)} %collective-permute-done.6), channel_id=1, source_target_pairs={{4,0},{8,12},{6,2},{10,14},{5,1},{9,13},{7,3},{11,15},{20,16},{24,... | collective-permute-start | bytes 3538952 | tf_op jit(solution)/shard_map/ppermute | solution.py:28
  203.0 1.3 copy-start.4
  212.2 8.8 %collective-permute-start.11 = (bf16[256,512]{1,0:T(8,128)(2,1)S(1)}, bf16[256,512]{1,0:T(8,128)(2,1)S(1)}, u32[]{:S(2)}, u32[]{:S(2)}) collective-permute-start(bf16[256,512]{1,0:T(8,128)(2,1)S(1)} %get-tuple-element.14), channel_id=1, source_target_pairs={{0,2},{2,0},{4,6},{6,4},{8,10},{10,8},{12,14},{14,12},{1,3},{3,1},... | collective-permute-start | bytes 786440 | tf_op jit(solution)/shard_map/ppermute | solution.py:20
  213.8 43.6 %collective-permute-start.3 = (bf16[1152,512]{1,0:T(8,128)(2,1)S(1)}, bf16[1152,512]{1,0:T(8,128)(2,1)S(1)}, u32[]{:S(2)}, u32[]{:S(2)}) collective-permute-start(bf16[1152,512]{1,0:T(8,128)(2,1)S(1)} %collective-permute-done.2), channel_id=1, source_target_pairs={{4,0},{8,12},{6,2},{10,14},{5,1},{9,13},{7,3},{11,15},{20,16},{24,... | collective-permute-start | bytes 3538952 | tf_op jit(solution)/shard_map/ppermute | solution.py:28
  228.3 30.2 %collective-permute-start.12 = (bf16[256,512]{1,0:T(8,128)(2,1)S(1)}, bf16[256,512]{1,0:T(8,128)(2,1)S(1)}, u32[]{:S(2)}, u32[]{:S(2)}) collective-permute-start(bf16[256,512]{1,0:T(8,128)(2,1)S(1)} %get-tuple-element.16), channel_id=1, source_target_pairs={{0,2},{2,0},{4,6},{6,4},{8,10},{10,8},{12,14},{14,12},{1,3},{3,1},... | collective-permute-start | bytes 786440 | tf_op jit(solution)/shard_map/ppermute | solution.py:20
  232.7 25.8 %copy-start.2 = (bf16[4,320,512]{2,1,0:T(8,128)(2,1)S(1)}, bf16[4,320,512]{2,1,0:T(8,128)(2,1)}, u32[]{:S(2)}) copy-start(bf16[4,320,512]{2,1,0:T(8,128)(2,1)} %get-tuple-element.13.refs_2_.refs_1_) | copy-start | bytes 3932164
  232.7 25.8 %collective-permute-start.8 = (bf16[1152,512]{1,0:T(8,128)(2,1)S(1)}, bf16[1152,512]{1,0:T(8,128)(2,1)S(1)}, u32[]{:S(2)}, u32[]{:S(2)}) collective-permute-start(bf16[1152,512]{1,0:T(8,128)(2,1)S(1)} %broadcast_select_fusion.refs_3_), channel_id=1, source_target_pairs={{0,1},{1,0},{2,3},{3,2},{4,5},{5,4},{6,7},{7,6},{8,9},{9,8},{10,11... | collective-permute-start | bytes 3538952 | tf_op jit(solution)/shard_map/ppermute | solution.py:20
  257.6 9.1 %collective-permute-start.4 = (bf16[1152,512]{1,0:T(8,128)(2,1)S(1)}, bf16[1152,512]{1,0:T(8,128)(2,1)S(1)}, u32[]{:S(2)}, u32[]{:S(2)}) collective-permute-start(bf16[1152,512]{1,0:T(8,128)(2,1)S(1)} %broadcast_select_fusion.1.refs_2_), channel_id=1, source_target_pairs={{0,1},{1,0},{2,3},{3,2},{4,5},{5,4},{6,7},{7,6},{8,9},{9,8},{10,11... | collective-permute-start | bytes 3538952 | tf_op jit(solution)/shard_map/ppermute | solution.py:20
  257.7 14.3 %collective-permute-start.21 = (f32[2,7168]{1,0:T(2,128)S(1)}, f32[2,7168]{1,0:T(2,128)S(1)}, u32[]{:S(2)}, u32[]{:S(2)}) collective-permute-start(f32[2,7168]{1,0:T(2,128)S(1)} %get-tuple-element.25), channel_id=1, source_target_pairs={{0,8},{2,10},{4,12},{6,14},{8,0},{10,2},{12,4},{14,6},{1,9},{3,11}... | collective-permute-start | bytes 172040 | tf_op jit(solution)/shard_map/ppermute | solution.py:453
  265.0 9.6 %collective-permute-start.13 = (bf16[256,512]{1,0:T(8,128)(2,1)S(1)}, bf16[256,512]{1,0:T(8,128)(2,1)S(1)}, u32[]{:S(2)}, u32[]{:S(2)}) collective-permute-start(bf16[256,512]{1,0:T(8,128)(2,1)S(1)} %get-tuple-element.18), channel_id=1, source_target_pairs={{0,2},{2,0},{4,6},{6,4},{8,10},{10,8},{12,14},{14,12},{1,3},{3,1},... | collective-permute-start | bytes 786440 | tf_op jit(solution)/shard_map/ppermute | solution.py:20
  266.6 4.8 %copy-start.5 = (bf16[1152,512]{1,0:T(8,128)(2,1)}, bf16[1152,512]{1,0:T(8,128)(2,1)S(1)}, u32[]{:S(2)}) copy-start(bf16[1152,512]{1,0:T(8,128)(2,1)S(1)} %collective-permute-done.4.refs_3_) | copy-start | bytes 3538948
  271.4 9.9 %collective-permute-start.5 = (bf16[256,512]{1,0:T(8,128)(2,1)}, bf16[256,512]{1,0:T(8,128)(2,1)}, u32[]{:S(2)}, u32[]{:S(2)}) collective-permute-start(bf16[256,512]{1,0:T(8,128)(2,1)} %attend_give.1), channel_id=1, source_target_pairs={{0,2},{2,0},{4,6},{6,4},{8,10},{10,8},{12,14},{14,12},{1,3},{3,1},... | collective-permute-start | bytes 786440 | tf_op jit(solution)/shard_map/ppermute | solution.py:20
  274.6 1.3 copy-start.3
  275.9 1.3 copy-start.6

commit v2 on v1

--- a/solution.py
+++ b/solution.py
@@ -28,66 +28,76 @@
     return lax.ppermute(x, "branch", pairs)
 
 
-def pack_cache_kernel(lat_ref, rope_ref, out_ref, sems):
+def pack_cache_kernel(lat_ref, rope_ref, out_ref):
     rows = lat_ref.shape[0]
-    first = pltpu.make_async_copy(lat_ref, out_ref.at[pl.ds(0, rows)], sems.at[0])
-    second = pltpu.make_async_copy(
-        rope_ref, out_ref.at[pl.ds(rows, rope_ref.shape[0])], sems.at[1]
-    )
-    first.start()
-    second.start()
-    first.wait()
-    second.wait()
+    out_ref[0:rows, :] = lat_ref[...]
+    out_ref[rows:, :] = rope_ref[...]
 
 
 def pack_cache(lat, rope):
     return pl.pallas_call(
         pack_cache_kernel,
         out_shape=jax.ShapeDtypeStruct((lat.shape[0] + rope.shape[0], lat.shape[1]), lat.dtype),
-        in_specs=[pl.BlockSpec(memory_space=pl.ANY)] * 2,
-        out_specs=pl.BlockSpec(memory_space=pl.ANY),
-        scratch_shapes=[pltpu.SemaphoreType.DMA((2,))],
+        in_specs=[pl.BlockSpec(memory_space=pltpu.VMEM)] * 2,
+        out_specs=pl.BlockSpec(memory_space=pltpu.VMEM),
         cost_estimate=pl.CostEstimate(flops=0, bytes_accessed=2 * 2 * lat.size, transcendentals=0),
+        compiler_params=pltpu.CompilerParams(vmem_limit_bytes=16 * 1024 * 1024),
         name="pack_cache",
     )(lat, rope)
 
 
-def pack_queries_kernel(stay_row, leave_row, q_ref, rope_ref, new_ref, stay_ref, leave_ref, sems):
-    slots = stay_ref.shape[0]
-    copies = []
-    for out, rows, group in ((leave_ref, leave_row, 0), (stay_ref, stay_row, 1)):
-        for slot in range(slots):
-            start = 0
-            for part, source in enumerate((q_ref, rope_ref, new_ref)):
-                count = source.shape[1]
-                copies.append(
-                    pltpu.make_async_copy(
-                        source.at[rows[slot]],
-                        out.at[slot, pl.ds(start, count)],
-                        sems.at[group, slot, part],
-                    )
-                )
-                start += count
-    for copy in copies:
-        copy.start()
-    for copy in copies:
-        copy.wait()
-
-
-def pack_queries(stay_row, leave_row, q_lat, q_rope, new):
-    slots = stay_row.shape[0]
-    rows = q_lat.shape[1] + q_rope.shape[1] + new.shape[1]
-    shape = jax.ShapeDtypeStruct((slots, rows, q_lat.shape[2]), q_lat.dtype)
+def row_for(slot, parity, slot_ref, own_ref):
+    count = slot_ref.shape[0]
+    line = count // 2
+    own = own_ref[0]
+    high = lax.div(own, 2)
+    low = lax.rem(own, 2)
+    mine = high
+    pair = high + 1 - 2 * lax.rem(high, 2)
+    first_half = high < line // 2
+    nearer = jnp.where(first_half, line // 2, line // 2 - 1)
+    farther = jnp.where(first_half, line - 1, 0)
+    position = mine
+    for number, place_there in ((1, pair), (2, nearer), (3, farther)):
+        position = jnp.where(slot == number, place_there, position)
+    wanted = 2 * position + (low if parity == 0 else 1 - low)
+    row = jnp.int32(0)
+    for r in range(1, count):
+        row = row + jnp.where(slot_ref[r] == wanted, r, 0)
+    return row
+
+
+def pack_leaving_kernel(slot_ref, own_ref, q_ref, rope_ref, new_ref, out_ref):
+    start = 0
+    for source in (q_ref, rope_ref, new_ref):
+        count = source.shape[1]
+        out_ref[0, start : start + count, :] = source[0]
+        start += count
+
+
+def pack_leaving(branch_slot, own, q_lat, q_rope, new):
+    slots = branch_slot.shape[0] // 2
+    sources = (q_lat, q_rope, new)
+    rows = sum(x.shape[1] for x in sources)
+    width = q_lat.shape[2]
+
+    def chosen(i, slot_ref, own_ref):
+        return (row_for(i, 1, slot_ref, own_ref), 0, 0)
+
     return pl.pallas_call(
-        pack_queries_kernel,
-        out_shape=(shape, shape),
-        in_specs=[pl.BlockSpec(memory_space=pltpu.SMEM)] * 2
-        + [pl.BlockSpec(memory_space=pl.ANY)] * 3,
-        out_specs=(pl.BlockSpec(memory_space=pl.ANY),) * 2,
-        scratch_shapes=[pltpu.SemaphoreType.DMA((2, slots, 3))],
-        cost_estimate=pl.CostEstimate(flops=0, bytes_accessed=4 * q_lat.size, transcendentals=0),
-        name="pack_queries",
-    )(stay_row, leave_row, q_lat, q_rope, new)
+        pack_leaving_kernel,
+        out_shape=jax.ShapeDtypeStruct((slots, rows, width), q_lat.dtype),
+        grid_spec=pltpu.PrefetchScalarGridSpec(
+            num_scalar_prefetch=2,
+            grid=(slots,),
+            in_specs=[pl.BlockSpec((1, x.shape[1], width), chosen) for x in sources],
+            out_specs=pl.BlockSpec((1, rows, width), lambda i, *_: (i, 0, 0)),
+        ),
+        cost_estimate=pl.CostEstimate(
+            flops=0, bytes_accessed=4 * slots * rows * width, transcendentals=0
+        ),
+        name="pack_leaving",
+    )(branch_slot, own, *sources)
 
 
 def spread_matrix(raw_rows, width):
@@ -115,12 +125,11 @@
     q_rows = heads * steps
     token_rope = q_rows // 8
 
-    def one_token(q_ref, keys):
-        lat = q_ref[0:q_rows, :]
+    def one_token(lat, raw_rope, fresh_all, keys):
         matrix = spread_matrix(raw_group, width)
         pieces = []
         for start in range(0, token_rope, raw_group):
-            part = spread(matrix, q_ref[q_rows + start : q_rows + start + raw_group, :])
+            part = spread(matrix, raw_rope[start : start + raw_group, :])
             pieces.append(part + pltpu.roll(part, LANES // 2, 1))
         rope = pieces[0] if len(pieces) == 1 else jnp.concatenate(pieces, axis=0)
         rope = rope.astype(jnp.bfloat16)
@@ -128,9 +137,8 @@
         contract = (((1,), (1,)), ((), ()))
         scores = lax.dot_general(query, keys[...], contract, preferred_element_type=jnp.float32)
         peak = jnp.max(scores, axis=1, keepdims=True)
-        base = q_rows + token_rope
-        fresh = q_ref[base : base + PAD, :]
-        fresh_rope = q_ref[base + PAD : base + 2 * PAD, 0:LANES]
+        fresh = fresh_all[0:PAD, :]
+        fresh_rope = fresh_all[PAD : 2 * PAD, 0:LANES]
         own = lax.dot_general(lat, fresh, contract, preferred_element_type=jnp.float32)
         own = own + lax.dot_general(rope, fresh_rope, contract, preferred_element_type=jnp.float32)
         factor = softmax_scale * log2e
@@ -179,16 +187,21 @@
                 first = i * half + start * (width // (LANES // 2))
                 keys[first : first + grown, width : width + LANES] = part.astype(jnp.bfloat16)
 
-    def kernel(kinds, n_arrived, has_placed, *refs):
+    def kernel(slot, kinds, given_slots, has_placed, *refs):
         refs = list(refs)
-        index = refs.pop(0)
-        queries = [refs.pop(0) for _ in kinds]
+        slot_ref, own_ref = refs.pop(0), refs.pop(0)
+        queries = []
+        for kind in kinds:
+            if kind == "give":
+                queries.append(refs.pop(0))
+            else:
+                queries.append([refs.pop(0) for _ in range(3)])
         caches = [refs.pop(0) for _ in range(2)]
-        arrived = [refs.pop(0) for _ in range(n_arrived)]
+        arrived = [refs.pop(0) for _ in given_slots]
         if has_placed:
             refs.pop(0)
         gives = [refs.pop(0) for kind in kinds if kind == "give"]
-        placed = refs.pop(0) if ("keep" in kinds or n_arrived) else None
+        placed = refs.pop(0) if ("keep" in kinds or given_slots) else None
         keys, rope_scratch, result, sems, place_sems = refs
         copies = load_keys(caches, keys, sems)
         rope_copies = []
@@ -199,8 +212,10 @@
             copy.start()
             rope_copies.append(copy)
         placing = []
-        for i, source in enumerate(arrived):
-            copy = pltpu.make_async_copy(source, placed.at[index[1 + i]], place_sems.at[1 + i])
+        for i, (number, source) in enumerate(zip(given_slots, arrived)):
+            copy = pltpu.make_async_copy(
+                source, placed.at[row_for(number, 1, slot_ref, own_ref)], place_sems.at[1 + i]
+            )
             copy.start()
             placing.append(copy)
         for copy in rope_copies:
@@ -209,55 +224,79 @@
         for copy in copies:
             copy.wait()
         for kind, query in zip(kinds, queries):
-            value = one_token(query.at[0], keys)
             if kind == "give":
+                packed = query.at[0]
+                middle = q_rows + token_rope
+                value = one_token(
+                    packed[0:q_rows, :],
+                    packed[q_rows:middle, :],
+                    packed[middle : middle + 2 * PAD, :],
+                    keys,
+                )
                 gives.pop(0)[...] = value
             else:
+                value = one_token(query[0][0], query[1][0], query[2][0], keys)
                 result[...] = value
-                copy = pltpu.make_async_copy(result, placed.at[index[0]], place_sems.at[0])
+                copy = pltpu.make_async_copy(
+                    result, placed.at[row_for(slot, 0, slot_ref, own_ref)], place_sems.at[0]
+                )
                 copy.start()
                 placing.append(copy)
         for copy in placing:
             copy.wait()
 
-    def call(index, kinds, slot, packed, caches, arrived, placed, count):
+    def call(scalars, kinds, slot, guest, stay, caches, arrived, placed):
+        count = scalars[0].shape[0]
         n_tok = len(kinds)
-        rows = packed[0].shape[1]
         any_spec = pl.BlockSpec(memory_space=pl.ANY)
-        in_specs = [pl.BlockSpec(memory_space=pltpu.SMEM)]
-        in_specs += [
-            pl.BlockSpec((1, rows, width), lambda i: (slot, 0, 0)) for _ in range(n_tok)
-        ]
+
+        def chosen(i, slot_ref, own_ref):
+            return (row_for(slot, 0, slot_ref, own_ref), 0, 0)
+
+        in_specs, operands = [], []
+        for kind in kinds:
+            if kind == "give":
+                in_specs.append(
+                    pl.BlockSpec((1, guest.shape[1], width), lambda i, *_: (slot, 0, 0))
+                )
+                operands.append(guest)
+            else:
+                in_specs += [pl.BlockSpec((1, x.shape[1], width), chosen) for x in stay]
+                operands += stay
+        given_slots = tuple(number for number, _ in arrived)
         in_specs += [any_spec] * (2 + len(arrived))
-        operands = [index, *packed, *caches, *arrived]
+        operands += [*caches, *(value for _, value in arrived)]
         has_placed = placed is not None
         out_shape, out_specs, alias = [], [], {}
         for kind in kinds:
             if kind == "give":
                 out_shape.append(jax.ShapeDtypeStruct((q_rows, width), jnp.bfloat16))
-                out_specs.append(pl.BlockSpec((q_rows, width), lambda i: (0, 0)))
+                out_specs.append(pl.BlockSpec((q_rows, width), lambda i, *_: (0, 0)))
         if "keep" in kinds or arrived:
             out_shape.append(jax.ShapeDtypeStruct((count, q_rows, width), jnp.bfloat16))
             out_specs.append(any_spec)
             if has_placed:
-                alias = {len(operands): len(out_shape) - 1}
+                alias = {2 + len(operands): len(out_shape) - 1}
         if has_placed:
             in_specs.append(any_spec)
             operands.append(placed)
         all_rows = 2 * half
         return pl.pallas_call(
-            functools.partial(kernel, kinds, len(arrived), has_placed),
-            grid=(1,),
+            functools.partial(kernel, slot, kinds, given_slots, has_placed),
             out_shape=tuple(out_shape),
-            in_specs=in_specs,
-            out_specs=tuple(out_specs),
-            scratch_shapes=[
-                pltpu.VMEM((all_rows, width + LANES), jnp.bfloat16),
-                pltpu.VMEM((2, rope_rows, width), jnp.bfloat16),
-                pltpu.VMEM((q_rows, width), jnp.bfloat16),
-                pltpu.SemaphoreType.DMA((4,)),
-                pltpu.SemaphoreType.DMA((1 + max(1, len(arrived)),)),
-            ],
+            grid_spec=pltpu.PrefetchScalarGridSpec(
+                num_scalar_prefetch=2,
+                grid=(1,),
+                in_specs=in_specs,
+                out_specs=tuple(out_specs),
+                scratch_shapes=[
+                    pltpu.VMEM((all_rows, width + LANES), jnp.bfloat16),
+                    pltpu.VMEM((2, rope_rows, width), jnp.bfloat16),
+                    pltpu.VMEM((q_rows, width), jnp.bfloat16),
+                    pltpu.SemaphoreType.DMA((4,)),
+                    pltpu.SemaphoreType.DMA((1 + max(1, len(arrived)),)),
+                ],
+            ),
             input_output_aliases=alias,
             cost_estimate=pl.CostEstimate(
                 flops=2 * n_tok * q_rows * all_rows * (2 * width + LANES),
@@ -266,28 +305,34 @@
             ),
             compiler_params=pltpu.CompilerParams(vmem_limit_bytes=32 * 1024 * 1024),
             name="attend_" + "_".join(kinds),
-        )(*operands)
+        )(*scalars, *operands)
 
     return call
 
 
-def place_kernel(index, source, before, placed, sem):
-    copy = pltpu.make_async_copy(source, placed.at[index[0]], sem)
-    copy.start()
-    copy.wait()
-
-
-def place(index, source, placed):
+def place_kernel(slot_ref, own_ref, source_ref, before, placed_ref):
+    placed_ref[0] = source_ref[...]
+
+
+def place(scalars, slot, source, placed):
+    def chosen(i, slot_ref, own_ref):
+        return (row_for(slot, 1, slot_ref, own_ref), 0, 0)
+
     return pl.pallas_call(
         place_kernel,
         out_shape=jax.ShapeDtypeStruct(placed.shape, placed.dtype),
-        in_specs=[pl.BlockSpec(memory_space=pltpu.SMEM)]
-        + [pl.BlockSpec(memory_space=pl.ANY)] * 2,
-        out_specs=pl.BlockSpec(memory_space=pl.ANY),
-        scratch_shapes=[pltpu.SemaphoreType.DMA],
-        input_output_aliases={2: 0},
+        grid_spec=pltpu.PrefetchScalarGridSpec(
+            num_scalar_prefetch=2,
+            grid=(1,),
+            in_specs=[
+                pl.BlockSpec(source.shape, lambda i, *_: (0, 0)),
+                pl.BlockSpec(memory_space=pl.ANY),
+            ],
+            out_specs=pl.BlockSpec((1,) + source.shape, chosen),
+        ),
+        input_output_aliases={3: 0},
         name="place",
-    )(index, source, placed)
+    )(*scalars, source, placed)
 
 
 def dispatch_kernel(experts, block_ref, routes_ref, gate_ref, tokens_ref, out_ref, share_ref):
@@ -381,20 +426,6 @@
     caches = [own_cache, cache_a, cache_b, cache_c]
     caches = [(cache, swapped(cache, "expert", 0)) for cache in caches]
 
-    nearer = jnp.where(high < line // 2, line // 2, line // 2 - 1)
-    farther = jnp.where(high < line // 2, line - 1, 0)
-    order = jnp.stack([high, high ^ 1, nearer, farther])
-    row_of = jnp.sum(
-        jnp.where(
-            branch_slot[None, :] == jnp.arange(tok_rows, dtype=jnp.int32)[:, None],
-            jnp.arange(tok_rows, dtype=jnp.int32)[None, :],
-            0,
-        ),
-        axis=1,
-    )
-    stay_row = row_of[2 * order + low]
-    leave_row = row_of[2 * order + 1 - low]
-
     q_lat = q_latent.reshape(tok_rows, q_rows, width)
     rope_raw = q_rope.reshape(tok_rows, q_rows * rope_width // width, width)
     fresh = jnp.concatenate(
@@ -404,33 +435,35 @@
         ],
         axis=1,
     )
-    stay, leave = pack_queries(stay_row, leave_row, q_lat, rope_raw, fresh)
+    scalars = (branch_slot, own[None])
+    stay = (q_lat, rope_raw, fresh)
+    leave = pack_leaving(*scalars, *stay)
     guest = swapped(leave, "branch", 0)
 
     attend = build_attend(head_count, step_count, width, half, rope_rows, 32)
     placed = None
     waiting = []
     for slot in range(line):
-        index = jnp.stack([stay_row[slot]] + [leave_row[s] for s, _ in waiting])
-        arrived = [value for _, value in waiting]
-        if slot < line - 1:
-            given, placed = attend(
-                index,
-                ("give", "keep"),
+        kinds = [("give", "keep")] if slot < line - 1 else [("give",), ("keep",)]
+        given = None
+        for kind in kinds:
+            keeps = "keep" in kind
+            results = attend(
+                scalars,
+                kind,
                 slot,
-                (guest, stay),
+                guest,
+                stay,
                 caches[slot],
-                arrived,
-                placed,
-                tok_rows,
+                waiting if keeps else [],
+                placed if keeps else None,
             )
-        else:
-            (given,) = attend(index, ("give",), slot, (guest,), caches[slot], [], None, tok_rows)
-            (placed,) = attend(
-                index, ("keep",), slot, (stay,), caches[slot], arrived, placed, tok_rows
-            )
+            if "give" in kind:
+                given = results[0]
+            if keeps:
+                placed = results[-1]
         waiting = [(slot, swapped(given, "branch", 0))]
-    placed = place(leave_row[line - 1 :], waiting[0][1], placed)
+    placed = place(scalars, line - 1, waiting[0][1], placed)
     attended = placed.reshape(tok_rows, step_count, head_count, width)
 
     model_width = moe_input.shape[-1]
@@ -448,18 +481,24 @@
         experts,
     )
 
-    def to_block(x, shift):
+    around = shard_branches // 2
+
+    def along(x, shift, flip):
         count = lax.axis_size("branch")
-        return lax.ppermute(
-            x, "branch", [(i, (i + shift * shard_branches) % count) for i in range(count)]
-        )
-
-    rows = [outgoing[:CAP]]
-    for k in range(1, experts):
-        rows.append(to_block(outgoing[k * CAP : (k + 1) * CAP], k))
+        there = [
+            ((i // shard_branches + shift) % experts) * shard_branches
+            + ((i % shard_branches) ^ (flip * 2))
+            for i in range(count)
+        ]
+        return lax.ppermute(x, "branch", list(enumerate(there)))
+
+    ways = [(k, m) for k in range(experts) for m in range(around)]
+    rows = []
+    for k, m in ways:
+        piece = outgoing[k * CAP : (k + 1) * CAP]
+        rows.append(piece if (k, m) == (0, 0) else along(piece, k, m))
     rows = jnp.concatenate(rows, axis=0)
-    bits = [("branch", b) for b in reversed(range(shard_branches.bit_length() - 1))]
-    bits += [("expert", b) for b in reversed(range(cores.bit_length() - 1))]
+    bits = [("branch", 0)] + [("expert", b) for b in reversed(range(cores.bit_length() - 1))]
     for axis, bit in bits:
         rows = jnp.concatenate([rows, swapped(rows, axis, bit)], axis=0)
     gate_value = jnp.dot(rows, w_gate[0], preferred_element_type=jnp.float32)
@@ -471,9 +510,12 @@
         parts = parts[:count] + swapped(
             parts[count:].astype(jnp.bfloat16), axis, bit
         ).astype(jnp.float32)
-    sums = [parts[:CAP]]
-    for k in range(1, experts):
-        sums.append(to_block(parts[k * CAP : (k + 1) * CAP], -k))
+    sums = [0.0] * experts
+    for number, (k, m) in enumerate(ways):
+        piece = parts[number * CAP : (number + 1) * CAP]
+        if (k, m) != (0, 0):
+            piece = along(piece.astype(jnp.bfloat16), -k, m).astype(jnp.float32)
+        sums[k] = sums[k] + piece
     sums = jnp.concatenate(sums, axis=0)
     combined = jnp.sum(share[:, :, None] * sums[None, :, :], axis=1)
     moe_out = combined.astype(jnp.bfloat16).reshape(tok_rows, step_count, model_width)

time: 292 us -> 162 us (0.55)
  Pallas kernels: 160 us -> 47.4 us
  waiting for transfers between devices: 80.6 us -> 69.8 us
  other arithmetic: 8.35 us -> 4.31 us
    pallas_call x6, Pallas kernels: 112 us -> 43.1 us  [the longest x5 38.8 us: call(): pl.pallas_call(functools.partial(kernel, slot, kinds, given_slots, has_pl...]
    pallas_call x1, Pallas kernels: 36.9 us -> 0.08 us  [pack_cache(): pl.pallas_call(pack_cache_kernel, out_shape=jax.ShapeDtypeStruct((lat.sha...]
    ppermute x2 -> x6, waiting for transfers between devices: 23.9 us -> 5.67 us  [along(): return lax.ppermute(x, 'branch', list(enumerate(there)))]
    ppermute x5, waiting for transfers between devices: 27.3 us -> 44.1 us  [line_hop(): return lax.ppermute(x, 'branch', pairs)]
    ppermute x15 -> x13, waiting for transfers between devices: 29.4 us -> 20 us  [swapped(): lax.ppermute(x, axis, [(i, i ^ 1 << bit) for i in range(lax.axis_size(axi...]
    pallas_call x1, Pallas kernels: 9.68 us -> 2.33 us  [place(): pl.pallas_call(place_kernel, out_shape=jax.ShapeDtypeStruct(placed.shape,...]
    ppermute x2 -> x6, starting transfers between devices: 3.67 us -> 8.75 us  [along(): return lax.ppermute(x, 'branch', list(enumerate(there)))]
    ppermute x15 -> x13, starting transfers between devices: 10.3 us -> 7.64 us  [swapped(): lax.ppermute(x, axis, [(i, i ^ 1 << bit) for i in range(lax.axis_size(axi...]
  transfers between devices with their start and end apart: 22 -> 24, of which waited for: 7 -> 9; matrix products, arithmetic and copies ran while one was open for 8% -> 5% of each run, Pallas kernels for 39% -> 27%
where the time goes in v2:
time: 162 us
  waiting for transfers between devices  69.8 us (43%)
  Pallas kernels  47.4 us (29%)
  starting transfers between devices  21.6 us (13%)
  local copies, waits for them, and re-layouts  13.3 us (8%)
  other arithmetic  4.31 us (3%)
  matrix products  4.21 us (3%)
    ppermute x5, waiting for transfers between devices, line_hop(): return lax.ppermute(x, 'branch', pairs)  44.1 us
    pallas_call x5, Pallas kernels, call(): pl.pallas_call(functools.partial(kernel, slot, kinds, given_slots, has_pl...  38.8 us
    ppermute x13, waiting for transfers between devices, swapped(): lax.ppermute(x, axis, [(i, i ^ 1 << bit) for i in range(lax.axis_size(axi...  20 us
    ppermute x6, starting transfers between devices, along(): return lax.ppermute(x, 'branch', list(enumerate(there)))  8.75 us
    ppermute x13, starting transfers between devices, swapped(): lax.ppermute(x, axis, [(i, i ^ 1 << bit) for i in range(lax.axis_size(axi...  7.64 us
    unnamed x32, local copies, waits for them, and re-layouts  5.81 us
    ppermute x6, waiting for transfers between devices, along(): return lax.ppermute(x, 'branch', list(enumerate(there)))  5.67 us
    ppermute x5, starting transfers between devices, line_hop(): return lax.ppermute(x, 'branch', pairs)  5.16 us
  transfers between devices with their start and end apart: 24, of which 9 were waited for; matrix products, arithmetic and copies ran while one was open for 5% of the time, Pallas kernels for 27%

profile of v2, /device:TPU:0, one launch (start us, length us, event | category | flops | bytes accessed | tf_op | source)
XLA Modules:
  0.0 161.5 jit_solution(1653652376654200813)
XLA Ops:
  0.7 1.8 %reshape.32.tokens_ref = bf16[16,7168]{1,0:T(8,128)(2,1)} reshape(bf16[8,2,7168]{2,1,0:T(2,128)(2,1)} %param.20) | data formatting | bytes 458752 | tf_op jit(solution)/shard_map/reshape | solution.py:480
  2.5 1.9 %dispatch.1 = (bf16[4,7168]{1,0:T(4,128)(2,1)}, f32[16,4]{1,0:T(8,128)}) custom-call(s32[1]{0:T(128)} %bitcast.5.block_ref, s32[16,8]{1,0:T(8,128)} %bitcast.31, f32[16,8]{1,0:T(8,128)} %bitcast.32, bf16[16,7168]{1,0:T(8,128)(2,1)} %reshape.32.tokens_ref), custom_call_target="tpu_custom_call" | custom-call | flops 917504 | bytes 344064 | tf_op jit(solution)/shard_map/dispatch/pallas_call | solution.py:371
  4.4 0.9 fusion.17
  5.3 3.1 %collective-permute-start.14 = (bf16[2,7168]{1,0:T(2,128)(2,1)S(1)}, bf16[2,7168]{1,0:T(2,128)(2,1)S(1)}, u32[]{:S(2)}, u32[]{:S(2)}) collective-permute-start(bf16[2,7168]{1,0:T(2,128)(2,1)S(1)} %get-tuple-element.24), channel_id=1, source_target_pairs={{0,4},{2,6},{4,0},{6,2},{8,12},{10,14},{12,8},{14,10},{1,5},{3,7},... | collective-permute-start | bytes 86024 | tf_op jit(solution)/shard_map/ppermute | solution.py:493
  8.4 2.6 %collective-permute-start.15 = (bf16[2,7168]{1,0:T(2,128)(2,1)S(1)}, bf16[2,7168]{1,0:T(2,128)(2,1)S(1)}, u32[]{:S(2)}, u32[]{:S(2)}) collective-permute-start(bf16[2,7168]{1,0:T(2,128)(2,1)S(1)} %get-tuple-element.23), channel_id=1, source_target_pairs={{0,8},{2,10},{4,12},{6,14},{8,0},{10,2},{12,4},{14,6},{1,9},{3,11}... | collective-permute-start | bytes 86024 | tf_op jit(solution)/shard_map/ppermute | solution.py:493
  11.0 2.7 %collective-permute-done.15 = bf16[2,7168]{1,0:T(2,128)(2,1)S(1)} collective-permute-done((bf16[2,7168]{1,0:T(2,128)(2,1)S(1)}, bf16[2,7168]{1,0:T(2,128)(2,1)S(1)}, u32[]{:S(2)}, u32[]{:S(2)}) %collective-permute-start.15) | collective-permute-done | bytes 28704 | tf_op jit(solution)/shard_map/ppermute | solution.py:493
  13.7 3.0 %collective-permute-done.16 = bf16[2,7168]{1,0:T(2,128)(2,1)S(1)} collective-permute-done((bf16[2,7168]{1,0:T(2,128)(2,1)S(1)}, bf16[2,7168]{1,0:T(2,128)(2,1)S(1)}, u32[]{:S(2)}, u32[]{:S(2)}) %collective-permute-start.16) | collective-permute-done | bytes 28704 | tf_op jit(solution)/shard_map/ppermute | solution.py:493
  16.8 1.6 collective-permute-start.17
  18.4 3.3 %collective-permute-done.17 = bf16[8,7168]{1,0:T(8,128)(2,1)S(1)} collective-permute-done((bf16[8,7168]{1,0:T(8,128)(2,1)S(1)}, bf16[8,7168]{1,0:T(8,128)(2,1)S(1)}, u32[]{:S(2)}, u32[]{:S(2)}) %collective-permute-start.17) | collective-permute-done | bytes 114720 | tf_op jit(solution)/shard_map/ppermute | solution.py:20
  21.9 1.5 collective-permute-done.18
  23.7 1.9 %fusion.2 = f32[32,128]{1,0:T(8,128)S(1)} fusion(bf16[32,7168]{1,0:T(8,128)(2,1)S(1)} %concatenate.20, bf16[1,7168,128]{2,1,0:T(8,128)(2,1)} %param.24), kind=kOutput, calls=%fused_computation.2 | convolution fusion | flops 58720256 | bytes 2310144 | tf_op jit(solution)/shard_map/dot_general | solution.py:505
  25.6 2.3 %fusion = f32[32,7168]{1,0:T(8,128)S(1)} fusion(bf16[1,128,7168]{2,1,0:T(8,128)(2,1)S(1)} %copy-done, f32[32,128]{1,0:T(8,128)S(1)} %fusion.2, bf16[32,7168]{1,0:T(8,128)(2,1)S(1)} %concatenate.20, bf16[1,7168,128]{2,1,0:T(8,128)(2,1)} %param.23), kind=kOutput, calls=%fused_computation | convolution fusion | flops 117465088 | bytes 5062656 | tf_op jit(solution)/shard_map/dot_general | solution.py:507
  27.9 0.8 slice.60
  28.9 1.2 copy-done.7
  30.6 1.7 %collective-permute-start.6 = (bf16[1152,512]{1,0:T(8,128)(2,1)S(1)}, bf16[1152,512]{1,0:T(8,128)(2,1)}, u32[]{:S(2)}, u32[]{:S(2)}) collective-permute-start(bf16[1152,512]{1,0:T(8,128)(2,1)S(1)} %pack_cache.1.refs_6_), channel_id=1, source_target_pairs={{4,8},{8,4},{6,10},{10,6},{5,9},{9,5},{7,11},{11,7},{20,24},{24,20... | collective-permute-start | bytes 3538952 | tf_op jit(solution)/shard_map/ppermute | solution.py:28
  32.3 0.9 reshape.28.rope_ref.refs_4_.refs_3_
  33.2 1.1 slice_add_fusion
  34.3 0.7 slice.61
  35.1 1.5 collective-permute-start.20
  36.6 0.7 fusion.8.new_ref.refs_5_.refs_4_
  37.4 4.3 %pack_leaving.1 = bf16[4,320,512]{2,1,0:T(8,128)(2,1)} custom-call(s32[8]{0:T(128)} %slot_ref.3, s32[1]{0:T(128)} %bitcast.own_ref.refs_1_, bf16[8,256,512]{2,1,0:T(8,128)(2,1)} %bitcast.23, bf16[8,32,512]{2,1,0:T(8,128)(2,1)} %reshape.28.rope_ref.refs_4_.refs_3_, bf16[8,32,512]{2,1,0:T(8,128)(2,1)} %fusion.8.new_ref.refs_5_.refs_4_), custom_call_target="tpu_custom_call" | custom-call | bytes 2621440 | tf_op jit(solution)/shard_map/pack_leaving/pallas_call | solution.py:87
  41.7 0.5 collective-permute-start
  42.3 1.0 fusion.15
  43.3 15.5 %collective-permute-done.1.refs_6_ = bf16[1152,512]{1,0:T(8,128)(2,1)} collective-permute-done((bf16[1152,512]{1,0:T(8,128)(2,1)S(1)}, bf16[1152,512]{1,0:T(8,128)(2,1)}, u32[]{:S(2)}, u32[]{:S(2)}) %collective-permute-start.1) | collective-permute-done | bytes 1179680 | tf_op jit(solution)/shard_map/ppermute | solution.py:28
  58.8 0.7 collective-permute-start.2
  59.6 1.5 collective-permute-start.21
  61.1 1.5 collective-permute-start.22
  62.7 9.9 %collective-permute-done.refs_2_ = bf16[4,320,512]{2,1,0:T(8,128)(2,1)} collective-permute-done((bf16[4,320,512]{2,1,0:T(8,128)(2,1)}, bf16[4,320,512]{2,1,0:T(8,128)(2,1)}, u32[]{:S(2)}, u32[]{:S(2)}) %collective-permute-start) | collective-permute-done | bytes 1310752 | tf_op jit(solution)/shard_map/ppermute | solution.py:20
  72.6 1.3 collective-permute-start.7
  74.0 1.6 copy-done.1
  75.5 7.9 %attend_give_keep.3 = (bf16[256,512]{1,0:T(8,128)(2,1)S(1)}, bf16[8,256,512]{2,1,0:T(8,128)(2,1)}) custom-call(s32[8]{0:T(128)S(1)} %copy-done.9, s32[1]{0:T(128)} %bitcast.own_ref.refs_1_, bf16[4,320,512]{2,1,0:T(8,128)(2,1)} %collective-permute-done.refs_2_, bf16[8,256,512]{2,1,0:T(8,128)(2,1)S(1)} %bitcast.24, bf16[8,32,512]{2,1,0:T(8,128)(2,1)S(1)} %copy-done.3, ...), custom_call_target="tpu_custom_call" | custom-call | flops 2415919104 | bytes 3670016 | tf_op jit(solution)/shard_map/attend_give_keep/pallas_call | solution.py:284
  83.5 0.6 collective-permute-start.11
  84.0 1.5 collective-permute-start.3
  85.5 5.3 %collective-permute-done.11.refs_8_ = bf16[256,512]{1,0:T(8,128)(2,1)S(1)} collective-permute-done((bf16[256,512]{1,0:T(8,128)(2,1)S(1)}, bf16[256,512]{1,0:T(8,128)(2,1)S(1)}, u32[]{:S(2)}, u32[]{:S(2)}) %collective-permute-start.11) | collective-permute-done | bytes 262176 | tf_op jit(solution)/shard_map/ppermute | solution.py:20
  90.8 7.9 %attend_give_keep.4 = (bf16[256,512]{1,0:T(8,128)(2,1)S(1)}, bf16[8,256,512]{2,1,0:T(8,128)(2,1)}) custom-call(s32[8]{0:T(128)S(1)} %copy-done.9, s32[1]{0:T(128)} %bitcast.own_ref.refs_1_, bf16[4,320,512]{2,1,0:T(8,128)(2,1)} %collective-permute-done.refs_2_, bf16[8,256,512]{2,1,0:T(8,128)(2,1)S(1)} %bitcast.25, ...), custom_call_target="tpu_custom_call", output_to_operand_aliasing={{1}: (9, {})} | custom-call | flops 2415919104 | bytes 3670016 | tf_op jit(solution)/shard_map/attend_give_keep/pallas_call | solution.py:284
  98.7 0.6 collective-permute-start.12
  99.3 5.6 %collective-permute-done.7 = bf16[1152,512]{1,0:T(8,128)(2,1)S(1)} collective-permute-done((bf16[1152,512]{1,0:T(8,128)(2,1)}, bf16[1152,512]{1,0:T(8,128)(2,1)S(1)}, u32[]{:S(2)}, u32[]{:S(2)}) %collective-permute-start.7) | collective-permute-done | bytes 1179680 | tf_op jit(solution)/shard_map/ppermute | solution.py:28
  105.1 23.1 %collective-permute-done.3 = bf16[1152,512]{1,0:T(8,128)(2,1)S(1)} collective-permute-done((bf16[1152,512]{1,0:T(8,128)(2,1)S(1)}, bf16[1152,512]{1,0:T(8,128)(2,1)S(1)}, u32[]{:S(2)}, u32[]{:S(2)}) %collective-permute-start.3) | collective-permute-done | bytes 1179680 | tf_op jit(solution)/shard_map/ppermute | solution.py:28
  128.5 7.8 %attend_give_keep.5 = (bf16[256,512]{1,0:T(8,128)(2,1)}, bf16[8,256,512]{2,1,0:T(8,128)(2,1)}) custom-call(s32[8]{0:T(128)S(1)} %copy-done.9, s32[1]{0:T(128)} %bitcast.own_ref.refs_1_, bf16[4,320,512]{2,1,0:T(8,128)(2,1)} %collective-permute-done.refs_2_, bf16[8,256,512]{2,1,0:T(8,128)(2,1)S(1)} %bitcast.26, ...), custom_call_target="tpu_custom_call", output_to_operand_aliasing={{1}: (9, {})} | custom-call | flops 2415919104 | bytes 3670016 | tf_op jit(solution)/shard_map/attend_give_keep/pallas_call | solution.py:284
  136.3 0.6 collective-permute-start.13
  136.8 5.0 %attend_give.1 = bf16[256,512]{1,0:T(8,128)(2,1)} custom-call(s32[8]{0:T(128)S(1)} %copy-done.9, s32[1]{0:T(128)} %bitcast.own_ref.refs_1_, bf16[4,320,512]{2,1,0:T(8,128)(2,1)} %collective-permute-done.refs_2_, bf16[1152,512]{1,0:T(8,128)(2,1)S(1)} %broadcast_select_fusion.1.refs_3_.refs_5_, bf16[1152,512]{1,0:T(8,128)(2,1)S(1)} %collective-permute-done.4.refs_4_.refs_6_), custom_call_target="tpu_custom_call" | custom-call | flops 1207959552 | bytes 3145728 | tf_op jit(solution)/shard_map/attend_give/pallas_call | solution.py:284
  141.9 1.6 %collective-permute-start.5 = (bf16[256,512]{1,0:T(8,128)(2,1)}, bf16[256,512]{1,0:T(8,128)(2,1)}, u32[]{:S(2)}, u32[]{:S(2)}) collective-permute-start(bf16[256,512]{1,0:T(8,128)(2,1)} %attend_give.1), channel_id=1, source_target_pairs={{0,2},{2,0},{4,6},{6,4},{8,10},{10,8},{12,14},{14,12},{1,3},{3,1},... | collective-permute-start | bytes 786440 | tf_op jit(solution)/shard_map/ppermute | solution.py:20
  143.6 0.9 multiply_reduce_fusion
  144.4 1.7 %convert_element_type.41 = bf16[8,2,7168]{2,1,0:T(2,128)(2,1)} reshape(bf16[16,7168]{1,0:T(8,128)(2,1)} %multiply_reduce_fusion) | data formatting | bytes 458752 | tf_op jit(solution)/shard_map/convert_element_type | solution.py:521
  146.2 1.6 copy-done.2
  147.7 1.3 copy-done.6
  149.0 10.1 %attend_keep.1.before = bf16[8,256,512]{2,1,0:T(8,128)(2,1)} custom-call(s32[8]{0:T(128)S(1)} %copy-done.9, s32[1]{0:T(128)} %bitcast.own_ref.refs_1_, bf16[8,256,512]{2,1,0:T(8,128)(2,1)S(1)} %bitcast.27, bf16[8,32,512]{2,1,0:T(8,128)(2,1)S(1)} %copy-done.3, bf16[8,32,512]{2,1,0:T(8,128)(2,1)S(1)} %copy-done.4, ...), custom_call_target="tpu_custom_call", output_to_operand_aliasing={{}: (8, {})} | custom-call | flops 1207959552 | bytes 3145728 | tf_op jit(solution)/shard_map/attend_keep/pallas_call | solution.py:284
  159.2 2.3 %place.1 = bf16[8,256,512]{2,1,0:T(8,128)(2,1)} custom-call(s32[8]{0:T(128)} %slot_ref.3, s32[1]{0:T(128)} %bitcast.own_ref.refs_1_, bf16[256,512]{1,0:T(8,128)(2,1)} %collective-permute-done.5.source_ref, bf16[8,256,512]{2,1,0:T(8,128)(2,1)} %attend_keep.1.before), custom_call_target="tpu_custom_call", output_to_operand_aliasing={{}: (3, {})} | custom-call | tf_op jit(solution)/shard_map/place/pallas_call | solution.py:321
  (63 shorter events, 2.1 us)
Async XLA Ops:
  0.6 25.0 %copy-start = (bf16[1,128,7168]{2,1,0:T(8,128)(2,1)S(1)}, bf16[1,128,7168]{2,1,0:T(8,128)(2,1)}, u32[]{:S(2)}) copy-start(bf16[1,128,7168]{2,1,0:T(8,128)(2,1)} %param.25) | copy-start | bytes 5505028
  5.3 5.7 %collective-permute-start.14 = (bf16[2,7168]{1,0:T(2,128)(2,1)S(1)}, bf16[2,7168]{1,0:T(2,128)(2,1)S(1)}, u32[]{:S(2)}, u32[]{:S(2)}) collective-permute-start(bf16[2,7168]{1,0:T(2,128)(2,1)S(1)} %get-tuple-element.24), channel_id=1, source_target_pairs={{0,4},{2,6},{4,0},{6,2},{8,12},{10,14},{12,8},{14,10},{1,5},{3,7},... | collective-permute-start | bytes 86024 | tf_op jit(solution)/shard_map/ppermute | solution.py:493
  8.4 5.2 %collective-permute-start.15 = (bf16[2,7168]{1,0:T(2,128)(2,1)S(1)}, bf16[2,7168]{1,0:T(2,128)(2,1)S(1)}, u32[]{:S(2)}, u32[]{:S(2)}) collective-permute-start(bf16[2,7168]{1,0:T(2,128)(2,1)S(1)} %get-tuple-element.23), channel_id=1, source_target_pairs={{0,8},{2,10},{4,12},{6,14},{8,0},{10,2},{12,4},{14,6},{1,9},{3,11}... | collective-permute-start | bytes 86024 | tf_op jit(solution)/shard_map/ppermute | solution.py:493
  11.0 5.7 %collective-permute-start.16 = (bf16[2,7168]{1,0:T(2,128)(2,1)S(1)}, bf16[2,7168]{1,0:T(2,128)(2,1)S(1)}, u32[]{:S(2)}, u32[]{:S(2)}) collective-permute-start(bf16[2,7168]{1,0:T(2,128)(2,1)S(1)} %get-tuple-element.23), channel_id=1, source_target_pairs={{0,12},{2,14},{4,8},{6,10},{8,4},{10,6},{12,0},{14,2},{1,13},{3,15... | collective-permute-start | bytes 86024 | tf_op jit(solution)/shard_map/ppermute | solution.py:493
  16.8 4.9 %collective-permute-start.17 = (bf16[8,7168]{1,0:T(8,128)(2,1)S(1)}, bf16[8,7168]{1,0:T(8,128)(2,1)S(1)}, u32[]{:S(2)}, u32[]{:S(2)}) collective-permute-start(bf16[8,7168]{1,0:T(8,128)(2,1)S(1)} %pad_maximum_fusion), channel_id=1, source_target_pairs={{0,2},{2,0},{4,6},{6,4},{8,10},{10,8},{12,14},{14,12},{1,3},{3,1},... | collective-permute-start | bytes 344072 | tf_op jit(solution)/shard_map/ppermute | solution.py:20
  21.9 1.6 collective-permute-start.18
  25.6 3.3 %copy-start.8 = (bf16[1,128,512]{2,1,0:T(8,128)(2,1)S(1)}, bf16[1,128,512]{2,1,0:T(8,128)(2,1)}, u32[]{:S(2)}) copy-start(bf16[1,128,512]{2,1,0:T(8,128)(2,1)} %param.14) | copy-start | bytes 393220
  27.9 1.0 copy-start.10
  28.7 4.5 %collective-permute-start.19 = (bf16[16,7168]{1,0:T(8,128)(2,1)}, bf16[16,7168]{1,0:T(8,128)(2,1)}, u32[]{:S(2)}, u32[]{:S(2)}) collective-permute-start(bf16[16,7168]{1,0:T(8,128)(2,1)} %slice.60), channel_id=1, source_target_pairs={{0,1},{1,0},{2,3},{3,2},{4,5},{5,4},{6,7},{7,6},{8,9},{9,8},{10,11... | collective-permute-start | bytes 688136 | tf_op jit(solution)/shard_map/ppermute | solution.py:20
  28.9 1.2 copy-start.7
  30.2 2.1 %copy-start.12 = (bf16[8,2,8192]{2,1,0:T(2,128)(2,1)S(1)}, bf16[8,2,8192]{2,1,0:T(2,128)(2,1)}, u32[]{:S(2)}) copy-start(bf16[8,2,8192]{2,1,0:T(2,128)(2,1)} %param.16) | copy-start | bytes 786436
  30.2 6.4 %copy-start.13 = (bf16[8,2,512]{2,1,0:T(2,128)(2,1)S(1)}, bf16[8,2,512]{2,1,0:T(2,128)(2,1)}, u32[]{:S(2)}) copy-start(bf16[8,2,512]{2,1,0:T(2,128)(2,1)} %param.17) | copy-start | bytes 49156
  30.2 6.4 %copy-start.15 = (bf16[8,2,64]{2,1,0:T(2,128)(2,1)S(1)}, bf16[8,2,64]{2,1,0:T(2,128)(2,1)}, u32[]{:S(2)}) copy-start(bf16[8,2,64]{2,1,0:T(2,128)(2,1)} %param.18) | copy-start | bytes 6148
  30.2 30.9 %collective-permute-start.10 = (bf16[1152,512]{1,0:T(8,128)(2,1)S(1)}, bf16[1152,512]{1,0:T(8,128)(2,1)}, u32[]{:S(2)}, u32[]{:S(2)}) collective-permute-start(bf16[1152,512]{1,0:T(8,128)(2,1)S(1)} %pack_cache.1.refs_6_), channel_id=1, source_target_pairs={{0,1},{1,0},{2,3},{3,2},{4,5},{5,4},{6,7},{7,6},{8,9},{9,8},{10,11... | collective-permute-start | bytes 3538952 | tf_op jit(solution)/shard_map/ppermute | solution.py:20
  30.6 28.2 %collective-permute-start.1 = (bf16[1152,512]{1,0:T(8,128)(2,1)S(1)}, bf16[1152,512]{1,0:T(8,128)(2,1)}, u32[]{:S(2)}, u32[]{:S(2)}) collective-permute-start(bf16[1152,512]{1,0:T(8,128)(2,1)S(1)} %pack_cache.1.refs_6_), channel_id=1, source_target_pairs={{0,4},{4,0},{8,12},{12,8},{2,6},{6,2},{10,14},{14,10},{1,5},{5,1},... | collective-permute-start | bytes 3538952 | tf_op jit(solution)/shard_map/ppermute | solution.py:28
  30.6 32.1 %collective-permute-start.6 = (bf16[1152,512]{1,0:T(8,128)(2,1)S(1)}, bf16[1152,512]{1,0:T(8,128)(2,1)}, u32[]{:S(2)}, u32[]{:S(2)}) collective-permute-start(bf16[1152,512]{1,0:T(8,128)(2,1)S(1)} %pack_cache.1.refs_6_), channel_id=1, source_target_pairs={{4,8},{8,4},{6,10},{10,6},{5,9},{9,5},{7,11},{11,7},{20,24},{24,20... | collective-permute-start | bytes 3538952 | tf_op jit(solution)/shard_map/ppermute | solution.py:28
  34.3 3.0 %copy-start.11 = (f32[16,7168]{1,0:T(8,128)}, f32[16,7168]{1,0:T(8,128)S(1)}, u32[]{:S(2)}) copy-start(f32[16,7168]{1,0:T(8,128)S(1)} %slice_add_fusion) | copy-start | bytes 1376260
  35.1 7.2 %collective-permute-start.20 = (bf16[8,7168]{1,0:T(8,128)(2,1)}, bf16[8,7168]{1,0:T(8,128)(2,1)}, u32[]{:S(2)}, u32[]{:S(2)}) collective-permute-start(bf16[8,7168]{1,0:T(8,128)(2,1)} %slice.61), channel_id=1, source_target_pairs={{0,2},{2,0},{4,6},{6,4},{8,10},{10,8},{12,14},{14,12},{1,3},{3,1},... | collective-permute-start | bytes 344072 | tf_op jit(solution)/shard_map/ppermute | solution.py:20
  37.3 4.9 %copy-start.14 = (f32[16,4]{1,0:T(8,128)S(1)}, f32[16,4]{1,0:T(8,128)}, u32[]{:S(2)}) copy-start(f32[16,4]{1,0:T(8,128)} %get-tuple-element.16) | copy-start | bytes 772
  37.3 36.6 %copy-start.3 = (bf16[8,32,512]{2,1,0:T(8,128)(2,1)S(1)}, bf16[8,32,512]{2,1,0:T(8,128)(2,1)}, u32[]{:S(2)}) copy-start(bf16[8,32,512]{2,1,0:T(8,128)(2,1)} %reshape.28.rope_ref.refs_4_.refs_3_) | copy-start | bytes 786436
  37.3 36.6 %copy-start.4 = (bf16[8,32,512]{2,1,0:T(8,128)(2,1)S(1)}, bf16[8,32,512]{2,1,0:T(8,128)(2,1)}, u32[]{:S(2)}) copy-start(bf16[8,32,512]{2,1,0:T(8,128)(2,1)} %fusion.8.new_ref.refs_5_.refs_4_) | copy-start | bytes 786436
  37.3 36.6 %copy-start.9 = (s32[8]{0:T(128)S(1)}, s32[8]{0:T(128)}, u32[]{:S(2)}) copy-start(s32[8]{0:T(128)} %slot_ref.3) | copy-start | bytes 100
  41.7 30.9 %collective-permute-start = (bf16[4,320,512]{2,1,0:T(8,128)(2,1)}, bf16[4,320,512]{2,1,0:T(8,128)(2,1)}, u32[]{:S(2)}, u32[]{:S(2)}) collective-permute-start(bf16[4,320,512]{2,1,0:T(8,128)(2,1)} %pack_leaving.1), channel_id=1, source_target_pairs={{0,2},{2,0},{4,6},{6,4},{8,10},{10,8},{12,14},{14,12},{1,3},{3,1},... | collective-permute-start | bytes 3932168 | tf_op jit(solution)/shard_map/ppermute | solution.py:20
  58.8 25.2 %collective-permute-start.2 = (bf16[1152,512]{1,0:T(8,128)(2,1)}, bf16[1152,512]{1,0:T(8,128)(2,1)S(1)}, u32[]{:S(2)}, u32[]{:S(2)}) collective-permute-start(bf16[1152,512]{1,0:T(8,128)(2,1)} %collective-permute-done.1.refs_6_), channel_id=1, source_target_pairs={{4,8},{8,4},{6,10},{10,6},{5,9},{9,5},{7,11},{11,7},{20,24},{24,20... | collective-permute-start | bytes 3538952 | tf_op jit(solution)/shard_map/ppermute | solution.py:28
  59.6 23.8 %collective-permute-start.21 = (bf16[2,7168]{1,0:T(2,128)(2,1)S(1)}, bf16[2,7168]{1,0:T(2,128)(2,1)S(1)}, u32[]{:S(2)}, u32[]{:S(2)}) collective-permute-start(bf16[2,7168]{1,0:T(2,128)(2,1)S(1)} %get-tuple-element.20), channel_id=1, source_target_pairs={{0,4},{2,6},{4,0},{6,2},{8,12},{10,14},{12,8},{14,10},{1,5},{3,7},... | collective-permute-start | bytes 86024 | tf_op jit(solution)/shard_map/ppermute | solution.py:493
  61.1 67.2 %collective-permute-start.22 = (bf16[2,7168]{1,0:T(2,128)(2,1)S(1)}, bf16[2,7168]{1,0:T(2,128)(2,1)S(1)}, u32[]{:S(2)}, u32[]{:S(2)}) collective-permute-start(bf16[2,7168]{1,0:T(2,128)(2,1)S(1)} %get-tuple-element.22), channel_id=1, source_target_pairs={{0,8},{2,10},{4,12},{6,14},{8,0},{10,2},{12,4},{14,6},{1,9},{3,11}... | collective-permute-start | bytes 86024 | tf_op jit(solution)/shard_map/ppermute | solution.py:493
  62.7 28.1 %collective-permute-start.9 = (bf16[1152,512]{1,0:T(8,128)(2,1)}, bf16[1152,512]{1,0:T(8,128)(2,1)S(1)}, u32[]{:S(2)}, u32[]{:S(2)}) collective-permute-start(bf16[1152,512]{1,0:T(8,128)(2,1)} %collective-permute-done.1.refs_6_), channel_id=1, source_target_pairs={{0,1},{1,0},{2,3},{3,2},{4,5},{5,4},{6,7},{7,6},{8,9},{9,8},{10,11... | collective-permute-start | bytes 3538952 | tf_op jit(solution)/shard_map/ppermute | solution.py:20
  72.6 32.2 %collective-permute-start.7 = (bf16[1152,512]{1,0:T(8,128)(2,1)}, bf16[1152,512]{1,0:T(8,128)(2,1)S(1)}, u32[]{:S(2)}, u32[]{:S(2)}) collective-permute-start(bf16[1152,512]{1,0:T(8,128)(2,1)} %collective-permute-done.6), channel_id=1, source_target_pairs={{4,0},{8,12},{6,2},{10,14},{5,1},{9,13},{7,3},{11,15},{20,16},{24,... | collective-permute-start | bytes 3538952 | tf_op jit(solution)/shard_map/ppermute | solution.py:28
  74.0 1.6 copy-start.1
  83.5 7.4 %collective-permute-start.11 = (bf16[256,512]{1,0:T(8,128)(2,1)S(1)}, bf16[256,512]{1,0:T(8,128)(2,1)S(1)}, u32[]{:S(2)}, u32[]{:S(2)}) collective-permute-start(bf16[256,512]{1,0:T(8,128)(2,1)S(1)} %get-tuple-element.10), channel_id=1, source_target_pairs={{0,2},{2,0},{4,6},{6,4},{8,10},{10,8},{12,14},{14,12},{1,3},{3,1},... | collective-permute-start | bytes 786440 | tf_op jit(solution)/shard_map/ppermute | solution.py:20
  84.0 44.2 %collective-permute-start.3 = (bf16[1152,512]{1,0:T(8,128)(2,1)S(1)}, bf16[1152,512]{1,0:T(8,128)(2,1)S(1)}, u32[]{:S(2)}, u32[]{:S(2)}) collective-permute-start(bf16[1152,512]{1,0:T(8,128)(2,1)S(1)} %collective-permute-done.2), channel_id=1, source_target_pairs={{4,0},{8,12},{6,2},{10,14},{5,1},{9,13},{7,3},{11,15},{20,16},{24,... | collective-permute-start | bytes 3538952 | tf_op jit(solution)/shard_map/ppermute | solution.py:28
  90.8 37.6 %collective-permute-start.23 = (bf16[2,7168]{1,0:T(2,128)(2,1)S(1)}, bf16[2,7168]{1,0:T(2,128)(2,1)S(1)}, u32[]{:S(2)}, u32[]{:S(2)}) collective-permute-start(bf16[2,7168]{1,0:T(2,128)(2,1)S(1)} %get-tuple-element.21), channel_id=1, source_target_pairs={{0,12},{2,14},{4,8},{6,10},{8,4},{10,6},{12,0},{14,2},{1,13},{3,15... | collective-permute-start | bytes 86024 | tf_op jit(solution)/shard_map/ppermute | solution.py:493
  98.7 29.7 %collective-permute-start.12 = (bf16[256,512]{1,0:T(8,128)(2,1)S(1)}, bf16[256,512]{1,0:T(8,128)(2,1)S(1)}, u32[]{:S(2)}, u32[]{:S(2)}) collective-permute-start(bf16[256,512]{1,0:T(8,128)(2,1)S(1)} %get-tuple-element.12), channel_id=1, source_target_pairs={{0,2},{2,0},{4,6},{6,4},{8,10},{10,8},{12,14},{14,12},{1,3},{3,1},... | collective-permute-start | bytes 786440 | tf_op jit(solution)/shard_map/ppermute | solution.py:20
  105.0 23.4 %collective-permute-start.8 = (bf16[1152,512]{1,0:T(8,128)(2,1)S(1)}, bf16[1152,512]{1,0:T(8,128)(2,1)S(1)}, u32[]{:S(2)}, u32[]{:S(2)}) collective-permute-start(bf16[1152,512]{1,0:T(8,128)(2,1)S(1)} %broadcast_select_fusion.refs_6_), channel_id=1, source_target_pairs={{0,1},{1,0},{2,3},{3,2},{4,5},{5,4},{6,7},{7,6},{8,9},{9,8},{10,11... | collective-permute-start | bytes 3538952 | tf_op jit(solution)/shard_map/ppermute | solution.py:20
  128.3 8.5 %collective-permute-start.4 = (bf16[1152,512]{1,0:T(8,128)(2,1)S(1)}, bf16[1152,512]{1,0:T(8,128)(2,1)S(1)}, u32[]{:S(2)}, u32[]{:S(2)}) collective-permute-start(bf16[1152,512]{1,0:T(8,128)(2,1)S(1)} %broadcast_select_fusion.1.refs_3_.refs_5_), channel_id=1, source_target_pairs={{0,1},{1,0},{2,3},{3,2},{4,5},{5,4},{6,7},{7,6},{8,9},{9,8},{10,11... | collective-permute-start | bytes 3538952 | tf_op jit(solution)/shard_map/ppermute | solution.py:20
  136.3 9.9 %collective-permute-start.13 = (bf16[256,512]{1,0:T(8,128)(2,1)}, bf16[256,512]{1,0:T(8,128)(2,1)}, u32[]{:S(2)}, u32[]{:S(2)}) collective-permute-start(bf16[256,512]{1,0:T(8,128)(2,1)} %get-tuple-element.14), channel_id=1, source_target_pairs={{0,2},{2,0},{4,6},{6,4},{8,10},{10,8},{12,14},{14,12},{1,3},{3,1},... | collective-permute-start | bytes 786440 | tf_op jit(solution)/shard_map/ppermute | solution.py:20
  136.8 5.1 %copy-start.5 = (bf16[1152,512]{1,0:T(8,128)(2,1)}, bf16[1152,512]{1,0:T(8,128)(2,1)S(1)}, u32[]{:S(2)}) copy-start(bf16[1152,512]{1,0:T(8,128)(2,1)S(1)} %collective-permute-done.4.refs_4_.refs_6_) | copy-start | bytes 3538948
  141.9 17.3 %collective-permute-start.5 = (bf16[256,512]{1,0:T(8,128)(2,1)}, bf16[256,512]{1,0:T(8,128)(2,1)}, u32[]{:S(2)}, u32[]{:S(2)}) collective-permute-start(bf16[256,512]{1,0:T(8,128)(2,1)} %attend_give.1), channel_id=1, source_target_pairs={{0,2},{2,0},{4,6},{6,4},{8,10},{10,8},{12,14},{14,12},{1,3},{3,1},... | collective-permute-start | bytes 786440 | tf_op jit(solution)/shard_map/ppermute | solution.py:20
  146.2 1.6 copy-start.2
  147.7 1.3 copy-start.6

commit v3 on v2

--- a/solution.py
+++ b/solution.py
@@ -12,8 +12,14 @@
 LANES = 128
 PAD = 16
 
+SMALL = pl.CostEstimate(flops=0, bytes_accessed=1024, transcendentals=0)
+
 softmax_scale = 192.0 ** (-0.5)
 log2e = 1.4426950408889634
+
+
+def after(x, *earlier):
+    return lax.optimization_barrier((x, *earlier))[0]
 
 
 def swapped(x, axis, bit):
@@ -40,7 +46,7 @@
         out_shape=jax.ShapeDtypeStruct((lat.shape[0] + rope.shape[0], lat.shape[1]), lat.dtype),
         in_specs=[pl.BlockSpec(memory_space=pltpu.VMEM)] * 2,
         out_specs=pl.BlockSpec(memory_space=pltpu.VMEM),
-        cost_estimate=pl.CostEstimate(flops=0, bytes_accessed=2 * 2 * lat.size, transcendentals=0),
+        cost_estimate=SMALL,
         compiler_params=pltpu.CompilerParams(vmem_limit_bytes=16 * 1024 * 1024),
         name="pack_cache",
     )(lat, rope)
@@ -67,35 +73,36 @@
     return row
 
 
-def pack_leaving_kernel(slot_ref, own_ref, q_ref, rope_ref, new_ref, out_ref):
-    start = 0
-    for source in (q_ref, rope_ref, new_ref):
-        count = source.shape[1]
-        out_ref[0, start : start + count, :] = source[0]
-        start += count
+def pack_leaving_kernel(slot_ref, own_ref, q_ref, rope_ref, new_ref, out_ref, sems):
+    copies = []
+    for slot in range(out_ref.shape[0]):
+        row = row_for(slot, 1, slot_ref, own_ref)
+        start = 0
+        for part, source in enumerate((q_ref, rope_ref, new_ref)):
+            count = source.shape[1]
+            copy = pltpu.make_async_copy(
+                source.at[row], out_ref.at[slot, pl.ds(start, count)], sems.at[slot, part]
+            )
+            copy.start()
+            copies.append(copy)
+            start += count
+    for copy in copies:
+        copy.wait()
 
 
 def pack_leaving(branch_slot, own, q_lat, q_rope, new):
     slots = branch_slot.shape[0] // 2
     sources = (q_lat, q_rope, new)
     rows = sum(x.shape[1] for x in sources)
-    width = q_lat.shape[2]
-
-    def chosen(i, slot_ref, own_ref):
-        return (row_for(i, 1, slot_ref, own_ref), 0, 0)
-
     return pl.pallas_call(
         pack_leaving_kernel,
-        out_shape=jax.ShapeDtypeStruct((slots, rows, width), q_lat.dtype),
-        grid_spec=pltpu.PrefetchScalarGridSpec(
-            num_scalar_prefetch=2,
-            grid=(slots,),
-            in_specs=[pl.BlockSpec((1, x.shape[1], width), chosen) for x in sources],
-            out_specs=pl.BlockSpec((1, rows, width), lambda i, *_: (i, 0, 0)),
-        ),
-        cost_estimate=pl.CostEstimate(
-            flops=0, bytes_accessed=4 * slots * rows * width, transcendentals=0
-        ),
+        out_shape=jax.ShapeDtypeStruct((slots, rows, q_lat.shape[2]), q_lat.dtype),
+        in_specs=[pl.BlockSpec(memory_space=pltpu.SMEM)] * 2
+        + [pl.BlockSpec(memory_space=pl.ANY)] * 3,
+        out_specs=pl.BlockSpec(memory_space=pltpu.VMEM),
+        scratch_shapes=[pltpu.SemaphoreType.DMA((slots, 3))],
+        cost_estimate=SMALL,
+        compiler_params=pltpu.CompilerParams(vmem_limit_bytes=16 * 1024 * 1024),
         name="pack_leaving",
     )(branch_slot, own, *sources)
 
@@ -121,48 +128,51 @@
     return jnp.where(row % 2 == lane // (LANES // 2), rows, 0.0)
 
 
-def build_attend(heads, steps, width, half, rope_rows, raw_group):
+def build_attend(heads, steps, width, half, rope_rows, raw_group, chunk):
     q_rows = heads * steps
     token_rope = q_rows // 8
 
-    def one_token(lat, raw_rope, fresh_all, keys):
-        matrix = spread_matrix(raw_group, width)
-        pieces = []
-        for start in range(0, token_rope, raw_group):
+    factor = softmax_scale * log2e
+    contract = (((1,), (1,)), ((), ()))
+
+    def put_query(queries, number, lat, raw_rope, matrix):
+        first = number * q_rows
+        queries[first : first + q_rows, 0:width] = lat
+        grown = raw_group * width // (LANES // 2)
+        for i, start in enumerate(range(0, token_rope, raw_group)):
             part = spread(matrix, raw_rope[start : start + raw_group, :])
-            pieces.append(part + pltpu.roll(part, LANES // 2, 1))
-        rope = pieces[0] if len(pieces) == 1 else jnp.concatenate(pieces, axis=0)
-        rope = rope.astype(jnp.bfloat16)
-        query = jnp.concatenate([lat, rope], axis=1)
-        contract = (((1,), (1,)), ((), ()))
-        scores = lax.dot_general(query, keys[...], contract, preferred_element_type=jnp.float32)
-        peak = jnp.max(scores, axis=1, keepdims=True)
+            part = part + pltpu.roll(part, LANES // 2, 1)
+            row = first + i * grown
+            queries[row : row + grown, width : width + LANES] = part.astype(jnp.bfloat16)
+
+    def merge_own(query, fresh_all, peak, total, summed):
         fresh = fresh_all[0:PAD, :]
         fresh_rope = fresh_all[PAD : 2 * PAD, 0:LANES]
-        own = lax.dot_general(lat, fresh, contract, preferred_element_type=jnp.float32)
-        own = own + lax.dot_general(rope, fresh_rope, contract, preferred_element_type=jnp.float32)
-        factor = softmax_scale * log2e
-        weights = jnp.exp2(scores * factor - peak * factor)
-        total = jnp.sum(weights, axis=1, keepdims=True)
-        summed = jnp.dot(
-            weights.astype(jnp.bfloat16), keys[:, 0:width], preferred_element_type=jnp.float32
+        own = lax.dot_general(
+            query[:, 0:width], fresh, contract, preferred_element_type=jnp.float32
+        )
+        own = own + lax.dot_general(
+            query[:, width:], fresh_rope, contract, preferred_element_type=jnp.float32
         )
         row_step = lax.broadcasted_iota(jnp.int32, (q_rows, 1), 0) // heads
-        columns = [
-            jnp.where(row_step >= j, own[:, j : j + 1], -1e30) for j in range(steps)
-        ]
+        columns = [jnp.where(row_step >= j, own[:, j : j + 1], -1e30) for j in range(steps)]
         top = peak
         for column in columns:
             top = jnp.maximum(top, column)
         share = jnp.exp2((peak - top) * factor)
-        numerator = summed * share
+        parts = [
+            jnp.where(row_step >= j, jnp.exp2((column - top) * factor), 0.0)
+            for j, column in enumerate(columns)
+        ]
         denominator = total * share
+        for part in parts:
+            denominator = denominator + part
+        inverse = 1.0 / denominator
         fresh32 = fresh.astype(jnp.float32)
-        for j, column in enumerate(columns):
-            weight = jnp.where(row_step >= j, jnp.exp2((column - top) * factor), 0.0)
-            numerator = numerator + weight * fresh32[j : j + 1, :]
-            denominator = denominator + weight
-        return (numerator / denominator).astype(jnp.bfloat16)
+        value = summed * (share * inverse)
+        for j, part in enumerate(parts):
+            value = value + (part * inverse) * fresh32[j : j + 1, :]
+        return value.astype(jnp.bfloat16)
 
     def load_keys(caches, keys, sems):
         copies = []
@@ -178,14 +188,12 @@
             copy.start()
         return copies
 
-    def spread_keys(rope_scratch, keys):
-        matrix = spread_matrix(raw_group, width)
+    def spread_keys(i, rope_scratch, keys, matrix):
         grown = raw_group * width // (LANES // 2)
-        for i in range(2):
-            for start in range(0, rope_rows, raw_group):
-                part = spread(matrix, rope_scratch[i, start : start + raw_group, :])
-                first = i * half + start * (width // (LANES // 2))
-                keys[first : first + grown, width : width + LANES] = part.astype(jnp.bfloat16)
+        for start in range(0, rope_rows, raw_group):
+            part = spread(matrix, rope_scratch[i, start : start + raw_group, :])
+            first = i * half + start * (width // (LANES // 2))
+            keys[first : first + grown, width : width + LANES] = part.astype(jnp.bfloat16)
 
     def kernel(slot, kinds, given_slots, has_placed, *refs):
         refs = list(refs)
@@ -202,7 +210,7 @@
             refs.pop(0)
         gives = [refs.pop(0) for kind in kinds if kind == "give"]
         placed = refs.pop(0) if ("keep" in kinds or given_slots) else None
-        keys, rope_scratch, result, sems, place_sems = refs
+        keys, rope_scratch, query_all, scores, summed, result, sems, place_sems = refs
         copies = load_keys(caches, keys, sems)
         rope_copies = []
         for i in range(2):
@@ -218,24 +226,57 @@
             )
             copy.start()
             placing.append(copy)
-        for copy in rope_copies:
-            copy.wait()
-        spread_keys(rope_scratch, keys)
-        for copy in copies:
-            copy.wait()
-        for kind, query in zip(kinds, queries):
+        matrix = spread_matrix(raw_group, width)
+        fresh_parts = []
+        for number, (kind, query) in enumerate(zip(kinds, queries)):
             if kind == "give":
+                middle = q_rows + token_rope
                 packed = query.at[0]
-                middle = q_rows + token_rope
-                value = one_token(
-                    packed[0:q_rows, :],
-                    packed[q_rows:middle, :],
-                    packed[middle : middle + 2 * PAD, :],
-                    keys,
+                lat, raw = packed[0:q_rows, :], packed[q_rows:middle, :]
+                fresh_parts.append(packed[middle : middle + 2 * PAD, :])
+            else:
+                lat, raw = query[0][0], query[1][0]
+                fresh_parts.append(query[2][0])
+            put_query(query_all, number, lat, raw, matrix)
+        peak = None
+        for i in range(2):
+            rope_copies[i].wait()
+            spread_keys(i, rope_scratch, keys, matrix)
+            copies[i].wait()
+            for start in range(i * half, (i + 1) * half, chunk):
+                part = lax.dot_general(
+                    query_all[...],
+                    keys[start : start + chunk, :],
+                    contract,
+                    preferred_element_type=jnp.float32,
                 )
+                scores[:, start : start + chunk] = part
+                high = jnp.max(part, axis=1, keepdims=True)
+                peak = high if peak is None else jnp.maximum(peak, high)
+        scaled = peak * factor
+        total = None
+        for start in range(0, 2 * half, chunk):
+            weights = jnp.exp2(scores[:, start : start + chunk] * factor - scaled)
+            part = jnp.sum(weights, axis=1, keepdims=True)
+            value = jnp.dot(
+                weights.astype(jnp.bfloat16),
+                keys[start : start + chunk, 0:width],
+                preferred_element_type=jnp.float32,
+            )
+            if start == 0:
+                total = part
+                summed[...] = value
+            else:
+                total = total + part
+                summed[...] += value
+        for number, kind in enumerate(kinds):
+            rows = slice(number * q_rows, (number + 1) * q_rows)
+            value = merge_own(
+                query_all[rows, :], fresh_parts[number], peak[rows], total[rows], summed[rows, :]
+            )
+            if kind == "give":
                 gives.pop(0)[...] = value
             else:
-                value = one_token(query[0][0], query[1][0], query[2][0], keys)
                 result[...] = value
                 copy = pltpu.make_async_copy(
                     result, placed.at[row_for(slot, 0, slot_ref, own_ref)], place_sems.at[0]
@@ -264,7 +305,8 @@
                 in_specs += [pl.BlockSpec((1, x.shape[1], width), chosen) for x in stay]
                 operands += stay
         given_slots = tuple(number for number, _ in arrived)
-        in_specs += [any_spec] * (2 + len(arrived))
+        in_specs += [any_spec] * 2
+        in_specs += [pl.BlockSpec((q_rows, width), lambda i, *_: (0, 0)) for _ in arrived]
         operands += [*caches, *(value for _, value in arrived)]
         has_placed = placed is not None
         out_shape, out_specs, alias = [], [], {}
@@ -292,17 +334,16 @@
                 scratch_shapes=[
                     pltpu.VMEM((all_rows, width + LANES), jnp.bfloat16),
                     pltpu.VMEM((2, rope_rows, width), jnp.bfloat16),
+                    pltpu.VMEM((n_tok * q_rows, width + LANES), jnp.bfloat16),
+                    pltpu.VMEM((n_tok * q_rows, all_rows), jnp.float32),
+                    pltpu.VMEM((n_tok * q_rows, width), jnp.float32),
                     pltpu.VMEM((q_rows, width), jnp.bfloat16),
                     pltpu.SemaphoreType.DMA((4,)),
                     pltpu.SemaphoreType.DMA((1 + max(1, len(arrived)),)),
                 ],
             ),
             input_output_aliases=alias,
-            cost_estimate=pl.CostEstimate(
-                flops=2 * n_tok * q_rows * all_rows * (2 * width + LANES),
-                bytes_accessed=2 * all_rows * (width + LANES) + 4 * n_tok * q_rows * width,
-                transcendentals=n_tok * q_rows * all_rows,
-            ),
+            cost_estimate=SMALL,
             compiler_params=pltpu.CompilerParams(vmem_limit_bytes=32 * 1024 * 1024),
             name="attend_" + "_".join(kinds),
         )(*scalars, *operands)
@@ -377,11 +418,54 @@
         in_specs=[pl.BlockSpec(memory_space=pltpu.SMEM)]
         + [pl.BlockSpec(memory_space=pltpu.VMEM)] * 3,
         out_specs=(pl.BlockSpec(memory_space=pltpu.VMEM),) * 2,
-        cost_estimate=pl.CostEstimate(
-            flops=2 * slots * tokens.size, bytes_accessed=3 * tokens.size, transcendentals=0
-        ),
+        cost_estimate=SMALL,
         name="dispatch",
     )(block, routes, gates, tokens)
+
+
+def experts_kernel(mine_ref, theirs_ref, gate_ref, up_ref, down_ref, keep_ref, send_ref):
+    rows = jnp.concatenate([mine_ref[...], theirs_ref[...]], axis=0)
+    gate = jnp.dot(rows, gate_ref[0], preferred_element_type=jnp.float32)
+    lifted = jnp.dot(rows, up_ref[0], preferred_element_type=jnp.float32)
+    hidden = (gate / (1.0 + jnp.exp(-gate)) * lifted).astype(jnp.bfloat16)
+    parts = jnp.dot(hidden, down_ref[0], preferred_element_type=jnp.float32)
+    count = mine_ref.shape[0]
+    keep_ref[...] = parts[:count]
+    send_ref[...] = parts[count:].astype(jnp.bfloat16)
+
+
+def run_experts(mine, theirs, w_gate, w_up, w_down):
+    return pl.pallas_call(
+        experts_kernel,
+        out_shape=(
+            jax.ShapeDtypeStruct(mine.shape, jnp.float32),
+            jax.ShapeDtypeStruct(mine.shape, jnp.bfloat16),
+        ),
+        cost_estimate=SMALL,
+        compiler_params=pltpu.CompilerParams(vmem_limit_bytes=32 * 1024 * 1024),
+        name="experts",
+    )(mine, theirs, w_gate, w_up, w_down)
+
+
+def halve_kernel(sum_ref, arrived_ref, keep_ref, send_ref):
+    count = keep_ref.shape[0]
+    total = sum_ref[...] + arrived_ref[...].astype(jnp.float32)
+    keep_ref[...] = total[:count]
+    send_ref[...] = total[count:].astype(jnp.bfloat16)
+
+
+def halve(kept, arrived):
+    shape = (kept.shape[0] // 2, kept.shape[1])
+    return pl.pallas_call(
+        halve_kernel,
+        out_shape=(
+            jax.ShapeDtypeStruct(shape, jnp.float32),
+            jax.ShapeDtypeStruct(shape, jnp.bfloat16),
+        ),
+        cost_estimate=SMALL,
+        compiler_params=pltpu.CompilerParams(vmem_limit_bytes=16 * 1024 * 1024),
+        name="halve",
+    )(kept, arrived)
 
 
 def on_device(
@@ -421,10 +505,6 @@
     second_b = line_hop(first_b, tok_rows, outward)
     first_c = line_hop(cache_a, tok_rows, inner)
     second_c = line_hop(first_c, tok_rows, outward)
-    cache_b = jnp.where(middle, first_b, second_b)
-    cache_c = jnp.where(middle, first_c, second_c)
-    caches = [own_cache, cache_a, cache_b, cache_c]
-    caches = [(cache, swapped(cache, "expert", 0)) for cache in caches]
 
     q_lat = q_latent.reshape(tok_rows, q_rows, width)
     rope_raw = q_rope.reshape(tok_rows, q_rows * rope_width // width, width)
@@ -437,35 +517,8 @@
     )
     scalars = (branch_slot, own[None])
     stay = (q_lat, rope_raw, fresh)
-    leave = pack_leaving(*scalars, *stay)
-    guest = swapped(leave, "branch", 0)
-
-    attend = build_attend(head_count, step_count, width, half, rope_rows, 32)
-    placed = None
-    waiting = []
-    for slot in range(line):
-        kinds = [("give", "keep")] if slot < line - 1 else [("give",), ("keep",)]
-        given = None
-        for kind in kinds:
-            keeps = "keep" in kind
-            results = attend(
-                scalars,
-                kind,
-                slot,
-                guest,
-                stay,
-                caches[slot],
-                waiting if keeps else [],
-                placed if keeps else None,
-            )
-            if "give" in kind:
-                given = results[0]
-            if keeps:
-                placed = results[-1]
-        waiting = [(slot, swapped(given, "branch", 0))]
-    placed = place(scalars, line - 1, waiting[0][1], placed)
-    attended = placed.reshape(tok_rows, step_count, head_count, width)
-
+
+    attend = build_attend(head_count, step_count, width, half, rope_rows, 32, half // 2)
     model_width = moe_input.shape[-1]
     tok_total = tok_rows * step_count
     device = branch * lax.axis_size("expert") + lax.axis_index("expert")
@@ -474,7 +527,7 @@
     shard_branches = SHARDS // cores
     block = device // SHARDS
     outgoing, share = dispatch(
-        block[None],
+        after(block[None], own_cache),
         routes.reshape(tok_total, -1),
         route_gate.reshape(tok_total, -1),
         moe_input.reshape(tok_total, model_width),
@@ -492,24 +545,61 @@
         ]
         return lax.ppermute(x, "branch", list(enumerate(there)))
 
+    beside = swapped(outgoing, "branch", 0)
+    leave = pack_leaving(branch_slot, after(own[None], beside), *stay)
+    guest = swapped(leave, "branch", 0)
     ways = [(k, m) for k in range(experts) for m in range(around)]
-    rows = []
+    pieces = []
     for k, m in ways:
-        piece = outgoing[k * CAP : (k + 1) * CAP]
-        rows.append(piece if (k, m) == (0, 0) else along(piece, k, m))
-    rows = jnp.concatenate(rows, axis=0)
-    bits = [("branch", 0)] + [("expert", b) for b in reversed(range(cores.bit_length() - 1))]
-    for axis, bit in bits:
-        rows = jnp.concatenate([rows, swapped(rows, axis, bit)], axis=0)
-    gate_value = jnp.dot(rows, w_gate[0], preferred_element_type=jnp.float32)
-    lifted = jnp.dot(rows, w_up[0], preferred_element_type=jnp.float32)
-    hidden = (jax.nn.silu(gate_value) * lifted).astype(jnp.bfloat16)
-    parts = jnp.dot(hidden, w_down[0], preferred_element_type=jnp.float32)
-    for axis, bit in reversed(bits):
-        count = parts.shape[0] // 2
-        parts = parts[:count] + swapped(
-            parts[count:].astype(jnp.bfloat16), axis, bit
-        ).astype(jnp.float32)
+        piece = jnp.concatenate([x[k * CAP : (k + 1) * CAP] for x in (outgoing, beside)], axis=0)
+        pieces.append(piece if (k, m) == (0, 0) else along(piece, k, m))
+
+    def attend_slot(slot, cache, kinds, waiting, placed):
+        keeps = "keep" in kinds
+        results = attend(
+            scalars,
+            kinds,
+            slot,
+            guest,
+            stay,
+            cache,
+            waiting if keeps else [],
+            placed if keeps else None,
+        )
+        given = results[0] if "give" in kinds else None
+        return given, (results[-1] if keeps else placed)
+
+    def both_halves(cache):
+        return cache, swapped(cache, "expert", 0)
+
+    guest = after(guest, cache_a, first_b)
+    both = ("give", "keep")
+    given_0, placed = attend_slot(0, both_halves(own_cache), both, [], None)
+    back_0 = swapped(given_0, "branch", 0)
+    given_1, placed = attend_slot(1, both_halves(cache_a), both, [], placed)
+    back_1 = swapped(given_1, "branch", 0)
+
+
+    first_c, second_b, given_1, *pieces = lax.optimization_barrier(
+        (first_c, second_b, given_1, *pieces)
+    )
+    rows = jnp.concatenate([x[:CAP] for x in pieces] + [x[CAP:] for x in pieces], axis=0)
+    cache_b = jnp.where(middle, first_b, second_b)
+    kept, sent = run_experts(rows, swapped(rows, "expert", 0), w_gate, w_up, w_down)
+    kept, sent = halve(kept, swapped(sent, "expert", 0))
+    given_2, placed = attend_slot(2, both_halves(cache_b), both, [(0, back_0)], placed)
+    back_2 = swapped(given_2, "branch", 0)
+
+    second_c, given_2, kept, sent = lax.optimization_barrier((second_c, given_2, kept, sent))
+    cache_c = both_halves(jnp.where(middle, first_c, second_c))
+    given_3, _ = attend_slot(3, cache_c, ("give",), [], None)
+    back_3 = swapped(given_3, "branch", 0)
+    _, placed = attend_slot(3, cache_c, ("keep",), [(1, back_1), (2, back_2)], placed)
+    placed = place(scalars, 3, back_3, placed)
+    attended = placed.reshape(tok_rows, step_count, head_count, width)
+
+    parts = kept + swapped(sent, "branch", 0).astype(jnp.float32)
+    parts = after(parts, given_3)
     sums = [0.0] * experts
     for number, (k, m) in enumerate(ways):
         piece = parts[number * CAP : (number + 1) * CAP]

time: 162 us -> 141 us (0.87)
  waiting for transfers between devices: 69.8 us -> 30.3 us
  local copies, waits for them, and re-layouts: 13.3 us -> 27.3 us
  starting transfers between devices: 21.6 us -> 32.8 us
  Pallas kernels: 47.4 us -> 42.4 us
  matrix products: 4.21 us -> 0 us
    ppermute x5, waiting for transfers between devices: 44.1 us -> 17.4 us  [line_hop(): return lax.ppermute(x, 'branch', pairs)]
    unnamed x32 -> x64, local copies, waits for them, and re-layouts: 5.81 us -> 17.1 us
    ppermute x13, waiting for transfers between devices: 20 us -> 12.9 us  [swapped(): lax.ppermute(x, axis, [(i, i ^ 1 << bit) for i in range(lax.axis_size(axi...]
    ppermute x6, waiting for transfers between devices: 5.67 us -> 0.02 us  [along(): return lax.ppermute(x, 'branch', list(enumerate(there)))]
    dot_general x2 -> x0, matrix products: 4.21 us -> none  [the longest x1 2.31 us: on_device(): parts = jnp.dot(hidden, w_down[0], preferred_element_type=jnp.float32)]
    ppermute x5, starting transfers between devices: 5.16 us -> 9.17 us  [line_hop(): return lax.ppermute(x, 'branch', pairs)]
    pallas_call x5, Pallas kernels: 38.8 us -> 34.9 us  [call(): pl.pallas_call(functools.partial(kernel, slot, kinds, given_slots, has_pl...]
    ppermute x6, starting transfers between devices: 8.75 us -> 12.6 us  [along(): return lax.ppermute(x, 'branch', list(enumerate(there)))]
  transfers between devices with their start and end apart: 24 -> 24, of which waited for: 9 -> 6; matrix products, arithmetic and copies ran while one was open for 5% -> 10% of each run, Pallas kernels for 27% -> 28%
where the time goes in v3:
time: 141 us; the launch traced here: 140 us
  Pallas kernels  42.4 us (30%)
  starting transfers between devices  32.8 us (23%)
  waiting for transfers between devices  30.3 us (21%)
  local copies, waits for them, and re-layouts  27.3 us (19%)
  other arithmetic  5.9 us (4%)
    pallas_call x5, Pallas kernels, call(): pl.pallas_call(functools.partial(kernel, slot, kinds, given_slots, has_pl...  34.9 us
    ppermute x5, waiting for transfers between devices, line_hop(): return lax.ppermute(x, 'branch', pairs)  17.4 us
    unnamed x64, local copies, waits for them, and re-layouts  17.1 us
    ppermute x13, waiting for transfers between devices, swapped(): lax.ppermute(x, axis, [(i, i ^ 1 << bit) for i in range(lax.axis_size(axi...  12.9 us
    ppermute x6, starting transfers between devices, along(): return lax.ppermute(x, 'branch', list(enumerate(there)))  12.6 us
    ppermute x13, starting transfers between devices, swapped(): lax.ppermute(x, axis, [(i, i ^ 1 << bit) for i in range(lax.axis_size(axi...  11.1 us
    ppermute x5, starting transfers between devices, line_hop(): return lax.ppermute(x, 'branch', pairs)  9.17 us
    slice x2, local copies, waits for them, and re-layouts, on_device(): x[CAP:]  3.24 us
  transfers between devices with their start and end apart: 24, of which 6 were waited for; matrix products, arithmetic and copies ran while one was open for 10% of the time, Pallas kernels for 28%

profile of v3, /device:TPU:0, one launch (start us, length us, event | category | flops | bytes accessed | tf_op | source)
XLA Modules:
  0.0 139.8 jit_solution(11420176879354905457)
XLA Ops:
  0.6 1.2 copy-done.19
  2.8 1.1 pack_cache.1.refs_6_
  3.9 3.0 %collective-permute-start.2 = (bf16[1152,512]{1,0:T(8,128)(2,1)}, bf16[1152,512]{1,0:T(8,128)(2,1)}, u32[]{:S(2)}, u32[]{:S(2)}) collective-permute-start(bf16[1152,512]{1,0:T(8,128)(2,1)} %pack_cache.1.refs_6_), channel_id=1, source_target_pairs={{0,4},{4,0},{8,12},{12,8},{2,6},{6,2},{10,14},{14,10},{1,5},{5,1},... | collective-permute-start | bytes 3538952 | tf_op jit(solution)/shard_map/ppermute | solution.py:34
  6.9 1.7 %collective-permute-start.3 = (bf16[1152,512]{1,0:T(8,128)(2,1)}, bf16[1152,512]{1,0:T(8,128)(2,1)}, u32[]{:S(2)}, u32[]{:S(2)}) collective-permute-start(bf16[1152,512]{1,0:T(8,128)(2,1)} %pack_cache.1.refs_6_), channel_id=1, source_target_pairs={{4,8},{8,4},{6,10},{10,6},{5,9},{9,5},{7,11},{11,7},{20,24},{24,20... | collective-permute-start | bytes 3538952 | tf_op jit(solution)/shard_map/ppermute | solution.py:34
  8.6 1.7 %reshape.29.tokens_ref = bf16[16,7168]{1,0:T(8,128)(2,1)} reshape(bf16[8,2,7168]{2,1,0:T(2,128)(2,1)} %param.20) | data formatting | bytes 458752 | tf_op jit(solution)/shard_map/reshape | solution.py:533
  10.3 1.9 %dispatch.1 = (bf16[4,7168]{1,0:T(4,128)(2,1)}, f32[16,4]{1,0:T(8,128)}) custom-call(s32[1]{0:T(128)} %bitcast.1.block_ref, s32[16,8]{1,0:T(8,128)} %bitcast.16, f32[16,8]{1,0:T(8,128)} %bitcast.17, bf16[16,7168]{1,0:T(8,128)(2,1)} %reshape.29.tokens_ref), custom_call_target="tpu_custom_call" | custom-call | bytes 1024 | tf_op jit(solution)/shard_map/dispatch/pallas_call | solution.py:412
  12.2 1.5 %collective-permute-start = (bf16[4,7168]{1,0:T(4,128)(2,1)}, bf16[4,7168]{1,0:T(4,128)(2,1)S(1)}, u32[]{:S(2)}, u32[]{:S(2)}) collective-permute-start(bf16[4,7168]{1,0:T(4,128)(2,1)} %get-tuple-element.28), channel_id=1, source_target_pairs={{0,2},{2,0},{4,6},{6,4},{8,10},{10,8},{12,14},{14,12},{1,3},{3,1},... | collective-permute-start | bytes 172040 | tf_op jit(solution)/shard_map/ppermute | solution.py:26
  14.9 1.8 %collective-permute-done = bf16[4,7168]{1,0:T(4,128)(2,1)S(1)} collective-permute-done((bf16[4,7168]{1,0:T(4,128)(2,1)}, bf16[4,7168]{1,0:T(4,128)(2,1)S(1)}, u32[]{:S(2)}, u32[]{:S(2)}) %collective-permute-start) | collective-permute-done | bytes 57376 | tf_op jit(solution)/shard_map/ppermute | solution.py:26
  16.8 1.2 pack_leaving.1
  18.6 1.5 %collective-permute-start.1 = (bf16[4,320,512]{2,1,0:T(8,128)(2,1)S(1)}, bf16[4,320,512]{2,1,0:T(8,128)(2,1)S(1)}, u32[]{:S(2)}, u32[]{:S(2)}) collective-permute-start(bf16[4,320,512]{2,1,0:T(8,128)(2,1)S(1)} %pack_leaving.1), channel_id=1, source_target_pairs={{0,2},{2,0},{4,6},{6,4},{8,10},{10,8},{12,14},{14,12},{1,3},{3,1},... | collective-permute-start | bytes 3932168 | tf_op jit(solution)/shard_map/ppermute | solution.py:26
  20.2 13.0 %collective-permute-done.2.refs_6_ = bf16[1152,512]{1,0:T(8,128)(2,1)} collective-permute-done((bf16[1152,512]{1,0:T(8,128)(2,1)}, bf16[1152,512]{1,0:T(8,128)(2,1)}, u32[]{:S(2)}, u32[]{:S(2)}) %collective-permute-start.2) | collective-permute-done | bytes 1179680 | tf_op jit(solution)/shard_map/ppermute | solution.py:34
  33.2 1.7 %collective-permute-start.4 = (bf16[1152,512]{1,0:T(8,128)(2,1)}, bf16[1152,512]{1,0:T(8,128)(2,1)}, u32[]{:S(2)}, u32[]{:S(2)}) collective-permute-start(bf16[1152,512]{1,0:T(8,128)(2,1)} %collective-permute-done.2.refs_6_), channel_id=1, source_target_pairs={{4,8},{8,4},{6,10},{10,6},{5,9},{9,5},{7,11},{11,7},{20,24},{24,20... | collective-permute-start | bytes 3538952 | tf_op jit(solution)/shard_map/ppermute | solution.py:34
  34.9 1.3 collective-permute-start.5
  37.0 3.8 %collective-permute-start.10 = (bf16[4,7168]{1,0:T(4,128)(2,1)}, bf16[4,7168]{1,0:T(4,128)(2,1)}, u32[]{:S(2)}, u32[]{:S(2)}) collective-permute-start(bf16[4,7168]{1,0:T(4,128)(2,1)} %pad_maximum_fusion.2), channel_id=1, source_target_pairs={{0,12},{2,14},{4,8},{6,10},{8,4},{10,6},{12,0},{14,2},{1,13},{3,15... | collective-permute-start | bytes 172040 | tf_op jit(solution)/shard_map/ppermute | solution.py:546
  40.8 8.3 %collective-permute-done.1.refs_2_ = bf16[4,320,512]{2,1,0:T(8,128)(2,1)S(1)} collective-permute-done((bf16[4,320,512]{2,1,0:T(8,128)(2,1)S(1)}, bf16[4,320,512]{2,1,0:T(8,128)(2,1)S(1)}, u32[]{:S(2)}, u32[]{:S(2)}) %collective-permute-start.1) | collective-permute-done | bytes 1310752 | tf_op jit(solution)/shard_map/ppermute | solution.py:26
  49.1 3.4 %collective-permute-start.8 = (bf16[4,7168]{1,0:T(4,128)(2,1)S(1)}, bf16[4,7168]{1,0:T(4,128)(2,1)S(1)}, u32[]{:S(2)}, u32[]{:S(2)}) collective-permute-start(bf16[4,7168]{1,0:T(4,128)(2,1)S(1)} %pad_maximum_fusion.1), channel_id=1, source_target_pairs={{0,4},{2,6},{4,0},{6,2},{8,12},{10,14},{12,8},{14,10},{1,5},{3,7},... | collective-permute-start | bytes 172040 | tf_op jit(solution)/shard_map/ppermute | solution.py:546
  52.5 1.1 copy-done.17
  53.6 0.9 copy-done.4
  54.6 0.9 copy-done.8
  55.5 7.7 %attend_give_keep.3 = (bf16[256,512]{1,0:T(8,128)(2,1)S(1)}, bf16[8,256,512]{2,1,0:T(8,128)(2,1)}) custom-call(s32[8]{0:T(128)S(1)} %copy-done.23, s32[1]{0:T(128)} %bitcast.own_ref.refs_1_, bf16[4,320,512]{2,1,0:T(8,128)(2,1)S(1)} %collective-permute-done.1.refs_2_, bf16[8,256,512]{2,1,0:T(8,128)(2,1)S(1)} %bitcast.9, bf16[8,32,512]{2,1,0:T(8,128)(2,1)S(1)} %copy-done.8, ...), custom_call_target="tpu_custom_call" | custom-call | bytes 1024 | tf_op jit(solution)/shard_map/attend_give_keep/pallas_call | solution.py:326
  63.3 8.0 %attend_give_keep.4 = (bf16[256,512]{1,0:T(8,128)(2,1)}, bf16[8,256,512]{2,1,0:T(8,128)(2,1)}) custom-call(s32[8]{0:T(128)S(1)} %copy-done.23, s32[1]{0:T(128)} %bitcast.own_ref.refs_1_, bf16[4,320,512]{2,1,0:T(8,128)(2,1)S(1)} %collective-permute-done.1.refs_2_, bf16[8,256,512]{2,1,0:T(8,128)(2,1)S(1)} %bitcast.10, ...), custom_call_target="tpu_custom_call", output_to_operand_aliasing={{1}: (8, {})} | custom-call | bytes 1024 | tf_op jit(solution)/shard_map/attend_give_keep/pallas_call | solution.py:326
  71.4 2.4 %broadcast_select_fusion.1.refs_6_ = bf16[1152,512]{1,0:T(8,128)(2,1)} fusion(bf16[1152,512]{1,0:T(8,128)(2,1)} %collective-permute-done.3, bf16[1152,512]{1,0:T(8,128)(2,1)} %collective-permute-done.5, pred[]{:T(512)S(6)} %and.22), kind=kLoop, calls=%fused_computation.2 | loop fusion | flops 589824 | bytes 3538945 | tf_op jit(solution)/shard_map/jit(_where)/select_n | solution.py:587
  73.8 1.6 %fusion.4 = (bf16[2,7168]{1,0:T(2,128)(2,1)S(1)}, bf16[2,7168]{1,0:T(2,128)(2,1)S(1)}, bf16[2,7168]{1,0:T(2,128)(2,1)S(1)}, bf16[2,7168]{1,0:T(2,128)(2,1)}) fusion(bf16[4,7168]{1,0:T(4,128)(2,1)} %collective-permute-done.10, bf16[4,7168]{1,0:T(4,128)(2,1)} %collective-permute-done.9), kind=kLoop, calls=%fused_computation.15 | loop fusion | bytes 229376 | tf_op jit(solution)/shard_map/slice | solution.py:586
  75.4 1.5 %collective-permute-start.11 = (bf16[1152,512]{1,0:T(8,128)(2,1)}, bf16[1152,512]{1,0:T(8,128)(2,1)}, u32[]{:S(2)}, u32[]{:S(2)}) collective-permute-start(bf16[1152,512]{1,0:T(8,128)(2,1)} %collective-permute-done.4), channel_id=1, source_target_pairs={{4,0},{8,12},{6,2},{10,14},{5,1},{9,13},{7,3},{11,15},{20,16},{24,... | collective-permute-start | bytes 3538952 | tf_op jit(solution)/shard_map/ppermute | solution.py:34
  76.9 1.6 %fusion.6 = (bf16[2,7168]{1,0:T(2,128)(2,1)}, bf16[2,7168]{1,0:T(2,128)(2,1)}, bf16[2,7168]{1,0:T(2,128)(2,1)}, bf16[2,7168]{1,0:T(2,128)(2,1)}) fusion(bf16[4,7168]{1,0:T(4,128)(2,1)} %copy-done.28, bf16[4,7168]{1,0:T(4,128)(2,1)S(1)} %pad_maximum_fusion.1), kind=kLoop, calls=%fused_computation.17 | loop fusion | bytes 229376 | tf_op jit(solution)/shard_map/slice | solution.py:586
  78.5 3.2 %concatenate.20.mine_ref = bf16[16,7168]{1,0:T(8,128)(2,1)} concatenate(bf16[2,7168]{1,0:T(2,128)(2,1)} %get-tuple-element.69, bf16[2,7168]{1,0:T(2,128)(2,1)} %get-tuple-element.60, bf16[2,7168]{1,0:T(2,128)(2,1)S(1)} %get-tuple-element.67, bf16[2,7168]{1,0:T(2,128)(2,1)S(1)} %get-tuple-element.56, bf16[2,7168]{1,0:T(2,128)(2,1)} %get-tuple-element.70, ...), dimensions={0} | concatenate | bytes 458752 | tf_op jit(solution)/shard_map/concatenate | solution.py:586
  82.2 1.5 %collective-permute-start.13 = (bf16[256,512]{1,0:T(8,128)(2,1)}, bf16[256,512]{1,0:T(8,128)(2,1)S(1)}, u32[]{:S(2)}, u32[]{:S(2)}) collective-permute-start(bf16[256,512]{1,0:T(8,128)(2,1)} %copy-done.24), channel_id=1, source_target_pairs={{0,2},{2,0},{4,6},{6,4},{8,10},{10,8},{12,14},{14,12},{1,3},{3,1},... | collective-permute-start | bytes 786440 | tf_op jit(solution)/shard_map/ppermute | solution.py:26
  83.7 1.5 %copy-done.14 = bf16[1,7168,128]{2,1,0:T(8,128)(2,1)S(1)} copy-done((bf16[1,7168,128]{2,1,0:T(8,128)(2,1)S(1)}, bf16[1,7168,128]{2,1,0:T(8,128)(2,1)}, u32[]{:S(2)}) %copy-start.14) | copy-done | bytes 1835032
  85.2 1.5 %copy-done.15 = bf16[1,7168,128]{2,1,0:T(8,128)(2,1)S(1)} copy-done((bf16[1,7168,128]{2,1,0:T(8,128)(2,1)S(1)}, bf16[1,7168,128]{2,1,0:T(8,128)(2,1)}, u32[]{:S(2)}) %copy-start.15) | copy-done | bytes 1835032
  86.7 1.5 %copy-done.16 = bf16[1,128,7168]{2,1,0:T(8,128)(2,1)S(1)} copy-done((bf16[1,128,7168]{2,1,0:T(8,128)(2,1)S(1)}, bf16[1,128,7168]{2,1,0:T(8,128)(2,1)}, u32[]{:S(2)}) %copy-start.16) | copy-done | bytes 1835032
  89.1 1.0 experts.1
  90.4 1.5 %collective-permute-start.18 = (bf16[256,512]{1,0:T(8,128)(2,1)}, bf16[256,512]{1,0:T(8,128)(2,1)}, u32[]{:S(2)}, u32[]{:S(2)}) collective-permute-start(bf16[256,512]{1,0:T(8,128)(2,1)} %get-tuple-element.32), channel_id=1, source_target_pairs={{0,2},{2,0},{4,6},{6,4},{8,10},{10,8},{12,14},{14,12},{1,3},{3,1},... | collective-permute-start | bytes 786440 | tf_op jit(solution)/shard_map/ppermute | solution.py:26
  92.0 8.5 %attend_give_keep.5 = (bf16[256,512]{1,0:T(8,128)(2,1)}, bf16[8,256,512]{2,1,0:T(8,128)(2,1)}) custom-call(s32[8]{0:T(128)S(1)} %copy-done.23, s32[1]{0:T(128)} %bitcast.own_ref.refs_1_, bf16[4,320,512]{2,1,0:T(8,128)(2,1)S(1)} %collective-permute-done.1.refs_2_, bf16[8,256,512]{2,1,0:T(8,128)(2,1)S(1)} %bitcast.11, ...), custom_call_target="tpu_custom_call", output_to_operand_aliasing={{1}: (9, {})} | custom-call | bytes 1024 | tf_op jit(solution)/shard_map/attend_give_keep/pallas_call | solution.py:326
  100.5 1.2 collective-permute-start.19
  101.7 4.3 %collective-permute-done.11 = bf16[1152,512]{1,0:T(8,128)(2,1)} collective-permute-done((bf16[1152,512]{1,0:T(8,128)(2,1)}, bf16[1152,512]{1,0:T(8,128)(2,1)}, u32[]{:S(2)}, u32[]{:S(2)}) %collective-permute-start.11) | collective-permute-done | bytes 1179680 | tf_op jit(solution)/shard_map/ppermute | solution.py:34
  106.0 1.5 %collective-permute-start.20 = (bf16[8,7168]{1,0:T(8,128)(2,1)S(1)}, bf16[8,7168]{1,0:T(8,128)(2,1)S(1)}, u32[]{:S(2)}, u32[]{:S(2)}) collective-permute-start(bf16[8,7168]{1,0:T(8,128)(2,1)S(1)} %get-tuple-element.50), channel_id=1, source_target_pairs={{0,2},{2,0},{4,6},{6,4},{8,10},{10,8},{12,14},{14,12},{1,3},{3,1},... | collective-permute-start | bytes 344072 | tf_op jit(solution)/shard_map/ppermute | solution.py:26
  107.5 1.4 broadcast_select_fusion.refs_3_.refs_5_
  109.0 2.4 %collective-permute-done.20 = bf16[8,7168]{1,0:T(8,128)(2,1)S(1)} collective-permute-done((bf16[8,7168]{1,0:T(8,128)(2,1)S(1)}, bf16[8,7168]{1,0:T(8,128)(2,1)S(1)}, u32[]{:S(2)}, u32[]{:S(2)}) %collective-permute-start.20) | collective-permute-done | bytes 114720 | tf_op jit(solution)/shard_map/ppermute | solution.py:26
  111.8 4.5 %attend_give.1 = bf16[256,512]{1,0:T(8,128)(2,1)S(1)} custom-call(s32[8]{0:T(128)S(1)} %copy-done.23, s32[1]{0:T(128)} %bitcast.own_ref.refs_1_, bf16[4,320,512]{2,1,0:T(8,128)(2,1)S(1)} %collective-permute-done.1.refs_2_, bf16[1152,512]{1,0:T(8,128)(2,1)S(1)} %broadcast_select_fusion.refs_3_.refs_5_, ...), custom_call_target="tpu_custom_call" | custom-call | bytes 1024 | tf_op jit(solution)/shard_map/attend_give/pallas_call | solution.py:326
  117.1 2.9 %collective-permute-start.21 = (bf16[2,7168]{1,0:T(2,128)(2,1)S(1)}, bf16[2,7168]{1,0:T(2,128)(2,1)S(1)}, u32[]{:S(2)}, u32[]{:S(2)}) collective-permute-start(bf16[2,7168]{1,0:T(2,128)(2,1)S(1)} %get-tuple-element.52), channel_id=1, source_target_pairs={{0,4},{2,6},{4,0},{6,2},{8,12},{10,14},{12,8},{14,10},{1,5},{3,7},... | collective-permute-start | bytes 86024 | tf_op jit(solution)/shard_map/ppermute | solution.py:546
  120.2 1.5 %collective-permute-start.17 = (bf16[256,512]{1,0:T(8,128)(2,1)}, bf16[256,512]{1,0:T(8,128)(2,1)S(1)}, u32[]{:S(2)}, u32[]{:S(2)}) collective-permute-start(bf16[256,512]{1,0:T(8,128)(2,1)} %copy-done.21), channel_id=1, source_target_pairs={{0,2},{2,0},{4,6},{6,4},{8,10},{10,8},{12,14},{14,12},{1,3},{3,1},... | collective-permute-start | bytes 786440 | tf_op jit(solution)/shard_map/ppermute | solution.py:26
  122.6 1.5 %collective-permute-start.23 = (bf16[2,7168]{1,0:T(2,128)(2,1)S(1)}, bf16[2,7168]{1,0:T(2,128)(2,1)S(1)}, u32[]{:S(2)}, u32[]{:S(2)}) collective-permute-start(bf16[2,7168]{1,0:T(2,128)(2,1)S(1)} %get-tuple-element.53), channel_id=1, source_target_pairs={{0,12},{2,14},{4,8},{6,10},{8,4},{10,6},{12,0},{14,2},{1,13},{3,15... | collective-permute-start | bytes 86024 | tf_op jit(solution)/shard_map/ppermute | solution.py:546
  124.0 1.3 copy-done.2
  125.3 0.9 copy-done.6
  127.2 1.3 copy-done.13
  128.5 6.2 %attend_keep.1.before = bf16[8,256,512]{2,1,0:T(8,128)(2,1)} custom-call(s32[8]{0:T(128)S(1)} %copy-done.23, s32[1]{0:T(128)} %bitcast.own_ref.refs_1_, bf16[8,256,512]{2,1,0:T(8,128)(2,1)S(1)} %bitcast.12, bf16[8,32,512]{2,1,0:T(8,128)(2,1)S(1)} %copy-done.11, bf16[8,32,512]{2,1,0:T(8,128)(2,1)S(1)} %copy-done.6, ...), custom_call_target="tpu_custom_call", output_to_operand_aliasing={{}: (9, {})} | custom-call | bytes 1024 | tf_op jit(solution)/shard_map/attend_keep/pallas_call | solution.py:326
  134.7 1.0 convert_add_fusion.2
  137.5 2.3 %place.1 = bf16[8,256,512]{2,1,0:T(8,128)(2,1)} custom-call(s32[8]{0:T(128)} %slot_ref.3, s32[1]{0:T(128)} %bitcast.own_ref.refs_1_, bf16[256,512]{1,0:T(8,128)(2,1)} %copy-done.26, bf16[8,256,512]{2,1,0:T(8,128)(2,1)} %attend_keep.1.before), custom_call_target="tpu_custom_call", output_to_operand_aliasing={{}: (3, {})} | custom-call | tf_op jit(solution)/shard_map/place/pallas_call | solution.py:362
  (96 shorter events, 10.4 us)
Async XLA Ops:
  0.6 1.2 copy-start.19
  2.8 11.9 %copy-start.29 = (bf16[8,2,512]{2,1,0:T(2,128)(2,1)S(1)}, bf16[8,2,512]{2,1,0:T(2,128)(2,1)}, u32[]{:S(2)}) copy-start(bf16[8,2,512]{2,1,0:T(2,128)(2,1)} %param.17) | copy-start | bytes 49156
  2.8 11.9 %copy-start.31 = (bf16[8,2,64]{2,1,0:T(2,128)(2,1)S(1)}, bf16[8,2,64]{2,1,0:T(2,128)(2,1)}, u32[]{:S(2)}) copy-start(bf16[8,2,64]{2,1,0:T(2,128)(2,1)} %param.18) | copy-start | bytes 6148
  2.8 12.0 %copy-start.27 = (bf16[8,2,8192]{2,1,0:T(2,128)(2,1)S(1)}, bf16[8,2,8192]{2,1,0:T(2,128)(2,1)}, u32[]{:S(2)}) copy-start(bf16[8,2,8192]{2,1,0:T(2,128)(2,1)} %param.16) | copy-start | bytes 786436
  2.8 14.0 %copy-start = (bf16[8,2,128,512]{3,2,1,0:T(8,128)(2,1)S(1)}, bf16[8,2,128,512]{3,2,1,0:T(8,128)(2,1)}, u32[]{:S(2)}) copy-start(bf16[8,2,128,512]{3,2,1,0:T(8,128)(2,1)} %param.15) | copy-start | bytes 6291460
  3.9 12.8 %copy-start.23 = (s32[8]{0:T(128)S(1)}, s32[8]{0:T(128)}, u32[]{:S(2)}) copy-start(s32[8]{0:T(128)} %slot_ref.3) | copy-start | bytes 100
  3.9 29.3 %collective-permute-start.2 = (bf16[1152,512]{1,0:T(8,128)(2,1)}, bf16[1152,512]{1,0:T(8,128)(2,1)}, u32[]{:S(2)}, u32[]{:S(2)}) collective-permute-start(bf16[1152,512]{1,0:T(8,128)(2,1)} %pack_cache.1.refs_6_), channel_id=1, source_target_pairs={{0,4},{4,0},{8,12},{12,8},{2,6},{6,2},{10,14},{14,10},{1,5},{5,1},... | collective-permute-start | bytes 3538952 | tf_op jit(solution)/shard_map/ppermute | solution.py:34
  6.9 28.0 %collective-permute-start.3 = (bf16[1152,512]{1,0:T(8,128)(2,1)}, bf16[1152,512]{1,0:T(8,128)(2,1)}, u32[]{:S(2)}, u32[]{:S(2)}) collective-permute-start(bf16[1152,512]{1,0:T(8,128)(2,1)} %pack_cache.1.refs_6_), channel_id=1, source_target_pairs={{4,8},{8,4},{6,10},{10,6},{5,9},{9,5},{7,11},{11,7},{20,24},{24,20... | collective-permute-start | bytes 3538952 | tf_op jit(solution)/shard_map/ppermute | solution.py:34
  8.6 28.4 %collective-permute-start.7 = (bf16[1152,512]{1,0:T(8,128)(2,1)}, bf16[1152,512]{1,0:T(8,128)(2,1)}, u32[]{:S(2)}, u32[]{:S(2)}) collective-permute-start(bf16[1152,512]{1,0:T(8,128)(2,1)} %pack_cache.1.refs_6_), channel_id=1, source_target_pairs={{0,1},{1,0},{2,3},{3,2},{4,5},{5,4},{6,7},{7,6},{8,9},{9,8},{10,11... | collective-permute-start | bytes 3538952 | tf_op jit(solution)/shard_map/ppermute | solution.py:26
  12.2 4.5 %collective-permute-start = (bf16[4,7168]{1,0:T(4,128)(2,1)}, bf16[4,7168]{1,0:T(4,128)(2,1)S(1)}, u32[]{:S(2)}, u32[]{:S(2)}) collective-permute-start(bf16[4,7168]{1,0:T(4,128)(2,1)} %get-tuple-element.28), channel_id=1, source_target_pairs={{0,2},{2,0},{4,6},{6,4},{8,10},{10,8},{12,14},{14,12},{1,3},{3,1},... | collective-permute-start | bytes 172040 | tf_op jit(solution)/shard_map/ppermute | solution.py:26
  14.7 2.0 %copy-start.3 = (bf16[8,32,512]{2,1,0:T(8,128)(2,1)}, bf16[8,32,512]{2,1,0:T(8,128)(2,1)S(1)}, u32[]{:S(2)}) copy-start(bf16[8,32,512]{2,1,0:T(8,128)(2,1)S(1)} %fusion.2.new_ref.refs_5_.refs_4_) | copy-start | bytes 786436
  18.6 30.5 %collective-permute-start.1 = (bf16[4,320,512]{2,1,0:T(8,128)(2,1)S(1)}, bf16[4,320,512]{2,1,0:T(8,128)(2,1)S(1)}, u32[]{:S(2)}, u32[]{:S(2)}) collective-permute-start(bf16[4,320,512]{2,1,0:T(8,128)(2,1)S(1)} %pack_leaving.1), channel_id=1, source_target_pairs={{0,2},{2,0},{4,6},{6,4},{8,10},{10,8},{12,14},{14,12},{1,3},{3,1},... | collective-permute-start | bytes 3932168 | tf_op jit(solution)/shard_map/ppermute | solution.py:26
  33.2 19.3 %collective-permute-start.6 = (bf16[1152,512]{1,0:T(8,128)(2,1)}, bf16[1152,512]{1,0:T(8,128)(2,1)S(1)}, u32[]{:S(2)}, u32[]{:S(2)}) collective-permute-start(bf16[1152,512]{1,0:T(8,128)(2,1)} %collective-permute-done.2.refs_6_), channel_id=1, source_target_pairs={{0,1},{1,0},{2,3},{3,2},{4,5},{5,4},{6,7},{7,6},{8,9},{9,8},{10,11... | collective-permute-start | bytes 3538952 | tf_op jit(solution)/shard_map/ppermute | solution.py:26
  33.2 38.1 %collective-permute-start.4 = (bf16[1152,512]{1,0:T(8,128)(2,1)}, bf16[1152,512]{1,0:T(8,128)(2,1)}, u32[]{:S(2)}, u32[]{:S(2)}) collective-permute-start(bf16[1152,512]{1,0:T(8,128)(2,1)} %collective-permute-done.2.refs_6_), channel_id=1, source_target_pairs={{4,8},{8,4},{6,10},{10,6},{5,9},{9,5},{7,11},{11,7},{20,24},{24,20... | collective-permute-start | bytes 3538952 | tf_op jit(solution)/shard_map/ppermute | solution.py:34
  34.9 36.4 %collective-permute-start.5 = (bf16[1152,512]{1,0:T(8,128)(2,1)}, bf16[1152,512]{1,0:T(8,128)(2,1)}, u32[]{:S(2)}, u32[]{:S(2)}) collective-permute-start(bf16[1152,512]{1,0:T(8,128)(2,1)} %collective-permute-done.3), channel_id=1, source_target_pairs={{4,0},{8,12},{6,2},{10,14},{5,1},{9,13},{7,3},{11,15},{20,16},{24,... | collective-permute-start | bytes 3538952 | tf_op jit(solution)/shard_map/ppermute | solution.py:34
  37.0 34.3 %collective-permute-start.10 = (bf16[4,7168]{1,0:T(4,128)(2,1)}, bf16[4,7168]{1,0:T(4,128)(2,1)}, u32[]{:S(2)}, u32[]{:S(2)}) collective-permute-start(bf16[4,7168]{1,0:T(4,128)(2,1)} %pad_maximum_fusion.2), channel_id=1, source_target_pairs={{0,12},{2,14},{4,8},{6,10},{8,4},{10,6},{12,0},{14,2},{1,13},{3,15... | collective-permute-start | bytes 172040 | tf_op jit(solution)/shard_map/ppermute | solution.py:546
  49.1 22.2 %collective-permute-start.8 = (bf16[4,7168]{1,0:T(4,128)(2,1)S(1)}, bf16[4,7168]{1,0:T(4,128)(2,1)S(1)}, u32[]{:S(2)}, u32[]{:S(2)}) collective-permute-start(bf16[4,7168]{1,0:T(4,128)(2,1)S(1)} %pad_maximum_fusion.1), channel_id=1, source_target_pairs={{0,4},{2,6},{4,0},{6,2},{8,12},{10,14},{12,8},{14,10},{1,5},{3,7},... | collective-permute-start | bytes 172040 | tf_op jit(solution)/shard_map/ppermute | solution.py:546
  52.5 1.1 copy-start.17
  53.6 17.7 %collective-permute-start.9 = (bf16[4,7168]{1,0:T(4,128)(2,1)}, bf16[4,7168]{1,0:T(4,128)(2,1)}, u32[]{:S(2)}, u32[]{:S(2)}) collective-permute-start(bf16[4,7168]{1,0:T(4,128)(2,1)} %pad_maximum_fusion.2), channel_id=1, source_target_pairs={{0,8},{2,10},{4,12},{6,14},{8,0},{10,2},{12,4},{14,6},{1,9},{3,11}... | collective-permute-start | bytes 172040 | tf_op jit(solution)/shard_map/ppermute | solution.py:546
  53.6 1.0 copy-start.4
  55.5 7.7 %copy-start.9 = (bf16[8,32,512]{2,1,0:T(8,128)(2,1)S(1)}, bf16[8,32,512]{2,1,0:T(8,128)(2,1)}, u32[]{:S(2)}) copy-start(bf16[8,32,512]{2,1,0:T(8,128)(2,1)} %copy-done.7) | copy-start | bytes 786436
  55.5 7.7 %copy-start.18 = (bf16[1152,512]{1,0:T(8,128)(2,1)S(1)}, bf16[1152,512]{1,0:T(8,128)(2,1)}, u32[]{:S(2)}) copy-start(bf16[1152,512]{1,0:T(8,128)(2,1)} %copy-done.17) | copy-start | bytes 3538948
  63.2 8.1 %copy-start.24 = (bf16[256,512]{1,0:T(8,128)(2,1)}, bf16[256,512]{1,0:T(8,128)(2,1)S(1)}, u32[]{:S(2)}) copy-start(bf16[256,512]{1,0:T(8,128)(2,1)S(1)} %get-tuple-element.35) | copy-start | bytes 786436
  71.3 2.5 %copy-start.28 = (bf16[4,7168]{1,0:T(4,128)(2,1)}, bf16[4,7168]{1,0:T(4,128)(2,1)S(1)}, u32[]{:S(2)}) copy-start(bf16[4,7168]{1,0:T(4,128)(2,1)S(1)} %collective-permute-done.8) | copy-start | bytes 172036
  73.8 18.1 %collective-permute-start.12 = (bf16[1152,512]{1,0:T(8,128)(2,1)}, bf16[1152,512]{1,0:T(8,128)(2,1)}, u32[]{:S(2)}, u32[]{:S(2)}) collective-permute-start(bf16[1152,512]{1,0:T(8,128)(2,1)} %broadcast_select_fusion.1.refs_6_), channel_id=1, source_target_pairs={{0,1},{1,0},{2,3},{3,2},{4,5},{5,4},{6,7},{7,6},{8,9},{9,8},{10,11... | collective-permute-start | bytes 3538952 | tf_op jit(solution)/shard_map/ppermute | solution.py:26
  75.4 30.6 %collective-permute-start.11 = (bf16[1152,512]{1,0:T(8,128)(2,1)}, bf16[1152,512]{1,0:T(8,128)(2,1)}, u32[]{:S(2)}, u32[]{:S(2)}) collective-permute-start(bf16[1152,512]{1,0:T(8,128)(2,1)} %collective-permute-done.4), channel_id=1, source_target_pairs={{4,0},{8,12},{6,2},{10,14},{5,1},{9,13},{7,3},{11,15},{20,16},{24,... | collective-permute-start | bytes 3538952 | tf_op jit(solution)/shard_map/ppermute | solution.py:34
  81.7 2.0 %collective-permute-start.14 = (bf16[16,7168]{1,0:T(8,128)(2,1)}, bf16[16,7168]{1,0:T(8,128)(2,1)S(1)}, u32[]{:S(2)}, u32[]{:S(2)}) collective-permute-start(bf16[16,7168]{1,0:T(8,128)(2,1)} %concatenate.20.mine_ref), channel_id=1, source_target_pairs={{0,1},{1,0},{2,3},{3,2},{4,5},{5,4},{6,7},{7,6},{8,9},{9,8},{10,11... | collective-permute-start | bytes 688136 | tf_op jit(solution)/shard_map/ppermute | solution.py:26
  82.2 9.8 %copy-start.5 = (bf16[8,32,512]{2,1,0:T(8,128)(2,1)S(1)}, bf16[8,32,512]{2,1,0:T(8,128)(2,1)}, u32[]{:S(2)}) copy-start(bf16[8,32,512]{2,1,0:T(8,128)(2,1)} %copy-done.3) | copy-start | bytes 786436
  82.2 9.8 %copy-start.10 = (bf16[8,32,512]{2,1,0:T(8,128)(2,1)S(1)}, bf16[8,32,512]{2,1,0:T(8,128)(2,1)}, u32[]{:S(2)}) copy-start(bf16[8,32,512]{2,1,0:T(8,128)(2,1)} %copy-done.7) | copy-start | bytes 786436
  82.2 9.7 %collective-permute-start.13 = (bf16[256,512]{1,0:T(8,128)(2,1)}, bf16[256,512]{1,0:T(8,128)(2,1)S(1)}, u32[]{:S(2)}, u32[]{:S(2)}) collective-permute-start(bf16[256,512]{1,0:T(8,128)(2,1)} %copy-done.24), channel_id=1, source_target_pairs={{0,2},{2,0},{4,6},{6,4},{8,10},{10,8},{12,14},{14,12},{1,3},{3,1},... | collective-permute-start | bytes 786440 | tf_op jit(solution)/shard_map/ppermute | solution.py:26
  83.7 1.5 %copy-start.14 = (bf16[1,7168,128]{2,1,0:T(8,128)(2,1)S(1)}, bf16[1,7168,128]{2,1,0:T(8,128)(2,1)}, u32[]{:S(2)}) copy-start(bf16[1,7168,128]{2,1,0:T(8,128)(2,1)} %gate_ref.1) | copy-start | bytes 5505028
  85.2 1.5 %copy-start.15 = (bf16[1,7168,128]{2,1,0:T(8,128)(2,1)S(1)}, bf16[1,7168,128]{2,1,0:T(8,128)(2,1)}, u32[]{:S(2)}) copy-start(bf16[1,7168,128]{2,1,0:T(8,128)(2,1)} %up_ref.1) | copy-start | bytes 5505028
  86.7 1.5 %copy-start.16 = (bf16[1,128,7168]{2,1,0:T(8,128)(2,1)S(1)}, bf16[1,128,7168]{2,1,0:T(8,128)(2,1)}, u32[]{:S(2)}) copy-start(bf16[1,128,7168]{2,1,0:T(8,128)(2,1)} %down_ref.1) | copy-start | bytes 5505028
  90.1 1.8 %collective-permute-start.15 = (bf16[16,7168]{1,0:T(8,128)(2,1)S(1)}, bf16[16,7168]{1,0:T(8,128)(2,1)S(1)}, u32[]{:S(2)}, u32[]{:S(2)}) collective-permute-start(bf16[16,7168]{1,0:T(8,128)(2,1)S(1)} %get-tuple-element.43), channel_id=1, source_target_pairs={{0,1},{1,0},{2,3},{3,2},{4,5},{5,4},{6,7},{7,6},{8,9},{9,8},{10,11... | collective-permute-start | bytes 688136 | tf_op jit(solution)/shard_map/ppermute | solution.py:26
  90.4 32.2 %collective-permute-start.18 = (bf16[256,512]{1,0:T(8,128)(2,1)}, bf16[256,512]{1,0:T(8,128)(2,1)}, u32[]{:S(2)}, u32[]{:S(2)}) collective-permute-start(bf16[256,512]{1,0:T(8,128)(2,1)} %get-tuple-element.32), channel_id=1, source_target_pairs={{0,2},{2,0},{4,6},{6,4},{8,10},{10,8},{12,14},{14,12},{1,3},{3,1},... | collective-permute-start | bytes 786440 | tf_op jit(solution)/shard_map/ppermute | solution.py:26
  100.5 23.6 %collective-permute-start.19 = (bf16[256,512]{1,0:T(8,128)(2,1)}, bf16[256,512]{1,0:T(8,128)(2,1)}, u32[]{:S(2)}, u32[]{:S(2)}) collective-permute-start(bf16[256,512]{1,0:T(8,128)(2,1)} %get-tuple-element.37), channel_id=1, source_target_pairs={{0,2},{2,0},{4,6},{6,4},{8,10},{10,8},{12,14},{14,12},{1,3},{3,1},... | collective-permute-start | bytes 786440 | tf_op jit(solution)/shard_map/ppermute | solution.py:26
  106.0 5.4 %collective-permute-start.20 = (bf16[8,7168]{1,0:T(8,128)(2,1)S(1)}, bf16[8,7168]{1,0:T(8,128)(2,1)S(1)}, u32[]{:S(2)}, u32[]{:S(2)}) collective-permute-start(bf16[8,7168]{1,0:T(8,128)(2,1)S(1)} %get-tuple-element.50), channel_id=1, source_target_pairs={{0,2},{2,0},{4,6},{6,4},{8,10},{10,8},{12,14},{14,12},{1,3},{3,1},... | collective-permute-start | bytes 344072 | tf_op jit(solution)/shard_map/ppermute | solution.py:26
  108.9 7.4 %copy-start.1 = (bf16[1152,512]{1,0:T(8,128)(2,1)}, bf16[1152,512]{1,0:T(8,128)(2,1)S(1)}, u32[]{:S(2)}) copy-start(bf16[1152,512]{1,0:T(8,128)(2,1)S(1)} %broadcast_select_fusion.refs_3_.refs_5_) | copy-start | bytes 3538948
  108.9 2.9 %collective-permute-start.16 = (bf16[1152,512]{1,0:T(8,128)(2,1)S(1)}, bf16[1152,512]{1,0:T(8,128)(2,1)S(1)}, u32[]{:S(2)}, u32[]{:S(2)}) collective-permute-start(bf16[1152,512]{1,0:T(8,128)(2,1)S(1)} %broadcast_select_fusion.refs_3_.refs_5_), channel_id=1, source_target_pairs={{0,1},{1,0},{2,3},{3,2},{4,5},{5,4},{6,7},{7,6},{8,9},{9,8},{10,11... | collective-permute-start | bytes 3538952 | tf_op jit(solution)/shard_map/ppermute | solution.py:26
  111.4 4.9 %copy-start.25 = (f32[8,7168]{1,0:T(8,128)}, f32[8,7168]{1,0:T(8,128)S(1)}, u32[]{:S(2)}) copy-start(f32[8,7168]{1,0:T(8,128)S(1)} %convert_add_fusion) | copy-start | bytes 688132
  111.4 8.6 %copy-start.30 = (f32[16,4]{1,0:T(8,128)S(1)}, f32[16,4]{1,0:T(8,128)}, u32[]{:S(2)}) copy-start(f32[16,4]{1,0:T(8,128)} %get-tuple-element.48) | copy-start | bytes 772
  111.8 4.5 %copy-start.12 = (bf16[1152,512]{1,0:T(8,128)(2,1)}, bf16[1152,512]{1,0:T(8,128)(2,1)S(1)}, u32[]{:S(2)}) copy-start(bf16[1152,512]{1,0:T(8,128)(2,1)S(1)} %collective-permute-done.16.refs_4_.refs_6_) | copy-start | bytes 3538948
  117.1 17.6 %collective-permute-start.21 = (bf16[2,7168]{1,0:T(2,128)(2,1)S(1)}, bf16[2,7168]{1,0:T(2,128)(2,1)S(1)}, u32[]{:S(2)}, u32[]{:S(2)}) collective-permute-start(bf16[2,7168]{1,0:T(2,128)(2,1)S(1)} %get-tuple-element.52), channel_id=1, source_target_pairs={{0,4},{2,6},{4,0},{6,2},{8,12},{10,14},{12,8},{14,10},{1,5},{3,7},... | collective-permute-start | bytes 86024 | tf_op jit(solution)/shard_map/ppermute | solution.py:546
  120.2 16.6 %collective-permute-start.17 = (bf16[256,512]{1,0:T(8,128)(2,1)}, bf16[256,512]{1,0:T(8,128)(2,1)S(1)}, u32[]{:S(2)}, u32[]{:S(2)}) collective-permute-start(bf16[256,512]{1,0:T(8,128)(2,1)} %copy-done.21), channel_id=1, source_target_pairs={{0,2},{2,0},{4,6},{6,4},{8,10},{10,8},{12,14},{14,12},{1,3},{3,1},... | collective-permute-start | bytes 786440 | tf_op jit(solution)/shard_map/ppermute | solution.py:26
  121.6 14.0 %collective-permute-start.22 = (bf16[2,7168]{1,0:T(2,128)(2,1)S(1)}, bf16[2,7168]{1,0:T(2,128)(2,1)S(1)}, u32[]{:S(2)}, u32[]{:S(2)}) collective-permute-start(bf16[2,7168]{1,0:T(2,128)(2,1)S(1)} %get-tuple-element.54), channel_id=1, source_target_pairs={{0,8},{2,10},{4,12},{6,14},{8,0},{10,2},{12,4},{14,6},{1,9},{3,11}... | collective-permute-start | bytes 86024 | tf_op jit(solution)/shard_map/ppermute | solution.py:546
  122.6 13.1 %collective-permute-start.23 = (bf16[2,7168]{1,0:T(2,128)(2,1)S(1)}, bf16[2,7168]{1,0:T(2,128)(2,1)S(1)}, u32[]{:S(2)}, u32[]{:S(2)}) collective-permute-start(bf16[2,7168]{1,0:T(2,128)(2,1)S(1)} %get-tuple-element.53), channel_id=1, source_target_pairs={{0,12},{2,14},{4,8},{6,10},{8,4},{10,6},{12,0},{14,2},{1,13},{3,15... | collective-permute-start | bytes 86024 | tf_op jit(solution)/shard_map/ppermute | solution.py:546
  124.0 1.3 copy-start.2
  127.2 1.3 copy-start.13
  (8 other events, 6.8 us)

commit v4 on v3

--- a/solution.py
+++ b/solution.py
@@ -34,20 +34,27 @@
     return lax.ppermute(x, "branch", pairs)
 
 
-def pack_cache_kernel(lat_ref, rope_ref, out_ref):
+def pack_cache_kernel(lat_ref, rope_ref, out_ref, sems):
     rows = lat_ref.shape[0]
-    out_ref[0:rows, :] = lat_ref[...]
-    out_ref[rows:, :] = rope_ref[...]
+    copies = [
+        pltpu.make_async_copy(lat_ref, out_ref.at[pl.ds(0, rows)], sems.at[0]),
+        pltpu.make_async_copy(rope_ref, out_ref.at[pl.ds(rows, rope_ref.shape[0])], sems.at[1]),
+    ]
+    for copy in copies:
+        copy.start()
+    for copy in copies:
+        copy.wait()
 
 
 def pack_cache(lat, rope):
     return pl.pallas_call(
         pack_cache_kernel,
         out_shape=jax.ShapeDtypeStruct((lat.shape[0] + rope.shape[0], lat.shape[1]), lat.dtype),
-        in_specs=[pl.BlockSpec(memory_space=pltpu.VMEM)] * 2,
+        in_specs=[pl.BlockSpec(memory_space=pl.ANY)] * 2,
         out_specs=pl.BlockSpec(memory_space=pltpu.VMEM),
+        scratch_shapes=[pltpu.SemaphoreType.DMA((2,))],
         cost_estimate=SMALL,
-        compiler_params=pltpu.CompilerParams(vmem_limit_bytes=16 * 1024 * 1024),
+        compiler_params=pltpu.CompilerParams(vmem_limit_bytes=4 * 1024 * 1024),
         name="pack_cache",
     )(lat, rope)
 
@@ -102,7 +109,7 @@
         out_specs=pl.BlockSpec(memory_space=pltpu.VMEM),
         scratch_shapes=[pltpu.SemaphoreType.DMA((slots, 3))],
         cost_estimate=SMALL,
-        compiler_params=pltpu.CompilerParams(vmem_limit_bytes=16 * 1024 * 1024),
+        compiler_params=pltpu.CompilerParams(vmem_limit_bytes=4 * 1024 * 1024),
         name="pack_leaving",
     )(branch_slot, own, *sources)
 
@@ -174,51 +181,25 @@
             value = value + (part * inverse) * fresh32[j : j + 1, :]
         return value.astype(jnp.bfloat16)
 
-    def load_keys(caches, keys, sems):
-        copies = []
-        for i, cache in enumerate(caches):
-            copies.append(
-                pltpu.make_async_copy(
-                    cache.at[pl.ds(0, half)],
-                    keys.at[pl.ds(i * half, half), pl.ds(0, width)],
-                    sems.at[i],
-                )
-            )
-        for copy in copies:
-            copy.start()
-        return copies
-
-    def spread_keys(i, rope_scratch, keys, matrix):
+    def spread_keys(cache, rope_keys, matrix):
         grown = raw_group * width // (LANES // 2)
         for start in range(0, rope_rows, raw_group):
-            part = spread(matrix, rope_scratch[i, start : start + raw_group, :])
-            first = i * half + start * (width // (LANES // 2))
-            keys[first : first + grown, width : width + LANES] = part.astype(jnp.bfloat16)
+            part = spread(matrix, cache[half + start : half + start + raw_group, :])
+            first = start * (width // (LANES // 2))
+            rope_keys[first : first + grown, :] = part.astype(jnp.bfloat16)
 
     def kernel(slot, kinds, given_slots, has_placed, *refs):
         refs = list(refs)
         slot_ref, own_ref = refs.pop(0), refs.pop(0)
-        queries = []
-        for kind in kinds:
-            if kind == "give":
-                queries.append(refs.pop(0))
-            else:
-                queries.append([refs.pop(0) for _ in range(3)])
+        guest = refs.pop(0) if "give" in kinds else None
+        stay = [refs.pop(0) for _ in range(3)] if "keep" in kinds else None
         caches = [refs.pop(0) for _ in range(2)]
         arrived = [refs.pop(0) for _ in given_slots]
         if has_placed:
             refs.pop(0)
-        gives = [refs.pop(0) for kind in kinds if kind == "give"]
+        give = refs.pop(0) if "give" in kinds else None
         placed = refs.pop(0) if ("keep" in kinds or given_slots) else None
-        keys, rope_scratch, query_all, scores, summed, result, sems, place_sems = refs
-        copies = load_keys(caches, keys, sems)
-        rope_copies = []
-        for i in range(2):
-            copy = pltpu.make_async_copy(
-                caches[i].at[pl.ds(half, rope_rows)], rope_scratch.at[i], sems.at[2 + i]
-            )
-            copy.start()
-            rope_copies.append(copy)
+        rope_keys, query_all, scores, summed, result, place_sems = refs
         placing = []
         for i, (number, source) in enumerate(zip(given_slots, arrived)):
             copy = pltpu.make_async_copy(
@@ -226,31 +207,35 @@
             )
             copy.start()
             placing.append(copy)
+        kept_row = row_for(slot, 0, slot_ref, own_ref)
         matrix = spread_matrix(raw_group, width)
         fresh_parts = []
-        for number, (kind, query) in enumerate(zip(kinds, queries)):
+        for number, kind in enumerate(kinds):
             if kind == "give":
                 middle = q_rows + token_rope
-                packed = query.at[0]
-                lat, raw = packed[0:q_rows, :], packed[q_rows:middle, :]
-                fresh_parts.append(packed[middle : middle + 2 * PAD, :])
+                lat, raw = guest[slot, 0:q_rows, :], guest[slot, q_rows:middle, :]
+                fresh_parts.append(guest[slot, middle : middle + 2 * PAD, :])
             else:
-                lat, raw = query[0][0], query[1][0]
-                fresh_parts.append(query[2][0])
+                lat, raw = stay[0][kept_row], stay[1][kept_row]
+                fresh_parts.append(stay[2][kept_row])
             put_query(query_all, number, lat, raw, matrix)
         peak = None
-        for i in range(2):
-            rope_copies[i].wait()
-            spread_keys(i, rope_scratch, keys, matrix)
-            copies[i].wait()
-            for start in range(i * half, (i + 1) * half, chunk):
+        for i, cache in enumerate(caches):
+            spread_keys(cache, rope_keys, matrix)
+            for start in range(0, half, chunk):
                 part = lax.dot_general(
-                    query_all[...],
-                    keys[start : start + chunk, :],
+                    query_all[:, 0:width],
+                    cache[start : start + chunk, :],
                     contract,
                     preferred_element_type=jnp.float32,
                 )
-                scores[:, start : start + chunk] = part
+                part = part + lax.dot_general(
+                    query_all[:, width:],
+                    rope_keys[start : start + chunk, :],
+                    contract,
+                    preferred_element_type=jnp.float32,
+                )
+                scores[:, i * half + start : i * half + start + chunk] = part
                 high = jnp.max(part, axis=1, keepdims=True)
                 peak = high if peak is None else jnp.maximum(peak, high)
         scaled = peak * factor
@@ -260,7 +245,7 @@
             part = jnp.sum(weights, axis=1, keepdims=True)
             value = jnp.dot(
                 weights.astype(jnp.bfloat16),
-                keys[start : start + chunk, 0:width],
+                caches[start // half][start % half : start % half + chunk, :],
                 preferred_element_type=jnp.float32,
             )
             if start == 0:
@@ -275,12 +260,10 @@
                 query_all[rows, :], fresh_parts[number], peak[rows], total[rows], summed[rows, :]
             )
             if kind == "give":
-                gives.pop(0)[...] = value
+                give[...] = value
             else:
                 result[...] = value
-                copy = pltpu.make_async_copy(
-                    result, placed.at[row_for(slot, 0, slot_ref, own_ref)], place_sems.at[0]
-                )
+                copy = pltpu.make_async_copy(result, placed.at[kept_row], place_sems.at[0])
                 copy.start()
                 placing.append(copy)
         for copy in placing:
@@ -289,89 +272,67 @@
     def call(scalars, kinds, slot, guest, stay, caches, arrived, placed):
         count = scalars[0].shape[0]
         n_tok = len(kinds)
-        any_spec = pl.BlockSpec(memory_space=pl.ANY)
-
-        def chosen(i, slot_ref, own_ref):
-            return (row_for(slot, 0, slot_ref, own_ref), 0, 0)
-
-        in_specs, operands = [], []
-        for kind in kinds:
-            if kind == "give":
-                in_specs.append(
-                    pl.BlockSpec((1, guest.shape[1], width), lambda i, *_: (slot, 0, 0))
-                )
-                operands.append(guest)
-            else:
-                in_specs += [pl.BlockSpec((1, x.shape[1], width), chosen) for x in stay]
-                operands += stay
+        operands = [*scalars]
+        if "give" in kinds:
+            operands.append(guest)
+        if "keep" in kinds:
+            operands += stay
         given_slots = tuple(number for number, _ in arrived)
-        in_specs += [any_spec] * 2
-        in_specs += [pl.BlockSpec((q_rows, width), lambda i, *_: (0, 0)) for _ in arrived]
         operands += [*caches, *(value for _, value in arrived)]
-        has_placed = placed is not None
+        in_specs = [pl.BlockSpec(memory_space=pltpu.SMEM)] * len(scalars)
+        in_specs += [pl.BlockSpec(memory_space=pltpu.VMEM)] * (len(operands) - len(scalars))
         out_shape, out_specs, alias = [], [], {}
-        for kind in kinds:
-            if kind == "give":
-                out_shape.append(jax.ShapeDtypeStruct((q_rows, width), jnp.bfloat16))
-                out_specs.append(pl.BlockSpec((q_rows, width), lambda i, *_: (0, 0)))
+        if "give" in kinds:
+            out_shape.append(jax.ShapeDtypeStruct((q_rows, width), jnp.bfloat16))
+            out_specs.append(pl.BlockSpec(memory_space=pltpu.VMEM))
         if "keep" in kinds or arrived:
             out_shape.append(jax.ShapeDtypeStruct((count, q_rows, width), jnp.bfloat16))
-            out_specs.append(any_spec)
-            if has_placed:
-                alias = {2 + len(operands): len(out_shape) - 1}
+            out_specs.append(pl.BlockSpec(memory_space=pl.ANY))
+        has_placed = placed is not None
         if has_placed:
-            in_specs.append(any_spec)
+            alias = {len(operands): len(out_shape) - 1}
+            in_specs.append(pl.BlockSpec(memory_space=pl.ANY))
             operands.append(placed)
-        all_rows = 2 * half
         return pl.pallas_call(
             functools.partial(kernel, slot, kinds, given_slots, has_placed),
             out_shape=tuple(out_shape),
-            grid_spec=pltpu.PrefetchScalarGridSpec(
-                num_scalar_prefetch=2,
-                grid=(1,),
-                in_specs=in_specs,
-                out_specs=tuple(out_specs),
-                scratch_shapes=[
-                    pltpu.VMEM((all_rows, width + LANES), jnp.bfloat16),
-                    pltpu.VMEM((2, rope_rows, width), jnp.bfloat16),
-                    pltpu.VMEM((n_tok * q_rows, width + LANES), jnp.bfloat16),
-                    pltpu.VMEM((n_tok * q_rows, all_rows), jnp.float32),
-                    pltpu.VMEM((n_tok * q_rows, width), jnp.float32),
-                    pltpu.VMEM((q_rows, width), jnp.bfloat16),
-                    pltpu.SemaphoreType.DMA((4,)),
-                    pltpu.SemaphoreType.DMA((1 + max(1, len(arrived)),)),
-                ],
-            ),
+            in_specs=in_specs,
+            out_specs=tuple(out_specs),
+            scratch_shapes=[
+                pltpu.VMEM((half, LANES), jnp.bfloat16),
+                pltpu.VMEM((n_tok * q_rows, width + LANES), jnp.bfloat16),
+                pltpu.VMEM((n_tok * q_rows, 2 * half), jnp.float32),
+                pltpu.VMEM((n_tok * q_rows, width), jnp.float32),
+                pltpu.VMEM((q_rows, width), jnp.bfloat16),
+                pltpu.SemaphoreType.DMA((1 + max(1, len(arrived)),)),
+            ],
             input_output_aliases=alias,
             cost_estimate=SMALL,
-            compiler_params=pltpu.CompilerParams(vmem_limit_bytes=32 * 1024 * 1024),
+            compiler_params=pltpu.CompilerParams(vmem_limit_bytes=20 * 1024 * 1024),
             name="attend_" + "_".join(kinds),
-        )(*scalars, *operands)
+        )(*operands)
 
     return call
 
 
-def place_kernel(slot_ref, own_ref, source_ref, before, placed_ref):
-    placed_ref[0] = source_ref[...]
+def place_kernel(slot, slot_ref, own_ref, source_ref, before, placed_ref, sem):
+    row = row_for(slot, 1, slot_ref, own_ref)
+    copy = pltpu.make_async_copy(source_ref, placed_ref.at[row], sem)
+    copy.start()
+    copy.wait()
 
 
 def place(scalars, slot, source, placed):
-    def chosen(i, slot_ref, own_ref):
-        return (row_for(slot, 1, slot_ref, own_ref), 0, 0)
-
     return pl.pallas_call(
-        place_kernel,
+        functools.partial(place_kernel, slot),
         out_shape=jax.ShapeDtypeStruct(placed.shape, placed.dtype),
-        grid_spec=pltpu.PrefetchScalarGridSpec(
-            num_scalar_prefetch=2,
-            grid=(1,),
-            in_specs=[
-                pl.BlockSpec(source.shape, lambda i, *_: (0, 0)),
-                pl.BlockSpec(memory_space=pl.ANY),
-            ],
-            out_specs=pl.BlockSpec((1,) + source.shape, chosen),
-        ),
+        in_specs=[pl.BlockSpec(memory_space=pltpu.SMEM)] * 2
+        + [pl.BlockSpec(memory_space=pltpu.VMEM), pl.BlockSpec(memory_space=pl.ANY)],
+        out_specs=pl.BlockSpec(memory_space=pl.ANY),
+        scratch_shapes=[pltpu.SemaphoreType.DMA],
         input_output_aliases={3: 0},
+        cost_estimate=SMALL,
+        compiler_params=pltpu.CompilerParams(vmem_limit_bytes=4 * 1024 * 1024),
         name="place",
     )(*scalars, source, placed)
 
@@ -419,16 +380,66 @@
         + [pl.BlockSpec(memory_space=pltpu.VMEM)] * 3,
         out_specs=(pl.BlockSpec(memory_space=pltpu.VMEM),) * 2,
         cost_estimate=SMALL,
+        compiler_params=pltpu.CompilerParams(vmem_limit_bytes=8 * 1024 * 1024),
         name="dispatch",
     )(block, routes, gates, tokens)
 
 
-def experts_kernel(mine_ref, theirs_ref, gate_ref, up_ref, down_ref, keep_ref, send_ref):
+def moved_rows(pieces, places, rows):
+    total = None
+    for piece, places_of_piece in zip(pieces, places):
+        shape = (rows, piece.shape[0])
+        row = lax.broadcasted_iota(jnp.int32, shape, 0)
+        column = lax.broadcasted_iota(jnp.int32, shape, 1)
+        chosen = jnp.zeros(shape, jnp.float32)
+        for source, there in places_of_piece:
+            chosen += ((row == there) & (column == source)).astype(jnp.float32)
+        part = jnp.dot(
+            chosen.astype(jnp.bfloat16), piece[...], preferred_element_type=jnp.float32
+        )
+        total = part if total is None else total + part
+    return total.astype(jnp.bfloat16)
+
+
+def move_kernel(count, plans, *refs):
+    for plan, out_ref in zip(plans, refs[count:]):
+        used = [i for i in range(count) if plan[i]]
+        out_ref[...] = moved_rows(
+            [refs[i] for i in used], [plan[i] for i in used], out_ref.shape[0]
+        )
+
+
+def move_rows(arrays, plans, rows, name):
+    width = arrays[0].shape[1]
+    return pl.pallas_call(
+        functools.partial(move_kernel, len(arrays), plans),
+        out_shape=tuple(jax.ShapeDtypeStruct((rows, width), jnp.bfloat16) for _ in plans),
+        in_specs=[pl.BlockSpec(memory_space=pltpu.VMEM)] * len(arrays),
+        out_specs=tuple(pl.BlockSpec(memory_space=pltpu.VMEM) for _ in plans),
+        cost_estimate=SMALL,
+        compiler_params=pltpu.CompilerParams(vmem_limit_bytes=8 * 1024 * 1024),
+        name=name,
+    )(*arrays)
+
+
+def experts_kernel(mine_ref, theirs_ref, gate_hbm, up_hbm, down_hbm, keep_ref, send_ref, *scratch):
+    gate_ref, up_ref, down_ref, sems = scratch
+    copies = [
+        pltpu.make_async_copy(source.at[0], there, sems.at[i])
+        for i, (source, there) in enumerate(
+            ((gate_hbm, gate_ref), (up_hbm, up_ref), (down_hbm, down_ref))
+        )
+    ]
+    for copy in copies:
+        copy.start()
     rows = jnp.concatenate([mine_ref[...], theirs_ref[...]], axis=0)
-    gate = jnp.dot(rows, gate_ref[0], preferred_element_type=jnp.float32)
-    lifted = jnp.dot(rows, up_ref[0], preferred_element_type=jnp.float32)
+    copies[0].wait()
+    gate = jnp.dot(rows, gate_ref[...], preferred_element_type=jnp.float32)
+    copies[1].wait()
+    lifted = jnp.dot(rows, up_ref[...], preferred_element_type=jnp.float32)
     hidden = (gate / (1.0 + jnp.exp(-gate)) * lifted).astype(jnp.bfloat16)
-    parts = jnp.dot(hidden, down_ref[0], preferred_element_type=jnp.float32)
+    copies[2].wait()
+    parts = jnp.dot(hidden, down_ref[...], preferred_element_type=jnp.float32)
     count = mine_ref.shape[0]
     keep_ref[...] = parts[:count]
     send_ref[...] = parts[count:].astype(jnp.bfloat16)
@@ -441,8 +452,17 @@
             jax.ShapeDtypeStruct(mine.shape, jnp.float32),
             jax.ShapeDtypeStruct(mine.shape, jnp.bfloat16),
         ),
+        in_specs=[pl.BlockSpec(memory_space=pltpu.VMEM)] * 2
+        + [pl.BlockSpec(memory_space=pl.ANY)] * 3,
+        out_specs=(pl.BlockSpec(memory_space=pltpu.VMEM),) * 2,
+        scratch_shapes=[
+            pltpu.VMEM(w_gate.shape[1:], w_gate.dtype),
+            pltpu.VMEM(w_up.shape[1:], w_up.dtype),
+            pltpu.VMEM(w_down.shape[1:], w_down.dtype),
+            pltpu.SemaphoreType.DMA((3,)),
+        ],
         cost_estimate=SMALL,
-        compiler_params=pltpu.CompilerParams(vmem_limit_bytes=32 * 1024 * 1024),
+        compiler_params=pltpu.CompilerParams(vmem_limit_bytes=16 * 1024 * 1024),
         name="experts",
     )(mine, theirs, w_gate, w_up, w_down)
 
@@ -463,7 +483,7 @@
             jax.ShapeDtypeStruct(shape, jnp.bfloat16),
         ),
         cost_estimate=SMALL,
-        compiler_params=pltpu.CompilerParams(vmem_limit_bytes=16 * 1024 * 1024),
+        compiler_params=pltpu.CompilerParams(vmem_limit_bytes=8 * 1024 * 1024),
         name="halve",
     )(kept, arrived)
 
@@ -518,6 +538,8 @@
     scalars = (branch_slot, own[None])
     stay = (q_lat, rope_raw, fresh)
 
+    leave = pack_leaving(branch_slot, after(own[None], own_cache), *stay)
+    guest = swapped(leave, "branch", 0)
     attend = build_attend(head_count, step_count, width, half, rope_rows, 32, half // 2)
     model_width = moe_input.shape[-1]
     tok_total = tok_rows * step_count
@@ -527,7 +549,7 @@
     shard_branches = SHARDS // cores
     block = device // SHARDS
     outgoing, share = dispatch(
-        after(block[None], own_cache),
+        after(block[None], leave),
         routes.reshape(tok_total, -1),
         route_gate.reshape(tok_total, -1),
         moe_input.reshape(tok_total, model_width),
@@ -546,13 +568,11 @@
         return lax.ppermute(x, "branch", list(enumerate(there)))
 
     beside = swapped(outgoing, "branch", 0)
-    leave = pack_leaving(branch_slot, after(own[None], beside), *stay)
-    guest = swapped(leave, "branch", 0)
+    pair = tuple(
+        tuple(tuple((k * CAP + c, i * CAP + c) for c in range(CAP)) for i in range(2))
+        for k in range(experts)
+    )
     ways = [(k, m) for k in range(experts) for m in range(around)]
-    pieces = []
-    for k, m in ways:
-        piece = jnp.concatenate([x[k * CAP : (k + 1) * CAP] for x in (outgoing, beside)], axis=0)
-        pieces.append(piece if (k, m) == (0, 0) else along(piece, k, m))
 
     def attend_slot(slot, cache, kinds, waiting, placed):
         keeps = "keep" in kinds
@@ -576,6 +596,8 @@
     both = ("give", "keep")
     given_0, placed = attend_slot(0, both_halves(own_cache), both, [], None)
     back_0 = swapped(given_0, "branch", 0)
+    by_expert = move_rows((outgoing, after(beside, given_0)), pair, 2 * CAP, "pair_rows")
+    pieces = [by_expert[k] if (k, m) == (0, 0) else along(by_expert[k], k, m) for k, m in ways]
     given_1, placed = attend_slot(1, both_halves(cache_a), both, [], placed)
     back_1 = swapped(given_1, "branch", 0)
 
@@ -583,28 +605,37 @@
     first_c, second_b, given_1, *pieces = lax.optimization_barrier(
         (first_c, second_b, given_1, *pieces)
     )
-    rows = jnp.concatenate([x[:CAP] for x in pieces] + [x[CAP:] for x in pieces], axis=0)
+    count = len(ways) * CAP
+    stacked = tuple(
+        tuple((i * CAP + c, i * count + w * CAP + c) for i in range(2) for c in range(CAP))
+        for w in range(len(ways))
+    )
+    (rows,) = move_rows(tuple(pieces), (stacked,), 2 * count, "stack_rows")
     cache_b = jnp.where(middle, first_b, second_b)
     kept, sent = run_experts(rows, swapped(rows, "expert", 0), w_gate, w_up, w_down)
     kept, sent = halve(kept, swapped(sent, "expert", 0))
-    given_2, placed = attend_slot(2, both_halves(cache_b), both, [(0, back_0)], placed)
+    given_2, placed = attend_slot(2, both_halves(cache_b), both, [(0, back_0), (1, back_1)], placed)
     back_2 = swapped(given_2, "branch", 0)
 
-    second_c, given_2, kept, sent = lax.optimization_barrier((second_c, given_2, kept, sent))
+    second_c, back_2, kept, sent = lax.optimization_barrier((second_c, back_2, kept, sent))
     cache_c = both_halves(jnp.where(middle, first_c, second_c))
+    parts = kept + swapped(sent, "branch", 0).astype(jnp.float32)
+    homeward = [
+        parts[w * CAP : (w + 1) * CAP].astype(jnp.float32 if way == (0, 0) else jnp.bfloat16)
+        for w, way in enumerate(ways)
+    ]
+    guest, *homeward = lax.optimization_barrier((guest, *homeward))
     given_3, _ = attend_slot(3, cache_c, ("give",), [], None)
+    homeward = [after(x, given_3) for x in homeward]
     back_3 = swapped(given_3, "branch", 0)
-    _, placed = attend_slot(3, cache_c, ("keep",), [(1, back_1), (2, back_2)], placed)
+    _, placed = attend_slot(3, cache_c, ("keep",), [(2, back_2)], placed)
     placed = place(scalars, 3, back_3, placed)
     attended = placed.reshape(tok_rows, step_count, head_count, width)
 
-    parts = kept + swapped(sent, "branch", 0).astype(jnp.float32)
-    parts = after(parts, given_3)
     sums = [0.0] * experts
-    for number, (k, m) in enumerate(ways):
-        piece = parts[number * CAP : (number + 1) * CAP]
+    for (k, m), piece in zip(ways, homeward):
         if (k, m) != (0, 0):
-            piece = along(piece.astype(jnp.bfloat16), -k, m).astype(jnp.float32)
+            piece = along(piece, -k, m).astype(jnp.float32)
         sums[k] = sums[k] + piece
     sums = jnp.concatenate(sums, axis=0)
     combined = jnp.sum(share[:, :, None] * sums[None, :, :], axis=1)

time: 141 us -> 131 us (0.929)
  waiting for transfers between devices: 30.3 us -> 44 us
  local copies, waits for them, and re-layouts: 27.3 us -> 17.8 us
  Pallas kernels: 42.4 us -> 35.9 us
  other arithmetic: 5.9 us -> 2.01 us
  starting transfers between devices: 32.8 us -> 29.2 us
    pallas_call x5, Pallas kernels: 34.9 us -> 27 us  [call(): pl.pallas_call(functools.partial(kernel, slot, kinds, given_slots, has_pl...]
    ppermute x5, waiting for transfers between devices: 17.4 us -> 23.8 us  [line_hop(): return lax.ppermute(x, 'branch', pairs)]
    ppermute x13, waiting for transfers between devices: 12.9 us -> 18.6 us  [swapped(): lax.ppermute(x, axis, [(i, i ^ 1 << bit) for i in range(lax.axis_size(axi...]
    slice x5 -> x2, local copies, waits for them, and re-layouts: 4.3 us -> 0.71 us  [on_device(): parts[w * CAP:(w + 1) * CAP]]
    concatenate x1 -> x0, local copies, waits for them, and re-layouts: 3.15 us -> none  [on_device(): jnp.concatenate([x[:CAP] for x in pieces] + [x[CAP:] for x in pieces], ax...]
    unnamed x64 -> x60, local copies, waits for them, and re-layouts: 17.1 us -> 14.4 us
    ppermute x6, starting transfers between devices: 12.6 us -> 10.2 us  [along(): return lax.ppermute(x, 'branch', list(enumerate(there)))]
    ppermute x6, waiting for transfers between devices: 0.02 us -> 1.68 us  [along(): return lax.ppermute(x, 'branch', list(enumerate(there)))]
  transfers between devices with their start and end apart: 24 -> 24, of which waited for: 6 -> 9; matrix products, arithmetic and copies ran while one was open for 10% -> 3% of each run, Pallas kernels for 28% -> 23%
where the time goes in v4:
time: 131 us; the launch traced here: 130 us
  waiting for transfers between devices  44 us (34%)
  Pallas kernels  35.9 us (27%)
  starting transfers between devices  29.2 us (22%)
  local copies, waits for them, and re-layouts  17.8 us (14%)
  other arithmetic  2.01 us (2%)
    pallas_call x5, Pallas kernels, call(): pl.pallas_call(functools.partial(kernel, slot, kinds, given_slots, has_pl...  27 us
    ppermute x5, waiting for transfers between devices, line_hop(): return lax.ppermute(x, 'branch', pairs)  23.8 us
    ppermute x13, waiting for transfers between devices, swapped(): lax.ppermute(x, axis, [(i, i ^ 1 << bit) for i in range(lax.axis_size(axi...  18.6 us
    unnamed x60, local copies, waits for them, and re-layouts  14.4 us
    ppermute x6, starting transfers between devices, along(): return lax.ppermute(x, 'branch', list(enumerate(there)))  10.2 us
    ppermute x13, starting transfers between devices, swapped(): lax.ppermute(x, axis, [(i, i ^ 1 << bit) for i in range(lax.axis_size(axi...  9.74 us
    ppermute x5, starting transfers between devices, line_hop(): return lax.ppermute(x, 'branch', pairs)  9.22 us
  transfers between devices with their start and end apart: 24, of which 9 were waited for; matrix products, arithmetic and copies ran while one was open for 3% of the time, Pallas kernels for 23%

profile of v4, /device:TPU:0, one launch (start us, length us, event | category | flops | bytes accessed | tf_op | source)
XLA Modules:
  0.0 130.2 jit_solution(12410364579747568345)
XLA Ops:
  0.6 1.2 copy-done.16
  2.8 1.3 %pack_cache.1.refs_6_ = bf16[1152,512]{1,0:T(8,128)(2,1)} custom-call(bf16[1024,512]{1,0:T(8,128)(2,1)S(1)} %bitcast.13, bf16[128,512]{1,0:T(8,128)(2,1)S(1)} %bitcast.14), custom_call_target="tpu_custom_call" | custom-call | bytes 1024 | tf_op jit(solution)/shard_map/pack_cache/pallas_call | solution.py:50
  4.1 3.1 %collective-permute-start.1 = (bf16[1152,512]{1,0:T(8,128)(2,1)}, bf16[1152,512]{1,0:T(8,128)(2,1)}, u32[]{:S(2)}, u32[]{:S(2)}) collective-permute-start(bf16[1152,512]{1,0:T(8,128)(2,1)} %pack_cache.1.refs_6_), channel_id=1, source_target_pairs={{0,4},{4,0},{8,12},{12,8},{2,6},{6,2},{10,14},{14,10},{1,5},{5,1},... | collective-permute-start | bytes 3538952 | tf_op jit(solution)/shard_map/ppermute | solution.py:34
  7.2 1.7 %collective-permute-start.2 = (bf16[1152,512]{1,0:T(8,128)(2,1)}, bf16[1152,512]{1,0:T(8,128)(2,1)}, u32[]{:S(2)}, u32[]{:S(2)}) collective-permute-start(bf16[1152,512]{1,0:T(8,128)(2,1)} %pack_cache.1.refs_6_), channel_id=1, source_target_pairs={{4,8},{8,4},{6,10},{10,6},{5,9},{9,5},{7,11},{11,7},{20,24},{24,20... | collective-permute-start | bytes 3538952 | tf_op jit(solution)/shard_map/ppermute | solution.py:34
  9.8 2.2 %pack_leaving.1 = bf16[4,320,512]{2,1,0:T(8,128)(2,1)} custom-call(s32[8]{0:T(128)S(1)} %copy-done.22, s32[1]{0:T(128)} %bitcast.own_ref.refs_1_, bf16[8,256,512]{2,1,0:T(8,128)(2,1)S(1)} %bitcast.8, bf16[8,32,512]{2,1,0:T(8,128)(2,1)S(1)} %reshape.28.rope_ref.refs_4_.refs_3_, bf16[8,32,512]{2,1,0:T(8,128)(2,1)S(1)} %fusion.2.new_ref.refs_5_.refs_4_), custom_call_target="tpu_custom_call" | custom-call | bytes 1024 | tf_op jit(solution)/shard_map/pack_leaving/pallas_call | solution.py:104
  12.0 1.6 %collective-permute-start = (bf16[4,320,512]{2,1,0:T(8,128)(2,1)}, bf16[4,320,512]{2,1,0:T(8,128)(2,1)S(1)}, u32[]{:S(2)}, u32[]{:S(2)}) collective-permute-start(bf16[4,320,512]{2,1,0:T(8,128)(2,1)} %pack_leaving.1), channel_id=1, source_target_pairs={{0,2},{2,0},{4,6},{6,4},{8,10},{10,8},{12,14},{14,12},{1,3},{3,1},... | collective-permute-start | bytes 3932168 | tf_op jit(solution)/shard_map/ppermute | solution.py:26
  13.6 19.9 %collective-permute-done.1.refs_6_ = bf16[1152,512]{1,0:T(8,128)(2,1)} collective-permute-done((bf16[1152,512]{1,0:T(8,128)(2,1)}, bf16[1152,512]{1,0:T(8,128)(2,1)}, u32[]{:S(2)}, u32[]{:S(2)}) %collective-permute-start.1) | collective-permute-done | bytes 1179680 | tf_op jit(solution)/shard_map/ppermute | solution.py:34
  33.5 1.7 %collective-permute-start.3 = (bf16[1152,512]{1,0:T(8,128)(2,1)}, bf16[1152,512]{1,0:T(8,128)(2,1)}, u32[]{:S(2)}, u32[]{:S(2)}) collective-permute-start(bf16[1152,512]{1,0:T(8,128)(2,1)} %collective-permute-done.1.refs_6_), channel_id=1, source_target_pairs={{4,8},{8,4},{6,10},{10,6},{5,9},{9,5},{7,11},{11,7},{20,24},{24,20... | collective-permute-start | bytes 3538952 | tf_op jit(solution)/shard_map/ppermute | solution.py:34
  35.2 1.3 collective-permute-start.5
  36.5 1.7 %reshape.31.tokens_ref = bf16[16,7168]{1,0:T(8,128)(2,1)} reshape(bf16[8,2,7168]{2,1,0:T(2,128)(2,1)} %param.20) | data formatting | bytes 458752 | tf_op jit(solution)/shard_map/reshape | solution.py:555
  38.2 0.9 copy-done.17
  39.4 3.1 %collective-permute-done.refs_2_ = bf16[4,320,512]{2,1,0:T(8,128)(2,1)S(1)} collective-permute-done((bf16[4,320,512]{2,1,0:T(8,128)(2,1)}, bf16[4,320,512]{2,1,0:T(8,128)(2,1)S(1)}, u32[]{:S(2)}, u32[]{:S(2)}) %collective-permute-start) | collective-permute-done | bytes 1310752 | tf_op jit(solution)/shard_map/ppermute | solution.py:26
  42.6 1.5 %collective-permute-start.8 = (bf16[4,7168]{1,0:T(4,128)(2,1)S(1)}, bf16[4,7168]{1,0:T(4,128)(2,1)S(1)}, u32[]{:S(2)}, u32[]{:S(2)}) collective-permute-start(bf16[4,7168]{1,0:T(4,128)(2,1)S(1)} %get-tuple-element.44.refs_0_), channel_id=1, source_target_pairs={{0,2},{2,0},{4,6},{6,4},{8,10},{10,8},{12,14},{14,12},{1,3},{3,1},... | collective-permute-start | bytes 172040 | tf_op jit(solution)/shard_map/ppermute | solution.py:26
  44.1 0.9 copy-done.4
  45.0 0.9 copy-done.8
  46.0 6.8 %attend_give_keep.3 = (bf16[256,512]{1,0:T(8,128)(2,1)S(1)}, bf16[8,256,512]{2,1,0:T(8,128)(2,1)}) custom-call(s32[8]{0:T(128)S(1)} %copy-done.22, s32[1]{0:T(128)} %bitcast.own_ref.refs_1_, bf16[4,320,512]{2,1,0:T(8,128)(2,1)S(1)} %collective-permute-done.refs_2_, bf16[8,256,512]{2,1,0:T(8,128)(2,1)S(1)} %bitcast.9, bf16[8,32,512]{2,1,0:T(8,128)(2,1)S(1)} %copy-done.4, ...), custom_call_target="tpu_custom_call" | custom-call | bytes 1024 | tf_op jit(solution)/shard_map/attend_give_keep/pallas_call | solution.py:296
  53.5 1.0 pair_rows.1
  54.5 2.9 %collective-permute-start.10 = (bf16[4,7168]{1,0:T(4,128)(2,1)}, bf16[4,7168]{1,0:T(4,128)(2,1)S(1)}, u32[]{:S(2)}, u32[]{:S(2)}) collective-permute-start(bf16[4,7168]{1,0:T(4,128)(2,1)} %get-tuple-element.48), channel_id=1, source_target_pairs={{0,8},{2,10},{4,12},{6,14},{8,0},{10,2},{12,4},{14,6},{1,9},{3,11}... | collective-permute-start | bytes 172040 | tf_op jit(solution)/shard_map/ppermute | solution.py:568
  57.4 2.5 %collective-permute-start.11 = (bf16[4,7168]{1,0:T(4,128)(2,1)}, bf16[4,7168]{1,0:T(4,128)(2,1)}, u32[]{:S(2)}, u32[]{:S(2)}) collective-permute-start(bf16[4,7168]{1,0:T(4,128)(2,1)} %get-tuple-element.48), channel_id=1, source_target_pairs={{0,12},{2,14},{4,8},{6,10},{8,4},{10,6},{12,0},{14,2},{1,13},{3,15... | collective-permute-start | bytes 172040 | tf_op jit(solution)/shard_map/ppermute | solution.py:568
  60.0 0.9 copy-done.5
  60.9 0.9 copy-done.9
  61.9 6.8 %attend_give_keep.4 = (bf16[256,512]{1,0:T(8,128)(2,1)S(1)}, bf16[8,256,512]{2,1,0:T(8,128)(2,1)}) custom-call(s32[8]{0:T(128)S(1)} %copy-done.22, s32[1]{0:T(128)} %bitcast.own_ref.refs_1_, bf16[4,320,512]{2,1,0:T(8,128)(2,1)S(1)} %collective-permute-done.refs_2_, bf16[8,256,512]{2,1,0:T(8,128)(2,1)S(1)} %bitcast.10, ...), custom_call_target="tpu_custom_call", output_to_operand_aliasing={{1}: (8, {})} | custom-call | bytes 1024 | tf_op jit(solution)/shard_map/attend_give_keep/pallas_call | solution.py:296
  69.2 1.1 collective-permute-done.9.refs_1_
  70.4 1.4 %broadcast_select_fusion.1.refs_6_ = bf16[1152,512]{1,0:T(8,128)(2,1)S(1)} fusion(bf16[1152,512]{1,0:T(8,128)(2,1)} %collective-permute-done.2, bf16[1152,512]{1,0:T(8,128)(2,1)} %collective-permute-done.5, pred[]{:T(512)S(6)} %and.21), kind=kLoop, calls=%fused_computation.2 | loop fusion | flops 589824 | bytes 3538945 | tf_op jit(solution)/shard_map/jit(_where)/select_n | solution.py:614
  71.9 1.5 %collective-permute-start.4 = (bf16[1152,512]{1,0:T(8,128)(2,1)}, bf16[1152,512]{1,0:T(8,128)(2,1)S(1)}, u32[]{:S(2)}, u32[]{:S(2)}) collective-permute-start(bf16[1152,512]{1,0:T(8,128)(2,1)} %collective-permute-done.3), channel_id=1, source_target_pairs={{4,0},{8,12},{6,2},{10,14},{5,1},{9,13},{7,3},{11,15},{20,16},{24,... | collective-permute-start | bytes 3538952 | tf_op jit(solution)/shard_map/ppermute | solution.py:34
  73.4 1.6 %collective-permute-start.13 = (bf16[256,512]{1,0:T(8,128)(2,1)S(1)}, bf16[256,512]{1,0:T(8,128)(2,1)S(1)}, u32[]{:S(2)}, u32[]{:S(2)}) collective-permute-start(bf16[256,512]{1,0:T(8,128)(2,1)S(1)} %copy-done.26), channel_id=1, source_target_pairs={{0,2},{2,0},{4,6},{6,4},{8,10},{10,8},{12,14},{14,12},{1,3},{3,1},... | collective-permute-start | bytes 786440 | tf_op jit(solution)/shard_map/ppermute | solution.py:26
  75.5 1.2 stack_rows.1.mine_ref
  76.8 5.8 %collective-permute-done.13.refs_8_ = bf16[256,512]{1,0:T(8,128)(2,1)S(1)} collective-permute-done((bf16[256,512]{1,0:T(8,128)(2,1)S(1)}, bf16[256,512]{1,0:T(8,128)(2,1)S(1)}, u32[]{:S(2)}, u32[]{:S(2)}) %collective-permute-start.13) | collective-permute-done | bytes 262176 | tf_op jit(solution)/shard_map/ppermute | solution.py:26
  82.6 5.2 %collective-permute-done.14.refs_9_ = bf16[256,512]{1,0:T(8,128)(2,1)S(1)} collective-permute-done((bf16[256,512]{1,0:T(8,128)(2,1)S(1)}, bf16[256,512]{1,0:T(8,128)(2,1)S(1)}, u32[]{:S(2)}, u32[]{:S(2)}) %collective-permute-start.14) | collective-permute-done | bytes 262176 | tf_op jit(solution)/shard_map/ppermute | solution.py:26
  87.8 5.9 %attend_give_keep.5 = (bf16[256,512]{1,0:T(8,128)(2,1)S(1)}, bf16[8,256,512]{2,1,0:T(8,128)(2,1)}) custom-call(s32[8]{0:T(128)S(1)} %copy-done.22, s32[1]{0:T(128)} %bitcast.own_ref.refs_1_, bf16[4,320,512]{2,1,0:T(8,128)(2,1)S(1)} %collective-permute-done.refs_2_, bf16[8,256,512]{2,1,0:T(8,128)(2,1)S(1)} %bitcast.11, ...), custom_call_target="tpu_custom_call", output_to_operand_aliasing={{1}: (10, {})} | custom-call | bytes 1024 | tf_op jit(solution)/shard_map/attend_give_keep/pallas_call | solution.py:296
  93.7 1.6 %collective-permute-start.15 = (bf16[256,512]{1,0:T(8,128)(2,1)S(1)}, bf16[256,512]{1,0:T(8,128)(2,1)S(1)}, u32[]{:S(2)}, u32[]{:S(2)}) collective-permute-start(bf16[256,512]{1,0:T(8,128)(2,1)S(1)} %get-tuple-element.51), channel_id=1, source_target_pairs={{0,2},{2,0},{4,6},{6,4},{8,10},{10,8},{12,14},{14,12},{1,3},{3,1},... | collective-permute-start | bytes 786440 | tf_op jit(solution)/shard_map/ppermute | solution.py:26
  95.3 1.6 %experts.1 = (f32[16,7168]{1,0:T(8,128)S(1)}, bf16[16,7168]{1,0:T(8,128)(2,1)S(1)}) custom-call(bf16[16,7168]{1,0:T(8,128)(2,1)S(1)} %stack_rows.1.mine_ref, bf16[16,7168]{1,0:T(8,128)(2,1)S(1)} %collective-permute-done.16.theirs_ref, bf16[1,7168,128]{2,1,0:T(8,128)(2,1)S(1)} %copy-done.13, bf16[1,7168,128]{2,1,0:T(8,128)(2,1)S(1)} %copy-done.14, ...), custom_call_target="tpu_custom_call" | custom-call | bytes 1024 | tf_op jit(solution)/shard_map/experts/pallas_call | solution.py:449
  96.9 1.5 %collective-permute-done.17.arrived_ref = bf16[16,7168]{1,0:T(8,128)(2,1)S(1)} collective-permute-done((bf16[16,7168]{1,0:T(8,128)(2,1)S(1)}, bf16[16,7168]{1,0:T(8,128)(2,1)S(1)}, u32[]{:S(2)}, u32[]{:S(2)}) %collective-permute-start.17) | collective-permute-done | bytes 229408 | tf_op jit(solution)/shard_map/ppermute | solution.py:26
  98.5 3.9 %collective-permute-done.4 = bf16[1152,512]{1,0:T(8,128)(2,1)S(1)} collective-permute-done((bf16[1152,512]{1,0:T(8,128)(2,1)}, bf16[1152,512]{1,0:T(8,128)(2,1)S(1)}, u32[]{:S(2)}, u32[]{:S(2)}) %collective-permute-start.4) | collective-permute-done | bytes 1179680 | tf_op jit(solution)/shard_map/ppermute | solution.py:34
  102.4 1.5 %collective-permute-start.18 = (bf16[8,7168]{1,0:T(8,128)(2,1)S(1)}, bf16[8,7168]{1,0:T(8,128)(2,1)S(1)}, u32[]{:S(2)}, u32[]{:S(2)}) collective-permute-start(bf16[8,7168]{1,0:T(8,128)(2,1)S(1)} %get-tuple-element.61), channel_id=1, source_target_pairs={{0,2},{2,0},{4,6},{6,4},{8,10},{10,8},{12,14},{14,12},{1,3},{3,1},... | collective-permute-start | bytes 344072 | tf_op jit(solution)/shard_map/ppermute | solution.py:26
  104.2 3.0 %collective-permute-done.18 = bf16[8,7168]{1,0:T(8,128)(2,1)S(1)} collective-permute-done((bf16[8,7168]{1,0:T(8,128)(2,1)S(1)}, bf16[8,7168]{1,0:T(8,128)(2,1)S(1)}, u32[]{:S(2)}, u32[]{:S(2)}) %collective-permute-start.18) | collective-permute-done | bytes 114720 | tf_op jit(solution)/shard_map/ppermute | solution.py:26
  107.9 3.4 %attend_give.1 = bf16[256,512]{1,0:T(8,128)(2,1)S(1)} custom-call(s32[8]{0:T(128)S(1)} %copy-done.22, s32[1]{0:T(128)} %bitcast.own_ref.refs_1_, bf16[4,320,512]{2,1,0:T(8,128)(2,1)S(1)} %collective-permute-done.refs_2_, bf16[1152,512]{1,0:T(8,128)(2,1)S(1)} %broadcast_select_fusion.refs_3_.refs_5_, bf16[1152,512]{1,0:T(8,128)(2,1)S(1)} %collective-permute-done.19.refs_4_.refs_6_), custom_call_target="tpu_custom_call" | custom-call | bytes 1024 | tf_op jit(solution)/shard_map/attend_give/pallas_call | solution.py:296
  112.1 1.8 %collective-permute-start.21 = (bf16[2,7168]{1,0:T(2,128)(2,1)}, bf16[2,7168]{1,0:T(2,128)(2,1)S(1)}, u32[]{:S(2)}, u32[]{:S(2)}) collective-permute-start(bf16[2,7168]{1,0:T(2,128)(2,1)} %get-tuple-element.71), channel_id=1, source_target_pairs={{0,4},{2,6},{4,0},{6,2},{8,12},{10,14},{12,8},{14,10},{1,5},{3,7},... | collective-permute-start | bytes 86024 | tf_op jit(solution)/shard_map/ppermute | solution.py:568
  113.9 1.1 collective-permute-start.20
  115.1 2.0 %collective-permute-start.22 = (bf16[2,7168]{1,0:T(2,128)(2,1)S(1)}, bf16[2,7168]{1,0:T(2,128)(2,1)S(1)}, u32[]{:S(2)}, u32[]{:S(2)}) collective-permute-start(bf16[2,7168]{1,0:T(2,128)(2,1)S(1)} %get-tuple-element.73), channel_id=1, source_target_pairs={{0,8},{2,10},{4,12},{6,14},{8,0},{10,2},{12,4},{14,6},{1,9},{3,11}... | collective-permute-start | bytes 86024 | tf_op jit(solution)/shard_map/ppermute | solution.py:568
  117.1 1.0 collective-permute-start.23
  118.1 1.3 copy-done.2
  119.3 0.9 copy-done.6
  120.3 0.9 copy-done.10
  121.2 1.3 copy-done.12
  122.5 0.9 copy-done.19
  123.5 4.1 %attend_keep.1.before = bf16[8,256,512]{2,1,0:T(8,128)(2,1)} custom-call(s32[8]{0:T(128)S(1)} %copy-done.22, s32[1]{0:T(128)} %bitcast.own_ref.refs_1_, bf16[8,256,512]{2,1,0:T(8,128)(2,1)S(1)} %bitcast.12, bf16[8,32,512]{2,1,0:T(8,128)(2,1)S(1)} %copy-done.6, bf16[8,32,512]{2,1,0:T(8,128)(2,1)S(1)} %copy-done.10, ...), custom_call_target="tpu_custom_call", output_to_operand_aliasing={{}: (8, {})} | custom-call | bytes 1024 | tf_op jit(solution)/shard_map/attend_keep/pallas_call | solution.py:296
  128.7 1.3 place.1
  (87 shorter events, 7.0 us)
Async XLA Ops:
  0.6 1.2 copy-start.16
  2.8 6.1 %copy-start.27 = (bf16[8,2,8192]{2,1,0:T(2,128)(2,1)S(1)}, bf16[8,2,8192]{2,1,0:T(2,128)(2,1)}, u32[]{:S(2)}) copy-start(bf16[8,2,8192]{2,1,0:T(2,128)(2,1)} %param.16) | copy-start | bytes 786436
  2.8 6.3 %copy-start.28 = (bf16[8,2,512]{2,1,0:T(2,128)(2,1)S(1)}, bf16[8,2,512]{2,1,0:T(2,128)(2,1)}, u32[]{:S(2)}) copy-start(bf16[8,2,512]{2,1,0:T(2,128)(2,1)} %param.17) | copy-start | bytes 49156
  2.8 6.3 %copy-start.29 = (bf16[8,2,64]{2,1,0:T(2,128)(2,1)S(1)}, bf16[8,2,64]{2,1,0:T(2,128)(2,1)}, u32[]{:S(2)}) copy-start(bf16[8,2,64]{2,1,0:T(2,128)(2,1)} %param.18) | copy-start | bytes 6148
  2.8 7.0 %copy-start = (bf16[8,2,128,512]{3,2,1,0:T(8,128)(2,1)S(1)}, bf16[8,2,128,512]{3,2,1,0:T(8,128)(2,1)}, u32[]{:S(2)}) copy-start(bf16[8,2,128,512]{3,2,1,0:T(8,128)(2,1)} %param.15) | copy-start | bytes 6291460
  2.8 7.0 %copy-start.22 = (s32[8]{0:T(128)S(1)}, s32[8]{0:T(128)}, u32[]{:S(2)}) copy-start(s32[8]{0:T(128)} %slot_ref.3) | copy-start | bytes 100
  4.1 29.4 %collective-permute-start.1 = (bf16[1152,512]{1,0:T(8,128)(2,1)}, bf16[1152,512]{1,0:T(8,128)(2,1)}, u32[]{:S(2)}, u32[]{:S(2)}) collective-permute-start(bf16[1152,512]{1,0:T(8,128)(2,1)} %pack_cache.1.refs_6_), channel_id=1, source_target_pairs={{0,4},{4,0},{8,12},{12,8},{2,6},{6,2},{10,14},{14,10},{1,5},{5,1},... | collective-permute-start | bytes 3538952 | tf_op jit(solution)/shard_map/ppermute | solution.py:34
  7.2 28.0 %collective-permute-start.2 = (bf16[1152,512]{1,0:T(8,128)(2,1)}, bf16[1152,512]{1,0:T(8,128)(2,1)}, u32[]{:S(2)}, u32[]{:S(2)}) collective-permute-start(bf16[1152,512]{1,0:T(8,128)(2,1)} %pack_cache.1.refs_6_), channel_id=1, source_target_pairs={{4,8},{8,4},{6,10},{10,6},{5,9},{9,5},{7,11},{11,7},{20,24},{24,20... | collective-permute-start | bytes 3538952 | tf_op jit(solution)/shard_map/ppermute | solution.py:34
  9.1 2.9 %copy-start.7 = (bf16[8,32,512]{2,1,0:T(8,128)(2,1)}, bf16[8,32,512]{2,1,0:T(8,128)(2,1)S(1)}, u32[]{:S(2)}) copy-start(bf16[8,32,512]{2,1,0:T(8,128)(2,1)S(1)} %fusion.2.new_ref.refs_5_.refs_4_) | copy-start | bytes 786436
  9.8 28.4 %copy-start.23 = (s32[8,2,8]{2,1,0:T(2,128)S(1)}, s32[8,2,8]{2,1,0:T(2,128)}, u32[]{:S(2)}) copy-start(s32[8,2,8]{2,1,0:T(2,128)} %param.21) | copy-start | bytes 1540
  9.8 28.4 %copy-start.24 = (f32[8,2,8]{2,1,0:T(2,128)S(1)}, f32[8,2,8]{2,1,0:T(2,128)}, u32[]{:S(2)}) copy-start(f32[8,2,8]{2,1,0:T(2,128)} %param.22) | copy-start | bytes 1540
  12.0 30.5 %collective-permute-start = (bf16[4,320,512]{2,1,0:T(8,128)(2,1)}, bf16[4,320,512]{2,1,0:T(8,128)(2,1)S(1)}, u32[]{:S(2)}, u32[]{:S(2)}) collective-permute-start(bf16[4,320,512]{2,1,0:T(8,128)(2,1)} %pack_leaving.1), channel_id=1, source_target_pairs={{0,2},{2,0},{4,6},{6,4},{8,10},{10,8},{12,14},{14,12},{1,3},{3,1},... | collective-permute-start | bytes 3932168 | tf_op jit(solution)/shard_map/ppermute | solution.py:26
  13.6 30.5 %collective-permute-start.7 = (bf16[1152,512]{1,0:T(8,128)(2,1)}, bf16[1152,512]{1,0:T(8,128)(2,1)}, u32[]{:S(2)}, u32[]{:S(2)}) collective-permute-start(bf16[1152,512]{1,0:T(8,128)(2,1)} %pack_cache.1.refs_6_), channel_id=1, source_target_pairs={{0,1},{1,0},{2,3},{3,2},{4,5},{5,4},{6,7},{7,6},{8,9},{9,8},{10,11... | collective-permute-start | bytes 3538952 | tf_op jit(solution)/shard_map/ppermute | solution.py:26
  33.5 26.5 %collective-permute-start.6 = (bf16[1152,512]{1,0:T(8,128)(2,1)}, bf16[1152,512]{1,0:T(8,128)(2,1)}, u32[]{:S(2)}, u32[]{:S(2)}) collective-permute-start(bf16[1152,512]{1,0:T(8,128)(2,1)} %collective-permute-done.1.refs_6_), channel_id=1, source_target_pairs={{0,1},{1,0},{2,3},{3,2},{4,5},{5,4},{6,7},{7,6},{8,9},{9,8},{10,11... | collective-permute-start | bytes 3538952 | tf_op jit(solution)/shard_map/ppermute | solution.py:26
  33.5 36.9 %collective-permute-start.3 = (bf16[1152,512]{1,0:T(8,128)(2,1)}, bf16[1152,512]{1,0:T(8,128)(2,1)}, u32[]{:S(2)}, u32[]{:S(2)}) collective-permute-start(bf16[1152,512]{1,0:T(8,128)(2,1)} %collective-permute-done.1.refs_6_), channel_id=1, source_target_pairs={{4,8},{8,4},{6,10},{10,6},{5,9},{9,5},{7,11},{11,7},{20,24},{24,20... | collective-permute-start | bytes 3538952 | tf_op jit(solution)/shard_map/ppermute | solution.py:34
  35.2 35.2 %collective-permute-start.5 = (bf16[1152,512]{1,0:T(8,128)(2,1)}, bf16[1152,512]{1,0:T(8,128)(2,1)}, u32[]{:S(2)}, u32[]{:S(2)}) collective-permute-start(bf16[1152,512]{1,0:T(8,128)(2,1)} %collective-permute-done.2), channel_id=1, source_target_pairs={{4,0},{8,12},{6,2},{10,14},{5,1},{9,13},{7,3},{11,15},{20,16},{24,... | collective-permute-start | bytes 3538952 | tf_op jit(solution)/shard_map/ppermute | solution.py:34
  42.6 10.9 %collective-permute-start.8 = (bf16[4,7168]{1,0:T(4,128)(2,1)S(1)}, bf16[4,7168]{1,0:T(4,128)(2,1)S(1)}, u32[]{:S(2)}, u32[]{:S(2)}) collective-permute-start(bf16[4,7168]{1,0:T(4,128)(2,1)S(1)} %get-tuple-element.44.refs_0_), channel_id=1, source_target_pairs={{0,2},{2,0},{4,6},{6,4},{8,10},{10,8},{12,14},{14,12},{1,3},{3,1},... | collective-permute-start | bytes 172040 | tf_op jit(solution)/shard_map/ppermute | solution.py:26
  44.1 1.0 copy-start.4
  45.0 0.9 copy-start.8
  54.5 14.7 %collective-permute-start.10 = (bf16[4,7168]{1,0:T(4,128)(2,1)}, bf16[4,7168]{1,0:T(4,128)(2,1)S(1)}, u32[]{:S(2)}, u32[]{:S(2)}) collective-permute-start(bf16[4,7168]{1,0:T(4,128)(2,1)} %get-tuple-element.48), channel_id=1, source_target_pairs={{0,8},{2,10},{4,12},{6,14},{8,0},{10,2},{12,4},{14,6},{1,9},{3,11}... | collective-permute-start | bytes 172040 | tf_op jit(solution)/shard_map/ppermute | solution.py:568
  57.4 11.8 %collective-permute-start.11 = (bf16[4,7168]{1,0:T(4,128)(2,1)}, bf16[4,7168]{1,0:T(4,128)(2,1)}, u32[]{:S(2)}, u32[]{:S(2)}) collective-permute-start(bf16[4,7168]{1,0:T(4,128)(2,1)} %get-tuple-element.48), channel_id=1, source_target_pairs={{0,12},{2,14},{4,8},{6,10},{8,4},{10,6},{12,0},{14,2},{1,13},{3,15... | collective-permute-start | bytes 172040 | tf_op jit(solution)/shard_map/ppermute | solution.py:568
  60.0 10.4 %collective-permute-start.9 = (bf16[4,7168]{1,0:T(4,128)(2,1)S(1)}, bf16[4,7168]{1,0:T(4,128)(2,1)}, u32[]{:S(2)}, u32[]{:S(2)}) collective-permute-start(bf16[4,7168]{1,0:T(4,128)(2,1)S(1)} %get-tuple-element.52.refs_0_), channel_id=1, source_target_pairs={{0,4},{2,6},{4,0},{6,2},{8,12},{10,14},{12,8},{14,10},{1,5},{3,7},... | collective-permute-start | bytes 172040 | tf_op jit(solution)/shard_map/ppermute | solution.py:568
  60.0 1.0 copy-start.5
  60.9 0.9 copy-start.9
  70.4 3.0 %copy-start.26 = (bf16[256,512]{1,0:T(8,128)(2,1)S(1)}, bf16[256,512]{1,0:T(8,128)(2,1)}, u32[]{:S(2)}) copy-start(bf16[256,512]{1,0:T(8,128)(2,1)} %copy-done.25) | copy-start | bytes 786436
  71.8 16.0 %collective-permute-start.12 = (bf16[1152,512]{1,0:T(8,128)(2,1)S(1)}, bf16[1152,512]{1,0:T(8,128)(2,1)S(1)}, u32[]{:S(2)}, u32[]{:S(2)}) collective-permute-start(bf16[1152,512]{1,0:T(8,128)(2,1)S(1)} %broadcast_select_fusion.1.refs_6_), channel_id=1, source_target_pairs={{0,1},{1,0},{2,3},{3,2},{4,5},{5,4},{6,7},{7,6},{8,9},{9,8},{10,11... | collective-permute-start | bytes 3538952 | tf_op jit(solution)/shard_map/ppermute | solution.py:26
  71.9 30.5 %collective-permute-start.4 = (bf16[1152,512]{1,0:T(8,128)(2,1)}, bf16[1152,512]{1,0:T(8,128)(2,1)S(1)}, u32[]{:S(2)}, u32[]{:S(2)}) collective-permute-start(bf16[1152,512]{1,0:T(8,128)(2,1)} %collective-permute-done.3), channel_id=1, source_target_pairs={{4,0},{8,12},{6,2},{10,14},{5,1},{9,13},{7,3},{11,15},{20,16},{24,... | collective-permute-start | bytes 3538952 | tf_op jit(solution)/shard_map/ppermute | solution.py:34
  73.4 9.2 %collective-permute-start.13 = (bf16[256,512]{1,0:T(8,128)(2,1)S(1)}, bf16[256,512]{1,0:T(8,128)(2,1)S(1)}, u32[]{:S(2)}, u32[]{:S(2)}) collective-permute-start(bf16[256,512]{1,0:T(8,128)(2,1)S(1)} %copy-done.26), channel_id=1, source_target_pairs={{0,2},{2,0},{4,6},{6,4},{8,10},{10,8},{12,14},{14,12},{1,3},{3,1},... | collective-permute-start | bytes 786440 | tf_op jit(solution)/shard_map/ppermute | solution.py:26
  75.0 12.8 %collective-permute-start.14 = (bf16[256,512]{1,0:T(8,128)(2,1)S(1)}, bf16[256,512]{1,0:T(8,128)(2,1)S(1)}, u32[]{:S(2)}, u32[]{:S(2)}) collective-permute-start(bf16[256,512]{1,0:T(8,128)(2,1)S(1)} %get-tuple-element.42), channel_id=1, source_target_pairs={{0,2},{2,0},{4,6},{6,4},{8,10},{10,8},{12,14},{14,12},{1,3},{3,1},... | collective-permute-start | bytes 786440 | tf_op jit(solution)/shard_map/ppermute | solution.py:26
  76.7 18.5 %collective-permute-start.16 = (bf16[16,7168]{1,0:T(8,128)(2,1)S(1)}, bf16[16,7168]{1,0:T(8,128)(2,1)S(1)}, u32[]{:S(2)}, u32[]{:S(2)}) collective-permute-start(bf16[16,7168]{1,0:T(8,128)(2,1)S(1)} %stack_rows.1.mine_ref), channel_id=1, source_target_pairs={{0,1},{1,0},{2,3},{3,2},{4,5},{5,4},{6,7},{7,6},{8,9},{9,8},{10,11... | collective-permute-start | bytes 688136 | tf_op jit(solution)/shard_map/ppermute | solution.py:26
  87.8 7.5 %copy-start.13 = (bf16[1,7168,128]{2,1,0:T(8,128)(2,1)S(1)}, bf16[1,7168,128]{2,1,0:T(8,128)(2,1)}, u32[]{:S(2)}) copy-start(bf16[1,7168,128]{2,1,0:T(8,128)(2,1)} %gate_hbm.1) | copy-start | bytes 5505028
  87.8 7.5 %copy-start.14 = (bf16[1,7168,128]{2,1,0:T(8,128)(2,1)S(1)}, bf16[1,7168,128]{2,1,0:T(8,128)(2,1)}, u32[]{:S(2)}) copy-start(bf16[1,7168,128]{2,1,0:T(8,128)(2,1)} %up_hbm.1) | copy-start | bytes 5505028
  87.8 7.5 %copy-start.15 = (bf16[1,128,7168]{2,1,0:T(8,128)(2,1)S(1)}, bf16[1,128,7168]{2,1,0:T(8,128)(2,1)}, u32[]{:S(2)}) copy-start(bf16[1,128,7168]{2,1,0:T(8,128)(2,1)} %down_hbm.1) | copy-start | bytes 5505028
  93.7 8.7 %collective-permute-start.15 = (bf16[256,512]{1,0:T(8,128)(2,1)S(1)}, bf16[256,512]{1,0:T(8,128)(2,1)S(1)}, u32[]{:S(2)}, u32[]{:S(2)}) collective-permute-start(bf16[256,512]{1,0:T(8,128)(2,1)S(1)} %get-tuple-element.51), channel_id=1, source_target_pairs={{0,2},{2,0},{4,6},{6,4},{8,10},{10,8},{12,14},{14,12},{1,3},{3,1},... | collective-permute-start | bytes 786440 | tf_op jit(solution)/shard_map/ppermute | solution.py:26
  96.9 1.6 %collective-permute-start.17 = (bf16[16,7168]{1,0:T(8,128)(2,1)S(1)}, bf16[16,7168]{1,0:T(8,128)(2,1)S(1)}, u32[]{:S(2)}, u32[]{:S(2)}) collective-permute-start(bf16[16,7168]{1,0:T(8,128)(2,1)S(1)} %get-tuple-element.57), channel_id=1, source_target_pairs={{0,1},{1,0},{2,3},{3,2},{4,5},{5,4},{6,7},{7,6},{8,9},{9,8},{10,11... | collective-permute-start | bytes 688136 | tf_op jit(solution)/shard_map/ppermute | solution.py:26
  102.4 1.7 %copy-start.18 = (bf16[256,512]{1,0:T(8,128)(2,1)}, bf16[256,512]{1,0:T(8,128)(2,1)S(1)}, u32[]{:S(2)}) copy-start(bf16[256,512]{1,0:T(8,128)(2,1)S(1)} %collective-permute-done.15.refs_7_) | copy-start | bytes 786436
  102.4 4.8 %collective-permute-start.18 = (bf16[8,7168]{1,0:T(8,128)(2,1)S(1)}, bf16[8,7168]{1,0:T(8,128)(2,1)S(1)}, u32[]{:S(2)}, u32[]{:S(2)}) collective-permute-start(bf16[8,7168]{1,0:T(8,128)(2,1)S(1)} %get-tuple-element.61), channel_id=1, source_target_pairs={{0,2},{2,0},{4,6},{6,4},{8,10},{10,8},{12,14},{14,12},{1,3},{3,1},... | collective-permute-start | bytes 344072 | tf_op jit(solution)/shard_map/ppermute | solution.py:26
  104.1 7.3 %copy-start.1 = (bf16[1152,512]{1,0:T(8,128)(2,1)}, bf16[1152,512]{1,0:T(8,128)(2,1)S(1)}, u32[]{:S(2)}) copy-start(bf16[1152,512]{1,0:T(8,128)(2,1)S(1)} %broadcast_select_fusion.refs_3_.refs_5_) | copy-start | bytes 3538948
  104.1 3.8 %collective-permute-start.19 = (bf16[1152,512]{1,0:T(8,128)(2,1)S(1)}, bf16[1152,512]{1,0:T(8,128)(2,1)S(1)}, u32[]{:S(2)}, u32[]{:S(2)}) collective-permute-start(bf16[1152,512]{1,0:T(8,128)(2,1)S(1)} %broadcast_select_fusion.refs_3_.refs_5_), channel_id=1, source_target_pairs={{0,1},{1,0},{2,3},{3,2},{4,5},{5,4},{6,7},{7,6},{8,9},{9,8},{10,11... | collective-permute-start | bytes 3538952 | tf_op jit(solution)/shard_map/ppermute | solution.py:26
  107.9 3.5 %copy-start.11 = (bf16[1152,512]{1,0:T(8,128)(2,1)}, bf16[1152,512]{1,0:T(8,128)(2,1)S(1)}, u32[]{:S(2)}) copy-start(bf16[1152,512]{1,0:T(8,128)(2,1)S(1)} %collective-permute-done.19.refs_4_.refs_6_) | copy-start | bytes 3538948
  112.1 15.5 %collective-permute-start.21 = (bf16[2,7168]{1,0:T(2,128)(2,1)}, bf16[2,7168]{1,0:T(2,128)(2,1)S(1)}, u32[]{:S(2)}, u32[]{:S(2)}) collective-permute-start(bf16[2,7168]{1,0:T(2,128)(2,1)} %get-tuple-element.71), channel_id=1, source_target_pairs={{0,4},{2,6},{4,0},{6,2},{8,12},{10,14},{12,8},{14,10},{1,5},{3,7},... | collective-permute-start | bytes 86024 | tf_op jit(solution)/shard_map/ppermute | solution.py:568
  113.9 14.8 %collective-permute-start.20 = (bf16[256,512]{1,0:T(8,128)(2,1)}, bf16[256,512]{1,0:T(8,128)(2,1)S(1)}, u32[]{:S(2)}, u32[]{:S(2)}) collective-permute-start(bf16[256,512]{1,0:T(8,128)(2,1)} %copy-done.20), channel_id=1, source_target_pairs={{0,2},{2,0},{4,6},{6,4},{8,10},{10,8},{12,14},{14,12},{1,3},{3,1},... | collective-permute-start | bytes 786440 | tf_op jit(solution)/shard_map/ppermute | solution.py:26
  115.1 12.6 %collective-permute-start.22 = (bf16[2,7168]{1,0:T(2,128)(2,1)S(1)}, bf16[2,7168]{1,0:T(2,128)(2,1)S(1)}, u32[]{:S(2)}, u32[]{:S(2)}) collective-permute-start(bf16[2,7168]{1,0:T(2,128)(2,1)S(1)} %get-tuple-element.73), channel_id=1, source_target_pairs={{0,8},{2,10},{4,12},{6,14},{8,0},{10,2},{12,4},{14,6},{1,9},{3,11}... | collective-permute-start | bytes 86024 | tf_op jit(solution)/shard_map/ppermute | solution.py:568
  117.1 10.6 %collective-permute-start.23 = (bf16[2,7168]{1,0:T(2,128)(2,1)S(1)}, bf16[2,7168]{1,0:T(2,128)(2,1)S(1)}, u32[]{:S(2)}, u32[]{:S(2)}) collective-permute-start(bf16[2,7168]{1,0:T(2,128)(2,1)S(1)} %get-tuple-element.75), channel_id=1, source_target_pairs={{0,12},{2,14},{4,8},{6,10},{8,4},{10,6},{12,0},{14,2},{1,13},{3,15... | collective-permute-start | bytes 86024 | tf_op jit(solution)/shard_map/ppermute | solution.py:568
  118.1 1.3 copy-start.2
  119.3 0.9 copy-start.6
  120.3 0.9 copy-start.10
  121.2 1.3 copy-start.12
  (6 other events, 4.9 us)

commit v5 on v4

--- a/solution.py
+++ b/solution.py
@@ -50,7 +50,7 @@
     return pl.pallas_call(
         pack_cache_kernel,
         out_shape=jax.ShapeDtypeStruct((lat.shape[0] + rope.shape[0], lat.shape[1]), lat.dtype),
-        in_specs=[pl.BlockSpec(memory_space=pl.ANY)] * 2,
+        in_specs=[pl.BlockSpec(memory_space=pltpu.HBM)] * 2,
         out_specs=pl.BlockSpec(memory_space=pltpu.VMEM),
         scratch_shapes=[pltpu.SemaphoreType.DMA((2,))],
         cost_estimate=SMALL,
@@ -105,7 +105,7 @@
         pack_leaving_kernel,
         out_shape=jax.ShapeDtypeStruct((slots, rows, q_lat.shape[2]), q_lat.dtype),
         in_specs=[pl.BlockSpec(memory_space=pltpu.SMEM)] * 2
-        + [pl.BlockSpec(memory_space=pl.ANY)] * 3,
+        + [pl.BlockSpec(memory_space=pltpu.HBM)] * 3,
         out_specs=pl.BlockSpec(memory_space=pltpu.VMEM),
         scratch_shapes=[pltpu.SemaphoreType.DMA((slots, 3))],
         cost_estimate=SMALL,
@@ -142,15 +142,13 @@
     factor = softmax_scale * log2e
     contract = (((1,), (1,)), ((), ()))
 
-    def put_query(queries, number, lat, raw_rope, matrix):
-        first = number * q_rows
-        queries[first : first + q_rows, 0:width] = lat
+    def put_query_rope(query_all, number, raw_rope, matrix):
         grown = raw_group * width // (LANES // 2)
         for i, start in enumerate(range(0, token_rope, raw_group)):
             part = spread(matrix, raw_rope[start : start + raw_group, :])
             part = part + pltpu.roll(part, LANES // 2, 1)
-            row = first + i * grown
-            queries[row : row + grown, width : width + LANES] = part.astype(jnp.bfloat16)
+            row = number * q_rows + i * grown
+            query_all[row : row + grown, width : width + LANES] = part.astype(jnp.bfloat16)
 
     def merge_own(query, fresh_all, peak, total, summed):
         fresh = fresh_all[0:PAD, :]
@@ -181,12 +179,12 @@
             value = value + (part * inverse) * fresh32[j : j + 1, :]
         return value.astype(jnp.bfloat16)
 
-    def spread_keys(cache, rope_keys, matrix):
+    def put_key_rope(keys, first, raw_rope, matrix):
         grown = raw_group * width // (LANES // 2)
-        for start in range(0, rope_rows, raw_group):
-            part = spread(matrix, cache[half + start : half + start + raw_group, :])
-            first = start * (width // (LANES // 2))
-            rope_keys[first : first + grown, :] = part.astype(jnp.bfloat16)
+        for i, start in enumerate(range(0, rope_rows, raw_group)):
+            part = spread(matrix, raw_rope[start : start + raw_group, :])
+            row = first + i * grown
+            keys[row : row + grown, width : width + LANES] = part.astype(jnp.bfloat16)
 
     def kernel(slot, kinds, given_slots, has_placed, *refs):
         refs = list(refs)
@@ -199,56 +197,75 @@
             refs.pop(0)
         give = refs.pop(0) if "give" in kinds else None
         placed = refs.pop(0) if ("keep" in kinds or given_slots) else None
-        rope_keys, query_all, scores, summed, result, place_sems = refs
-        placing = []
-        for i, (number, source) in enumerate(zip(given_slots, arrived)):
-            copy = pltpu.make_async_copy(
-                source, placed.at[row_for(number, 1, slot_ref, own_ref)], place_sems.at[1 + i]
-            )
+        keys, key_rope, query_all, query_rope, fresh, scores, summed, result, staged, sems = refs
+        used = [0]
+
+        def start(source, there):
+            copy = pltpu.make_async_copy(source, there, sems.at[used[0]])
+            used[0] += 1
             copy.start()
-            placing.append(copy)
+            return copy
+
         kept_row = row_for(slot, 0, slot_ref, own_ref)
-        matrix = spread_matrix(raw_group, width)
-        fresh_parts = []
+        query_copies, rope_copies = [], []
+        middle = q_rows + token_rope
         for number, kind in enumerate(kinds):
             if kind == "give":
-                middle = q_rows + token_rope
-                lat, raw = guest[slot, 0:q_rows, :], guest[slot, q_rows:middle, :]
-                fresh_parts.append(guest[slot, middle : middle + 2 * PAD, :])
+                lat = guest.at[slot, pl.ds(0, q_rows)]
+                raw = guest.at[slot, pl.ds(q_rows, token_rope)]
+                new = guest.at[slot, pl.ds(middle, 2 * PAD)]
             else:
-                lat, raw = stay[0][kept_row], stay[1][kept_row]
-                fresh_parts.append(stay[2][kept_row])
-            put_query(query_all, number, lat, raw, matrix)
+                lat, raw, new = (source.at[kept_row] for source in stay)
+            rope_copies.append(start(raw, query_rope.at[number]))
+            there = query_all.at[pl.ds(number * q_rows, q_rows), pl.ds(0, width)]
+            query_copies.append(start(lat, there))
+            query_copies.append(start(new, fresh.at[number]))
+        key_copies, key_rope_copies = [], []
+        for i, cache in enumerate(caches):
+            key_rope_copies.append(start(cache.at[pl.ds(half, rope_rows)], key_rope.at[i]))
+            for first in range(0, half, chunk):
+                there = keys.at[pl.ds(i * half + first, chunk), pl.ds(0, width)]
+                key_copies.append(start(cache.at[pl.ds(first, chunk)], there))
+        staging = [start(source, staged.at[i]) for i, source in enumerate(arrived)]
+        matrix = spread_matrix(raw_group, width)
+        for number, copy in enumerate(rope_copies):
+            copy.wait()
+            put_query_rope(query_all, number, query_rope.at[number], matrix)
+        for i, copy in enumerate(key_rope_copies):
+            copy.wait()
+            put_key_rope(keys, i * half, key_rope.at[i], matrix)
+        for copy in query_copies:
+            copy.wait()
         peak = None
-        for i, cache in enumerate(caches):
-            spread_keys(cache, rope_keys, matrix)
-            for start in range(0, half, chunk):
-                part = lax.dot_general(
-                    query_all[:, 0:width],
-                    cache[start : start + chunk, :],
-                    contract,
-                    preferred_element_type=jnp.float32,
-                )
-                part = part + lax.dot_general(
-                    query_all[:, width:],
-                    rope_keys[start : start + chunk, :],
-                    contract,
-                    preferred_element_type=jnp.float32,
-                )
-                scores[:, i * half + start : i * half + start + chunk] = part
-                high = jnp.max(part, axis=1, keepdims=True)
-                peak = high if peak is None else jnp.maximum(peak, high)
+        for number, copy in enumerate(key_copies):
+            copy.wait()
+            first = number * chunk
+            part = lax.dot_general(
+                query_all[...],
+                keys[first : first + chunk, :],
+                contract,
+                preferred_element_type=jnp.float32,
+            )
+            scores[:, first : first + chunk] = part
+            high = jnp.max(part, axis=1, keepdims=True)
+            peak = high if peak is None else jnp.maximum(peak, high)
+        placing = []
+        for i, (number, copy) in enumerate(zip(given_slots, staging)):
+            copy.wait()
+            placing.append(
+                start(staged.at[i], placed.at[row_for(number, 1, slot_ref, own_ref)])
+            )
         scaled = peak * factor
         total = None
-        for start in range(0, 2 * half, chunk):
-            weights = jnp.exp2(scores[:, start : start + chunk] * factor - scaled)
+        for first in range(0, 2 * half, chunk):
+            weights = jnp.exp2(scores[:, first : first + chunk] * factor - scaled)
             part = jnp.sum(weights, axis=1, keepdims=True)
             value = jnp.dot(
                 weights.astype(jnp.bfloat16),
-                caches[start // half][start % half : start % half + chunk, :],
+                keys[first : first + chunk, 0:width],
                 preferred_element_type=jnp.float32,
             )
-            if start == 0:
+            if first == 0:
                 total = part
                 summed[...] = value
             else:
@@ -256,22 +273,18 @@
                 summed[...] += value
         for number, kind in enumerate(kinds):
             rows = slice(number * q_rows, (number + 1) * q_rows)
-            value = merge_own(
-                query_all[rows, :], fresh_parts[number], peak[rows], total[rows], summed[rows, :]
+            result[number] = merge_own(
+                query_all[rows, :], fresh[number], peak[rows], total[rows], summed[rows, :]
             )
-            if kind == "give":
-                give[...] = value
-            else:
-                result[...] = value
-                copy = pltpu.make_async_copy(result, placed.at[kept_row], place_sems.at[0])
-                copy.start()
-                placing.append(copy)
+            there = give if kind == "give" else placed.at[kept_row]
+            placing.append(start(result.at[number], there))
         for copy in placing:
             copy.wait()
 
     def call(scalars, kinds, slot, guest, stay, caches, arrived, placed):
         count = scalars[0].shape[0]
         n_tok = len(kinds)
+        hbm = pl.BlockSpec(memory_space=pltpu.HBM)
         operands = [*scalars]
         if "give" in kinds:
             operands.append(guest)
@@ -280,31 +293,34 @@
         given_slots = tuple(number for number, _ in arrived)
         operands += [*caches, *(value for _, value in arrived)]
         in_specs = [pl.BlockSpec(memory_space=pltpu.SMEM)] * len(scalars)
-        in_specs += [pl.BlockSpec(memory_space=pltpu.VMEM)] * (len(operands) - len(scalars))
-        out_shape, out_specs, alias = [], [], {}
+        in_specs += [hbm] * (len(operands) - len(scalars))
+        out_shape, alias = [], {}
         if "give" in kinds:
             out_shape.append(jax.ShapeDtypeStruct((q_rows, width), jnp.bfloat16))
-            out_specs.append(pl.BlockSpec(memory_space=pltpu.VMEM))
         if "keep" in kinds or arrived:
             out_shape.append(jax.ShapeDtypeStruct((count, q_rows, width), jnp.bfloat16))
-            out_specs.append(pl.BlockSpec(memory_space=pl.ANY))
         has_placed = placed is not None
         if has_placed:
             alias = {len(operands): len(out_shape) - 1}
-            in_specs.append(pl.BlockSpec(memory_space=pl.ANY))
+            in_specs.append(hbm)
             operands.append(placed)
+        copies = 4 * n_tok + 2 * (1 + half // chunk) + 2 * len(arrived)
         return pl.pallas_call(
             functools.partial(kernel, slot, kinds, given_slots, has_placed),
             out_shape=tuple(out_shape),
             in_specs=in_specs,
-            out_specs=tuple(out_specs),
+            out_specs=(hbm,) * len(out_shape),
             scratch_shapes=[
-                pltpu.VMEM((half, LANES), jnp.bfloat16),
+                pltpu.VMEM((2 * half, width + LANES), jnp.bfloat16),
+                pltpu.VMEM((2, rope_rows, width), jnp.bfloat16),
                 pltpu.VMEM((n_tok * q_rows, width + LANES), jnp.bfloat16),
+                pltpu.VMEM((n_tok, token_rope, width), jnp.bfloat16),
+                pltpu.VMEM((n_tok, 2 * PAD, width), jnp.bfloat16),
                 pltpu.VMEM((n_tok * q_rows, 2 * half), jnp.float32),
                 pltpu.VMEM((n_tok * q_rows, width), jnp.float32),
-                pltpu.VMEM((q_rows, width), jnp.bfloat16),
-                pltpu.SemaphoreType.DMA((1 + max(1, len(arrived)),)),
+                pltpu.VMEM((n_tok, q_rows, width), jnp.bfloat16),
+                pltpu.VMEM((max(1, len(arrived)), q_rows, width), jnp.bfloat16),
+                pltpu.SemaphoreType.DMA((copies,)),
             ],
             input_output_aliases=alias,
             cost_estimate=SMALL,
@@ -327,8 +343,8 @@
         functools.partial(place_kernel, slot),
         out_shape=jax.ShapeDtypeStruct(placed.shape, placed.dtype),
         in_specs=[pl.BlockSpec(memory_space=pltpu.SMEM)] * 2
-        + [pl.BlockSpec(memory_space=pltpu.VMEM), pl.BlockSpec(memory_space=pl.ANY)],
-        out_specs=pl.BlockSpec(memory_space=pl.ANY),
+        + [pl.BlockSpec(memory_space=pltpu.VMEM), pl.BlockSpec(memory_space=pltpu.HBM)],
+        out_specs=pl.BlockSpec(memory_space=pltpu.HBM),
         scratch_shapes=[pltpu.SemaphoreType.DMA],
         input_output_aliases={3: 0},
         cost_estimate=SMALL,
@@ -453,7 +469,7 @@
             jax.ShapeDtypeStruct(mine.shape, jnp.bfloat16),
         ),
         in_specs=[pl.BlockSpec(memory_space=pltpu.VMEM)] * 2
-        + [pl.BlockSpec(memory_space=pl.ANY)] * 3,
+        + [pl.BlockSpec(memory_space=pltpu.HBM)] * 3,
         out_specs=(pl.BlockSpec(memory_space=pltpu.VMEM),) * 2,
         scratch_shapes=[
             pltpu.VMEM(w_gate.shape[1:], w_gate.dtype),
@@ -522,9 +538,6 @@
     own_cache = pack_cache(latent_cache[0], rope_cache[0])
     cache_a = line_hop(own_cache, tok_rows, outer)
     first_b = line_hop(own_cache, tok_rows, inner)
-    second_b = line_hop(first_b, tok_rows, outward)
-    first_c = line_hop(cache_a, tok_rows, inner)
-    second_c = line_hop(first_c, tok_rows, outward)
 
     q_lat = q_latent.reshape(tok_rows, q_rows, width)
     rope_raw = q_rope.reshape(tok_rows, q_rows * rope_width // width, width)
@@ -568,6 +581,9 @@
         return lax.ppermute(x, "branch", list(enumerate(there)))
 
     beside = swapped(outgoing, "branch", 0)
+    cache_a, first_b, outgoing = lax.optimization_barrier((cache_a, first_b, outgoing))
+    second_b = line_hop(first_b, tok_rows, outward)
+    first_c = line_hop(cache_a, tok_rows, inner)
     pair = tuple(
         tuple(tuple((k * CAP + c, i * CAP + c) for c in range(CAP)) for i in range(2))
         for k in range(experts)
@@ -600,11 +616,13 @@
     pieces = [by_expert[k] if (k, m) == (0, 0) else along(by_expert[k], k, m) for k, m in ways]
     given_1, placed = attend_slot(1, both_halves(cache_a), both, [], placed)
     back_1 = swapped(given_1, "branch", 0)
+    pieces = [after(piece, given_1) for piece in pieces]
 
 
     first_c, second_b, given_1, *pieces = lax.optimization_barrier(
         (first_c, second_b, given_1, *pieces)
     )
+    second_c = line_hop(first_c, tok_rows, outward)
     count = len(ways) * CAP
     stacked = tuple(
         tuple((i * CAP + c, i * count + w * CAP + c) for i in range(2) for c in range(CAP))
@@ -612,9 +630,11 @@
     )
     (rows,) = move_rows(tuple(pieces), (stacked,), 2 * count, "stack_rows")
     cache_b = jnp.where(middle, first_b, second_b)
-    kept, sent = run_experts(rows, swapped(rows, "expert", 0), w_gate, w_up, w_down)
+    theirs = swapped(rows, "expert", 0)
+    rows, theirs, back_0, back_1 = lax.optimization_barrier((rows, theirs, back_0, back_1))
+    kept, sent = run_experts(rows, theirs, w_gate, w_up, w_down)
     kept, sent = halve(kept, swapped(sent, "expert", 0))
-    given_2, placed = attend_slot(2, both_halves(cache_b), both, [(0, back_0), (1, back_1)], placed)
+    given_2, placed = attend_slot(2, both_halves(cache_b), both, [], placed)
     back_2 = swapped(given_2, "branch", 0)
 
     second_c, back_2, kept, sent = lax.optimization_barrier((second_c, back_2, kept, sent))
@@ -628,7 +648,7 @@
     given_3, _ = attend_slot(3, cache_c, ("give",), [], None)
     homeward = [after(x, given_3) for x in homeward]
     back_3 = swapped(given_3, "branch", 0)
-    _, placed = attend_slot(3, cache_c, ("keep",), [(2, back_2)], placed)
+    _, placed = attend_slot(3, cache_c, ("keep",), [(0, back_0), (1, back_1), (2, back_2)], placed)
     placed = place(scalars, 3, back_3, placed)
     attended = placed.reshape(tok_rows, step_count, head_count, width)
 

time: 131 us -> 141 us (1.076)
  Pallas kernels: 35.9 us -> 45.7 us
  local copies, waits for them, and re-layouts: 17.8 us -> 22.8 us
  waiting for transfers between devices: 44 us -> 39.2 us
    pallas_call x5, Pallas kernels: 27 us -> 36.8 us  [call(): pl.pallas_call(functools.partial(kernel, slot, kinds, given_slots, has_pl...]
    ppermute x13, waiting for transfers between devices: 18.6 us -> 10.7 us  [swapped(): lax.ppermute(x, axis, [(i, i ^ 1 << bit) for i in range(lax.axis_size(axi...]
    unnamed x60 -> x72, local copies, waits for them, and re-layouts: 14.4 us -> 19.3 us
    ppermute x5, waiting for transfers between devices: 23.8 us -> 28.3 us  [line_hop(): return lax.ppermute(x, 'branch', pairs)]
    ppermute x6, waiting for transfers between devices: 1.68 us -> 0.16 us  [along(): return lax.ppermute(x, 'branch', list(enumerate(there)))]
  transfers between devices with their start and end apart: 24 -> 24, of which waited for: 9 -> 7; matrix products, arithmetic and copies ran while one was open for 3% -> 3% of each run, Pallas kernels for 23% -> 27%
where the time goes in v5:
time: 141 us; the launch traced here: 140 us
  Pallas kernels  45.7 us (32%)
  waiting for transfers between devices  39.2 us (28%)
  starting transfers between devices  28.4 us (20%)
  local copies, waits for them, and re-layouts  22.8 us (16%)
  other arithmetic  2.65 us (2%)
    pallas_call x5, Pallas kernels, call(): pl.pallas_call(functools.partial(kernel, slot, kinds, given_slots, has_pl...  36.8 us
    ppermute x5, waiting for transfers between devices, line_hop(): return lax.ppermute(x, 'branch', pairs)  28.3 us
    unnamed x72, local copies, waits for them, and re-layouts  19.3 us
    ppermute x13, waiting for transfers between devices, swapped(): lax.ppermute(x, axis, [(i, i ^ 1 << bit) for i in range(lax.axis_size(axi...  10.7 us
    ppermute x13, starting transfers between devices, swapped(): lax.ppermute(x, axis, [(i, i ^ 1 << bit) for i in range(lax.axis_size(axi...  10.2 us
    ppermute x5, starting transfers between devices, line_hop(): return lax.ppermute(x, 'branch', pairs)  9.23 us
    ppermute x6, starting transfers between devices, along(): return lax.ppermute(x, 'branch', list(enumerate(there)))  8.96 us
  transfers between devices with their start and end apart: 24, of which 7 were waited for; matrix products, arithmetic and copies ran while one was open for 3% of the time, Pallas kernels for 27%

profile of v5, /device:TPU:0, one launch (start us, length us, event | category | flops | bytes accessed | tf_op | source)
XLA Modules:
  0.0 139.9 jit_solution(17214508772499467798)
XLA Ops:
  0.6 1.2 copy-done.18
  2.8 1.3 pack_cache.1.refs_6_
  4.1 3.1 %collective-permute-start.1 = (bf16[1152,512]{1,0:T(8,128)(2,1)}, bf16[1152,512]{1,0:T(8,128)(2,1)}, u32[]{:S(2)}, u32[]{:S(2)}) collective-permute-start(bf16[1152,512]{1,0:T(8,128)(2,1)} %pack_cache.1.refs_6_), channel_id=1, source_target_pairs={{0,4},{4,0},{8,12},{12,8},{2,6},{6,2},{10,14},{14,10},{1,5},{5,1},... | collective-permute-start | bytes 3538952 | tf_op jit(solution)/shard_map/ppermute | solution.py:34
  7.2 1.7 %collective-permute-start.2 = (bf16[1152,512]{1,0:T(8,128)(2,1)}, bf16[1152,512]{1,0:T(8,128)(2,1)}, u32[]{:S(2)}, u32[]{:S(2)}) collective-permute-start(bf16[1152,512]{1,0:T(8,128)(2,1)} %pack_cache.1.refs_6_), channel_id=1, source_target_pairs={{4,8},{8,4},{6,10},{10,6},{5,9},{9,5},{7,11},{11,7},{20,24},{24,20... | collective-permute-start | bytes 3538952 | tf_op jit(solution)/shard_map/ppermute | solution.py:34
  9.8 2.2 %pack_leaving.1 = bf16[4,320,512]{2,1,0:T(8,128)(2,1)} custom-call(s32[8]{0:T(128)S(1)} %copy-done.28, s32[1]{0:T(128)} %bitcast.own_ref.refs_1_, bf16[8,256,512]{2,1,0:T(8,128)(2,1)S(1)} %bitcast.8, bf16[8,32,512]{2,1,0:T(8,128)(2,1)S(1)} %reshape.28.rope_ref.refs_4_.refs_3_, bf16[8,32,512]{2,1,0:T(8,128)(2,1)S(1)} %fusion.2.new_ref.refs_5_.refs_4_), custom_call_target="tpu_custom_call" | custom-call | bytes 1024 | tf_op jit(solution)/shard_map/pack_leaving/pallas_call | solution.py:104
  12.1 1.6 %collective-permute-start = (bf16[4,320,512]{2,1,0:T(8,128)(2,1)}, bf16[4,320,512]{2,1,0:T(8,128)(2,1)S(1)}, u32[]{:S(2)}, u32[]{:S(2)}) collective-permute-start(bf16[4,320,512]{2,1,0:T(8,128)(2,1)} %pack_leaving.1), channel_id=1, source_target_pairs={{0,2},{2,0},{4,6},{6,4},{8,10},{10,8},{12,14},{14,12},{1,3},{3,1},... | collective-permute-start | bytes 3932168 | tf_op jit(solution)/shard_map/ppermute | solution.py:26
  13.7 1.7 %reshape.31.tokens_ref = bf16[16,7168]{1,0:T(8,128)(2,1)} reshape(bf16[8,2,7168]{2,1,0:T(2,128)(2,1)} %param.20) | data formatting | bytes 458752 | tf_op jit(solution)/shard_map/reshape | solution.py:568
  15.4 0.9 copy-done.19
  16.6 16.9 %collective-permute-done.1.refs_6_ = bf16[1152,512]{1,0:T(8,128)(2,1)} collective-permute-done((bf16[1152,512]{1,0:T(8,128)(2,1)}, bf16[1152,512]{1,0:T(8,128)(2,1)}, u32[]{:S(2)}, u32[]{:S(2)}) %collective-permute-start.1) | collective-permute-done | bytes 1179680 | tf_op jit(solution)/shard_map/ppermute | solution.py:34
  33.5 1.7 %collective-permute-start.3 = (bf16[1152,512]{1,0:T(8,128)(2,1)}, bf16[1152,512]{1,0:T(8,128)(2,1)}, u32[]{:S(2)}, u32[]{:S(2)}) collective-permute-start(bf16[1152,512]{1,0:T(8,128)(2,1)} %collective-permute-done.1.refs_6_), channel_id=1, source_target_pairs={{4,8},{8,4},{6,10},{10,6},{5,9},{9,5},{7,11},{11,7},{20,24},{24,20... | collective-permute-start | bytes 3538952 | tf_op jit(solution)/shard_map/ppermute | solution.py:34
  35.2 1.3 collective-permute-start.4
  36.5 6.1 %collective-permute-done.refs_2_ = bf16[4,320,512]{2,1,0:T(8,128)(2,1)S(1)} collective-permute-done((bf16[4,320,512]{2,1,0:T(8,128)(2,1)}, bf16[4,320,512]{2,1,0:T(8,128)(2,1)S(1)}, u32[]{:S(2)}, u32[]{:S(2)}) %collective-permute-start) | collective-permute-done | bytes 1310752 | tf_op jit(solution)/shard_map/ppermute | solution.py:26
  42.6 1.5 %collective-permute-start.7 = (bf16[4,7168]{1,0:T(4,128)(2,1)S(1)}, bf16[4,7168]{1,0:T(4,128)(2,1)S(1)}, u32[]{:S(2)}, u32[]{:S(2)}) collective-permute-start(bf16[4,7168]{1,0:T(4,128)(2,1)S(1)} %get-tuple-element.58.refs_0_), channel_id=1, source_target_pairs={{0,2},{2,0},{4,6},{6,4},{8,10},{10,8},{12,14},{14,12},{1,3},{3,1},... | collective-permute-start | bytes 172040 | tf_op jit(solution)/shard_map/ppermute | solution.py:26
  44.1 0.9 copy-done.4
  45.1 0.9 copy-done.8
  46.0 8.5 %attend_give_keep.3 = (bf16[256,512]{1,0:T(8,128)(2,1)S(1)}, bf16[8,256,512]{2,1,0:T(8,128)(2,1)}) custom-call(s32[8]{0:T(128)S(1)} %copy-done.28, s32[1]{0:T(128)} %bitcast.own_ref.refs_1_, bf16[4,320,512]{2,1,0:T(8,128)(2,1)S(1)} %collective-permute-done.refs_2_, bf16[8,256,512]{2,1,0:T(8,128)(2,1)S(1)} %bitcast.9, bf16[8,32,512]{2,1,0:T(8,128)(2,1)S(1)} %copy-done.4, ...), custom_call_target="tpu_custom_call" | custom-call | bytes 1024 | tf_op jit(solution)/shard_map/attend_give_keep/pallas_call | solution.py:308
  55.2 1.0 pair_rows.1
  56.2 2.5 %collective-permute-start.10 = (bf16[4,7168]{1,0:T(4,128)(2,1)}, bf16[4,7168]{1,0:T(4,128)(2,1)S(1)}, u32[]{:S(2)}, u32[]{:S(2)}) collective-permute-start(bf16[4,7168]{1,0:T(4,128)(2,1)} %get-tuple-element.64), channel_id=1, source_target_pairs={{0,12},{2,14},{4,8},{6,10},{8,4},{10,6},{12,0},{14,2},{1,13},{3,15... | collective-permute-start | bytes 172040 | tf_op jit(solution)/shard_map/ppermute | solution.py:581
  58.7 2.1 %collective-permute-start.9 = (bf16[4,7168]{1,0:T(4,128)(2,1)}, bf16[4,7168]{1,0:T(4,128)(2,1)}, u32[]{:S(2)}, u32[]{:S(2)}) collective-permute-start(bf16[4,7168]{1,0:T(4,128)(2,1)} %get-tuple-element.64), channel_id=1, source_target_pairs={{0,8},{2,10},{4,12},{6,14},{8,0},{10,2},{12,4},{14,6},{1,9},{3,11}... | collective-permute-start | bytes 172040 | tf_op jit(solution)/shard_map/ppermute | solution.py:581
  60.8 1.1 copy-done.16
  61.9 0.9 copy-done.5
  62.8 0.9 copy-done.9
  63.8 1.3 copy-done.17
  65.0 8.3 %attend_give_keep.4 = (bf16[256,512]{1,0:T(8,128)(2,1)S(1)}, bf16[8,256,512]{2,1,0:T(8,128)(2,1)}) custom-call(s32[8]{0:T(128)S(1)} %copy-done.28, s32[1]{0:T(128)} %bitcast.own_ref.refs_1_, bf16[4,320,512]{2,1,0:T(8,128)(2,1)S(1)} %collective-permute-done.refs_2_, bf16[8,256,512]{2,1,0:T(8,128)(2,1)S(1)} %bitcast.10, ...), custom_call_target="tpu_custom_call", output_to_operand_aliasing={{1}: (8, {})} | custom-call | bytes 1024 | tf_op jit(solution)/shard_map/attend_give_keep/pallas_call | solution.py:308
  73.6 1.4 %broadcast_select_fusion.1.refs_6_ = bf16[1152,512]{1,0:T(8,128)(2,1)S(1)} fusion(bf16[1152,512]{1,0:T(8,128)(2,1)} %collective-permute-done.2, bf16[1152,512]{1,0:T(8,128)(2,1)} %collective-permute-done.4, pred[]{:T(512)S(6)} %and.22), kind=kLoop, calls=%fused_computation.2 | loop fusion | flops 589824 | bytes 3538945 | tf_op jit(solution)/shard_map/jit(_where)/select_n | solution.py:632
  75.0 1.5 %collective-permute-start.11 = (bf16[1152,512]{1,0:T(8,128)(2,1)}, bf16[1152,512]{1,0:T(8,128)(2,1)S(1)}, u32[]{:S(2)}, u32[]{:S(2)}) collective-permute-start(bf16[1152,512]{1,0:T(8,128)(2,1)} %collective-permute-done.3), channel_id=1, source_target_pairs={{4,0},{8,12},{6,2},{10,14},{5,1},{9,13},{7,3},{11,15},{20,16},{24,... | collective-permute-start | bytes 3538952 | tf_op jit(solution)/shard_map/ppermute | solution.py:34
  76.5 1.6 %collective-permute-start.15 = (bf16[256,512]{1,0:T(8,128)(2,1)S(1)}, bf16[256,512]{1,0:T(8,128)(2,1)S(1)}, u32[]{:S(2)}, u32[]{:S(2)}) collective-permute-start(bf16[256,512]{1,0:T(8,128)(2,1)S(1)} %copy-done.32), channel_id=1, source_target_pairs={{0,2},{2,0},{4,6},{6,4},{8,10},{10,8},{12,14},{14,12},{1,3},{3,1},... | collective-permute-start | bytes 786440 | tf_op jit(solution)/shard_map/ppermute | solution.py:26
  78.6 1.2 stack_rows.1.mine_ref
  80.0 8.5 %attend_give_keep.5 = (bf16[256,512]{1,0:T(8,128)(2,1)S(1)}, bf16[8,256,512]{2,1,0:T(8,128)(2,1)}) custom-call(s32[8]{0:T(128)S(1)} %copy-done.28, s32[1]{0:T(128)} %bitcast.own_ref.refs_1_, bf16[4,320,512]{2,1,0:T(8,128)(2,1)S(1)} %collective-permute-done.refs_2_, bf16[8,256,512]{2,1,0:T(8,128)(2,1)S(1)} %bitcast.11, ...), custom_call_target="tpu_custom_call", output_to_operand_aliasing={{1}: (8, {})} | custom-call | bytes 1024 | tf_op jit(solution)/shard_map/attend_give_keep/pallas_call | solution.py:308
  88.4 1.6 %collective-permute-start.13 = (bf16[256,512]{1,0:T(8,128)(2,1)S(1)}, bf16[256,512]{1,0:T(8,128)(2,1)S(1)}, u32[]{:S(2)}, u32[]{:S(2)}) collective-permute-start(bf16[256,512]{1,0:T(8,128)(2,1)S(1)} %get-tuple-element.70), channel_id=1, source_target_pairs={{0,2},{2,0},{4,6},{6,4},{8,10},{10,8},{12,14},{14,12},{1,3},{3,1},... | collective-permute-start | bytes 786440 | tf_op jit(solution)/shard_map/ppermute | solution.py:26
  90.9 1.6 %experts.1 = (f32[16,7168]{1,0:T(8,128)S(1)}, bf16[16,7168]{1,0:T(8,128)(2,1)S(1)}) custom-call(bf16[16,7168]{1,0:T(8,128)(2,1)S(1)} %stack_rows.1.mine_ref, bf16[16,7168]{1,0:T(8,128)(2,1)S(1)} %collective-permute-done.14.theirs_ref, bf16[1,7168,128]{2,1,0:T(8,128)(2,1)S(1)} %copy-done.13, bf16[1,7168,128]{2,1,0:T(8,128)(2,1)S(1)} %copy-done.14, ...), custom_call_target="tpu_custom_call" | custom-call | bytes 1024 | tf_op jit(solution)/shard_map/experts/pallas_call | solution.py:465
  92.6 1.4 %collective-permute-done.17.arrived_ref = bf16[16,7168]{1,0:T(8,128)(2,1)S(1)} collective-permute-done((bf16[16,7168]{1,0:T(8,128)(2,1)S(1)}, bf16[16,7168]{1,0:T(8,128)(2,1)S(1)}, u32[]{:S(2)}, u32[]{:S(2)}) %collective-permute-start.17) | collective-permute-done | bytes 229408 | tf_op jit(solution)/shard_map/ppermute | solution.py:26
  94.1 11.4 %collective-permute-done.11 = bf16[1152,512]{1,0:T(8,128)(2,1)S(1)} collective-permute-done((bf16[1152,512]{1,0:T(8,128)(2,1)}, bf16[1152,512]{1,0:T(8,128)(2,1)S(1)}, u32[]{:S(2)}, u32[]{:S(2)}) %collective-permute-start.11) | collective-permute-done | bytes 1179680 | tf_op jit(solution)/shard_map/ppermute | solution.py:34
  105.5 1.5 %collective-permute-start.18 = (bf16[8,7168]{1,0:T(8,128)(2,1)S(1)}, bf16[8,7168]{1,0:T(8,128)(2,1)S(1)}, u32[]{:S(2)}, u32[]{:S(2)}) collective-permute-start(bf16[8,7168]{1,0:T(8,128)(2,1)S(1)} %get-tuple-element.82), channel_id=1, source_target_pairs={{0,2},{2,0},{4,6},{6,4},{8,10},{10,8},{12,14},{14,12},{1,3},{3,1},... | collective-permute-start | bytes 344072 | tf_op jit(solution)/shard_map/ppermute | solution.py:26
  107.3 3.0 %collective-permute-done.18 = bf16[8,7168]{1,0:T(8,128)(2,1)S(1)} collective-permute-done((bf16[8,7168]{1,0:T(8,128)(2,1)S(1)}, bf16[8,7168]{1,0:T(8,128)(2,1)S(1)}, u32[]{:S(2)}, u32[]{:S(2)}) %collective-permute-start.18) | collective-permute-done | bytes 114720 | tf_op jit(solution)/shard_map/ppermute | solution.py:26
  111.0 5.2 %attend_give.1 = bf16[256,512]{1,0:T(8,128)(2,1)S(1)} custom-call(s32[8]{0:T(128)S(1)} %copy-done.28, s32[1]{0:T(128)} %bitcast.own_ref.refs_1_, bf16[4,320,512]{2,1,0:T(8,128)(2,1)S(1)} %collective-permute-done.refs_2_, bf16[1152,512]{1,0:T(8,128)(2,1)S(1)} %broadcast_select_fusion.refs_3_.refs_5_, bf16[1152,512]{1,0:T(8,128)(2,1)S(1)} %collective-permute-done.19.refs_4_.refs_6_), custom_call_target="tpu_custom_call" | custom-call | bytes 1024 | tf_op jit(solution)/shard_map/attend_give/pallas_call | solution.py:308
  117.1 1.5 %collective-permute-start.20 = (bf16[256,512]{1,0:T(8,128)(2,1)}, bf16[256,512]{1,0:T(8,128)(2,1)S(1)}, u32[]{:S(2)}, u32[]{:S(2)}) collective-permute-start(bf16[256,512]{1,0:T(8,128)(2,1)} %copy-done.26), channel_id=1, source_target_pairs={{0,2},{2,0},{4,6},{6,4},{8,10},{10,8},{12,14},{14,12},{1,3},{3,1},... | collective-permute-start | bytes 786440 | tf_op jit(solution)/shard_map/ppermute | solution.py:26
  118.6 2.9 %collective-permute-start.22 = (bf16[2,7168]{1,0:T(2,128)(2,1)S(1)}, bf16[2,7168]{1,0:T(2,128)(2,1)S(1)}, u32[]{:S(2)}, u32[]{:S(2)}) collective-permute-start(bf16[2,7168]{1,0:T(2,128)(2,1)S(1)} %get-tuple-element.95), channel_id=1, source_target_pairs={{0,8},{2,10},{4,12},{6,14},{8,0},{10,2},{12,4},{14,6},{1,9},{3,11}... | collective-permute-start | bytes 86024 | tf_op jit(solution)/shard_map/ppermute | solution.py:581
  121.5 1.5 %collective-permute-start.23 = (bf16[2,7168]{1,0:T(2,128)(2,1)S(1)}, bf16[2,7168]{1,0:T(2,128)(2,1)S(1)}, u32[]{:S(2)}, u32[]{:S(2)}) collective-permute-start(bf16[2,7168]{1,0:T(2,128)(2,1)S(1)} %get-tuple-element.97), channel_id=1, source_target_pairs={{0,12},{2,14},{4,8},{6,10},{8,4},{10,6},{12,0},{14,2},{1,13},{3,15... | collective-permute-start | bytes 86024 | tf_op jit(solution)/shard_map/ppermute | solution.py:581
  123.0 1.3 copy-done.2
  124.3 0.9 copy-done.6
  125.2 0.9 copy-done.10
  126.2 1.3 copy-done.12
  127.4 0.9 copy-done.21
  128.4 0.9 copy-done.23
  129.3 0.9 copy-done.25
  130.3 6.3 %attend_keep.1.before = bf16[8,256,512]{2,1,0:T(8,128)(2,1)} custom-call(s32[8]{0:T(128)S(1)} %copy-done.28, s32[1]{0:T(128)} %bitcast.own_ref.refs_1_, bf16[8,256,512]{2,1,0:T(8,128)(2,1)S(1)} %bitcast.12, bf16[8,32,512]{2,1,0:T(8,128)(2,1)S(1)} %copy-done.6, bf16[8,32,512]{2,1,0:T(8,128)(2,1)S(1)} %copy-done.10, ...), custom_call_target="tpu_custom_call", output_to_operand_aliasing={{}: (10, {})} | custom-call | bytes 1024 | tf_op jit(solution)/shard_map/attend_keep/pallas_call | solution.py:308
  138.5 1.3 place.1
  (99 shorter events, 8.3 us)
Async XLA Ops:
  0.6 1.2 copy-start.18
  2.8 6.1 %copy-start.33 = (bf16[8,2,8192]{2,1,0:T(2,128)(2,1)S(1)}, bf16[8,2,8192]{2,1,0:T(2,128)(2,1)}, u32[]{:S(2)}) copy-start(bf16[8,2,8192]{2,1,0:T(2,128)(2,1)} %param.16) | copy-start | bytes 786436
  2.8 6.3 %copy-start.34 = (bf16[8,2,512]{2,1,0:T(2,128)(2,1)S(1)}, bf16[8,2,512]{2,1,0:T(2,128)(2,1)}, u32[]{:S(2)}) copy-start(bf16[8,2,512]{2,1,0:T(2,128)(2,1)} %param.17) | copy-start | bytes 49156
  2.8 6.3 %copy-start.35 = (bf16[8,2,64]{2,1,0:T(2,128)(2,1)S(1)}, bf16[8,2,64]{2,1,0:T(2,128)(2,1)}, u32[]{:S(2)}) copy-start(bf16[8,2,64]{2,1,0:T(2,128)(2,1)} %param.18) | copy-start | bytes 6148
  2.8 7.1 %copy-start = (bf16[8,2,128,512]{3,2,1,0:T(8,128)(2,1)S(1)}, bf16[8,2,128,512]{3,2,1,0:T(8,128)(2,1)}, u32[]{:S(2)}) copy-start(bf16[8,2,128,512]{3,2,1,0:T(8,128)(2,1)} %param.15) | copy-start | bytes 6291460
  2.8 7.1 %copy-start.28 = (s32[8]{0:T(128)S(1)}, s32[8]{0:T(128)}, u32[]{:S(2)}) copy-start(s32[8]{0:T(128)} %slot_ref.3) | copy-start | bytes 100
  4.1 29.4 %collective-permute-start.1 = (bf16[1152,512]{1,0:T(8,128)(2,1)}, bf16[1152,512]{1,0:T(8,128)(2,1)}, u32[]{:S(2)}, u32[]{:S(2)}) collective-permute-start(bf16[1152,512]{1,0:T(8,128)(2,1)} %pack_cache.1.refs_6_), channel_id=1, source_target_pairs={{0,4},{4,0},{8,12},{12,8},{2,6},{6,2},{10,14},{14,10},{1,5},{5,1},... | collective-permute-start | bytes 3538952 | tf_op jit(solution)/shard_map/ppermute | solution.py:34
  7.2 26.3 %collective-permute-start.2 = (bf16[1152,512]{1,0:T(8,128)(2,1)}, bf16[1152,512]{1,0:T(8,128)(2,1)}, u32[]{:S(2)}, u32[]{:S(2)}) collective-permute-start(bf16[1152,512]{1,0:T(8,128)(2,1)} %pack_cache.1.refs_6_), channel_id=1, source_target_pairs={{4,8},{8,4},{6,10},{10,6},{5,9},{9,5},{7,11},{11,7},{20,24},{24,20... | collective-permute-start | bytes 3538952 | tf_op jit(solution)/shard_map/ppermute | solution.py:34
  9.1 2.9 %copy-start.7 = (bf16[8,32,512]{2,1,0:T(8,128)(2,1)}, bf16[8,32,512]{2,1,0:T(8,128)(2,1)S(1)}, u32[]{:S(2)}) copy-start(bf16[8,32,512]{2,1,0:T(8,128)(2,1)S(1)} %fusion.2.new_ref.refs_5_.refs_4_) | copy-start | bytes 786436
  9.8 5.5 %copy-start.29 = (s32[8,2,8]{2,1,0:T(2,128)S(1)}, s32[8,2,8]{2,1,0:T(2,128)}, u32[]{:S(2)}) copy-start(s32[8,2,8]{2,1,0:T(2,128)} %param.21) | copy-start | bytes 1540
  9.8 5.5 %copy-start.30 = (f32[8,2,8]{2,1,0:T(2,128)S(1)}, f32[8,2,8]{2,1,0:T(2,128)}, u32[]{:S(2)}) copy-start(f32[8,2,8]{2,1,0:T(2,128)} %param.22) | copy-start | bytes 1540
  12.1 30.5 %collective-permute-start = (bf16[4,320,512]{2,1,0:T(8,128)(2,1)}, bf16[4,320,512]{2,1,0:T(8,128)(2,1)S(1)}, u32[]{:S(2)}, u32[]{:S(2)}) collective-permute-start(bf16[4,320,512]{2,1,0:T(8,128)(2,1)} %pack_leaving.1), channel_id=1, source_target_pairs={{0,2},{2,0},{4,6},{6,4},{8,10},{10,8},{12,14},{14,12},{1,3},{3,1},... | collective-permute-start | bytes 3932168 | tf_op jit(solution)/shard_map/ppermute | solution.py:26
  13.7 30.5 %collective-permute-start.6 = (bf16[1152,512]{1,0:T(8,128)(2,1)}, bf16[1152,512]{1,0:T(8,128)(2,1)}, u32[]{:S(2)}, u32[]{:S(2)}) collective-permute-start(bf16[1152,512]{1,0:T(8,128)(2,1)} %pack_cache.1.refs_6_), channel_id=1, source_target_pairs={{0,1},{1,0},{2,3},{3,2},{4,5},{5,4},{6,7},{7,6},{8,9},{9,8},{10,11... | collective-permute-start | bytes 3538952 | tf_op jit(solution)/shard_map/ppermute | solution.py:26
  33.5 27.3 %collective-permute-start.5 = (bf16[1152,512]{1,0:T(8,128)(2,1)}, bf16[1152,512]{1,0:T(8,128)(2,1)S(1)}, u32[]{:S(2)}, u32[]{:S(2)}) collective-permute-start(bf16[1152,512]{1,0:T(8,128)(2,1)} %collective-permute-done.1.refs_6_), channel_id=1, source_target_pairs={{0,1},{1,0},{2,3},{3,2},{4,5},{5,4},{6,7},{7,6},{8,9},{9,8},{10,11... | collective-permute-start | bytes 3538952 | tf_op jit(solution)/shard_map/ppermute | solution.py:26
  33.5 40.0 %collective-permute-start.3 = (bf16[1152,512]{1,0:T(8,128)(2,1)}, bf16[1152,512]{1,0:T(8,128)(2,1)}, u32[]{:S(2)}, u32[]{:S(2)}) collective-permute-start(bf16[1152,512]{1,0:T(8,128)(2,1)} %collective-permute-done.1.refs_6_), channel_id=1, source_target_pairs={{4,8},{8,4},{6,10},{10,6},{5,9},{9,5},{7,11},{11,7},{20,24},{24,20... | collective-permute-start | bytes 3538952 | tf_op jit(solution)/shard_map/ppermute | solution.py:34
  35.2 38.3 %collective-permute-start.4 = (bf16[1152,512]{1,0:T(8,128)(2,1)}, bf16[1152,512]{1,0:T(8,128)(2,1)}, u32[]{:S(2)}, u32[]{:S(2)}) collective-permute-start(bf16[1152,512]{1,0:T(8,128)(2,1)} %collective-permute-done.2), channel_id=1, source_target_pairs={{4,0},{8,12},{6,2},{10,14},{5,1},{9,13},{7,3},{11,15},{20,16},{24,... | collective-permute-start | bytes 3538952 | tf_op jit(solution)/shard_map/ppermute | solution.py:34
  42.6 12.6 %collective-permute-start.7 = (bf16[4,7168]{1,0:T(4,128)(2,1)S(1)}, bf16[4,7168]{1,0:T(4,128)(2,1)S(1)}, u32[]{:S(2)}, u32[]{:S(2)}) collective-permute-start(bf16[4,7168]{1,0:T(4,128)(2,1)S(1)} %get-tuple-element.58.refs_0_), channel_id=1, source_target_pairs={{0,2},{2,0},{4,6},{6,4},{8,10},{10,8},{12,14},{14,12},{1,3},{3,1},... | collective-permute-start | bytes 172040 | tf_op jit(solution)/shard_map/ppermute | solution.py:26
  44.1 1.0 copy-start.4
  45.1 0.9 copy-start.8
  56.2 17.2 %collective-permute-start.10 = (bf16[4,7168]{1,0:T(4,128)(2,1)}, bf16[4,7168]{1,0:T(4,128)(2,1)S(1)}, u32[]{:S(2)}, u32[]{:S(2)}) collective-permute-start(bf16[4,7168]{1,0:T(4,128)(2,1)} %get-tuple-element.64), channel_id=1, source_target_pairs={{0,12},{2,14},{4,8},{6,10},{8,4},{10,6},{12,0},{14,2},{1,13},{3,15... | collective-permute-start | bytes 172040 | tf_op jit(solution)/shard_map/ppermute | solution.py:581
  58.7 14.7 %collective-permute-start.9 = (bf16[4,7168]{1,0:T(4,128)(2,1)}, bf16[4,7168]{1,0:T(4,128)(2,1)}, u32[]{:S(2)}, u32[]{:S(2)}) collective-permute-start(bf16[4,7168]{1,0:T(4,128)(2,1)} %get-tuple-element.64), channel_id=1, source_target_pairs={{0,8},{2,10},{4,12},{6,14},{8,0},{10,2},{12,4},{14,6},{1,9},{3,11}... | collective-permute-start | bytes 172040 | tf_op jit(solution)/shard_map/ppermute | solution.py:581
  60.8 1.1 copy-start.16
  61.9 11.7 %collective-permute-start.8 = (bf16[4,7168]{1,0:T(4,128)(2,1)S(1)}, bf16[4,7168]{1,0:T(4,128)(2,1)}, u32[]{:S(2)}, u32[]{:S(2)}) collective-permute-start(bf16[4,7168]{1,0:T(4,128)(2,1)S(1)} %get-tuple-element.71.refs_0_), channel_id=1, source_target_pairs={{0,4},{2,6},{4,0},{6,2},{8,12},{10,14},{12,8},{14,10},{1,5},{3,7},... | collective-permute-start | bytes 172040 | tf_op jit(solution)/shard_map/ppermute | solution.py:581
  61.9 1.0 copy-start.5
  63.8 1.3 copy-start.17
  73.4 3.1 %copy-start.32 = (bf16[256,512]{1,0:T(8,128)(2,1)S(1)}, bf16[256,512]{1,0:T(8,128)(2,1)}, u32[]{:S(2)}) copy-start(bf16[256,512]{1,0:T(8,128)(2,1)} %copy-done.31) | copy-start | bytes 786436
  75.0 5.0 %collective-permute-start.12 = (bf16[1152,512]{1,0:T(8,128)(2,1)S(1)}, bf16[1152,512]{1,0:T(8,128)(2,1)S(1)}, u32[]{:S(2)}, u32[]{:S(2)}) collective-permute-start(bf16[1152,512]{1,0:T(8,128)(2,1)S(1)} %broadcast_select_fusion.1.refs_6_), channel_id=1, source_target_pairs={{0,1},{1,0},{2,3},{3,2},{4,5},{5,4},{6,7},{7,6},{8,9},{9,8},{10,11... | collective-permute-start | bytes 3538952 | tf_op jit(solution)/shard_map/ppermute | solution.py:26
  75.0 30.5 %collective-permute-start.11 = (bf16[1152,512]{1,0:T(8,128)(2,1)}, bf16[1152,512]{1,0:T(8,128)(2,1)S(1)}, u32[]{:S(2)}, u32[]{:S(2)}) collective-permute-start(bf16[1152,512]{1,0:T(8,128)(2,1)} %collective-permute-done.3), channel_id=1, source_target_pairs={{4,0},{8,12},{6,2},{10,14},{5,1},{9,13},{7,3},{11,15},{20,16},{24,... | collective-permute-start | bytes 3538952 | tf_op jit(solution)/shard_map/ppermute | solution.py:34
  76.5 13.5 %collective-permute-start.15 = (bf16[256,512]{1,0:T(8,128)(2,1)S(1)}, bf16[256,512]{1,0:T(8,128)(2,1)S(1)}, u32[]{:S(2)}, u32[]{:S(2)}) collective-permute-start(bf16[256,512]{1,0:T(8,128)(2,1)S(1)} %copy-done.32), channel_id=1, source_target_pairs={{0,2},{2,0},{4,6},{6,4},{8,10},{10,8},{12,14},{14,12},{1,3},{3,1},... | collective-permute-start | bytes 786440 | tf_op jit(solution)/shard_map/ppermute | solution.py:26
  78.1 12.8 %collective-permute-start.16 = (bf16[256,512]{1,0:T(8,128)(2,1)S(1)}, bf16[256,512]{1,0:T(8,128)(2,1)S(1)}, u32[]{:S(2)}, u32[]{:S(2)}) collective-permute-start(bf16[256,512]{1,0:T(8,128)(2,1)S(1)} %get-tuple-element.57), channel_id=1, source_target_pairs={{0,2},{2,0},{4,6},{6,4},{8,10},{10,8},{12,14},{14,12},{1,3},{3,1},... | collective-permute-start | bytes 786440 | tf_op jit(solution)/shard_map/ppermute | solution.py:26
  79.8 10.9 %collective-permute-start.14 = (bf16[16,7168]{1,0:T(8,128)(2,1)S(1)}, bf16[16,7168]{1,0:T(8,128)(2,1)S(1)}, u32[]{:S(2)}, u32[]{:S(2)}) collective-permute-start(bf16[16,7168]{1,0:T(8,128)(2,1)S(1)} %stack_rows.1.mine_ref), channel_id=1, source_target_pairs={{0,1},{1,0},{2,3},{3,2},{4,5},{5,4},{6,7},{7,6},{8,9},{9,8},{10,11... | collective-permute-start | bytes 688136 | tf_op jit(solution)/shard_map/ppermute | solution.py:26
  79.9 11.0 %copy-start.13 = (bf16[1,7168,128]{2,1,0:T(8,128)(2,1)S(1)}, bf16[1,7168,128]{2,1,0:T(8,128)(2,1)}, u32[]{:S(2)}) copy-start(bf16[1,7168,128]{2,1,0:T(8,128)(2,1)} %gate_hbm.1) | copy-start | bytes 5505028
  79.9 11.0 %copy-start.14 = (bf16[1,7168,128]{2,1,0:T(8,128)(2,1)S(1)}, bf16[1,7168,128]{2,1,0:T(8,128)(2,1)}, u32[]{:S(2)}) copy-start(bf16[1,7168,128]{2,1,0:T(8,128)(2,1)} %up_hbm.1) | copy-start | bytes 5505028
  80.0 11.0 %copy-start.15 = (bf16[1,128,7168]{2,1,0:T(8,128)(2,1)S(1)}, bf16[1,128,7168]{2,1,0:T(8,128)(2,1)}, u32[]{:S(2)}) copy-start(bf16[1,128,7168]{2,1,0:T(8,128)(2,1)} %down_hbm.1) | copy-start | bytes 5505028
  88.4 17.1 %collective-permute-start.13 = (bf16[256,512]{1,0:T(8,128)(2,1)S(1)}, bf16[256,512]{1,0:T(8,128)(2,1)S(1)}, u32[]{:S(2)}, u32[]{:S(2)}) collective-permute-start(bf16[256,512]{1,0:T(8,128)(2,1)S(1)} %get-tuple-element.70), channel_id=1, source_target_pairs={{0,2},{2,0},{4,6},{6,4},{8,10},{10,8},{12,14},{14,12},{1,3},{3,1},... | collective-permute-start | bytes 786440 | tf_op jit(solution)/shard_map/ppermute | solution.py:26
  90.9 1.6 %copy-start.22 = (bf16[256,512]{1,0:T(8,128)(2,1)}, bf16[256,512]{1,0:T(8,128)(2,1)S(1)}, u32[]{:S(2)}) copy-start(bf16[256,512]{1,0:T(8,128)(2,1)S(1)} %collective-permute-done.16.refs_8_) | copy-start | bytes 786436
  92.5 1.6 %collective-permute-start.17 = (bf16[16,7168]{1,0:T(8,128)(2,1)S(1)}, bf16[16,7168]{1,0:T(8,128)(2,1)S(1)}, u32[]{:S(2)}, u32[]{:S(2)}) collective-permute-start(bf16[16,7168]{1,0:T(8,128)(2,1)S(1)} %get-tuple-element.78), channel_id=1, source_target_pairs={{0,1},{1,0},{2,3},{3,2},{4,5},{5,4},{6,7},{7,6},{8,9},{9,8},{10,11... | collective-permute-start | bytes 688136 | tf_op jit(solution)/shard_map/ppermute | solution.py:26
  105.5 1.7 %copy-start.24 = (bf16[256,512]{1,0:T(8,128)(2,1)}, bf16[256,512]{1,0:T(8,128)(2,1)S(1)}, u32[]{:S(2)}) copy-start(bf16[256,512]{1,0:T(8,128)(2,1)S(1)} %collective-permute-done.13.refs_9_) | copy-start | bytes 786436
  105.5 4.8 %collective-permute-start.18 = (bf16[8,7168]{1,0:T(8,128)(2,1)S(1)}, bf16[8,7168]{1,0:T(8,128)(2,1)S(1)}, u32[]{:S(2)}, u32[]{:S(2)}) collective-permute-start(bf16[8,7168]{1,0:T(8,128)(2,1)S(1)} %get-tuple-element.82), channel_id=1, source_target_pairs={{0,2},{2,0},{4,6},{6,4},{8,10},{10,8},{12,14},{14,12},{1,3},{3,1},... | collective-permute-start | bytes 344072 | tf_op jit(solution)/shard_map/ppermute | solution.py:26
  107.2 9.1 %copy-start.1 = (bf16[1152,512]{1,0:T(8,128)(2,1)}, bf16[1152,512]{1,0:T(8,128)(2,1)S(1)}, u32[]{:S(2)}) copy-start(bf16[1152,512]{1,0:T(8,128)(2,1)S(1)} %broadcast_select_fusion.refs_3_.refs_5_) | copy-start | bytes 3538948
  107.2 3.9 %collective-permute-start.19 = (bf16[1152,512]{1,0:T(8,128)(2,1)S(1)}, bf16[1152,512]{1,0:T(8,128)(2,1)S(1)}, u32[]{:S(2)}, u32[]{:S(2)}) collective-permute-start(bf16[1152,512]{1,0:T(8,128)(2,1)S(1)} %broadcast_select_fusion.refs_3_.refs_5_), channel_id=1, source_target_pairs={{0,1},{1,0},{2,3},{3,2},{4,5},{5,4},{6,7},{7,6},{8,9},{9,8},{10,11... | collective-permute-start | bytes 3538952 | tf_op jit(solution)/shard_map/ppermute | solution.py:26
  111.0 5.3 %copy-start.11 = (bf16[1152,512]{1,0:T(8,128)(2,1)}, bf16[1152,512]{1,0:T(8,128)(2,1)S(1)}, u32[]{:S(2)}) copy-start(bf16[1152,512]{1,0:T(8,128)(2,1)S(1)} %collective-permute-done.19.refs_4_.refs_6_) | copy-start | bytes 3538948
  117.0 19.6 %collective-permute-start.21 = (bf16[2,7168]{1,0:T(2,128)(2,1)}, bf16[2,7168]{1,0:T(2,128)(2,1)}, u32[]{:S(2)}, u32[]{:S(2)}) collective-permute-start(bf16[2,7168]{1,0:T(2,128)(2,1)} %get-tuple-element.93), channel_id=1, source_target_pairs={{0,4},{2,6},{4,0},{6,2},{8,12},{10,14},{12,8},{14,10},{1,5},{3,7},... | collective-permute-start | bytes 86024 | tf_op jit(solution)/shard_map/ppermute | solution.py:581
  117.1 21.4 %collective-permute-start.20 = (bf16[256,512]{1,0:T(8,128)(2,1)}, bf16[256,512]{1,0:T(8,128)(2,1)S(1)}, u32[]{:S(2)}, u32[]{:S(2)}) collective-permute-start(bf16[256,512]{1,0:T(8,128)(2,1)} %copy-done.26), channel_id=1, source_target_pairs={{0,2},{2,0},{4,6},{6,4},{8,10},{10,8},{12,14},{14,12},{1,3},{3,1},... | collective-permute-start | bytes 786440 | tf_op jit(solution)/shard_map/ppermute | solution.py:26
  118.6 18.8 %collective-permute-start.22 = (bf16[2,7168]{1,0:T(2,128)(2,1)S(1)}, bf16[2,7168]{1,0:T(2,128)(2,1)S(1)}, u32[]{:S(2)}, u32[]{:S(2)}) collective-permute-start(bf16[2,7168]{1,0:T(2,128)(2,1)S(1)} %get-tuple-element.95), channel_id=1, source_target_pairs={{0,8},{2,10},{4,12},{6,14},{8,0},{10,2},{12,4},{14,6},{1,9},{3,11}... | collective-permute-start | bytes 86024 | tf_op jit(solution)/shard_map/ppermute | solution.py:581
  121.5 15.9 %collective-permute-start.23 = (bf16[2,7168]{1,0:T(2,128)(2,1)S(1)}, bf16[2,7168]{1,0:T(2,128)(2,1)S(1)}, u32[]{:S(2)}, u32[]{:S(2)}) collective-permute-start(bf16[2,7168]{1,0:T(2,128)(2,1)S(1)} %get-tuple-element.97), channel_id=1, source_target_pairs={{0,12},{2,14},{4,8},{6,10},{8,4},{10,6},{12,0},{14,2},{1,13},{3,15... | collective-permute-start | bytes 86024 | tf_op jit(solution)/shard_map/ppermute | solution.py:581
  123.0 1.3 copy-start.2
  126.2 1.3 copy-start.12
  (12 other events, 10.4 us)

commit v6 on v5

--- a/solution.py
+++ b/solution.py
@@ -13,6 +13,8 @@
 PAD = 16
 
 SMALL = pl.CostEstimate(flops=0, bytes_accessed=1024, transcendentals=0)
+
+LARGE = 62 * 1024 * 1024
 
 softmax_scale = 192.0 ** (-0.5)
 log2e = 1.4426950408889634
@@ -54,7 +56,7 @@
         out_specs=pl.BlockSpec(memory_space=pltpu.VMEM),
         scratch_shapes=[pltpu.SemaphoreType.DMA((2,))],
         cost_estimate=SMALL,
-        compiler_params=pltpu.CompilerParams(vmem_limit_bytes=4 * 1024 * 1024),
+        compiler_params=pltpu.CompilerParams(vmem_limit_bytes=LARGE),
         name="pack_cache",
     )(lat, rope)
 
@@ -109,7 +111,7 @@
         out_specs=pl.BlockSpec(memory_space=pltpu.VMEM),
         scratch_shapes=[pltpu.SemaphoreType.DMA((slots, 3))],
         cost_estimate=SMALL,
-        compiler_params=pltpu.CompilerParams(vmem_limit_bytes=4 * 1024 * 1024),
+        compiler_params=pltpu.CompilerParams(vmem_limit_bytes=LARGE),
         name="pack_leaving",
     )(branch_slot, own, *sources)
 
@@ -142,22 +144,22 @@
     factor = softmax_scale * log2e
     contract = (((1,), (1,)), ((), ()))
 
-    def put_query_rope(query_all, number, raw_rope, matrix):
+    def put_query_rope(rope_queries, number, raw_rope, matrix):
         grown = raw_group * width // (LANES // 2)
         for i, start in enumerate(range(0, token_rope, raw_group)):
             part = spread(matrix, raw_rope[start : start + raw_group, :])
             part = part + pltpu.roll(part, LANES // 2, 1)
             row = number * q_rows + i * grown
-            query_all[row : row + grown, width : width + LANES] = part.astype(jnp.bfloat16)
-
-    def merge_own(query, fresh_all, peak, total, summed):
+            rope_queries[row : row + grown, :] = part.astype(jnp.bfloat16)
+
+    def merge_own(query, rope_query, fresh_all, peak, total, summed):
         fresh = fresh_all[0:PAD, :]
         fresh_rope = fresh_all[PAD : 2 * PAD, 0:LANES]
         own = lax.dot_general(
-            query[:, 0:width], fresh, contract, preferred_element_type=jnp.float32
+            query, fresh, contract, preferred_element_type=jnp.float32
         )
         own = own + lax.dot_general(
-            query[:, width:], fresh_rope, contract, preferred_element_type=jnp.float32
+            rope_query, fresh_rope, contract, preferred_element_type=jnp.float32
         )
         row_step = lax.broadcasted_iota(jnp.int32, (q_rows, 1), 0) // heads
         columns = [jnp.where(row_step >= j, own[:, j : j + 1], -1e30) for j in range(steps)]
@@ -179,12 +181,12 @@
             value = value + (part * inverse) * fresh32[j : j + 1, :]
         return value.astype(jnp.bfloat16)
 
-    def put_key_rope(keys, first, raw_rope, matrix):
+    def put_key_rope(rope_keys, first, raw_rope, matrix):
         grown = raw_group * width // (LANES // 2)
         for i, start in enumerate(range(0, rope_rows, raw_group)):
             part = spread(matrix, raw_rope[start : start + raw_group, :])
             row = first + i * grown
-            keys[row : row + grown, width : width + LANES] = part.astype(jnp.bfloat16)
+            rope_keys[row : row + grown, :] = part.astype(jnp.bfloat16)
 
     def kernel(slot, kinds, given_slots, has_placed, *refs):
         refs = list(refs)
@@ -197,7 +199,8 @@
             refs.pop(0)
         give = refs.pop(0) if "give" in kinds else None
         placed = refs.pop(0) if ("keep" in kinds or given_slots) else None
-        keys, key_rope, query_all, query_rope, fresh, scores, summed, result, staged, sems = refs
+        keys, rope_keys, key_rope, query_all, rope_queries, query_rope = refs[:6]
+        fresh, scores, summed, result, staged, sems = refs[6:]
         used = [0]
 
         def start(source, there):
@@ -217,23 +220,23 @@
             else:
                 lat, raw, new = (source.at[kept_row] for source in stay)
             rope_copies.append(start(raw, query_rope.at[number]))
-            there = query_all.at[pl.ds(number * q_rows, q_rows), pl.ds(0, width)]
+            there = query_all.at[pl.ds(number * q_rows, q_rows)]
             query_copies.append(start(lat, there))
             query_copies.append(start(new, fresh.at[number]))
         key_copies, key_rope_copies = [], []
         for i, cache in enumerate(caches):
             key_rope_copies.append(start(cache.at[pl.ds(half, rope_rows)], key_rope.at[i]))
             for first in range(0, half, chunk):
-                there = keys.at[pl.ds(i * half + first, chunk), pl.ds(0, width)]
+                there = keys.at[pl.ds(i * half + first, chunk)]
                 key_copies.append(start(cache.at[pl.ds(first, chunk)], there))
         staging = [start(source, staged.at[i]) for i, source in enumerate(arrived)]
         matrix = spread_matrix(raw_group, width)
         for number, copy in enumerate(rope_copies):
             copy.wait()
-            put_query_rope(query_all, number, query_rope.at[number], matrix)
+            put_query_rope(rope_queries, number, query_rope.at[number], matrix)
         for i, copy in enumerate(key_rope_copies):
             copy.wait()
-            put_key_rope(keys, i * half, key_rope.at[i], matrix)
+            put_key_rope(rope_keys, i * half, key_rope.at[i], matrix)
         for copy in query_copies:
             copy.wait()
         peak = None
@@ -243,6 +246,12 @@
             part = lax.dot_general(
                 query_all[...],
                 keys[first : first + chunk, :],
+                contract,
+                preferred_element_type=jnp.float32,
+            )
+            part = part + lax.dot_general(
+                rope_queries[...],
+                rope_keys[first : first + chunk, :],
                 contract,
                 preferred_element_type=jnp.float32,
             )
@@ -262,7 +271,7 @@
             part = jnp.sum(weights, axis=1, keepdims=True)
             value = jnp.dot(
                 weights.astype(jnp.bfloat16),
-                keys[first : first + chunk, 0:width],
+                keys[first : first + chunk, :],
                 preferred_element_type=jnp.float32,
             )
             if first == 0:
@@ -274,7 +283,12 @@
         for number, kind in enumerate(kinds):
             rows = slice(number * q_rows, (number + 1) * q_rows)
             result[number] = merge_own(
-                query_all[rows, :], fresh[number], peak[rows], total[rows], summed[rows, :]
+                query_all[rows, :],
+                rope_queries[rows, :],
+                fresh[number],
+                peak[rows],
+                total[rows],
+                summed[rows, :],
             )
             there = give if kind == "give" else placed.at[kept_row]
             placing.append(start(result.at[number], there))
@@ -311,9 +325,11 @@
             in_specs=in_specs,
             out_specs=(hbm,) * len(out_shape),
             scratch_shapes=[
-                pltpu.VMEM((2 * half, width + LANES), jnp.bfloat16),
+                pltpu.VMEM((2 * half, width), jnp.bfloat16),
+                pltpu.VMEM((2 * half, LANES), jnp.bfloat16),
                 pltpu.VMEM((2, rope_rows, width), jnp.bfloat16),
-                pltpu.VMEM((n_tok * q_rows, width + LANES), jnp.bfloat16),
+                pltpu.VMEM((n_tok * q_rows, width), jnp.bfloat16),
+                pltpu.VMEM((n_tok * q_rows, LANES), jnp.bfloat16),
                 pltpu.VMEM((n_tok, token_rope, width), jnp.bfloat16),
                 pltpu.VMEM((n_tok, 2 * PAD, width), jnp.bfloat16),
                 pltpu.VMEM((n_tok * q_rows, 2 * half), jnp.float32),
@@ -324,7 +340,7 @@
             ],
             input_output_aliases=alias,
             cost_estimate=SMALL,
-            compiler_params=pltpu.CompilerParams(vmem_limit_bytes=20 * 1024 * 1024),
+            compiler_params=pltpu.CompilerParams(vmem_limit_bytes=LARGE),
             name="attend_" + "_".join(kinds),
         )(*operands)
 
@@ -348,7 +364,7 @@
         scratch_shapes=[pltpu.SemaphoreType.DMA],
         input_output_aliases={3: 0},
         cost_estimate=SMALL,
-        compiler_params=pltpu.CompilerParams(vmem_limit_bytes=4 * 1024 * 1024),
+        compiler_params=pltpu.CompilerParams(vmem_limit_bytes=LARGE),
         name="place",
     )(*scalars, source, placed)
 
@@ -619,9 +635,8 @@
     pieces = [after(piece, given_1) for piece in pieces]
 
 
-    first_c, second_b, given_1, *pieces = lax.optimization_barrier(
-        (first_c, second_b, given_1, *pieces)
-    )
+    second_b, given_1, *pieces = lax.optimization_barrier((second_b, given_1, *pieces))
+    first_c, second_b = lax.optimization_barrier((first_c, second_b))
     second_c = line_hop(first_c, tok_rows, outward)
     count = len(ways) * CAP
     stacked = tuple(

time: 141 us -> 134 us (0.950)
  local copies, waits for them, and re-layouts: 22.8 us -> 6.68 us
  waiting for transfers between devices: 39.2 us -> 46.4 us
  Pallas kernels: 45.7 us -> 48 us
    unnamed x72 -> x30, local copies, waits for them, and re-layouts: 19.3 us -> 4.78 us
    ppermute x6, waiting for transfers between devices: 0.16 us -> 8.61 us  [along(): return lax.ppermute(x, 'branch', list(enumerate(there)))]
    ppermute x5, waiting for transfers between devices: 28.3 us -> 24.9 us  [line_hop(): return lax.ppermute(x, 'branch', pairs)]
    ppermute x13, waiting for transfers between devices: 10.7 us -> 12.9 us  [swapped(): lax.ppermute(x, axis, [(i, i ^ 1 << bit) for i in range(lax.axis_size(axi...]
    reshape x1, local copies, waits for them, and re-layouts: 1.71 us -> 0.09 us  [on_device(): moe_input.reshape(tok_total, model_width)]
  transfers between devices with their start and end apart: 24 -> 24, of which waited for: 7 -> 8; matrix products, arithmetic and copies ran while one was open for 3% -> 3% of each run, Pallas kernels for 27% -> 28%
where the time goes in v6:
time: 134 us
  Pallas kernels  48 us (36%)
  waiting for transfers between devices  46.4 us (35%)
  starting transfers between devices  27.4 us (20%)
  local copies, waits for them, and re-layouts  6.68 us (5%)
  other arithmetic  3.88 us (3%)
    pallas_call x5, Pallas kernels, call(): pl.pallas_call(functools.partial(kernel, slot, kinds, given_slots, has_pl...  36.4 us
    ppermute x5, waiting for transfers between devices, line_hop(): return lax.ppermute(x, 'branch', pairs)  24.9 us
    ppermute x13, waiting for transfers between devices, swapped(): lax.ppermute(x, axis, [(i, i ^ 1 << bit) for i in range(lax.axis_size(axi...  12.9 us
    ppermute x5, starting transfers between devices, line_hop(): return lax.ppermute(x, 'branch', pairs)  9.22 us
    ppermute x6, starting transfers between devices, along(): return lax.ppermute(x, 'branch', list(enumerate(there)))  9.1 us
    ppermute x13, starting transfers between devices, swapped(): lax.ppermute(x, axis, [(i, i ^ 1 << bit) for i in range(lax.axis_size(axi...  9.04 us
    ppermute x6, waiting for transfers between devices, along(): return lax.ppermute(x, 'branch', list(enumerate(there)))  8.61 us
    unnamed x30, local copies, waits for them, and re-layouts  4.78 us
  transfers between devices with their start and end apart: 24, of which 8 were waited for; matrix products, arithmetic and copies ran while one was open for 3% of the time, Pallas kernels for 28%

profile of v6, /device:TPU:0, one launch (start us, length us, event | category | flops | bytes accessed | tf_op | source)
XLA Modules:
  0.0 133.5 jit_solution(9677833324448724496)
XLA Ops:
  0.7 2.3 %pack_cache.1.refs_6_ = bf16[1152,512]{1,0:T(8,128)(2,1)} custom-call(bf16[1024,512]{1,0:T(8,128)(2,1)} %bitcast.16, bf16[128,512]{1,0:T(8,128)(2,1)} %bitcast.17), custom_call_target="tpu_custom_call" | custom-call | bytes 1024 | tf_op jit(solution)/shard_map/pack_cache/pallas_call | solution.py:52
  3.0 3.1 %collective-permute-start.1 = (bf16[1152,512]{1,0:T(8,128)(2,1)}, bf16[1152,512]{1,0:T(8,128)(2,1)}, u32[]{:S(2)}, u32[]{:S(2)}) collective-permute-start(bf16[1152,512]{1,0:T(8,128)(2,1)} %pack_cache.1.refs_6_), channel_id=1, source_target_pairs={{0,4},{4,0},{8,12},{12,8},{2,6},{6,2},{10,14},{14,10},{1,5},{5,1},... | collective-permute-start | bytes 3538952 | tf_op jit(solution)/shard_map/ppermute | solution.py:36
  6.1 1.7 %collective-permute-start.2 = (bf16[1152,512]{1,0:T(8,128)(2,1)}, bf16[1152,512]{1,0:T(8,128)(2,1)}, u32[]{:S(2)}, u32[]{:S(2)}) collective-permute-start(bf16[1152,512]{1,0:T(8,128)(2,1)} %pack_cache.1.refs_6_), channel_id=1, source_target_pairs={{4,8},{8,4},{6,10},{10,6},{5,9},{9,5},{7,11},{11,7},{20,24},{24,20... | collective-permute-start | bytes 3538952 | tf_op jit(solution)/shard_map/ppermute | solution.py:36
  7.8 0.9 reshape.28.rope_ref.refs_4_.refs_3_
  8.6 0.7 fusion.2.new_ref.refs_5_.refs_4_
  9.4 3.3 %pack_leaving.1 = bf16[4,320,512]{2,1,0:T(8,128)(2,1)} custom-call(s32[8]{0:T(128)} %slot_ref.3, s32[1]{0:T(128)} %bitcast.own_ref.refs_1_, bf16[8,256,512]{2,1,0:T(8,128)(2,1)} %bitcast.10, bf16[8,32,512]{2,1,0:T(8,128)(2,1)} %reshape.28.rope_ref.refs_4_.refs_3_, bf16[8,32,512]{2,1,0:T(8,128)(2,1)} %fusion.2.new_ref.refs_5_.refs_4_), custom_call_target="tpu_custom_call" | custom-call | bytes 1024 | tf_op jit(solution)/shard_map/pack_leaving/pallas_call | solution.py:106
  12.6 1.6 %collective-permute-start = (bf16[4,320,512]{2,1,0:T(8,128)(2,1)}, bf16[4,320,512]{2,1,0:T(8,128)(2,1)S(1)}, u32[]{:S(2)}, u32[]{:S(2)}) collective-permute-start(bf16[4,320,512]{2,1,0:T(8,128)(2,1)} %pack_leaving.1), channel_id=1, source_target_pairs={{0,2},{2,0},{4,6},{6,4},{8,10},{10,8},{12,14},{14,12},{1,3},{3,1},... | collective-permute-start | bytes 3932168 | tf_op jit(solution)/shard_map/ppermute | solution.py:28
  14.2 0.1 reshape.31.tokens_ref
  14.3 0.3 dispatch.1
  14.6 17.7 %collective-permute-done.1.refs_6_ = bf16[1152,512]{1,0:T(8,128)(2,1)} collective-permute-done((bf16[1152,512]{1,0:T(8,128)(2,1)}, bf16[1152,512]{1,0:T(8,128)(2,1)}, u32[]{:S(2)}, u32[]{:S(2)}) %collective-permute-start.1) | collective-permute-done | bytes 1179680 | tf_op jit(solution)/shard_map/ppermute | solution.py:36
  32.4 1.3 collective-permute-start.4
  33.7 1.7 %collective-permute-start.3 = (bf16[1152,512]{1,0:T(8,128)(2,1)}, bf16[1152,512]{1,0:T(8,128)(2,1)}, u32[]{:S(2)}, u32[]{:S(2)}) collective-permute-start(bf16[1152,512]{1,0:T(8,128)(2,1)} %collective-permute-done.1.refs_6_), channel_id=1, source_target_pairs={{4,8},{8,4},{6,10},{10,6},{5,9},{9,5},{7,11},{11,7},{20,24},{24,20... | collective-permute-start | bytes 3538952 | tf_op jit(solution)/shard_map/ppermute | solution.py:36
  35.4 7.8 %collective-permute-done.refs_2_ = bf16[4,320,512]{2,1,0:T(8,128)(2,1)S(1)} collective-permute-done((bf16[4,320,512]{2,1,0:T(8,128)(2,1)}, bf16[4,320,512]{2,1,0:T(8,128)(2,1)S(1)}, u32[]{:S(2)}, u32[]{:S(2)}) %collective-permute-start) | collective-permute-done | bytes 1310752 | tf_op jit(solution)/shard_map/ppermute | solution.py:28
  43.1 1.5 %collective-permute-start.7 = (bf16[4,7168]{1,0:T(4,128)(2,1)S(1)}, bf16[4,7168]{1,0:T(4,128)(2,1)S(1)}, u32[]{:S(2)}, u32[]{:S(2)}) collective-permute-start(bf16[4,7168]{1,0:T(4,128)(2,1)S(1)} %get-tuple-element.59.refs_0_), channel_id=1, source_target_pairs={{0,2},{2,0},{4,6},{6,4},{8,10},{10,8},{12,14},{14,12},{1,3},{3,1},... | collective-permute-start | bytes 172040 | tf_op jit(solution)/shard_map/ppermute | solution.py:28
  44.7 7.9 %attend_give_keep.3 = (bf16[256,512]{1,0:T(8,128)(2,1)}, bf16[8,256,512]{2,1,0:T(8,128)(2,1)}) custom-call(s32[8]{0:T(128)} %slot_ref.3, s32[1]{0:T(128)} %bitcast.own_ref.refs_1_, bf16[4,320,512]{2,1,0:T(8,128)(2,1)} %copy-done.5, bf16[8,256,512]{2,1,0:T(8,128)(2,1)} %bitcast.11, bf16[8,32,512]{2,1,0:T(8,128)(2,1)} %reshape.28.rope_ref.refs_4_.refs_3_, ...), custom_call_target="tpu_custom_call" | custom-call | bytes 1024 | tf_op jit(solution)/shard_map/attend_give_keep/pallas_call | solution.py:322
  52.6 0.4 pair_rows.1
  53.0 2.5 %collective-permute-start.10 = (bf16[4,7168]{1,0:T(4,128)(2,1)S(1)}, bf16[4,7168]{1,0:T(4,128)(2,1)S(1)}, u32[]{:S(2)}, u32[]{:S(2)}) collective-permute-start(bf16[4,7168]{1,0:T(4,128)(2,1)S(1)} %get-tuple-element.65), channel_id=1, source_target_pairs={{0,12},{2,14},{4,8},{6,10},{8,4},{10,6},{12,0},{14,2},{1,13},{3,15... | collective-permute-start | bytes 172040 | tf_op jit(solution)/shard_map/ppermute | solution.py:597
  55.5 2.1 %collective-permute-start.9 = (bf16[4,7168]{1,0:T(4,128)(2,1)S(1)}, bf16[4,7168]{1,0:T(4,128)(2,1)S(1)}, u32[]{:S(2)}, u32[]{:S(2)}) collective-permute-start(bf16[4,7168]{1,0:T(4,128)(2,1)S(1)} %get-tuple-element.65), channel_id=1, source_target_pairs={{0,8},{2,10},{4,12},{6,14},{8,0},{10,2},{12,4},{14,6},{1,9},{3,11}... | collective-permute-start | bytes 172040 | tf_op jit(solution)/shard_map/ppermute | solution.py:597
  57.7 7.9 %attend_give_keep.4 = (bf16[256,512]{1,0:T(8,128)(2,1)}, bf16[8,256,512]{2,1,0:T(8,128)(2,1)}) custom-call(s32[8]{0:T(128)} %slot_ref.3, s32[1]{0:T(128)} %bitcast.own_ref.refs_1_, bf16[4,320,512]{2,1,0:T(8,128)(2,1)} %copy-done.5, bf16[8,256,512]{2,1,0:T(8,128)(2,1)} %bitcast.12, ...), custom_call_target="tpu_custom_call", output_to_operand_aliasing={{1}: (8, {})} | custom-call | bytes 1024 | tf_op jit(solution)/shard_map/attend_give_keep/pallas_call | solution.py:322
  65.6 8.6 %collective-permute-done.9.refs_2_ = bf16[4,7168]{1,0:T(4,128)(2,1)S(1)} collective-permute-done((bf16[4,7168]{1,0:T(4,128)(2,1)S(1)}, bf16[4,7168]{1,0:T(4,128)(2,1)S(1)}, u32[]{:S(2)}, u32[]{:S(2)}) %collective-permute-start.9) | collective-permute-done | bytes 57376 | tf_op jit(solution)/shard_map/ppermute | solution.py:597
  74.2 1.4 %broadcast_select_fusion.1.refs_6_ = bf16[1152,512]{1,0:T(8,128)(2,1)S(1)} fusion(bf16[1152,512]{1,0:T(8,128)(2,1)} %collective-permute-done.2, bf16[1152,512]{1,0:T(8,128)(2,1)} %collective-permute-done.4, pred[]{:T(512)S(6)} %and.22), kind=kLoop, calls=%fused_computation.2 | loop fusion | flops 589824 | bytes 3538945 | tf_op jit(solution)/shard_map/jit(_where)/select_n | solution.py:647
  75.8 1.5 %collective-permute-start.11 = (bf16[1152,512]{1,0:T(8,128)(2,1)}, bf16[1152,512]{1,0:T(8,128)(2,1)}, u32[]{:S(2)}, u32[]{:S(2)}) collective-permute-start(bf16[1152,512]{1,0:T(8,128)(2,1)} %collective-permute-done.3), channel_id=1, source_target_pairs={{4,0},{8,12},{6,2},{10,14},{5,1},{9,13},{7,3},{11,15},{20,16},{24,... | collective-permute-start | bytes 3538952 | tf_op jit(solution)/shard_map/ppermute | solution.py:36
  77.2 1.6 %collective-permute-start.15 = (bf16[256,512]{1,0:T(8,128)(2,1)}, bf16[256,512]{1,0:T(8,128)(2,1)}, u32[]{:S(2)}, u32[]{:S(2)}) collective-permute-start(bf16[256,512]{1,0:T(8,128)(2,1)} %get-tuple-element.60), channel_id=1, source_target_pairs={{0,2},{2,0},{4,6},{6,4},{8,10},{10,8},{12,14},{14,12},{1,3},{3,1},... | collective-permute-start | bytes 786440 | tf_op jit(solution)/shard_map/ppermute | solution.py:28
  78.8 0.5 collective-permute-start.16
  79.3 1.1 stack_rows.1.mine_ref
  80.4 1.0 copy-done.8
  81.4 8.1 %attend_give_keep.5 = (bf16[256,512]{1,0:T(8,128)(2,1)}, bf16[8,256,512]{2,1,0:T(8,128)(2,1)}) custom-call(s32[8]{0:T(128)} %slot_ref.3, s32[1]{0:T(128)} %bitcast.own_ref.refs_1_, bf16[4,320,512]{2,1,0:T(8,128)(2,1)} %copy-done.5, bf16[8,256,512]{2,1,0:T(8,128)(2,1)} %bitcast.13, ...), custom_call_target="tpu_custom_call", output_to_operand_aliasing={{1}: (8, {})} | custom-call | bytes 1024 | tf_op jit(solution)/shard_map/attend_give_keep/pallas_call | solution.py:322
  89.5 1.6 %collective-permute-start.13 = (bf16[256,512]{1,0:T(8,128)(2,1)}, bf16[256,512]{1,0:T(8,128)(2,1)S(1)}, u32[]{:S(2)}, u32[]{:S(2)}) collective-permute-start(bf16[256,512]{1,0:T(8,128)(2,1)} %get-tuple-element.72), channel_id=1, source_target_pairs={{0,2},{2,0},{4,6},{6,4},{8,10},{10,8},{12,14},{14,12},{1,3},{3,1},... | collective-permute-start | bytes 786440 | tf_op jit(solution)/shard_map/ppermute | solution.py:28
  91.1 0.8 collective-permute-done.16.refs_8_
  91.9 1.5 %copy-done.1 = bf16[1,7168,128]{2,1,0:T(8,128)(2,1)S(1)} copy-done((bf16[1,7168,128]{2,1,0:T(8,128)(2,1)S(1)}, bf16[1,7168,128]{2,1,0:T(8,128)(2,1)}, u32[]{:S(2)}) %copy-start.1) | copy-done | bytes 1835032
  93.4 1.5 %copy-done.2 = bf16[1,128,7168]{2,1,0:T(8,128)(2,1)S(1)} copy-done((bf16[1,128,7168]{2,1,0:T(8,128)(2,1)S(1)}, bf16[1,128,7168]{2,1,0:T(8,128)(2,1)}, u32[]{:S(2)}) %copy-start.2) | copy-done | bytes 1835032
  94.9 2.6 %experts.1 = (f32[16,7168]{1,0:T(8,128)S(1)}, bf16[16,7168]{1,0:T(8,128)(2,1)S(1)}) custom-call(bf16[16,7168]{1,0:T(8,128)(2,1)} %stack_rows.1.mine_ref, bf16[16,7168]{1,0:T(8,128)(2,1)} %collective-permute-done.14.theirs_ref, bf16[1,7168,128]{2,1,0:T(8,128)(2,1)S(1)} %copy-done, bf16[1,7168,128]{2,1,0:T(8,128)(2,1)S(1)} %copy-done.1, ...), custom_call_target="tpu_custom_call" | custom-call | bytes 1024 | tf_op jit(solution)/shard_map/experts/pallas_call | solution.py:481
  97.6 1.5 %collective-permute-done.17.arrived_ref = bf16[16,7168]{1,0:T(8,128)(2,1)S(1)} collective-permute-done((bf16[16,7168]{1,0:T(8,128)(2,1)S(1)}, bf16[16,7168]{1,0:T(8,128)(2,1)S(1)}, u32[]{:S(2)}, u32[]{:S(2)}) %collective-permute-start.17) | collective-permute-done | bytes 229408 | tf_op jit(solution)/shard_map/ppermute | solution.py:28
  99.1 7.2 %collective-permute-done.11 = bf16[1152,512]{1,0:T(8,128)(2,1)} collective-permute-done((bf16[1152,512]{1,0:T(8,128)(2,1)}, bf16[1152,512]{1,0:T(8,128)(2,1)}, u32[]{:S(2)}, u32[]{:S(2)}) %collective-permute-start.11) | collective-permute-done | bytes 1179680 | tf_op jit(solution)/shard_map/ppermute | solution.py:36
  106.3 1.5 %collective-permute-start.18 = (bf16[8,7168]{1,0:T(8,128)(2,1)S(1)}, bf16[8,7168]{1,0:T(8,128)(2,1)S(1)}, u32[]{:S(2)}, u32[]{:S(2)}) collective-permute-start(bf16[8,7168]{1,0:T(8,128)(2,1)S(1)} %get-tuple-element.84), channel_id=1, source_target_pairs={{0,2},{2,0},{4,6},{6,4},{8,10},{10,8},{12,14},{14,12},{1,3},{3,1},... | collective-permute-start | bytes 344072 | tf_op jit(solution)/shard_map/ppermute | solution.py:28
  107.8 1.4 %broadcast_select_fusion.refs_3_.refs_5_ = bf16[1152,512]{1,0:T(8,128)(2,1)S(1)} fusion(bf16[1152,512]{1,0:T(8,128)(2,1)} %collective-permute-done.3, bf16[1152,512]{1,0:T(8,128)(2,1)} %collective-permute-done.11, pred[]{:T(512)S(6)} %and.22), kind=kLoop, calls=%fused_computation.1 | loop fusion | flops 589824 | bytes 3538945 | tf_op jit(solution)/shard_map/jit(_where)/select_n | solution.py:656
  109.3 1.8 %collective-permute-done.18 = bf16[8,7168]{1,0:T(8,128)(2,1)S(1)} collective-permute-done((bf16[8,7168]{1,0:T(8,128)(2,1)S(1)}, bf16[8,7168]{1,0:T(8,128)(2,1)S(1)}, u32[]{:S(2)}, u32[]{:S(2)}) %collective-permute-start.18) | collective-permute-done | bytes 114720 | tf_op jit(solution)/shard_map/ppermute | solution.py:28
  111.3 1.0 collective-permute-done.19.refs_4_.refs_6_
  112.3 6.2 %attend_give.1 = bf16[256,512]{1,0:T(8,128)(2,1)} custom-call(s32[8]{0:T(128)} %slot_ref.3, s32[1]{0:T(128)} %bitcast.own_ref.refs_1_, bf16[4,320,512]{2,1,0:T(8,128)(2,1)} %copy-done.5, bf16[1152,512]{1,0:T(8,128)(2,1)} %copy-done.6, bf16[1152,512]{1,0:T(8,128)(2,1)} %collective-permute-done.19.refs_4_.refs_6_), custom_call_target="tpu_custom_call" | custom-call | bytes 1024 | tf_op jit(solution)/shard_map/attend_give/pallas_call | solution.py:322
  118.6 0.1 copy.19
  118.7 0.5 collective-permute-start.20
  119.2 3.2 %collective-permute-start.22 = (bf16[2,7168]{1,0:T(2,128)(2,1)S(1)}, bf16[2,7168]{1,0:T(2,128)(2,1)S(1)}, u32[]{:S(2)}, u32[]{:S(2)}) collective-permute-start(bf16[2,7168]{1,0:T(2,128)(2,1)S(1)} %get-tuple-element.97), channel_id=1, source_target_pairs={{0,8},{2,10},{4,12},{6,14},{8,0},{10,2},{12,4},{14,6},{1,9},{3,11}... | collective-permute-start | bytes 86024 | tf_op jit(solution)/shard_map/ppermute | solution.py:597
  122.4 1.2 collective-permute-start.23
  123.6 6.2 %attend_keep.1.before = bf16[8,256,512]{2,1,0:T(8,128)(2,1)} custom-call(s32[8]{0:T(128)} %slot_ref.3, s32[1]{0:T(128)} %bitcast.own_ref.refs_1_, bf16[8,256,512]{2,1,0:T(8,128)(2,1)} %bitcast.14, bf16[8,32,512]{2,1,0:T(8,128)(2,1)} %reshape.28.rope_ref.refs_4_.refs_3_, ...), custom_call_target="tpu_custom_call", output_to_operand_aliasing={{}: (10, {})} | custom-call | bytes 1024 | tf_op jit(solution)/shard_map/attend_keep/pallas_call | solution.py:322
  130.0 0.2 multiply_reduce_fusion
  130.2 0.8 convert_element_type.31
  131.0 0.7 copy-done.10
  131.7 1.7 %place.1 = bf16[8,256,512]{2,1,0:T(8,128)(2,1)} custom-call(s32[8]{0:T(128)} %slot_ref.3, s32[1]{0:T(128)} %bitcast.own_ref.refs_1_, bf16[256,512]{1,0:T(8,128)(2,1)} %copy-done.10, bf16[8,256,512]{2,1,0:T(8,128)(2,1)} %attend_keep.1.before), custom_call_target="tpu_custom_call", output_to_operand_aliasing={{}: (3, {})} | custom-call | bytes 1024 | tf_op jit(solution)/shard_map/place/pallas_call | solution.py:358
  (57 shorter events, 0.7 us)
Async XLA Ops:
  0.6 7.1 %copy-start.11 = (bf16[8,2,8192]{2,1,0:T(2,128)(2,1)S(1)}, bf16[8,2,8192]{2,1,0:T(2,128)(2,1)}, u32[]{:S(2)}) copy-start(bf16[8,2,8192]{2,1,0:T(2,128)(2,1)} %param.16) | copy-start | bytes 786436
  0.6 8.0 %copy-start.13 = (bf16[8,2,512]{2,1,0:T(2,128)(2,1)S(1)}, bf16[8,2,512]{2,1,0:T(2,128)(2,1)}, u32[]{:S(2)}) copy-start(bf16[8,2,512]{2,1,0:T(2,128)(2,1)} %param.17) | copy-start | bytes 49156
  0.7 8.0 %copy-start.14 = (bf16[8,2,64]{2,1,0:T(2,128)(2,1)S(1)}, bf16[8,2,64]{2,1,0:T(2,128)(2,1)}, u32[]{:S(2)}) copy-start(bf16[8,2,64]{2,1,0:T(2,128)(2,1)} %param.18) | copy-start | bytes 6148
  3.0 29.4 %collective-permute-start.1 = (bf16[1152,512]{1,0:T(8,128)(2,1)}, bf16[1152,512]{1,0:T(8,128)(2,1)}, u32[]{:S(2)}, u32[]{:S(2)}) collective-permute-start(bf16[1152,512]{1,0:T(8,128)(2,1)} %pack_cache.1.refs_6_), channel_id=1, source_target_pairs={{0,4},{4,0},{8,12},{12,8},{2,6},{6,2},{10,14},{14,10},{1,5},{5,1},... | collective-permute-start | bytes 3538952 | tf_op jit(solution)/shard_map/ppermute | solution.py:36
  6.1 26.3 %collective-permute-start.2 = (bf16[1152,512]{1,0:T(8,128)(2,1)}, bf16[1152,512]{1,0:T(8,128)(2,1)}, u32[]{:S(2)}, u32[]{:S(2)}) collective-permute-start(bf16[1152,512]{1,0:T(8,128)(2,1)} %pack_cache.1.refs_6_), channel_id=1, source_target_pairs={{4,8},{8,4},{6,10},{10,6},{5,9},{9,5},{7,11},{11,7},{20,24},{24,20... | collective-permute-start | bytes 3538952 | tf_op jit(solution)/shard_map/ppermute | solution.py:36
  9.3 4.9 %copy-start.12 = (bf16[8,2,7168]{2,1,0:T(2,128)(2,1)S(1)}, bf16[8,2,7168]{2,1,0:T(2,128)(2,1)}, u32[]{:S(2)}) copy-start(bf16[8,2,7168]{2,1,0:T(2,128)(2,1)} %param.20) | copy-start | bytes 688132
  9.3 5.0 %copy-start.3 = (s32[8,2,8]{2,1,0:T(2,128)S(1)}, s32[8,2,8]{2,1,0:T(2,128)}, u32[]{:S(2)}) copy-start(s32[8,2,8]{2,1,0:T(2,128)} %param.21) | copy-start | bytes 1540
  9.4 5.0 %copy-start.4 = (f32[8,2,8]{2,1,0:T(2,128)S(1)}, f32[8,2,8]{2,1,0:T(2,128)}, u32[]{:S(2)}) copy-start(f32[8,2,8]{2,1,0:T(2,128)} %param.22) | copy-start | bytes 1540
  12.6 30.5 %collective-permute-start = (bf16[4,320,512]{2,1,0:T(8,128)(2,1)}, bf16[4,320,512]{2,1,0:T(8,128)(2,1)S(1)}, u32[]{:S(2)}, u32[]{:S(2)}) collective-permute-start(bf16[4,320,512]{2,1,0:T(8,128)(2,1)} %pack_leaving.1), channel_id=1, source_target_pairs={{0,2},{2,0},{4,6},{6,4},{8,10},{10,8},{12,14},{14,12},{1,3},{3,1},... | collective-permute-start | bytes 3932168 | tf_op jit(solution)/shard_map/ppermute | solution.py:28
  14.2 30.5 %collective-permute-start.6 = (bf16[1152,512]{1,0:T(8,128)(2,1)}, bf16[1152,512]{1,0:T(8,128)(2,1)}, u32[]{:S(2)}, u32[]{:S(2)}) collective-permute-start(bf16[1152,512]{1,0:T(8,128)(2,1)} %pack_cache.1.refs_6_), channel_id=1, source_target_pairs={{0,1},{1,0},{2,3},{3,2},{4,5},{5,4},{6,7},{7,6},{8,9},{9,8},{10,11... | collective-permute-start | bytes 3538952 | tf_op jit(solution)/shard_map/ppermute | solution.py:28
  32.4 25.3 %collective-permute-start.5 = (bf16[1152,512]{1,0:T(8,128)(2,1)}, bf16[1152,512]{1,0:T(8,128)(2,1)}, u32[]{:S(2)}, u32[]{:S(2)}) collective-permute-start(bf16[1152,512]{1,0:T(8,128)(2,1)} %collective-permute-done.1.refs_6_), channel_id=1, source_target_pairs={{0,1},{1,0},{2,3},{3,2},{4,5},{5,4},{6,7},{7,6},{8,9},{9,8},{10,11... | collective-permute-start | bytes 3538952 | tf_op jit(solution)/shard_map/ppermute | solution.py:28
  32.4 41.9 %collective-permute-start.4 = (bf16[1152,512]{1,0:T(8,128)(2,1)}, bf16[1152,512]{1,0:T(8,128)(2,1)}, u32[]{:S(2)}, u32[]{:S(2)}) collective-permute-start(bf16[1152,512]{1,0:T(8,128)(2,1)} %collective-permute-done.2), channel_id=1, source_target_pairs={{4,0},{8,12},{6,2},{10,14},{5,1},{9,13},{7,3},{11,15},{20,16},{24,... | collective-permute-start | bytes 3538952 | tf_op jit(solution)/shard_map/ppermute | solution.py:36
  33.7 40.6 %collective-permute-start.3 = (bf16[1152,512]{1,0:T(8,128)(2,1)}, bf16[1152,512]{1,0:T(8,128)(2,1)}, u32[]{:S(2)}, u32[]{:S(2)}) collective-permute-start(bf16[1152,512]{1,0:T(8,128)(2,1)} %collective-permute-done.1.refs_6_), channel_id=1, source_target_pairs={{4,8},{8,4},{6,10},{10,6},{5,9},{9,5},{7,11},{11,7},{20,24},{24,20... | collective-permute-start | bytes 3538952 | tf_op jit(solution)/shard_map/ppermute | solution.py:36
  43.1 1.5 %copy-start.5 = (bf16[4,320,512]{2,1,0:T(8,128)(2,1)}, bf16[4,320,512]{2,1,0:T(8,128)(2,1)S(1)}, u32[]{:S(2)}) copy-start(bf16[4,320,512]{2,1,0:T(8,128)(2,1)S(1)} %collective-permute-done.refs_2_) | copy-start | bytes 3932164
  43.1 9.5 %collective-permute-start.7 = (bf16[4,7168]{1,0:T(4,128)(2,1)S(1)}, bf16[4,7168]{1,0:T(4,128)(2,1)S(1)}, u32[]{:S(2)}, u32[]{:S(2)}) collective-permute-start(bf16[4,7168]{1,0:T(4,128)(2,1)S(1)} %get-tuple-element.59.refs_0_), channel_id=1, source_target_pairs={{0,2},{2,0},{4,6},{6,4},{8,10},{10,8},{12,14},{14,12},{1,3},{3,1},... | collective-permute-start | bytes 172040 | tf_op jit(solution)/shard_map/ppermute | solution.py:28
  53.0 12.6 %collective-permute-start.10 = (bf16[4,7168]{1,0:T(4,128)(2,1)S(1)}, bf16[4,7168]{1,0:T(4,128)(2,1)S(1)}, u32[]{:S(2)}, u32[]{:S(2)}) collective-permute-start(bf16[4,7168]{1,0:T(4,128)(2,1)S(1)} %get-tuple-element.65), channel_id=1, source_target_pairs={{0,12},{2,14},{4,8},{6,10},{8,4},{10,6},{12,0},{14,2},{1,13},{3,15... | collective-permute-start | bytes 172040 | tf_op jit(solution)/shard_map/ppermute | solution.py:597
  55.5 18.7 %collective-permute-start.9 = (bf16[4,7168]{1,0:T(4,128)(2,1)S(1)}, bf16[4,7168]{1,0:T(4,128)(2,1)S(1)}, u32[]{:S(2)}, u32[]{:S(2)}) collective-permute-start(bf16[4,7168]{1,0:T(4,128)(2,1)S(1)} %get-tuple-element.65), channel_id=1, source_target_pairs={{0,8},{2,10},{4,12},{6,14},{8,0},{10,2},{12,4},{14,6},{1,9},{3,11}... | collective-permute-start | bytes 172040 | tf_op jit(solution)/shard_map/ppermute | solution.py:597
  57.7 16.6 %collective-permute-start.8 = (bf16[4,7168]{1,0:T(4,128)(2,1)S(1)}, bf16[4,7168]{1,0:T(4,128)(2,1)S(1)}, u32[]{:S(2)}, u32[]{:S(2)}) collective-permute-start(bf16[4,7168]{1,0:T(4,128)(2,1)S(1)} %get-tuple-element.73.refs_0_), channel_id=1, source_target_pairs={{0,4},{2,6},{4,0},{6,2},{8,12},{10,14},{12,8},{14,10},{1,5},{3,7},... | collective-permute-start | bytes 172040 | tf_op jit(solution)/shard_map/ppermute | solution.py:597
  75.7 4.7 %copy-start.7 = (bf16[1152,512]{1,0:T(8,128)(2,1)}, bf16[1152,512]{1,0:T(8,128)(2,1)S(1)}, u32[]{:S(2)}) copy-start(bf16[1152,512]{1,0:T(8,128)(2,1)S(1)} %broadcast_select_fusion.1.refs_6_) | copy-start | bytes 3538948
  75.7 4.7 %collective-permute-start.12 = (bf16[1152,512]{1,0:T(8,128)(2,1)S(1)}, bf16[1152,512]{1,0:T(8,128)(2,1)S(1)}, u32[]{:S(2)}, u32[]{:S(2)}) collective-permute-start(bf16[1152,512]{1,0:T(8,128)(2,1)S(1)} %broadcast_select_fusion.1.refs_6_), channel_id=1, source_target_pairs={{0,1},{1,0},{2,3},{3,2},{4,5},{5,4},{6,7},{7,6},{8,9},{9,8},{10,11... | collective-permute-start | bytes 3538952 | tf_op jit(solution)/shard_map/ppermute | solution.py:28
  75.8 30.6 %collective-permute-start.11 = (bf16[1152,512]{1,0:T(8,128)(2,1)}, bf16[1152,512]{1,0:T(8,128)(2,1)}, u32[]{:S(2)}, u32[]{:S(2)}) collective-permute-start(bf16[1152,512]{1,0:T(8,128)(2,1)} %collective-permute-done.3), channel_id=1, source_target_pairs={{4,0},{8,12},{6,2},{10,14},{5,1},{9,13},{7,3},{11,15},{20,16},{24,... | collective-permute-start | bytes 3538952 | tf_op jit(solution)/shard_map/ppermute | solution.py:36
  77.2 13.9 %collective-permute-start.15 = (bf16[256,512]{1,0:T(8,128)(2,1)}, bf16[256,512]{1,0:T(8,128)(2,1)}, u32[]{:S(2)}, u32[]{:S(2)}) collective-permute-start(bf16[256,512]{1,0:T(8,128)(2,1)} %get-tuple-element.60), channel_id=1, source_target_pairs={{0,2},{2,0},{4,6},{6,4},{8,10},{10,8},{12,14},{14,12},{1,3},{3,1},... | collective-permute-start | bytes 786440 | tf_op jit(solution)/shard_map/ppermute | solution.py:28
  78.8 13.1 %collective-permute-start.16 = (bf16[256,512]{1,0:T(8,128)(2,1)}, bf16[256,512]{1,0:T(8,128)(2,1)}, u32[]{:S(2)}, u32[]{:S(2)}) collective-permute-start(bf16[256,512]{1,0:T(8,128)(2,1)} %get-tuple-element.58), channel_id=1, source_target_pairs={{0,2},{2,0},{4,6},{6,4},{8,10},{10,8},{12,14},{14,12},{1,3},{3,1},... | collective-permute-start | bytes 786440 | tf_op jit(solution)/shard_map/ppermute | solution.py:28
  80.4 10.7 %collective-permute-start.14 = (bf16[16,7168]{1,0:T(8,128)(2,1)}, bf16[16,7168]{1,0:T(8,128)(2,1)}, u32[]{:S(2)}, u32[]{:S(2)}) collective-permute-start(bf16[16,7168]{1,0:T(8,128)(2,1)} %stack_rows.1.mine_ref), channel_id=1, source_target_pairs={{0,1},{1,0},{2,3},{3,2},{4,5},{5,4},{6,7},{7,6},{8,9},{9,8},{10,11... | collective-permute-start | bytes 688136 | tf_op jit(solution)/shard_map/ppermute | solution.py:28
  80.4 1.0 copy-start.8
  81.4 10.5 %copy-start = (bf16[1,7168,128]{2,1,0:T(8,128)(2,1)S(1)}, bf16[1,7168,128]{2,1,0:T(8,128)(2,1)}, u32[]{:S(2)}) copy-start(bf16[1,7168,128]{2,1,0:T(8,128)(2,1)} %gate_hbm.1) | copy-start | bytes 5505028
  89.5 16.8 %collective-permute-start.13 = (bf16[256,512]{1,0:T(8,128)(2,1)}, bf16[256,512]{1,0:T(8,128)(2,1)S(1)}, u32[]{:S(2)}, u32[]{:S(2)}) collective-permute-start(bf16[256,512]{1,0:T(8,128)(2,1)} %get-tuple-element.72), channel_id=1, source_target_pairs={{0,2},{2,0},{4,6},{6,4},{8,10},{10,8},{12,14},{14,12},{1,3},{3,1},... | collective-permute-start | bytes 786440 | tf_op jit(solution)/shard_map/ppermute | solution.py:28
  91.9 1.5 %copy-start.1 = (bf16[1,7168,128]{2,1,0:T(8,128)(2,1)S(1)}, bf16[1,7168,128]{2,1,0:T(8,128)(2,1)}, u32[]{:S(2)}) copy-start(bf16[1,7168,128]{2,1,0:T(8,128)(2,1)} %up_hbm.1) | copy-start | bytes 5505028
  93.4 1.5 %copy-start.2 = (bf16[1,128,7168]{2,1,0:T(8,128)(2,1)S(1)}, bf16[1,128,7168]{2,1,0:T(8,128)(2,1)}, u32[]{:S(2)}) copy-start(bf16[1,128,7168]{2,1,0:T(8,128)(2,1)} %down_hbm.1) | copy-start | bytes 5505028
  97.5 1.6 %collective-permute-start.17 = (bf16[16,7168]{1,0:T(8,128)(2,1)S(1)}, bf16[16,7168]{1,0:T(8,128)(2,1)S(1)}, u32[]{:S(2)}, u32[]{:S(2)}) collective-permute-start(bf16[16,7168]{1,0:T(8,128)(2,1)S(1)} %get-tuple-element.80), channel_id=1, source_target_pairs={{0,1},{1,0},{2,3},{3,2},{4,5},{5,4},{6,7},{7,6},{8,9},{9,8},{10,11... | collective-permute-start | bytes 688136 | tf_op jit(solution)/shard_map/ppermute | solution.py:28
  106.3 2.9 %copy-start.9 = (bf16[256,512]{1,0:T(8,128)(2,1)}, bf16[256,512]{1,0:T(8,128)(2,1)S(1)}, u32[]{:S(2)}) copy-start(bf16[256,512]{1,0:T(8,128)(2,1)S(1)} %collective-permute-done.13.refs_9_) | copy-start | bytes 786436
  106.3 4.8 %collective-permute-start.18 = (bf16[8,7168]{1,0:T(8,128)(2,1)S(1)}, bf16[8,7168]{1,0:T(8,128)(2,1)S(1)}, u32[]{:S(2)}, u32[]{:S(2)}) collective-permute-start(bf16[8,7168]{1,0:T(8,128)(2,1)S(1)} %get-tuple-element.84), channel_id=1, source_target_pairs={{0,2},{2,0},{4,6},{6,4},{8,10},{10,8},{12,14},{14,12},{1,3},{3,1},... | collective-permute-start | bytes 344072 | tf_op jit(solution)/shard_map/ppermute | solution.py:28
  109.3 3.1 %copy-start.6 = (bf16[1152,512]{1,0:T(8,128)(2,1)}, bf16[1152,512]{1,0:T(8,128)(2,1)S(1)}, u32[]{:S(2)}) copy-start(bf16[1152,512]{1,0:T(8,128)(2,1)S(1)} %broadcast_select_fusion.refs_3_.refs_5_) | copy-start | bytes 3538948
  109.3 3.0 %collective-permute-start.19 = (bf16[1152,512]{1,0:T(8,128)(2,1)S(1)}, bf16[1152,512]{1,0:T(8,128)(2,1)}, u32[]{:S(2)}, u32[]{:S(2)}) collective-permute-start(bf16[1152,512]{1,0:T(8,128)(2,1)S(1)} %broadcast_select_fusion.refs_3_.refs_5_), channel_id=1, source_target_pairs={{0,1},{1,0},{2,3},{3,2},{4,5},{5,4},{6,7},{7,6},{8,9},{9,8},{10,11... | collective-permute-start | bytes 3538952 | tf_op jit(solution)/shard_map/ppermute | solution.py:28
  118.5 11.3 %collective-permute-start.21 = (bf16[2,7168]{1,0:T(2,128)(2,1)S(1)}, bf16[2,7168]{1,0:T(2,128)(2,1)S(1)}, u32[]{:S(2)}, u32[]{:S(2)}) collective-permute-start(bf16[2,7168]{1,0:T(2,128)(2,1)S(1)} %get-tuple-element.95), channel_id=1, source_target_pairs={{0,4},{2,6},{4,0},{6,2},{8,12},{10,14},{12,8},{14,10},{1,5},{3,7},... | collective-permute-start | bytes 86024 | tf_op jit(solution)/shard_map/ppermute | solution.py:597
  118.7 12.3 %collective-permute-start.20 = (bf16[256,512]{1,0:T(8,128)(2,1)}, bf16[256,512]{1,0:T(8,128)(2,1)S(1)}, u32[]{:S(2)}, u32[]{:S(2)}) collective-permute-start(bf16[256,512]{1,0:T(8,128)(2,1)} %attend_give.1), channel_id=1, source_target_pairs={{0,2},{2,0},{4,6},{6,4},{8,10},{10,8},{12,14},{14,12},{1,3},{3,1},... | collective-permute-start | bytes 786440 | tf_op jit(solution)/shard_map/ppermute | solution.py:28
  119.2 10.7 %collective-permute-start.22 = (bf16[2,7168]{1,0:T(2,128)(2,1)S(1)}, bf16[2,7168]{1,0:T(2,128)(2,1)S(1)}, u32[]{:S(2)}, u32[]{:S(2)}) collective-permute-start(bf16[2,7168]{1,0:T(2,128)(2,1)S(1)} %get-tuple-element.97), channel_id=1, source_target_pairs={{0,8},{2,10},{4,12},{6,14},{8,0},{10,2},{12,4},{14,6},{1,9},{3,11}... | collective-permute-start | bytes 86024 | tf_op jit(solution)/shard_map/ppermute | solution.py:597
  122.4 7.5 %collective-permute-start.23 = (bf16[2,7168]{1,0:T(2,128)(2,1)S(1)}, bf16[2,7168]{1,0:T(2,128)(2,1)S(1)}, u32[]{:S(2)}, u32[]{:S(2)}) collective-permute-start(bf16[2,7168]{1,0:T(2,128)(2,1)S(1)} %get-tuple-element.99), channel_id=1, source_target_pairs={{0,12},{2,14},{4,8},{6,10},{8,4},{10,6},{12,0},{14,2},{1,13},{3,15... | collective-permute-start | bytes 86024 | tf_op jit(solution)/shard_map/ppermute | solution.py:597
  131.0 0.7 copy-start.10

commit v7 on v4

v7 whole, which is shorter than its diff:
```python
import functools

import jax
import jax.numpy as jnp
from jax import lax
from jax.experimental import pallas as pl
from jax.experimental.pallas import tpu as pltpu
from jax.sharding import PartitionSpec as P

SHARDS = 8
CAP = 2
LANES = 128
PAD = 16

SMALL = pl.CostEstimate(flops=0, bytes_accessed=1024, transcendentals=0)

LARGE = 62 * 1024 * 1024

softmax_scale = 192.0 ** (-0.5)
log2e = 1.4426950408889634


def after(x, *earlier):
    return lax.optimization_barrier((x, *earlier))[0]


def swapped(x, axis, bit):
    return lax.ppermute(x, axis, [(i, i ^ 1 << bit) for i in range(lax.axis_size(axis))])


def line_hop(x, block, moves):
    pairs = []
    for base in range(0, lax.axis_size("branch"), block):
        for low in range(2):
            pairs += [(base + 2 * i + low, base + 2 * j + low) for i, j in moves]
    return lax.ppermute(x, "branch", pairs)


def pack_cache_kernel(lat_ref, rope_ref, out_ref, sems):
    rows = lat_ref.shape[0]
    copies = [
        pltpu.make_async_copy(lat_ref, out_ref.at[pl.ds(0, rows)], sems.at[0]),
        pltpu.make_async_copy(rope_ref, out_ref.at[pl.ds(rows, rope_ref.shape[0])], sems.at[1]),
    ]
    for copy in copies:
        copy.start()
    for copy in copies:
        copy.wait()


def pack_cache(lat, rope):
    return pl.pallas_call(
        pack_cache_kernel,
        out_shape=jax.ShapeDtypeStruct((lat.shape[0] + rope.shape[0], lat.shape[1]), lat.dtype),
        in_specs=[pl.BlockSpec(memory_space=pltpu.HBM)] * 2,
        out_specs=pl.BlockSpec(memory_space=pltpu.VMEM),
        scratch_shapes=[pltpu.SemaphoreType.DMA((2,))],
        cost_estimate=SMALL,
        compiler_params=pltpu.CompilerParams(vmem_limit_bytes=LARGE),
        name="pack_cache",
    )(lat, rope)


def row_for(slot, parity, slot_ref, own_ref):
    count = slot_ref.shape[0]
    line = count // 2
    own = own_ref[0]
    high = lax.div(own, 2)
    low = lax.rem(own, 2)
    mine = high
    pair = high + 1 - 2 * lax.rem(high, 2)
    first_half = high < line // 2
    nearer = jnp.where(first_half, line // 2, line // 2 - 1)
    farther = jnp.where(first_half, line - 1, 0)
    position = mine
    for number, place_there in ((1, pair), (2, nearer), (3, farther)):
        position = jnp.where(slot == number, place_there, position)
    wanted = 2 * position + (low if parity == 0 else 1 - low)
    row = jnp.int32(0)
    for r in range(1, count):
        row = row + jnp.where(slot_ref[r] == wanted, r, 0)
    return row


def pack_tokens_kernel(parity, slot_ref, own_ref, q_ref, rope_ref, new_ref, out_ref, sems):
    copies = []
    for slot in range(out_ref.shape[0]):
        row = row_for(slot, parity, slot_ref, own_ref)
        start = 0
        for part, source in enumerate((q_ref, rope_ref, new_ref)):
            count = source.shape[1]
            copy = pltpu.make_async_copy(
                source.at[row], out_ref.at[slot, pl.ds(start, count)], sems.at[slot, part]
            )
            copy.start()
            copies.append(copy)
            start += count
    for copy in copies:
        copy.wait()


def pack_tokens(parity, branch_slot, own, q_lat, q_rope, new):
    slots = branch_slot.shape[0] // 2
    sources = (q_lat, q_rope, new)
    rows = sum(x.shape[1] for x in sources)
    return pl.pallas_call(
        functools.partial(pack_tokens_kernel, parity),
        out_shape=jax.ShapeDtypeStruct((slots, rows, q_lat.shape[2]), q_lat.dtype),
        in_specs=[pl.BlockSpec(memory_space=pltpu.SMEM)] * 2
        + [pl.BlockSpec(memory_space=pl.ANY)] * 3,
        out_specs=pl.BlockSpec(memory_space=pltpu.VMEM),
        scratch_shapes=[pltpu.SemaphoreType.DMA((slots, 3))],
        cost_estimate=SMALL,
        compiler_params=pltpu.CompilerParams(vmem_limit_bytes=4 * 1024 * 1024),
        name="pack_tokens",
    )(branch_slot, own, *sources)


def spread_matrix(raw_rows, width):
    per_row = width // (LANES // 2)
    blocks = width // LANES
    shape = (raw_rows * per_row, raw_rows * blocks)
    row = lax.broadcasted_iota(jnp.int32, shape, 0)
    column = lax.broadcasted_iota(jnp.int32, shape, 1)
    wanted = ((row % per_row) // 2) * raw_rows + row // per_row
    return (column == wanted).astype(jnp.bfloat16)


def spread(matrix, raw):
    blocks = raw.shape[1] // LANES
    stacked = jnp.concatenate(
        [raw[:, b * LANES : (b + 1) * LANES] for b in range(blocks)], axis=0
    )
    rows = jnp.dot(matrix, stacked, preferred_element_type=jnp.float32)
    row = lax.broadcasted_iota(jnp.int32, rows.shape, 0)
    lane = lax.broadcasted_iota(jnp.int32, rows.shape, 1)
    return jnp.where(row % 2 == lane // (LANES // 2), rows, 0.0)


def build_attend(heads, steps, width, half, rope_rows, raw_group, chunk):
    q_rows = heads * steps
    token_rope = q_rows // 8

    factor = softmax_scale * log2e
    contract = (((1,), (1,)), ((), ()))

    def put_query_rope(rope_queries, number, raw_rope, matrix):
        grown = raw_group * width // (LANES // 2)
        for i, start in enumerate(range(0, token_rope, raw_group)):
            part = spread(matrix, raw_rope[start : start + raw_group, :])
            part = part + pltpu.roll(part, LANES // 2, 1)
            row = number * q_rows + i * grown
            rope_queries[row : row + grown, :] = part.astype(jnp.bfloat16)

    def merge_own(query, rope_query, fresh_all, peak, total, summed):
        fresh = fresh_all[0:PAD, :]
        fresh_rope = fresh_all[PAD : 2 * PAD, 0:LANES]
        own = lax.dot_general(
            query, fresh, contract, preferred_element_type=jnp.float32
        )
        own = own + lax.dot_general(
            rope_query, fresh_rope, contract, preferred_element_type=jnp.float32
        )
        row_step = lax.broadcasted_iota(jnp.int32, (q_rows, 1), 0) // heads
        columns = [jnp.where(row_step >= j, own[:, j : j + 1], -1e30) for j in range(steps)]
        top = peak
        for column in columns:
            top = jnp.maximum(top, column)
        share = jnp.exp2((peak - top) * factor)
        parts = [
            jnp.where(row_step >= j, jnp.exp2((column - top) * factor), 0.0)
            for j, column in enumerate(columns)
        ]
        denominator = total * share
        for part in parts:
            denominator = denominator + part
        inverse = 1.0 / denominator
        fresh32 = fresh.astype(jnp.float32)
        value = summed * (share * inverse)
        for j, part in enumerate(parts):
            value = value + (part * inverse) * fresh32[j : j + 1, :]
        return value.astype(jnp.bfloat16)

    def put_key_rope(rope_keys, first, raw_rope, matrix):
        grown = raw_group * width // (LANES // 2)
        for i, start in enumerate(range(0, rope_rows, raw_group)):
            part = spread(matrix, raw_rope[start : start + raw_group, :])
            row = first + i * grown
            rope_keys[row : row + grown, :] = part.astype(jnp.bfloat16)

    def kernel(slot, has_placed, slot_ref, own_ref, guest, stay, *refs):
        own_half, other_half = refs[:2]
        refs = refs[3:] if has_placed else refs[2:]
        give, placed, rope_keys, query_rope, scores, summed, result, sem = refs
        tokens = (guest.at[slot], stay.at[slot])
        matrix = spread_matrix(raw_group, width)
        middle = q_rows + token_rope
        for number, token in enumerate(tokens):
            put_query_rope(query_rope, number, token.at[pl.ds(q_rows, token_rope)], matrix)
        peak = None
        for i, cache in enumerate((own_half, other_half)):
            put_key_rope(rope_keys, 0, cache.at[pl.ds(half, rope_rows)], matrix)
            for first in range(0, half, chunk):
                highs = []
                for number, token in enumerate(tokens):
                    rows = slice(number * q_rows, (number + 1) * q_rows)
                    part = lax.dot_general(
                        token[0:q_rows, :],
                        cache[first : first + chunk, :],
                        contract,
                        preferred_element_type=jnp.float32,
                    )
                    part = part + lax.dot_general(
                        query_rope[rows, :],
                        rope_keys[first : first + chunk, :],
                        contract,
                        preferred_element_type=jnp.float32,
                    )
                    scores[rows, i * half + first : i * half + first + chunk] = part
                    highs.append(jnp.max(part, axis=1, keepdims=True))
                high = jnp.concatenate(highs, axis=0)
                peak = high if peak is None else jnp.maximum(peak, high)
        scaled = peak * factor
        total = None
        for first in range(0, 2 * half, chunk):
            cache = own_half if first < half else other_half
            weights = jnp.exp2(scores[:, first : first + chunk] * factor - scaled)
            part = jnp.sum(weights, axis=1, keepdims=True)
            value = jnp.dot(
                weights.astype(jnp.bfloat16),
                cache[first % half : first % half + chunk, :],
                preferred_element_type=jnp.float32,
            )
            if first == 0:
                total = part
                summed[...] = value
            else:
                total = total + part
                summed[...] += value
        for number, token in enumerate(tokens):
            rows = slice(number * q_rows, (number + 1) * q_rows)
            value = merge_own(
                token[0:q_rows, :],
                query_rope[rows, :],
                token[middle : middle + 2 * PAD, :],
                peak[rows],
                total[rows],
                summed[rows, :],
            )
            if number == 0:
                give[...] = value
            else:
                result[...] = value
        row = row_for(slot, 0, slot_ref, own_ref)
        copy = pltpu.make_async_copy(result, placed.at[row], sem)
        copy.start()
        copy.wait()

    def call(scalars, slot, guest, stay, caches, placed):
        count = scalars[0].shape[0]
        vmem = pl.BlockSpec(memory_space=pltpu.VMEM)
        anywhere = pl.BlockSpec(memory_space=pl.ANY)
        operands = [*scalars, guest, stay, *caches]
        in_specs = [pl.BlockSpec(memory_space=pltpu.SMEM)] * 2 + [vmem] * 4
        alias = {}
        if placed is not None:
            alias = {len(operands): 1}
            in_specs.append(anywhere)
            operands.append(placed)
        return pl.pallas_call(
            functools.partial(kernel, slot, placed is not None),
            out_shape=(
                jax.ShapeDtypeStruct((q_rows, width), jnp.bfloat16),
                jax.ShapeDtypeStruct((count, q_rows, width), jnp.bfloat16),
            ),
            in_specs=in_specs,
            out_specs=(vmem, anywhere),
            scratch_shapes=[
                pltpu.VMEM((half, LANES), jnp.bfloat16),
                pltpu.VMEM((2 * q_rows, LANES), jnp.bfloat16),
                pltpu.VMEM((2 * q_rows, 2 * half), jnp.float32),
                pltpu.VMEM((2 * q_rows, width), jnp.float32),
                pltpu.VMEM((q_rows, width), jnp.bfloat16),
                pltpu.SemaphoreType.DMA,
            ],
            input_output_aliases=alias,
            cost_estimate=SMALL,
            compiler_params=pltpu.CompilerParams(vmem_limit_bytes=16 * 1024 * 1024),
            name="attend",
        )(*operands)

    return call


def place_kernel(slot_ref, own_ref, *refs):
    sources, (before, placed_ref, sems) = refs[:-3], refs[-3:]
    copies = []
    for slot, source in enumerate(sources):
        row = row_for(slot, 1, slot_ref, own_ref)
        copies.append(pltpu.make_async_copy(source, placed_ref.at[row], sems.at[slot]))
    for copy in copies:
        copy.start()
    for copy in copies:
        copy.wait()


def place(scalars, sources, placed):
    vmem = pl.BlockSpec(memory_space=pltpu.VMEM)
    return pl.pallas_call(
        place_kernel,
        out_shape=jax.ShapeDtypeStruct(placed.shape, placed.dtype),
        in_specs=[pl.BlockSpec(memory_space=pltpu.SMEM)] * 2
        + [vmem] * len(sources)
        + [pl.BlockSpec(memory_space=pl.ANY)],
        out_specs=pl.BlockSpec(memory_space=pl.ANY),
        scratch_shapes=[pltpu.SemaphoreType.DMA((len(sources),))],
        input_output_aliases={2 + len(sources): 0},
        cost_estimate=SMALL,
        compiler_params=pltpu.CompilerParams(vmem_limit_bytes=4 * 1024 * 1024),
        name="place",
    )(*scalars, *sources, placed)


def dispatch_kernel(experts, block_ref, routes_ref, gate_ref, tokens_ref, out_ref, share_ref):
    block = block_ref[0]
    routes = routes_ref[...]
    gates = gate_ref[...]
    rows = routes.shape[0]
    down = lax.broadcasted_iota(jnp.int32, (rows, rows), 0)
    across = lax.broadcasted_iota(jnp.int32, (rows, rows), 1)
    same = (down == across).astype(jnp.float32)
    slots = experts * CAP
    slot_row = lax.broadcasted_iota(jnp.int32, (slots, rows), 0)
    slot_column = lax.broadcasted_iota(jnp.int32, (rows, slots), 1)
    placing = jnp.zeros((slots, rows), jnp.float32)
    share = jnp.zeros((rows, slots), jnp.float32)
    for expert in range(experts):
        hit = routes == expert
        has = jnp.sum(hit.astype(jnp.float32), axis=1, keepdims=True)
        weight = jnp.sum(jnp.where(hit, gates, 0.0), axis=1, keepdims=True)
        has_row = jnp.sum(has * same, axis=0, keepdims=True)
        before_row = jnp.sum(jnp.where(down < across, has, 0.0), axis=0, keepdims=True)
        before = jnp.sum(jnp.where(across < down, has_row, 0.0), axis=1, keepdims=True)
        away = lax.rem(expert + experts - block, experts)
        for c in range(CAP):
            slot = expert * CAP + c
            placing += jnp.where((slot_row == slot) & (before_row == c), has_row, 0.0)
            share += jnp.where((slot_column == away * CAP + c) & (before == c), weight, 0.0)
    out_ref[...] = jnp.dot(
        placing.astype(jnp.bfloat16), tokens_ref[...], preferred_element_type=jnp.float32
    ).astype(jnp.bfloat16)
    share_ref[...] = share


def dispatch(block, routes, gates, tokens, experts):
    slots = experts * CAP
    return pl.pallas_call(
        functools.partial(dispatch_kernel, experts),
        out_shape=(
            jax.ShapeDtypeStruct((slots, tokens.shape[1]), tokens.dtype),
            jax.ShapeDtypeStruct((tokens.shape[0], slots), jnp.float32),
        ),
        in_specs=[pl.BlockSpec(memory_space=pltpu.SMEM)]
        + [pl.BlockSpec(memory_space=pltpu.VMEM)] * 3,
        out_specs=(pl.BlockSpec(memory_space=pltpu.VMEM),) * 2,
        cost_estimate=SMALL,
        compiler_params=pltpu.CompilerParams(vmem_limit_bytes=8 * 1024 * 1024),
        name="dispatch",
    )(block, routes, gates, tokens)


def order_kernel(experts, device_ref, rows_ref, mine_ref, theirs_ref):
    device = device_ref[0]
    total = rows_ref.shape[0]
    count = mine_ref.shape[0]
    cores = total // count
    lines = SHARDS // (2 * cores)
    ways = experts * lines
    block = lax.div(device, SHARDS)
    within = lax.rem(device, SHARDS)
    shape = (count, total)
    row = lax.broadcasted_iota(jnp.int32, shape, 0)
    column = lax.broadcasted_iota(jnp.int32, shape, 1)
    slot = row % CAP
    way = (row // CAP) % ways
    beside = row // (CAP * ways)
    from_block = (block + experts - way // lines) % experts
    flip = (way % lines) * (2 * cores) + beside * cores
    for core, out_ref in enumerate((mine_ref, theirs_ref)):
        source = from_block * SHARDS + jnp.bitwise_xor(within, flip + core)
        chosen = (column == source * CAP + slot).astype(jnp.bfloat16)
        out_ref[...] = jnp.dot(
            chosen, rows_ref[...], preferred_element_type=jnp.float32
        ).astype(jnp.bfloat16)


def order_rows(device, rows, experts, cores):
    shape = jax.ShapeDtypeStruct((rows.shape[0] // cores, rows.shape[1]), rows.dtype)
    return pl.pallas_call(
        functools.partial(order_kernel, experts),
        out_shape=(shape, shape),
        in_specs=[
            pl.BlockSpec(memory_space=pltpu.SMEM),
            pl.BlockSpec(memory_space=pltpu.VMEM),
        ],
        out_specs=(pl.BlockSpec(memory_space=pltpu.VMEM),) * 2,
        cost_estimate=SMALL,
        compiler_params=pltpu.CompilerParams(vmem_limit_bytes=16 * 1024 * 1024),
        name="order_rows",
    )(device, rows)


def experts_kernel(mine_ref, theirs_ref, gate_hbm, up_hbm, down_hbm, keep_ref, send_ref, *scratch):
    gate_ref, up_ref, down_ref, sems = scratch
    copies = [
        pltpu.make_async_copy(source.at[0], there, sems.at[i])
        for i, (source, there) in enumerate(
            ((gate_hbm, gate_ref), (up_hbm, up_ref), (down_hbm, down_ref))
        )
    ]
    for copy in copies:
        copy.start()
    rows = jnp.concatenate([mine_ref[...], theirs_ref[...]], axis=0)
    copies[0].wait()
    gate = jnp.dot(rows, gate_ref[...], preferred_element_type=jnp.float32)
    copies[1].wait()
    lifted = jnp.dot(rows, up_ref[...], preferred_element_type=jnp.float32)
    hidden = (gate / (1.0 + jnp.exp(-gate)) * lifted).astype(jnp.bfloat16)
    copies[2].wait()
    parts = jnp.dot(hidden, down_ref[...], preferred_element_type=jnp.float32)
    count = mine_ref.shape[0]
    keep_ref[...] = parts[:count]
    send_ref[...] = parts[count:].astype(jnp.bfloat16)


def run_experts(mine, theirs, w_gate, w_up, w_down):
    return pl.pallas_call(
        experts_kernel,
        out_shape=(
            jax.ShapeDtypeStruct(mine.shape, jnp.float32),
            jax.ShapeDtypeStruct(mine.shape, jnp.bfloat16),
        ),
        in_specs=[pl.BlockSpec(memory_space=pltpu.VMEM)] * 2
        + [pl.BlockSpec(memory_space=pltpu.HBM)] * 3,
        out_specs=(pl.BlockSpec(memory_space=pltpu.VMEM),) * 2,
        scratch_shapes=[
            pltpu.VMEM(w_gate.shape[1:], w_gate.dtype),
            pltpu.VMEM(w_up.shape[1:], w_up.dtype),
            pltpu.VMEM(w_down.shape[1:], w_down.dtype),
            pltpu.SemaphoreType.DMA((3,)),
        ],
        cost_estimate=SMALL,
        compiler_params=pltpu.CompilerParams(vmem_limit_bytes=16 * 1024 * 1024),
        name="experts",
    )(mine, theirs, w_gate, w_up, w_down)


def halve_kernel(sum_ref, arrived_ref, keep_ref, send_ref):
    count = keep_ref.shape[0]
    total = sum_ref[...] + arrived_ref[...].astype(jnp.float32)
    keep_ref[...] = total[:count]
    send_ref[...] = total[count:].astype(jnp.bfloat16)


def halve(kept, arrived):
    shape = (kept.shape[0] // 2, kept.shape[1])
    return pl.pallas_call(
        halve_kernel,
        out_shape=(
            jax.ShapeDtypeStruct(shape, jnp.float32),
            jax.ShapeDtypeStruct(shape, jnp.bfloat16),
        ),
        cost_estimate=SMALL,
        compiler_params=pltpu.CompilerParams(vmem_limit_bytes=8 * 1024 * 1024),
        name="halve",
    )(kept, arrived)


def on_device(
    latent_cache,
    rope_cache,
    q_latent,
    q_rope,
    new_latent,
    new_rope,
    branch_slot,
    moe_input,
    routes,
    route_gate,
    w_gate,
    w_up,
    w_down,
):
    tok_rows, step_count, head_count, width = q_latent.shape
    rope_width = new_rope.shape[-1]
    line = tok_rows // 2
    q_rows = step_count * head_count
    half = latent_cache.shape[1]
    rope_rows = rope_cache.shape[1]
    branch = lax.axis_index("branch")
    own = branch % tok_rows
    low = own % 2
    high = own // 2
    middle = jnp.logical_and(high > 0, high < line - 1)

    outer = [(i, i ^ 1) for i in range(line)]
    inner = [(i, i + 1) for i in range(1, line - 1, 2)]
    inner = inner + [(j, i) for i, j in inner]
    outward = [(i, i ^ 1) for i in range(1, line - 1)]
    own_cache = pack_cache(latent_cache[0], rope_cache[0])
    cache_a = line_hop(own_cache, tok_rows, outer)
    first_b = line_hop(own_cache, tok_rows, inner)

    q_lat = q_latent.reshape(tok_rows, q_rows, width)
    rope_raw = q_rope.reshape(tok_rows, q_rows * rope_width // width, width)
    fresh = jnp.concatenate(
        [
            jnp.pad(new_latent, ((0, 0), (0, PAD - step_count), (0, 0))),
            jnp.pad(new_rope, ((0, 0), (0, PAD - step_count), (0, width - rope_width))),
        ],
        axis=1,
    )
    scalars = (branch_slot, own[None])
    sources = (q_lat, rope_raw, fresh)
    leave = pack_tokens(1, branch_slot, after(own[None], own_cache), *sources)
    guest = swapped(leave, "branch", 0)
    stay = pack_tokens(0, branch_slot, after(own[None], leave), *sources)
    attend = build_attend(head_count, step_count, width, half, rope_rows, 32, half // 2)
    model_width = moe_input.shape[-1]
    tok_total = tok_rows * step_count
    device = branch * lax.axis_size("expert") + lax.axis_index("expert")
    experts = lax.axis_size("branch") * lax.axis_size("expert") // SHARDS
    cores = lax.axis_size("expert")
    shard_branches = SHARDS // cores
    block = device // SHARDS
    outgoing, share = dispatch(
        after(block[None], leave),
        routes.reshape(tok_total, -1),
        route_gate.reshape(tok_total, -1),
        moe_input.reshape(tok_total, model_width),
        experts,
    )

    around = shard_branches // 2

    def along(x, shift, flip):
        count = lax.axis_size("branch")
        there = [
            ((i // shard_branches + shift) % experts) * shard_branches
            + ((i % shard_branches) ^ (flip * 2))
            for i in range(count)
        ]
        return lax.ppermute(x, "branch", list(enumerate(there)))

    gathered = lax.all_gather(outgoing, ("branch", "expert"), axis=0, tiled=False)
    cache_a, first_b, outgoing = lax.optimization_barrier((cache_a, first_b, outgoing))
    second_b = line_hop(first_b, tok_rows, outward)
    first_c = line_hop(cache_a, tok_rows, inner)
    ways = [(k, m) for k in range(experts) for m in range(around)]

    def both_halves(cache):
        return cache, swapped(cache, "expert", 0)

    guest = after(guest, cache_a, first_b)
    given_0, placed = attend(scalars, 0, guest, stay, both_halves(own_cache), None)
    back_0 = swapped(given_0, "branch", 0)
    gathered = after(gathered, given_0)
    picked = lax.dynamic_slice_in_dim(gathered, block * CAP, CAP, axis=1)
    mine, theirs = order_rows(
        device[None], picked.reshape(-1, model_width), experts, cores
    )
    kept, sent = run_experts(mine, theirs, w_gate, w_up, w_down)
    kept, sent = halve(kept, swapped(sent, "expert", 0))
    given_1, placed = attend(scalars, 1, guest, stay, both_halves(cache_a), placed)
    back_1 = swapped(given_1, "branch", 0)

    second_b, given_1, kept, sent = lax.optimization_barrier((second_b, given_1, kept, sent))
    first_c, second_b = lax.optimization_barrier((first_c, second_b))
    second_c = line_hop(first_c, tok_rows, outward)
    cache_b = jnp.where(middle, first_b, second_b)
    given_2, placed = attend(scalars, 2, guest, stay, both_halves(cache_b), placed)
    back_2 = swapped(given_2, "branch", 0)
    parts = kept + swapped(sent, "branch", 0).astype(jnp.float32)

    second_c, back_0, back_1, back_2, parts = lax.optimization_barrier(
        (second_c, back_0, back_1, back_2, parts)
    )
    cache_c = both_halves(jnp.where(middle, first_c, second_c))
    homeward = [
        parts[w * CAP : (w + 1) * CAP].astype(jnp.float32 if way == (0, 0) else jnp.bfloat16)
        for w, way in enumerate(ways)
    ]
    guest, *homeward = lax.optimization_barrier((guest, *homeward))
    given_3, placed = attend(scalars, 3, guest, stay, cache_c, placed)
    back_3 = swapped(given_3, "branch", 0)
    homeward = [after(x, given_3) for x in homeward]
    placed = place(scalars, (back_0, back_1, back_2, back_3), placed)
    attended = placed.reshape(tok_rows, step_count, head_count, width)

    sums = [0.0] * experts
    for (k, m), piece in zip(ways, homeward):
        if (k, m) != (0, 0):
            piece = along(piece, -k, m).astype(jnp.float32)
        sums[k] = sums[k] + piece
    sums = jnp.concatenate(sums, axis=0)
    combined = jnp.sum(share[:, :, None] * sums[None, :, :], axis=1)
    moe_out = combined.astype(jnp.bfloat16).reshape(tok_rows, step_count, model_width)
    return (attended, moe_out)


def solution(mesh):
    return jax.shard_map(
        on_device,
        mesh=mesh,
        in_specs=(
            P(("group", "branch"), "expert", None),
            P(("group", "branch"), "expert", None),
            P(("group", "branch", "expert"), None, None, None),
            P(("group", "branch", "expert"), None, None),
            P(("group", "branch", "expert"), None, None),
            P(("group", "branch", "expert"), None, None),
            P(("group", "branch", "expert")),
            P(("group", "branch", "expert"), None, None),
            P(("group", "branch", "expert"), None, None),
            P(("group", "branch", "expert"), None, None),
            P(("branch", "expert"), None, None),
            P(("branch", "expert"), None, None),
            P(("branch", "expert"), None, None),
        ),
        out_specs=(
            P(("group", "branch", "expert"), None, None, None),
            P(("group", "branch", "expert"), None, None),
        ),
        check_vma=False,
    )
```

time: 131 us -> 167 us (1.27)
  blocking collectives: 0 us -> 49.9 us
  starting transfers between devices: 29.2 us -> 21.9 us
  local copies, waits for them, and re-layouts: 17.8 us -> 11.5 us
    all_gather x0 -> x1, blocking collectives: none -> 49.9 us  [on_device(): lax.all_gather(outgoing, ('branch', 'expert'), axis=0, tiled=False)]
    ppermute x13 -> x11, waiting for transfers between devices: 18.6 us -> 9.29 us  [swapped(): lax.ppermute(x, axis, [(i, i ^ 1 << bit) for i in range(lax.axis_size(axi...]
    ppermute x5, waiting for transfers between devices: 23.8 us -> 33 us  [line_hop(): return lax.ppermute(x, 'branch', pairs)]
    ppermute x6 -> x3, starting transfers between devices: 10.2 us -> 4.38 us  [along(): return lax.ppermute(x, 'branch', list(enumerate(there)))]
    unnamed x60 -> x34, local copies, waits for them, and re-layouts: 14.4 us -> 9.09 us
    pallas_call x9 -> x8, Pallas kernels: 32.7 us -> 30.6 us  [the longest x4 25.4 us: call(): pl.pallas_call(functools.partial(kernel, slot, placed is not None), out_s...]
    ppermute x13 -> x11, starting transfers between devices: 9.74 us -> 8.28 us  [swapped(): lax.ppermute(x, axis, [(i, i ^ 1 << bit) for i in range(lax.axis_size(axi...]
  transfers between devices with their start and end apart: 24 -> 19, of which waited for: 9 -> 8; matrix products, arithmetic and copies ran while one was open for 3% -> 2% of each run, Pallas kernels for 23% -> 16%
where the time goes in v7:
time: 167 us; the launch traced here: 166 us
  blocking collectives  49.9 us (30%)
  waiting for transfers between devices  44.5 us (27%)
  Pallas kernels  35.5 us (21%)
  starting transfers between devices  21.9 us (13%)
  local copies, waits for them, and re-layouts  11.5 us (7%)
  other arithmetic  1.97 us (1%)
    all_gather x1, blocking collectives, on_device(): lax.all_gather(outgoing, ('branch', 'expert'), axis=0, tiled=False)  49.9 us
    ppermute x5, waiting for transfers between devices, line_hop(): return lax.ppermute(x, 'branch', pairs)  33 us
    pallas_call x4, Pallas kernels, call(): pl.pallas_call(functools.partial(kernel, slot, placed is not None), out_s...  25.4 us
    ppermute x11, waiting for transfers between devices, swapped(): lax.ppermute(x, axis, [(i, i ^ 1 << bit) for i in range(lax.axis_size(axi...  9.29 us
    ppermute x5, starting transfers between devices, line_hop(): return lax.ppermute(x, 'branch', pairs)  9.19 us
    unnamed x34, local copies, waits for them, and re-layouts  9.09 us
    ppermute x11, starting transfers between devices, swapped(): lax.ppermute(x, axis, [(i, i ^ 1 << bit) for i in range(lax.axis_size(axi...  8.28 us
    ppermute x3, starting transfers between devices, along(): return lax.ppermute(x, 'branch', list(enumerate(there)))  4.38 us
  transfers between devices with their start and end apart: 19, of which 8 were waited for; matrix products, arithmetic and copies ran while one was open for 2% of the time, Pallas kernels for 16%

profile of v7, /device:TPU:0, one launch (start us, length us, event | category | flops | bytes accessed | tf_op | source)
XLA Modules:
  0.0 166.4 jit_solution(1546171253443045475)
XLA Ops:
  0.7 2.3 %pack_cache.1.refs_0_ = bf16[1152,512]{1,0:T(8,128)(2,1)} custom-call(bf16[1024,512]{1,0:T(8,128)(2,1)} %bitcast.16, bf16[128,512]{1,0:T(8,128)(2,1)} %bitcast.17), custom_call_target="tpu_custom_call" | custom-call | bytes 1024 | tf_op jit(solution)/shard_map/pack_cache/pallas_call | solution.py:52
  3.0 3.1 %collective-permute-start = (bf16[1152,512]{1,0:T(8,128)(2,1)}, bf16[1152,512]{1,0:T(8,128)(2,1)}, u32[]{:S(2)}, u32[]{:S(2)}) collective-permute-start(bf16[1152,512]{1,0:T(8,128)(2,1)} %pack_cache.1.refs_0_), channel_id=1, source_target_pairs={{0,4},{4,0},{8,12},{12,8},{2,6},{6,2},{10,14},{14,10},{1,5},{5,1},... | collective-permute-start | bytes 3538952 | tf_op jit(solution)/shard_map/ppermute | solution.py:36
  6.1 1.7 %collective-permute-start.1 = (bf16[1152,512]{1,0:T(8,128)(2,1)}, bf16[1152,512]{1,0:T(8,128)(2,1)}, u32[]{:S(2)}, u32[]{:S(2)}) collective-permute-start(bf16[1152,512]{1,0:T(8,128)(2,1)} %pack_cache.1.refs_0_), channel_id=1, source_target_pairs={{4,8},{8,4},{6,10},{10,6},{5,9},{9,5},{7,11},{11,7},{20,24},{24,20... | collective-permute-start | bytes 3538952 | tf_op jit(solution)/shard_map/ppermute | solution.py:36
  7.7 0.2 reshape.31.rope_ref
  8.0 1.6 copy-done
  9.6 2.2 %pack_tokens.2 = bf16[4,320,512]{2,1,0:T(8,128)(2,1)} custom-call(s32[8]{0:T(128)S(1)} %copy-done.5, s32[1]{0:T(128)} %bitcast.own_ref, bf16[8,256,512]{2,1,0:T(8,128)(2,1)S(1)} %bitcast.10, bf16[8,32,512]{2,1,0:T(8,128)(2,1)S(1)} %reshape.31.rope_ref, bf16[8,32,512]{2,1,0:T(8,128)(2,1)S(1)} %fusion.2.new_ref), custom_call_target="tpu_custom_call" | custom-call | bytes 1024 | tf_op jit(solution)/shard_map/pack_tokens/pallas_call | solution.py:106
  11.8 1.6 collective-permute-start.4
  13.5 0.3 dispatch.1
  13.8 18.6 %collective-permute-done.refs_0_ = bf16[1152,512]{1,0:T(8,128)(2,1)} collective-permute-done((bf16[1152,512]{1,0:T(8,128)(2,1)}, bf16[1152,512]{1,0:T(8,128)(2,1)}, u32[]{:S(2)}, u32[]{:S(2)}) %collective-permute-start) | collective-permute-done | bytes 1179680 | tf_op jit(solution)/shard_map/ppermute | solution.py:36
  32.3 1.7 %collective-permute-start.2 = (bf16[1152,512]{1,0:T(8,128)(2,1)}, bf16[1152,512]{1,0:T(8,128)(2,1)}, u32[]{:S(2)}, u32[]{:S(2)}) collective-permute-start(bf16[1152,512]{1,0:T(8,128)(2,1)} %collective-permute-done.refs_0_), channel_id=1, source_target_pairs={{4,8},{8,4},{6,10},{10,6},{5,9},{9,5},{7,11},{11,7},{20,24},{24,20... | collective-permute-start | bytes 3538952 | tf_op jit(solution)/shard_map/ppermute | solution.py:36
  34.0 1.3 collective-permute-start.3
  35.3 49.9 %all-gather.1 = bf16[16,4,7168]{2,1,0:T(4,128)(2,1)} all-gather(bf16[1,4,7168]{2,1,0:T(4,128)(2,1)S(1)} %bitcast.12), channel_id=2, replica_groups=mesh['group'=2,'branch'=8,'expert'=2] {'branch','expert'}, dimensions={0}, use_global_device_ids=true | all-gather | bytes 974848 | tf_op jit(solution)/shard_map/all_gather | solution.py:555
  85.2 1.6 copy-done.1
  86.8 1.1 pack_tokens.3.stay
  88.0 7.0 %attend.4 = (bf16[256,512]{1,0:T(8,128)(2,1)S(1)}, bf16[8,256,512]{2,1,0:T(8,128)(2,1)}) custom-call(s32[8]{0:T(128)S(1)} %copy-done.5, s32[1]{0:T(128)} %bitcast.own_ref, bf16[4,320,512]{2,1,0:T(8,128)(2,1)S(1)} %collective-permute-done.4.guest, bf16[4,320,512]{2,1,0:T(8,128)(2,1)S(1)} %pack_tokens.3.stay, bf16[1152,512]{1,0:T(8,128)(2,1)} %pack_cache.1.refs_0_, ...), custom_call_target="tpu_custom_call" | custom-call | bytes 1024 | tf_op jit(solution)/shard_map/attend/pallas_call | solution.py:270
  95.0 0.7 copy-done.8
  95.7 0.5 constant_dynamic-slice_fusion
  96.2 0.2 reshape.35.rows_ref
  96.4 0.3 order_rows.1
  96.7 1.5 copy-done.2
  98.2 1.5 copy-done.3
  99.7 1.5 copy-done.4
  101.2 2.2 %experts.1 = (f32[16,7168]{1,0:T(8,128)S(1)}, bf16[16,7168]{1,0:T(8,128)(2,1)}) custom-call(bf16[16,7168]{1,0:T(8,128)(2,1)S(1)} %get-tuple-element.55.mine_ref, bf16[16,7168]{1,0:T(8,128)(2,1)S(1)} %get-tuple-element.56.theirs_ref, bf16[1,7168,128]{2,1,0:T(8,128)(2,1)S(1)} %copy-done.2, bf16[1,7168,128]{2,1,0:T(8,128)(2,1)S(1)} %copy-done.3, ...), custom_call_target="tpu_custom_call" | custom-call | bytes 1024 | tf_op jit(solution)/shard_map/experts/pallas_call | solution.py:437
  103.4 0.4 collective-permute-start.7
  103.8 1.4 collective-permute-done.7.arrived_ref
  105.2 6.9 %attend.5 = (bf16[256,512]{1,0:T(8,128)(2,1)S(1)}, bf16[8,256,512]{2,1,0:T(8,128)(2,1)}) custom-call(s32[8]{0:T(128)S(1)} %copy-done.5, s32[1]{0:T(128)} %bitcast.own_ref, bf16[4,320,512]{2,1,0:T(8,128)(2,1)S(1)} %collective-permute-done.4.guest, bf16[4,320,512]{2,1,0:T(8,128)(2,1)S(1)} %pack_tokens.3.stay, ...), custom_call_target="tpu_custom_call", output_to_operand_aliasing={{1}: (6, {})} | custom-call | bytes 1024 | tf_op jit(solution)/shard_map/attend/pallas_call | solution.py:270
  112.2 1.4 broadcast_select_fusion.1.refs_0_
  113.6 0.4 collective-permute-start.11
  114.0 2.0 %collective-permute-start.9 = (bf16[256,512]{1,0:T(8,128)(2,1)S(1)}, bf16[256,512]{1,0:T(8,128)(2,1)S(1)}, u32[]{:S(2)}, u32[]{:S(2)}) collective-permute-start(bf16[256,512]{1,0:T(8,128)(2,1)S(1)} %copy-done.9), channel_id=1, source_target_pairs={{0,2},{2,0},{4,6},{6,4},{8,10},{10,8},{12,14},{14,12},{1,3},{3,1},... | collective-permute-start | bytes 786440 | tf_op jit(solution)/shard_map/ppermute | solution.py:28
  116.1 1.5 collective-permute-start.8
  117.6 5.8 %attend.6 = (bf16[256,512]{1,0:T(8,128)(2,1)S(1)}, bf16[8,256,512]{2,1,0:T(8,128)(2,1)}) custom-call(s32[8]{0:T(128)S(1)} %copy-done.5, s32[1]{0:T(128)} %bitcast.own_ref, bf16[4,320,512]{2,1,0:T(8,128)(2,1)S(1)} %collective-permute-done.4.guest, bf16[4,320,512]{2,1,0:T(8,128)(2,1)S(1)} %pack_tokens.3.stay, ...), custom_call_target="tpu_custom_call", output_to_operand_aliasing={{1}: (6, {})} | custom-call | bytes 1024 | tf_op jit(solution)/shard_map/attend/pallas_call | solution.py:270
  123.4 2.0 %collective-permute-start.12 = (bf16[256,512]{1,0:T(8,128)(2,1)S(1)}, bf16[256,512]{1,0:T(8,128)(2,1)S(1)}, u32[]{:S(2)}, u32[]{:S(2)}) collective-permute-start(bf16[256,512]{1,0:T(8,128)(2,1)S(1)} %get-tuple-element.65), channel_id=1, source_target_pairs={{0,2},{2,0},{4,6},{6,4},{8,10},{10,8},{12,14},{14,12},{1,3},{3,1},... | collective-permute-start | bytes 786440 | tf_op jit(solution)/shard_map/ppermute | solution.py:28
  125.5 0.2 collective-permute-done.9.refs_0_
  125.6 5.6 %collective-permute-done.10.refs_1_ = bf16[256,512]{1,0:T(8,128)(2,1)S(1)} collective-permute-done((bf16[256,512]{1,0:T(8,128)(2,1)S(1)}, bf16[256,512]{1,0:T(8,128)(2,1)S(1)}, u32[]{:S(2)}, u32[]{:S(2)}) %collective-permute-start.10) | collective-permute-done | bytes 262176 | tf_op jit(solution)/shard_map/ppermute | solution.py:28
  131.2 14.4 %collective-permute-done.8 = bf16[1152,512]{1,0:T(8,128)(2,1)S(1)} collective-permute-done((bf16[1152,512]{1,0:T(8,128)(2,1)}, bf16[1152,512]{1,0:T(8,128)(2,1)S(1)}, u32[]{:S(2)}, u32[]{:S(2)}) %collective-permute-start.8) | collective-permute-done | bytes 1179680 | tf_op jit(solution)/shard_map/ppermute | solution.py:36
  145.7 0.1 broadcast_select_fusion.refs_0_
  145.9 0.7 fusion.3
  146.6 2.1 %collective-permute-done.14.refs_1_ = bf16[1152,512]{1,0:T(8,128)(2,1)S(1)} collective-permute-done((bf16[1152,512]{1,0:T(8,128)(2,1)S(1)}, bf16[1152,512]{1,0:T(8,128)(2,1)S(1)}, u32[]{:S(2)}, u32[]{:S(2)}) %collective-permute-start.14) | collective-permute-done | bytes 1179680 | tf_op jit(solution)/shard_map/ppermute | solution.py:28
  148.8 5.8 %attend.7 = (bf16[256,512]{1,0:T(8,128)(2,1)S(1)}, bf16[8,256,512]{2,1,0:T(8,128)(2,1)}) custom-call(s32[8]{0:T(128)S(1)} %copy-done.5, s32[1]{0:T(128)} %bitcast.own_ref, bf16[4,320,512]{2,1,0:T(8,128)(2,1)S(1)} %collective-permute-done.4.guest, bf16[4,320,512]{2,1,0:T(8,128)(2,1)S(1)} %pack_tokens.3.stay, ...), custom_call_target="tpu_custom_call", output_to_operand_aliasing={{1}: (6, {})} | custom-call | bytes 1024 | tf_op jit(solution)/shard_map/attend/pallas_call | solution.py:270
  154.6 0.7 copy-done.10
  155.3 0.9 collective-permute-start.16
  156.3 1.7 %collective-permute-start.15 = (bf16[256,512]{1,0:T(8,128)(2,1)}, bf16[256,512]{1,0:T(8,128)(2,1)S(1)}, u32[]{:S(2)}, u32[]{:S(2)}) collective-permute-start(bf16[256,512]{1,0:T(8,128)(2,1)} %copy-done.10), channel_id=1, source_target_pairs={{0,2},{2,0},{4,6},{6,4},{8,10},{10,8},{12,14},{14,12},{1,3},{3,1},... | collective-permute-start | bytes 786440 | tf_op jit(solution)/shard_map/ppermute | solution.py:28
  158.0 3.5 %collective-permute-start.18 = (bf16[2,7168]{1,0:T(2,128)(2,1)S(1)}, bf16[2,7168]{1,0:T(2,128)(2,1)S(1)}, u32[]{:S(2)}, u32[]{:S(2)}) collective-permute-start(bf16[2,7168]{1,0:T(2,128)(2,1)S(1)} %get-tuple-element.85), channel_id=1, source_target_pairs={{0,12},{2,14},{4,8},{6,10},{8,4},{10,6},{12,0},{14,2},{1,13},{3,15... | collective-permute-start | bytes 86024 | tf_op jit(solution)/shard_map/ppermute | solution.py:553
  161.5 1.3 collective-permute-done.17
  162.7 0.9 collective-permute-done.18
  163.8 0.2 multiply_reduce_fusion
  163.9 0.8 convert_element_type.31
  164.7 1.5 place.1
  (55 shorter events, 0.6 us)
Async XLA Ops:
  0.6 7.1 %copy-start.13 = (bf16[8,2,8192]{2,1,0:T(2,128)(2,1)S(1)}, bf16[8,2,8192]{2,1,0:T(2,128)(2,1)}, u32[]{:S(2)}) copy-start(bf16[8,2,8192]{2,1,0:T(2,128)(2,1)} %param.16) | copy-start | bytes 786436
  0.6 7.3 %copy-start.15 = (bf16[8,2,512]{2,1,0:T(2,128)(2,1)S(1)}, bf16[8,2,512]{2,1,0:T(2,128)(2,1)}, u32[]{:S(2)}) copy-start(bf16[8,2,512]{2,1,0:T(2,128)(2,1)} %param.17) | copy-start | bytes 49156
  0.7 7.3 %copy-start.16 = (bf16[8,2,64]{2,1,0:T(2,128)(2,1)S(1)}, bf16[8,2,64]{2,1,0:T(2,128)(2,1)}, u32[]{:S(2)}) copy-start(bf16[8,2,64]{2,1,0:T(2,128)(2,1)} %param.18) | copy-start | bytes 6148
  0.7 7.3 %copy-start.5 = (s32[8]{0:T(128)S(1)}, s32[8]{0:T(128)}, u32[]{:S(2)}) copy-start(s32[8]{0:T(128)} %slot_ref.13) | copy-start | bytes 100
  3.0 29.4 %collective-permute-start = (bf16[1152,512]{1,0:T(8,128)(2,1)}, bf16[1152,512]{1,0:T(8,128)(2,1)}, u32[]{:S(2)}, u32[]{:S(2)}) collective-permute-start(bf16[1152,512]{1,0:T(8,128)(2,1)} %pack_cache.1.refs_0_), channel_id=1, source_target_pairs={{0,4},{4,0},{8,12},{12,8},{2,6},{6,2},{10,14},{14,10},{1,5},{5,1},... | collective-permute-start | bytes 3538952 | tf_op jit(solution)/shard_map/ppermute | solution.py:36
  6.1 26.3 %collective-permute-start.1 = (bf16[1152,512]{1,0:T(8,128)(2,1)}, bf16[1152,512]{1,0:T(8,128)(2,1)}, u32[]{:S(2)}, u32[]{:S(2)}) collective-permute-start(bf16[1152,512]{1,0:T(8,128)(2,1)} %pack_cache.1.refs_0_), channel_id=1, source_target_pairs={{4,8},{8,4},{6,10},{10,6},{5,9},{9,5},{7,11},{11,7},{20,24},{24,20... | collective-permute-start | bytes 3538952 | tf_op jit(solution)/shard_map/ppermute | solution.py:36
  8.0 1.6 copy-start
  9.6 3.8 %copy-start.14 = (bf16[8,2,7168]{2,1,0:T(2,128)(2,1)S(1)}, bf16[8,2,7168]{2,1,0:T(2,128)(2,1)}, u32[]{:S(2)}) copy-start(bf16[8,2,7168]{2,1,0:T(2,128)(2,1)} %param.20) | copy-start | bytes 688132
  9.6 3.9 %copy-start.6 = (s32[8,2,8]{2,1,0:T(2,128)S(1)}, s32[8,2,8]{2,1,0:T(2,128)}, u32[]{:S(2)}) copy-start(s32[8,2,8]{2,1,0:T(2,128)} %param.21) | copy-start | bytes 1540
  9.6 3.9 %copy-start.7 = (f32[8,2,8]{2,1,0:T(2,128)S(1)}, f32[8,2,8]{2,1,0:T(2,128)}, u32[]{:S(2)}) copy-start(f32[8,2,8]{2,1,0:T(2,128)} %param.22) | copy-start | bytes 1540
  11.8 76.2 %collective-permute-start.4 = (bf16[4,320,512]{2,1,0:T(8,128)(2,1)}, bf16[4,320,512]{2,1,0:T(8,128)(2,1)S(1)}, u32[]{:S(2)}, u32[]{:S(2)}) collective-permute-start(bf16[4,320,512]{2,1,0:T(8,128)(2,1)} %pack_tokens.2), channel_id=1, source_target_pairs={{0,2},{2,0},{4,6},{6,4},{8,10},{10,8},{12,14},{14,12},{1,3},{3,1},... | collective-permute-start | bytes 3932168 | tf_op jit(solution)/shard_map/ppermute | solution.py:28
  13.4 74.7 %collective-permute-start.6 = (bf16[1152,512]{1,0:T(8,128)(2,1)}, bf16[1152,512]{1,0:T(8,128)(2,1)}, u32[]{:S(2)}, u32[]{:S(2)}) collective-permute-start(bf16[1152,512]{1,0:T(8,128)(2,1)} %pack_cache.1.refs_0_), channel_id=1, source_target_pairs={{0,1},{1,0},{2,3},{3,2},{4,5},{5,4},{6,7},{7,6},{8,9},{9,8},{10,11... | collective-permute-start | bytes 3538952 | tf_op jit(solution)/shard_map/ppermute | solution.py:28
  32.3 72.9 %collective-permute-start.5 = (bf16[1152,512]{1,0:T(8,128)(2,1)}, bf16[1152,512]{1,0:T(8,128)(2,1)}, u32[]{:S(2)}, u32[]{:S(2)}) collective-permute-start(bf16[1152,512]{1,0:T(8,128)(2,1)} %collective-permute-done.refs_0_), channel_id=1, source_target_pairs={{0,1},{1,0},{2,3},{3,2},{4,5},{5,4},{6,7},{7,6},{8,9},{9,8},{10,11... | collective-permute-start | bytes 3538952 | tf_op jit(solution)/shard_map/ppermute | solution.py:28
  32.3 79.8 %collective-permute-start.2 = (bf16[1152,512]{1,0:T(8,128)(2,1)}, bf16[1152,512]{1,0:T(8,128)(2,1)}, u32[]{:S(2)}, u32[]{:S(2)}) collective-permute-start(bf16[1152,512]{1,0:T(8,128)(2,1)} %collective-permute-done.refs_0_), channel_id=1, source_target_pairs={{4,8},{8,4},{6,10},{10,6},{5,9},{9,5},{7,11},{11,7},{20,24},{24,20... | collective-permute-start | bytes 3538952 | tf_op jit(solution)/shard_map/ppermute | solution.py:36
  34.0 78.1 %collective-permute-start.3 = (bf16[1152,512]{1,0:T(8,128)(2,1)}, bf16[1152,512]{1,0:T(8,128)(2,1)}, u32[]{:S(2)}, u32[]{:S(2)}) collective-permute-start(bf16[1152,512]{1,0:T(8,128)(2,1)} %collective-permute-done.1), channel_id=1, source_target_pairs={{4,0},{8,12},{6,2},{10,14},{5,1},{9,13},{7,3},{11,15},{20,16},{24,... | collective-permute-start | bytes 3538952 | tf_op jit(solution)/shard_map/ppermute | solution.py:36
  85.2 1.6 copy-start.1
  88.0 7.7 %copy-start.11 = (bf16[16,4,7168]{2,1,0:T(4,128)(2,1)S(1)}, bf16[16,4,7168]{2,1,0:T(4,128)(2,1)}, u32[]{:S(2)}) copy-start(bf16[16,4,7168]{2,1,0:T(4,128)(2,1)} %all-gather.1) | copy-start | bytes 2752516
  95.0 0.7 copy-start.8
  96.7 1.5 copy-start.2
  98.2 1.5 copy-start.3
  99.7 1.5 copy-start.4
  103.4 1.8 %collective-permute-start.7 = (bf16[16,7168]{1,0:T(8,128)(2,1)}, bf16[16,7168]{1,0:T(8,128)(2,1)S(1)}, u32[]{:S(2)}, u32[]{:S(2)}) collective-permute-start(bf16[16,7168]{1,0:T(8,128)(2,1)} %get-tuple-element.58), channel_id=1, source_target_pairs={{0,1},{1,0},{2,3},{3,2},{4,5},{5,4},{6,7},{7,6},{8,9},{9,8},{10,11... | collective-permute-start | bytes 688136 | tf_op jit(solution)/shard_map/ppermute | solution.py:28
  112.1 1.9 %copy-start.9 = (bf16[256,512]{1,0:T(8,128)(2,1)S(1)}, bf16[256,512]{1,0:T(8,128)(2,1)}, u32[]{:S(2)}) copy-start(bf16[256,512]{1,0:T(8,128)(2,1)} %copy-done.8) | copy-start | bytes 786436
  113.6 3.9 %collective-permute-start.11 = (bf16[1152,512]{1,0:T(8,128)(2,1)S(1)}, bf16[1152,512]{1,0:T(8,128)(2,1)S(1)}, u32[]{:S(2)}, u32[]{:S(2)}) collective-permute-start(bf16[1152,512]{1,0:T(8,128)(2,1)S(1)} %broadcast_select_fusion.1.refs_0_), channel_id=1, source_target_pairs={{0,1},{1,0},{2,3},{3,2},{4,5},{5,4},{6,7},{7,6},{8,9},{9,8},{10,11... | collective-permute-start | bytes 3538952 | tf_op jit(solution)/shard_map/ppermute | solution.py:28
  114.0 11.4 %collective-permute-start.13 = (bf16[8,7168]{1,0:T(8,128)(2,1)S(1)}, bf16[8,7168]{1,0:T(8,128)(2,1)S(1)}, u32[]{:S(2)}, u32[]{:S(2)}) collective-permute-start(bf16[8,7168]{1,0:T(8,128)(2,1)S(1)} %get-tuple-element.67), channel_id=1, source_target_pairs={{0,2},{2,0},{4,6},{6,4},{8,10},{10,8},{12,14},{14,12},{1,3},{3,1},... | collective-permute-start | bytes 344072 | tf_op jit(solution)/shard_map/ppermute | solution.py:28
  114.0 11.6 %collective-permute-start.9 = (bf16[256,512]{1,0:T(8,128)(2,1)S(1)}, bf16[256,512]{1,0:T(8,128)(2,1)S(1)}, u32[]{:S(2)}, u32[]{:S(2)}) collective-permute-start(bf16[256,512]{1,0:T(8,128)(2,1)S(1)} %copy-done.9), channel_id=1, source_target_pairs={{0,2},{2,0},{4,6},{6,4},{8,10},{10,8},{12,14},{14,12},{1,3},{3,1},... | collective-permute-start | bytes 786440 | tf_op jit(solution)/shard_map/ppermute | solution.py:28
  116.0 15.2 %collective-permute-start.10 = (bf16[256,512]{1,0:T(8,128)(2,1)S(1)}, bf16[256,512]{1,0:T(8,128)(2,1)S(1)}, u32[]{:S(2)}, u32[]{:S(2)}) collective-permute-start(bf16[256,512]{1,0:T(8,128)(2,1)S(1)} %get-tuple-element.52), channel_id=1, source_target_pairs={{0,2},{2,0},{4,6},{6,4},{8,10},{10,8},{12,14},{14,12},{1,3},{3,1},... | collective-permute-start | bytes 786440 | tf_op jit(solution)/shard_map/ppermute | solution.py:28
  116.1 29.6 %collective-permute-start.8 = (bf16[1152,512]{1,0:T(8,128)(2,1)}, bf16[1152,512]{1,0:T(8,128)(2,1)S(1)}, u32[]{:S(2)}, u32[]{:S(2)}) collective-permute-start(bf16[1152,512]{1,0:T(8,128)(2,1)} %collective-permute-done.2), channel_id=1, source_target_pairs={{4,0},{8,12},{6,2},{10,14},{5,1},{9,13},{7,3},{11,15},{20,16},{24,... | collective-permute-start | bytes 3538952 | tf_op jit(solution)/shard_map/ppermute | solution.py:36
  123.4 22.3 %collective-permute-start.12 = (bf16[256,512]{1,0:T(8,128)(2,1)S(1)}, bf16[256,512]{1,0:T(8,128)(2,1)S(1)}, u32[]{:S(2)}, u32[]{:S(2)}) collective-permute-start(bf16[256,512]{1,0:T(8,128)(2,1)S(1)} %get-tuple-element.65), channel_id=1, source_target_pairs={{0,2},{2,0},{4,6},{6,4},{8,10},{10,8},{12,14},{14,12},{1,3},{3,1},... | collective-permute-start | bytes 786440 | tf_op jit(solution)/shard_map/ppermute | solution.py:28
  125.4 20.2 %copy-start.12 = (f32[8,7168]{1,0:T(8,128)}, f32[8,7168]{1,0:T(8,128)S(1)}, u32[]{:S(2)}) copy-start(f32[8,7168]{1,0:T(8,128)S(1)} %convert_add_fusion) | copy-start | bytes 688132
  145.8 2.9 %collective-permute-start.14 = (bf16[1152,512]{1,0:T(8,128)(2,1)S(1)}, bf16[1152,512]{1,0:T(8,128)(2,1)S(1)}, u32[]{:S(2)}, u32[]{:S(2)}) collective-permute-start(bf16[1152,512]{1,0:T(8,128)(2,1)S(1)} %broadcast_select_fusion.refs_0_), channel_id=1, source_target_pairs={{0,1},{1,0},{2,3},{3,2},{4,5},{5,4},{6,7},{7,6},{8,9},{9,8},{10,11... | collective-permute-start | bytes 3538952 | tf_op jit(solution)/shard_map/ppermute | solution.py:28
  148.8 12.7 %slice-start = ((f32[8,7168]{1,0:T(8,128)}), f32[2,7168]{1,0:T(2,128)S(1)}, s32[]{:S(2)}) async-start(f32[8,7168]{1,0:T(8,128)} %copy-done.12), calls=%async_computation | async-start | bytes 114688 | tf_op jit(solution)/shard_map/slice | solution.py:590
  154.6 0.7 copy-start.10
  155.3 6.2 %collective-permute-start.16 = (bf16[2,7168]{1,0:T(2,128)(2,1)}, bf16[2,7168]{1,0:T(2,128)(2,1)S(1)}, u32[]{:S(2)}, u32[]{:S(2)}) collective-permute-start(bf16[2,7168]{1,0:T(2,128)(2,1)} %get-tuple-element.81), channel_id=1, source_target_pairs={{0,4},{2,6},{4,0},{6,2},{8,12},{10,14},{12,8},{14,10},{1,5},{3,7},... | collective-permute-start | bytes 86024 | tf_op jit(solution)/shard_map/ppermute | solution.py:553
  156.3 8.5 %collective-permute-start.15 = (bf16[256,512]{1,0:T(8,128)(2,1)}, bf16[256,512]{1,0:T(8,128)(2,1)S(1)}, u32[]{:S(2)}, u32[]{:S(2)}) collective-permute-start(bf16[256,512]{1,0:T(8,128)(2,1)} %copy-done.10), channel_id=1, source_target_pairs={{0,2},{2,0},{4,6},{6,4},{8,10},{10,8},{12,14},{14,12},{1,3},{3,1},... | collective-permute-start | bytes 786440 | tf_op jit(solution)/shard_map/ppermute | solution.py:28
  158.0 4.8 %collective-permute-start.17 = (bf16[2,7168]{1,0:T(2,128)(2,1)S(1)}, bf16[2,7168]{1,0:T(2,128)(2,1)S(1)}, u32[]{:S(2)}, u32[]{:S(2)}) collective-permute-start(bf16[2,7168]{1,0:T(2,128)(2,1)S(1)} %get-tuple-element.83), channel_id=1, source_target_pairs={{0,8},{2,10},{4,12},{6,14},{8,0},{10,2},{12,4},{14,6},{1,9},{3,11}... | collective-permute-start | bytes 86024 | tf_op jit(solution)/shard_map/ppermute | solution.py:553
  158.0 5.7 %collective-permute-start.18 = (bf16[2,7168]{1,0:T(2,128)(2,1)S(1)}, bf16[2,7168]{1,0:T(2,128)(2,1)S(1)}, u32[]{:S(2)}, u32[]{:S(2)}) collective-permute-start(bf16[2,7168]{1,0:T(2,128)(2,1)S(1)} %get-tuple-element.85), channel_id=1, source_target_pairs={{0,12},{2,14},{4,8},{6,10},{8,4},{10,6},{12,0},{14,2},{1,13},{3,15... | collective-permute-start | bytes 86024 | tf_op jit(solution)/shard_map/ppermute | solution.py:553

commit v8 on v7

--- a/solution.py
+++ b/solution.py
@@ -321,7 +321,7 @@
     )(*scalars, *sources, placed)
 
 
-def dispatch_kernel(experts, block_ref, routes_ref, gate_ref, tokens_ref, out_ref, share_ref):
+def dispatch_kernel(experts, block_ref, routes_ref, gate_ref, tokens_ref, *out_refs):
     block = block_ref[0]
     routes = routes_ref[...]
     gates = gate_ref[...]
@@ -334,22 +334,25 @@
     slot_column = lax.broadcasted_iota(jnp.int32, (rows, slots), 1)
     placing = jnp.zeros((slots, rows), jnp.float32)
     share = jnp.zeros((rows, slots), jnp.float32)
-    for expert in range(experts):
+    for k in range(experts):
+        expert = lax.rem(block + k, experts)
         hit = routes == expert
         has = jnp.sum(hit.astype(jnp.float32), axis=1, keepdims=True)
         weight = jnp.sum(jnp.where(hit, gates, 0.0), axis=1, keepdims=True)
         has_row = jnp.sum(has * same, axis=0, keepdims=True)
         before_row = jnp.sum(jnp.where(down < across, has, 0.0), axis=0, keepdims=True)
         before = jnp.sum(jnp.where(across < down, has_row, 0.0), axis=1, keepdims=True)
-        away = lax.rem(expert + experts - block, experts)
         for c in range(CAP):
-            slot = expert * CAP + c
+            slot = k * CAP + c
             placing += jnp.where((slot_row == slot) & (before_row == c), has_row, 0.0)
-            share += jnp.where((slot_column == away * CAP + c) & (before == c), weight, 0.0)
-    out_ref[...] = jnp.dot(
-        placing.astype(jnp.bfloat16), tokens_ref[...], preferred_element_type=jnp.float32
-    ).astype(jnp.bfloat16)
-    share_ref[...] = share
+            share += jnp.where((slot_column == slot) & (before == c), weight, 0.0)
+    for k in range(experts):
+        out_refs[k][...] = jnp.dot(
+            placing[k * CAP : (k + 1) * CAP].astype(jnp.bfloat16),
+            tokens_ref[...],
+            preferred_element_type=jnp.float32,
+        ).astype(jnp.bfloat16)
+    out_refs[experts][...] = share
 
 
 def dispatch(block, routes, gates, tokens, experts):
@@ -357,57 +360,54 @@
     return pl.pallas_call(
         functools.partial(dispatch_kernel, experts),
         out_shape=(
-            jax.ShapeDtypeStruct((slots, tokens.shape[1]), tokens.dtype),
+            *(jax.ShapeDtypeStruct((CAP, tokens.shape[1]), tokens.dtype) for _ in range(experts)),
             jax.ShapeDtypeStruct((tokens.shape[0], slots), jnp.float32),
         ),
         in_specs=[pl.BlockSpec(memory_space=pltpu.SMEM)]
         + [pl.BlockSpec(memory_space=pltpu.VMEM)] * 3,
-        out_specs=(pl.BlockSpec(memory_space=pltpu.VMEM),) * 2,
+        out_specs=(pl.BlockSpec(memory_space=pltpu.VMEM),) * (experts + 1),
         cost_estimate=SMALL,
         compiler_params=pltpu.CompilerParams(vmem_limit_bytes=8 * 1024 * 1024),
         name="dispatch",
     )(block, routes, gates, tokens)
 
 
-def order_kernel(experts, device_ref, rows_ref, mine_ref, theirs_ref):
-    device = device_ref[0]
-    total = rows_ref.shape[0]
-    count = mine_ref.shape[0]
-    cores = total // count
-    lines = SHARDS // (2 * cores)
-    ways = experts * lines
-    block = lax.div(device, SHARDS)
-    within = lax.rem(device, SHARDS)
-    shape = (count, total)
-    row = lax.broadcasted_iota(jnp.int32, shape, 0)
-    column = lax.broadcasted_iota(jnp.int32, shape, 1)
-    slot = row % CAP
-    way = (row // CAP) % ways
-    beside = row // (CAP * ways)
-    from_block = (block + experts - way // lines) % experts
-    flip = (way % lines) * (2 * cores) + beside * cores
-    for core, out_ref in enumerate((mine_ref, theirs_ref)):
-        source = from_block * SHARDS + jnp.bitwise_xor(within, flip + core)
-        chosen = (column == source * CAP + slot).astype(jnp.bfloat16)
-        out_ref[...] = jnp.dot(
-            chosen, rows_ref[...], preferred_element_type=jnp.float32
-        ).astype(jnp.bfloat16)
-
-
-def order_rows(device, rows, experts, cores):
-    shape = jax.ShapeDtypeStruct((rows.shape[0] // cores, rows.shape[1]), rows.dtype)
+def moved_rows(pieces, places, rows):
+    total = None
+    for piece, places_of_piece in zip(pieces, places):
+        shape = (rows, piece.shape[0])
+        row = lax.broadcasted_iota(jnp.int32, shape, 0)
+        column = lax.broadcasted_iota(jnp.int32, shape, 1)
+        chosen = jnp.zeros(shape, jnp.float32)
+        for source, there in places_of_piece:
+            chosen += ((row == there) & (column == source)).astype(jnp.float32)
+        part = jnp.dot(
+            chosen.astype(jnp.bfloat16), piece[...], preferred_element_type=jnp.float32
+        )
+        total = part if total is None else total + part
+    return total.astype(jnp.bfloat16)
+
+
+def stack_kernel(*refs):
+    arrays, out_ref = refs[:-1], refs[-1]
+    places, start = [], 0
+    for array in arrays:
+        places.append([(r, start + r) for r in range(array.shape[0])])
+        start += array.shape[0]
+    out_ref[...] = moved_rows(arrays, places, start)
+
+
+def stack_rows(*arrays):
+    rows = sum(array.shape[0] for array in arrays)
     return pl.pallas_call(
-        functools.partial(order_kernel, experts),
-        out_shape=(shape, shape),
-        in_specs=[
-            pl.BlockSpec(memory_space=pltpu.SMEM),
-            pl.BlockSpec(memory_space=pltpu.VMEM),
-        ],
-        out_specs=(pl.BlockSpec(memory_space=pltpu.VMEM),) * 2,
+        stack_kernel,
+        out_shape=jax.ShapeDtypeStruct((rows, arrays[0].shape[1]), arrays[0].dtype),
+        in_specs=[pl.BlockSpec(memory_space=pltpu.VMEM)] * len(arrays),
+        out_specs=pl.BlockSpec(memory_space=pltpu.VMEM),
         cost_estimate=SMALL,
-        compiler_params=pltpu.CompilerParams(vmem_limit_bytes=16 * 1024 * 1024),
-        name="order_rows",
-    )(device, rows)
+        compiler_params=pltpu.CompilerParams(vmem_limit_bytes=8 * 1024 * 1024),
+        name="stack_rows",
+    )(*arrays)
 
 
 def experts_kernel(mine_ref, theirs_ref, gate_hbm, up_hbm, down_hbm, keep_ref, send_ref, *scratch):
@@ -533,7 +533,7 @@
     cores = lax.axis_size("expert")
     shard_branches = SHARDS // cores
     block = device // SHARDS
-    outgoing, share = dispatch(
+    *outgoing, share = dispatch(
         after(block[None], leave),
         routes.reshape(tok_total, -1),
         route_gate.reshape(tok_total, -1),
@@ -552,40 +552,39 @@
         ]
         return lax.ppermute(x, "branch", list(enumerate(there)))
 
-    gathered = lax.all_gather(outgoing, ("branch", "expert"), axis=0, tiled=False)
-    cache_a, first_b, outgoing = lax.optimization_barrier((cache_a, first_b, outgoing))
+    ways = [(k, m) for m in range(around) for k in range(experts)]
+    pieces = outgoing[:1] + [along(outgoing[k], k, 0) for k in range(1, experts)]
+    cache_a, first_b, *pieces = lax.optimization_barrier((cache_a, first_b, *pieces))
     second_b = line_hop(first_b, tok_rows, outward)
     first_c = line_hop(cache_a, tok_rows, inner)
-    ways = [(k, m) for k in range(experts) for m in range(around)]
 
     def both_halves(cache):
         return cache, swapped(cache, "expert", 0)
 
     guest = after(guest, cache_a, first_b)
+    rows = stack_rows(*pieces)
+    rows = stack_rows(rows, *(along(rows, 0, m) for m in range(1, around)))
     given_0, placed = attend(scalars, 0, guest, stay, both_halves(own_cache), None)
     back_0 = swapped(given_0, "branch", 0)
-    gathered = after(gathered, given_0)
-    picked = lax.dynamic_slice_in_dim(gathered, block * CAP, CAP, axis=1)
-    mine, theirs = order_rows(
-        device[None], picked.reshape(-1, model_width), experts, cores
-    )
-    kept, sent = run_experts(mine, theirs, w_gate, w_up, w_down)
-    kept, sent = halve(kept, swapped(sent, "expert", 0))
     given_1, placed = attend(scalars, 1, guest, stay, both_halves(cache_a), placed)
     back_1 = swapped(given_1, "branch", 0)
-
-    second_b, given_1, kept, sent = lax.optimization_barrier((second_b, given_1, kept, sent))
+    rows = after(rows, given_0)
+    rows = stack_rows(rows, swapped(rows, "branch", 0))
+
+    second_b, given_1, rows = lax.optimization_barrier((second_b, given_1, rows))
     first_c, second_b = lax.optimization_barrier((first_c, second_b))
     second_c = line_hop(first_c, tok_rows, outward)
     cache_b = jnp.where(middle, first_b, second_b)
     given_2, placed = attend(scalars, 2, guest, stay, both_halves(cache_b), placed)
     back_2 = swapped(given_2, "branch", 0)
+    theirs = swapped(rows, "expert", 0)
+    rows, theirs, back_0, back_1 = lax.optimization_barrier((rows, theirs, back_0, back_1))
+    kept, sent = run_experts(rows, theirs, w_gate, w_up, w_down)
+    kept, sent = halve(kept, swapped(sent, "expert", 0))
+
+    second_c, back_2, kept, sent = lax.optimization_barrier((second_c, back_2, kept, sent))
+    cache_c = both_halves(jnp.where(middle, first_c, second_c))
     parts = kept + swapped(sent, "branch", 0).astype(jnp.float32)
-
-    second_c, back_0, back_1, back_2, parts = lax.optimization_barrier(
-        (second_c, back_0, back_1, back_2, parts)
-    )
-    cache_c = both_halves(jnp.where(middle, first_c, second_c))
     homeward = [
         parts[w * CAP : (w + 1) * CAP].astype(jnp.float32 if way == (0, 0) else jnp.bfloat16)
         for w, way in enumerate(ways)

time: 167 us -> 129 us (0.77)
  blocking collectives: 49.9 us -> 0 us
  waiting for transfers between devices: 44.5 us -> 57 us
  local copies, waits for them, and re-layouts: 11.5 us -> 5.72 us
  starting transfers between devices: 21.9 us -> 27 us
    all_gather x1 -> x0, blocking collectives: 49.9 us -> none  [on_device(): lax.all_gather(outgoing, ('branch', 'expert'), axis=0, tiled=False)]
    ppermute x3 -> x5, waiting for transfers between devices: 2.18 us -> 27.9 us  [along(): return lax.ppermute(x, 'branch', list(enumerate(there)))]
    ppermute x5, waiting for transfers between devices: 33 us -> 15.6 us  [line_hop(): return lax.ppermute(x, 'branch', pairs)]
    unnamed x34 -> x26, local copies, waits for them, and re-layouts: 9.09 us -> 3.91 us
    ppermute x11 -> x13, waiting for transfers between devices: 9.29 us -> 13.5 us  [swapped(): lax.ppermute(x, axis, [(i, i ^ 1 << bit) for i in range(lax.axis_size(axi...]
    ppermute x3 -> x5, starting transfers between devices: 4.38 us -> 7.73 us  [along(): return lax.ppermute(x, 'branch', list(enumerate(there)))]
    ppermute x11 -> x13, starting transfers between devices: 8.28 us -> 10.1 us  [swapped(): lax.ppermute(x, axis, [(i, i ^ 1 << bit) for i in range(lax.axis_size(axi...]
  transfers between devices with their start and end apart: 19 -> 23, of which waited for: 8 -> 10; matrix products, arithmetic and copies ran while one was open for 2% -> 2% of each run, Pallas kernels for 16% -> 20%
where the time goes in v8:
time: 129 us
  waiting for transfers between devices  57 us (44%)
  Pallas kernels  35.9 us (28%)
  starting transfers between devices  27 us (21%)
  local copies, waits for them, and re-layouts  5.72 us (4%)
  other arithmetic  1.88 us (1%)
    ppermute x5, waiting for transfers between devices, along(): return lax.ppermute(x, 'branch', list(enumerate(there)))  27.9 us
    pallas_call x4, Pallas kernels, call(): pl.pallas_call(functools.partial(kernel, slot, placed is not None), out_s...  26 us
    ppermute x5, waiting for transfers between devices, line_hop(): return lax.ppermute(x, 'branch', pairs)  15.6 us
    ppermute x13, waiting for transfers between devices, swapped(): lax.ppermute(x, axis, [(i, i ^ 1 << bit) for i in range(lax.axis_size(axi...  13.5 us
    ppermute x13, starting transfers between devices, swapped(): lax.ppermute(x, axis, [(i, i ^ 1 << bit) for i in range(lax.axis_size(axi...  10.1 us
    ppermute x5, starting transfers between devices, line_hop(): return lax.ppermute(x, 'branch', pairs)  9.18 us
    ppermute x5, starting transfers between devices, along(): return lax.ppermute(x, 'branch', list(enumerate(there)))  7.73 us
    unnamed x26, local copies, waits for them, and re-layouts  3.91 us
  transfers between devices with their start and end apart: 23, of which 10 were waited for; matrix products, arithmetic and copies ran while one was open for 2% of the time, Pallas kernels for 20%

profile of v8, /device:TPU:0, one launch (start us, length us, event | category | flops | bytes accessed | tf_op | source)
XLA Modules:
  0.0 128.7 jit_solution(5908116243093990310)
XLA Ops:
  0.7 2.3 %pack_cache.1.refs_0_ = bf16[1152,512]{1,0:T(8,128)(2,1)} custom-call(bf16[1024,512]{1,0:T(8,128)(2,1)} %bitcast.13, bf16[128,512]{1,0:T(8,128)(2,1)} %bitcast.14), custom_call_target="tpu_custom_call" | custom-call | bytes 1024 | tf_op jit(solution)/shard_map/pack_cache/pallas_call | solution.py:52
  3.0 3.1 %collective-permute-start = (bf16[1152,512]{1,0:T(8,128)(2,1)}, bf16[1152,512]{1,0:T(8,128)(2,1)}, u32[]{:S(2)}, u32[]{:S(2)}) collective-permute-start(bf16[1152,512]{1,0:T(8,128)(2,1)} %pack_cache.1.refs_0_), channel_id=1, source_target_pairs={{0,4},{4,0},{8,12},{12,8},{2,6},{6,2},{10,14},{14,10},{1,5},{5,1},... | collective-permute-start | bytes 3538952 | tf_op jit(solution)/shard_map/ppermute | solution.py:36
  6.1 1.7 %collective-permute-start.1 = (bf16[1152,512]{1,0:T(8,128)(2,1)}, bf16[1152,512]{1,0:T(8,128)(2,1)}, u32[]{:S(2)}, u32[]{:S(2)}) collective-permute-start(bf16[1152,512]{1,0:T(8,128)(2,1)} %pack_cache.1.refs_0_), channel_id=1, source_target_pairs={{4,8},{8,4},{6,10},{10,6},{5,9},{9,5},{7,11},{11,7},{20,24},{24,20... | collective-permute-start | bytes 3538952 | tf_op jit(solution)/shard_map/ppermute | solution.py:36
  7.8 0.2 reshape.28.rope_ref
  8.0 1.6 %copy-done = bf16[8,2,128,512]{3,2,1,0:T(8,128)(2,1)S(1)} copy-done((bf16[8,2,128,512]{3,2,1,0:T(8,128)(2,1)S(1)}, bf16[8,2,128,512]{3,2,1,0:T(8,128)(2,1)}, u32[]{:S(2)}) %copy-start) | copy-done | bytes 2097176
  9.6 2.2 %pack_tokens.2 = bf16[4,320,512]{2,1,0:T(8,128)(2,1)} custom-call(s32[8]{0:T(128)S(1)} %copy-done.5, s32[1]{0:T(128)} %bitcast.own_ref, bf16[8,256,512]{2,1,0:T(8,128)(2,1)S(1)} %bitcast.8, bf16[8,32,512]{2,1,0:T(8,128)(2,1)S(1)} %reshape.28.rope_ref, bf16[8,32,512]{2,1,0:T(8,128)(2,1)S(1)} %fusion.2.new_ref), custom_call_target="tpu_custom_call" | custom-call | bytes 1024 | tf_op jit(solution)/shard_map/pack_tokens/pallas_call | solution.py:106
  11.8 1.6 %collective-permute-start.4 = (bf16[4,320,512]{2,1,0:T(8,128)(2,1)}, bf16[4,320,512]{2,1,0:T(8,128)(2,1)S(1)}, u32[]{:S(2)}, u32[]{:S(2)}) collective-permute-start(bf16[4,320,512]{2,1,0:T(8,128)(2,1)} %pack_tokens.2), channel_id=1, source_target_pairs={{0,2},{2,0},{4,6},{6,4},{8,10},{10,8},{12,14},{14,12},{1,3},{3,1},... | collective-permute-start | bytes 3932168 | tf_op jit(solution)/shard_map/ppermute | solution.py:28
  13.5 0.3 dispatch.1
  13.9 2.9 %collective-permute-start.2 = (bf16[2,7168]{1,0:T(2,128)(2,1)S(1)}, bf16[2,7168]{1,0:T(2,128)(2,1)S(1)}, u32[]{:S(2)}, u32[]{:S(2)}) collective-permute-start(bf16[2,7168]{1,0:T(2,128)(2,1)S(1)} %get-tuple-element.50), channel_id=1, source_target_pairs={{0,8},{2,10},{4,12},{6,14},{8,0},{10,2},{12,4},{14,6},{1,9},{3,11}... | collective-permute-start | bytes 86024 | tf_op jit(solution)/shard_map/ppermute | solution.py:553
  16.8 20.9 %collective-permute-done.2.refs_1_ = bf16[2,7168]{1,0:T(2,128)(2,1)S(1)} collective-permute-done((bf16[2,7168]{1,0:T(2,128)(2,1)S(1)}, bf16[2,7168]{1,0:T(2,128)(2,1)S(1)}, u32[]{:S(2)}, u32[]{:S(2)}) %collective-permute-start.2) | collective-permute-done | bytes 28704 | tf_op jit(solution)/shard_map/ppermute | solution.py:553
  37.7 0.3 stack_rows.3.refs_0_
  38.0 0.4 collective-permute-start.7
  38.4 1.3 collective-permute-start.3
  39.7 2.5 %collective-permute-done.7.refs_1_ = bf16[4,7168]{1,0:T(4,128)(2,1)S(1)} collective-permute-done((bf16[4,7168]{1,0:T(4,128)(2,1)S(1)}, bf16[4,7168]{1,0:T(4,128)(2,1)S(1)}, u32[]{:S(2)}, u32[]{:S(2)}) %collective-permute-start.7) | collective-permute-done | bytes 57376 | tf_op jit(solution)/shard_map/ppermute | solution.py:553
  42.2 1.7 %collective-permute-start.12 = (bf16[1152,512]{1,0:T(8,128)(2,1)}, bf16[1152,512]{1,0:T(8,128)(2,1)}, u32[]{:S(2)}, u32[]{:S(2)}) collective-permute-start(bf16[1152,512]{1,0:T(8,128)(2,1)} %collective-permute-done.refs_0_), channel_id=1, source_target_pairs={{4,8},{8,4},{6,10},{10,6},{5,9},{9,5},{7,11},{11,7},{20,24},{24,20... | collective-permute-start | bytes 3538952 | tf_op jit(solution)/shard_map/ppermute | solution.py:36
  43.9 1.6 %copy-done.1 = bf16[8,2,128,512]{3,2,1,0:T(8,128)(2,1)S(1)} copy-done((bf16[8,2,128,512]{3,2,1,0:T(8,128)(2,1)S(1)}, bf16[8,2,128,512]{3,2,1,0:T(8,128)(2,1)}, u32[]{:S(2)}) %copy-start.1) | copy-done | bytes 2097176
  45.5 1.1 pack_tokens.3.stay
  46.6 0.3 stack_rows.4.refs_0_
  46.9 7.6 %attend.4 = (bf16[256,512]{1,0:T(8,128)(2,1)}, bf16[8,256,512]{2,1,0:T(8,128)(2,1)}) custom-call(s32[8]{0:T(128)S(1)} %copy-done.5, s32[1]{0:T(128)} %bitcast.own_ref, bf16[4,320,512]{2,1,0:T(8,128)(2,1)S(1)} %collective-permute-done.4.guest, bf16[4,320,512]{2,1,0:T(8,128)(2,1)S(1)} %pack_tokens.3.stay, bf16[1152,512]{1,0:T(8,128)(2,1)} %pack_cache.1.refs_0_, ...), custom_call_target="tpu_custom_call" | custom-call | bytes 1024 | tf_op jit(solution)/shard_map/attend/pallas_call | solution.py:270
  54.5 1.6 %collective-permute-start.8 = (bf16[8,7168]{1,0:T(8,128)(2,1)S(1)}, bf16[8,7168]{1,0:T(8,128)(2,1)S(1)}, u32[]{:S(2)}, u32[]{:S(2)}) collective-permute-start(bf16[8,7168]{1,0:T(8,128)(2,1)S(1)} %stack_rows.4.refs_0_), channel_id=1, source_target_pairs={{0,2},{2,0},{4,6},{6,4},{8,10},{10,8},{12,14},{14,12},{1,3},{3,1},... | collective-permute-start | bytes 344072 | tf_op jit(solution)/shard_map/ppermute | solution.py:28
  56.1 3.3 %collective-permute-done.8.refs_1_ = bf16[8,7168]{1,0:T(8,128)(2,1)S(1)} collective-permute-done((bf16[8,7168]{1,0:T(8,128)(2,1)S(1)}, bf16[8,7168]{1,0:T(8,128)(2,1)S(1)}, u32[]{:S(2)}, u32[]{:S(2)}) %collective-permute-start.8) | collective-permute-done | bytes 114720 | tf_op jit(solution)/shard_map/ppermute | solution.py:28
  59.3 0.3 stack_rows.5.mine_ref
  59.6 6.9 %attend.5 = (bf16[256,512]{1,0:T(8,128)(2,1)S(1)}, bf16[8,256,512]{2,1,0:T(8,128)(2,1)}) custom-call(s32[8]{0:T(128)S(1)} %copy-done.5, s32[1]{0:T(128)} %bitcast.own_ref, bf16[4,320,512]{2,1,0:T(8,128)(2,1)S(1)} %collective-permute-done.4.guest, bf16[4,320,512]{2,1,0:T(8,128)(2,1)S(1)} %pack_tokens.3.stay, ...), custom_call_target="tpu_custom_call", output_to_operand_aliasing={{1}: (6, {})} | custom-call | bytes 1024 | tf_op jit(solution)/shard_map/attend/pallas_call | solution.py:270
  66.5 2.5 %collective-permute-done.3 = bf16[1152,512]{1,0:T(8,128)(2,1)} collective-permute-done((bf16[1152,512]{1,0:T(8,128)(2,1)}, bf16[1152,512]{1,0:T(8,128)(2,1)}, u32[]{:S(2)}, u32[]{:S(2)}) %collective-permute-start.3) | collective-permute-done | bytes 1179680 | tf_op jit(solution)/shard_map/ppermute | solution.py:36
  69.0 1.4 %broadcast_select_fusion.1.refs_0_ = bf16[1152,512]{1,0:T(8,128)(2,1)S(1)} fusion(bf16[1152,512]{1,0:T(8,128)(2,1)} %collective-permute-done.1, bf16[1152,512]{1,0:T(8,128)(2,1)} %collective-permute-done.3, pred[]{:T(512)S(6)} %and.22), kind=kLoop, calls=%fused_computation.2 | loop fusion | flops 589824 | bytes 3538945 | tf_op jit(solution)/shard_map/jit(_where)/select_n | solution.py:577
  70.4 1.5 %collective-permute-start.13 = (bf16[1152,512]{1,0:T(8,128)(2,1)}, bf16[1152,512]{1,0:T(8,128)(2,1)S(1)}, u32[]{:S(2)}, u32[]{:S(2)}) collective-permute-start(bf16[1152,512]{1,0:T(8,128)(2,1)} %collective-permute-done.12), channel_id=1, source_target_pairs={{4,0},{8,12},{6,2},{10,14},{5,1},{9,13},{7,3},{11,15},{20,16},{24,... | collective-permute-start | bytes 3538952 | tf_op jit(solution)/shard_map/ppermute | solution.py:36
  71.9 1.6 %collective-permute-start.10 = (bf16[256,512]{1,0:T(8,128)(2,1)}, bf16[256,512]{1,0:T(8,128)(2,1)S(1)}, u32[]{:S(2)}, u32[]{:S(2)}) collective-permute-start(bf16[256,512]{1,0:T(8,128)(2,1)} %get-tuple-element.59), channel_id=1, source_target_pairs={{0,2},{2,0},{4,6},{6,4},{8,10},{10,8},{12,14},{14,12},{1,3},{3,1},... | collective-permute-start | bytes 786440 | tf_op jit(solution)/shard_map/ppermute | solution.py:28
  73.5 0.5 collective-permute-start.11
  74.1 5.8 %attend.6 = (bf16[256,512]{1,0:T(8,128)(2,1)S(1)}, bf16[8,256,512]{2,1,0:T(8,128)(2,1)}) custom-call(s32[8]{0:T(128)S(1)} %copy-done.5, s32[1]{0:T(128)} %bitcast.own_ref, bf16[4,320,512]{2,1,0:T(8,128)(2,1)S(1)} %collective-permute-done.4.guest, bf16[4,320,512]{2,1,0:T(8,128)(2,1)S(1)} %pack_tokens.3.stay, ...), custom_call_target="tpu_custom_call", output_to_operand_aliasing={{1}: (6, {})} | custom-call | bytes 1024 | tf_op jit(solution)/shard_map/attend/pallas_call | solution.py:270
  79.8 1.6 %collective-permute-start.15 = (bf16[256,512]{1,0:T(8,128)(2,1)S(1)}, bf16[256,512]{1,0:T(8,128)(2,1)S(1)}, u32[]{:S(2)}, u32[]{:S(2)}) collective-permute-start(bf16[256,512]{1,0:T(8,128)(2,1)S(1)} %get-tuple-element.68), channel_id=1, source_target_pairs={{0,2},{2,0},{4,6},{6,4},{8,10},{10,8},{12,14},{14,12},{1,3},{3,1},... | collective-permute-start | bytes 786440 | tf_op jit(solution)/shard_map/ppermute | solution.py:28
  81.4 5.5 %collective-permute-done.11.refs_1_ = bf16[256,512]{1,0:T(8,128)(2,1)S(1)} collective-permute-done((bf16[256,512]{1,0:T(8,128)(2,1)S(1)}, bf16[256,512]{1,0:T(8,128)(2,1)S(1)}, u32[]{:S(2)}, u32[]{:S(2)}) %collective-permute-start.11) | collective-permute-done | bytes 262176 | tf_op jit(solution)/shard_map/ppermute | solution.py:28
  86.9 1.6 %experts.1 = (f32[16,7168]{1,0:T(8,128)S(1)}, bf16[16,7168]{1,0:T(8,128)(2,1)S(1)}) custom-call(bf16[16,7168]{1,0:T(8,128)(2,1)S(1)} %stack_rows.5.mine_ref, bf16[16,7168]{1,0:T(8,128)(2,1)S(1)} %collective-permute-done.9.theirs_ref, bf16[1,7168,128]{2,1,0:T(8,128)(2,1)S(1)} %copy-done.2, bf16[1,7168,128]{2,1,0:T(8,128)(2,1)S(1)} %copy-done.3, ...), custom_call_target="tpu_custom_call" | custom-call | bytes 1024 | tf_op jit(solution)/shard_map/experts/pallas_call | solution.py:437
  88.6 1.5 %collective-permute-done.16.arrived_ref = bf16[16,7168]{1,0:T(8,128)(2,1)S(1)} collective-permute-done((bf16[16,7168]{1,0:T(8,128)(2,1)S(1)}, bf16[16,7168]{1,0:T(8,128)(2,1)S(1)}, u32[]{:S(2)}, u32[]{:S(2)}) %collective-permute-start.16) | collective-permute-done | bytes 229408 | tf_op jit(solution)/shard_map/ppermute | solution.py:28
  90.1 13.2 %collective-permute-done.13 = bf16[1152,512]{1,0:T(8,128)(2,1)S(1)} collective-permute-done((bf16[1152,512]{1,0:T(8,128)(2,1)}, bf16[1152,512]{1,0:T(8,128)(2,1)S(1)}, u32[]{:S(2)}, u32[]{:S(2)}) %collective-permute-start.13) | collective-permute-done | bytes 1179680 | tf_op jit(solution)/shard_map/ppermute | solution.py:36
  103.3 1.5 %collective-permute-start.17 = (bf16[8,7168]{1,0:T(8,128)(2,1)S(1)}, bf16[8,7168]{1,0:T(8,128)(2,1)S(1)}, u32[]{:S(2)}, u32[]{:S(2)}) collective-permute-start(bf16[8,7168]{1,0:T(8,128)(2,1)S(1)} %get-tuple-element.77), channel_id=1, source_target_pairs={{0,2},{2,0},{4,6},{6,4},{8,10},{10,8},{12,14},{14,12},{1,3},{3,1},... | collective-permute-start | bytes 344072 | tf_op jit(solution)/shard_map/ppermute | solution.py:28
  104.8 0.1 broadcast_select_fusion.refs_0_
  105.0 3.2 %collective-permute-done.17 = bf16[8,7168]{1,0:T(8,128)(2,1)S(1)} collective-permute-done((bf16[8,7168]{1,0:T(8,128)(2,1)S(1)}, bf16[8,7168]{1,0:T(8,128)(2,1)S(1)}, u32[]{:S(2)}, u32[]{:S(2)}) %collective-permute-start.17) | collective-permute-done | bytes 114720 | tf_op jit(solution)/shard_map/ppermute | solution.py:28
  108.3 0.7 fusion.4
  109.0 5.8 %attend.7 = (bf16[256,512]{1,0:T(8,128)(2,1)S(1)}, bf16[8,256,512]{2,1,0:T(8,128)(2,1)}) custom-call(s32[8]{0:T(128)S(1)} %copy-done.5, s32[1]{0:T(128)} %bitcast.own_ref, bf16[4,320,512]{2,1,0:T(8,128)(2,1)S(1)} %collective-permute-done.4.guest, bf16[4,320,512]{2,1,0:T(8,128)(2,1)S(1)} %pack_tokens.3.stay, ...), custom_call_target="tpu_custom_call", output_to_operand_aliasing={{1}: (6, {})} | custom-call | bytes 1024 | tf_op jit(solution)/shard_map/attend/pallas_call | solution.py:270
  114.8 0.7 copy-done.8
  115.5 1.5 %collective-permute-start.19 = (bf16[256,512]{1,0:T(8,128)(2,1)}, bf16[256,512]{1,0:T(8,128)(2,1)S(1)}, u32[]{:S(2)}, u32[]{:S(2)}) collective-permute-start(bf16[256,512]{1,0:T(8,128)(2,1)} %copy-done.8), channel_id=1, source_target_pairs={{0,2},{2,0},{4,6},{6,4},{8,10},{10,8},{12,14},{14,12},{1,3},{3,1},... | collective-permute-start | bytes 786440 | tf_op jit(solution)/shard_map/ppermute | solution.py:28
  117.0 3.2 %collective-permute-start.21 = (bf16[2,7168]{1,0:T(2,128)(2,1)S(1)}, bf16[2,7168]{1,0:T(2,128)(2,1)S(1)}, u32[]{:S(2)}, u32[]{:S(2)}) collective-permute-start(bf16[2,7168]{1,0:T(2,128)(2,1)S(1)} %get-tuple-element.89), channel_id=1, source_target_pairs={{0,8},{2,10},{4,12},{6,14},{8,0},{10,2},{12,4},{14,6},{1,9},{3,11}... | collective-permute-start | bytes 86024 | tf_op jit(solution)/shard_map/ppermute | solution.py:553
  120.2 1.2 collective-permute-start.22
  121.5 0.6 collective-permute-done.21
  122.1 3.8 %collective-permute-done.22 = bf16[2,7168]{1,0:T(2,128)(2,1)S(1)} collective-permute-done((bf16[2,7168]{1,0:T(2,128)(2,1)S(1)}, bf16[2,7168]{1,0:T(2,128)(2,1)S(1)}, u32[]{:S(2)}, u32[]{:S(2)}) %collective-permute-start.22) | collective-permute-done | bytes 28704 | tf_op jit(solution)/shard_map/ppermute | solution.py:553
  126.0 0.2 multiply_reduce_fusion
  126.2 0.8 convert_element_type.31
  127.0 1.5 %place.1 = bf16[8,256,512]{2,1,0:T(8,128)(2,1)} custom-call(s32[8]{0:T(128)S(1)} %copy-done.5, s32[1]{0:T(128)} %bitcast.own_ref, bf16[256,512]{1,0:T(8,128)(2,1)S(1)} %collective-permute-done.10.refs_0_, bf16[256,512]{1,0:T(8,128)(2,1)S(1)} %collective-permute-done.11.refs_1_, ...), custom_call_target="tpu_custom_call", output_to_operand_aliasing={{}: (6, {})} | custom-call | bytes 1024 | tf_op jit(solution)/shard_map/place/pallas_call | solution.py:309
  (52 shorter events, 0.7 us)
Async XLA Ops:
  0.6 7.1 %copy-start.9 = (bf16[8,2,8192]{2,1,0:T(2,128)(2,1)S(1)}, bf16[8,2,8192]{2,1,0:T(2,128)(2,1)}, u32[]{:S(2)}) copy-start(bf16[8,2,8192]{2,1,0:T(2,128)(2,1)} %param.16) | copy-start | bytes 786436
  0.6 7.3 %copy-start.11 = (bf16[8,2,512]{2,1,0:T(2,128)(2,1)S(1)}, bf16[8,2,512]{2,1,0:T(2,128)(2,1)}, u32[]{:S(2)}) copy-start(bf16[8,2,512]{2,1,0:T(2,128)(2,1)} %param.17) | copy-start | bytes 49156
  0.7 7.3 %copy-start.12 = (bf16[8,2,64]{2,1,0:T(2,128)(2,1)S(1)}, bf16[8,2,64]{2,1,0:T(2,128)(2,1)}, u32[]{:S(2)}) copy-start(bf16[8,2,64]{2,1,0:T(2,128)(2,1)} %param.18) | copy-start | bytes 6148
  0.7 7.3 %copy-start.5 = (s32[8]{0:T(128)S(1)}, s32[8]{0:T(128)}, u32[]{:S(2)}) copy-start(s32[8]{0:T(128)} %slot_ref.13) | copy-start | bytes 100
  3.0 34.7 %collective-permute-start = (bf16[1152,512]{1,0:T(8,128)(2,1)}, bf16[1152,512]{1,0:T(8,128)(2,1)}, u32[]{:S(2)}, u32[]{:S(2)}) collective-permute-start(bf16[1152,512]{1,0:T(8,128)(2,1)} %pack_cache.1.refs_0_), channel_id=1, source_target_pairs={{0,4},{4,0},{8,12},{12,8},{2,6},{6,2},{10,14},{14,10},{1,5},{5,1},... | collective-permute-start | bytes 3538952 | tf_op jit(solution)/shard_map/ppermute | solution.py:36
  6.1 31.6 %collective-permute-start.1 = (bf16[1152,512]{1,0:T(8,128)(2,1)}, bf16[1152,512]{1,0:T(8,128)(2,1)}, u32[]{:S(2)}, u32[]{:S(2)}) collective-permute-start(bf16[1152,512]{1,0:T(8,128)(2,1)} %pack_cache.1.refs_0_), channel_id=1, source_target_pairs={{4,8},{8,4},{6,10},{10,6},{5,9},{9,5},{7,11},{11,7},{20,24},{24,20... | collective-permute-start | bytes 3538952 | tf_op jit(solution)/shard_map/ppermute | solution.py:36
  8.0 1.6 %copy-start = (bf16[8,2,128,512]{3,2,1,0:T(8,128)(2,1)S(1)}, bf16[8,2,128,512]{3,2,1,0:T(8,128)(2,1)}, u32[]{:S(2)}) copy-start(bf16[8,2,128,512]{3,2,1,0:T(8,128)(2,1)} %param.15) | copy-start | bytes 6291460
  9.6 3.8 %copy-start.10 = (bf16[8,2,7168]{2,1,0:T(2,128)(2,1)S(1)}, bf16[8,2,7168]{2,1,0:T(2,128)(2,1)}, u32[]{:S(2)}) copy-start(bf16[8,2,7168]{2,1,0:T(2,128)(2,1)} %param.20) | copy-start | bytes 688132
  9.6 3.9 %copy-start.6 = (s32[8,2,8]{2,1,0:T(2,128)S(1)}, s32[8,2,8]{2,1,0:T(2,128)}, u32[]{:S(2)}) copy-start(s32[8,2,8]{2,1,0:T(2,128)} %param.21) | copy-start | bytes 1540
  9.6 3.9 %copy-start.7 = (f32[8,2,8]{2,1,0:T(2,128)S(1)}, f32[8,2,8]{2,1,0:T(2,128)}, u32[]{:S(2)}) copy-start(f32[8,2,8]{2,1,0:T(2,128)} %param.22) | copy-start | bytes 1540
  11.8 35.1 %collective-permute-start.4 = (bf16[4,320,512]{2,1,0:T(8,128)(2,1)}, bf16[4,320,512]{2,1,0:T(8,128)(2,1)S(1)}, u32[]{:S(2)}, u32[]{:S(2)}) collective-permute-start(bf16[4,320,512]{2,1,0:T(8,128)(2,1)} %pack_tokens.2), channel_id=1, source_target_pairs={{0,2},{2,0},{4,6},{6,4},{8,10},{10,8},{12,14},{14,12},{1,3},{3,1},... | collective-permute-start | bytes 3932168 | tf_op jit(solution)/shard_map/ppermute | solution.py:28
  13.4 33.5 %collective-permute-start.6 = (bf16[1152,512]{1,0:T(8,128)(2,1)}, bf16[1152,512]{1,0:T(8,128)(2,1)}, u32[]{:S(2)}, u32[]{:S(2)}) collective-permute-start(bf16[1152,512]{1,0:T(8,128)(2,1)} %pack_cache.1.refs_0_), channel_id=1, source_target_pairs={{0,1},{1,0},{2,3},{3,2},{4,5},{5,4},{6,7},{7,6},{8,9},{9,8},{10,11... | collective-permute-start | bytes 3538952 | tf_op jit(solution)/shard_map/ppermute | solution.py:28
  13.9 23.8 %collective-permute-start.2 = (bf16[2,7168]{1,0:T(2,128)(2,1)S(1)}, bf16[2,7168]{1,0:T(2,128)(2,1)S(1)}, u32[]{:S(2)}, u32[]{:S(2)}) collective-permute-start(bf16[2,7168]{1,0:T(2,128)(2,1)S(1)} %get-tuple-element.50), channel_id=1, source_target_pairs={{0,8},{2,10},{4,12},{6,14},{8,0},{10,2},{12,4},{14,6},{1,9},{3,11}... | collective-permute-start | bytes 86024 | tf_op jit(solution)/shard_map/ppermute | solution.py:553
  38.0 4.2 %collective-permute-start.7 = (bf16[4,7168]{1,0:T(4,128)(2,1)S(1)}, bf16[4,7168]{1,0:T(4,128)(2,1)S(1)}, u32[]{:S(2)}, u32[]{:S(2)}) collective-permute-start(bf16[4,7168]{1,0:T(4,128)(2,1)S(1)} %stack_rows.3.refs_0_), channel_id=1, source_target_pairs={{0,4},{2,6},{4,0},{6,2},{8,12},{10,14},{12,8},{14,10},{1,5},{3,7},... | collective-permute-start | bytes 172040 | tf_op jit(solution)/shard_map/ppermute | solution.py:553
  38.4 21.2 %collective-permute-start.5 = (bf16[1152,512]{1,0:T(8,128)(2,1)}, bf16[1152,512]{1,0:T(8,128)(2,1)}, u32[]{:S(2)}, u32[]{:S(2)}) collective-permute-start(bf16[1152,512]{1,0:T(8,128)(2,1)} %collective-permute-done.refs_0_), channel_id=1, source_target_pairs={{0,1},{1,0},{2,3},{3,2},{4,5},{5,4},{6,7},{7,6},{8,9},{9,8},{10,11... | collective-permute-start | bytes 3538952 | tf_op jit(solution)/shard_map/ppermute | solution.py:28
  38.4 30.6 %collective-permute-start.3 = (bf16[1152,512]{1,0:T(8,128)(2,1)}, bf16[1152,512]{1,0:T(8,128)(2,1)}, u32[]{:S(2)}, u32[]{:S(2)}) collective-permute-start(bf16[1152,512]{1,0:T(8,128)(2,1)} %collective-permute-done.1), channel_id=1, source_target_pairs={{4,0},{8,12},{6,2},{10,14},{5,1},{9,13},{7,3},{11,15},{20,16},{24,... | collective-permute-start | bytes 3538952 | tf_op jit(solution)/shard_map/ppermute | solution.py:36
  42.2 26.8 %collective-permute-start.12 = (bf16[1152,512]{1,0:T(8,128)(2,1)}, bf16[1152,512]{1,0:T(8,128)(2,1)}, u32[]{:S(2)}, u32[]{:S(2)}) collective-permute-start(bf16[1152,512]{1,0:T(8,128)(2,1)} %collective-permute-done.refs_0_), channel_id=1, source_target_pairs={{4,8},{8,4},{6,10},{10,6},{5,9},{9,5},{7,11},{11,7},{20,24},{24,20... | collective-permute-start | bytes 3538952 | tf_op jit(solution)/shard_map/ppermute | solution.py:36
  43.9 1.6 %copy-start.1 = (bf16[8,2,128,512]{3,2,1,0:T(8,128)(2,1)S(1)}, bf16[8,2,128,512]{3,2,1,0:T(8,128)(2,1)}, u32[]{:S(2)}) copy-start(bf16[8,2,128,512]{3,2,1,0:T(8,128)(2,1)} %param.15) | copy-start | bytes 6291460
  54.5 4.9 %collective-permute-start.8 = (bf16[8,7168]{1,0:T(8,128)(2,1)S(1)}, bf16[8,7168]{1,0:T(8,128)(2,1)S(1)}, u32[]{:S(2)}, u32[]{:S(2)}) collective-permute-start(bf16[8,7168]{1,0:T(8,128)(2,1)S(1)} %stack_rows.4.refs_0_), channel_id=1, source_target_pairs={{0,2},{2,0},{4,6},{6,4},{8,10},{10,8},{12,14},{14,12},{1,3},{3,1},... | collective-permute-start | bytes 344072 | tf_op jit(solution)/shard_map/ppermute | solution.py:28
  70.4 3.7 %collective-permute-start.14 = (bf16[1152,512]{1,0:T(8,128)(2,1)S(1)}, bf16[1152,512]{1,0:T(8,128)(2,1)S(1)}, u32[]{:S(2)}, u32[]{:S(2)}) collective-permute-start(bf16[1152,512]{1,0:T(8,128)(2,1)S(1)} %broadcast_select_fusion.1.refs_0_), channel_id=1, source_target_pairs={{0,1},{1,0},{2,3},{3,2},{4,5},{5,4},{6,7},{7,6},{8,9},{9,8},{10,11... | collective-permute-start | bytes 3538952 | tf_op jit(solution)/shard_map/ppermute | solution.py:28
  70.4 32.8 %collective-permute-start.13 = (bf16[1152,512]{1,0:T(8,128)(2,1)}, bf16[1152,512]{1,0:T(8,128)(2,1)S(1)}, u32[]{:S(2)}, u32[]{:S(2)}) collective-permute-start(bf16[1152,512]{1,0:T(8,128)(2,1)} %collective-permute-done.12), channel_id=1, source_target_pairs={{4,0},{8,12},{6,2},{10,14},{5,1},{9,13},{7,3},{11,15},{20,16},{24,... | collective-permute-start | bytes 3538952 | tf_op jit(solution)/shard_map/ppermute | solution.py:36
  71.9 9.5 %collective-permute-start.10 = (bf16[256,512]{1,0:T(8,128)(2,1)}, bf16[256,512]{1,0:T(8,128)(2,1)S(1)}, u32[]{:S(2)}, u32[]{:S(2)}) collective-permute-start(bf16[256,512]{1,0:T(8,128)(2,1)} %get-tuple-element.59), channel_id=1, source_target_pairs={{0,2},{2,0},{4,6},{6,4},{8,10},{10,8},{12,14},{14,12},{1,3},{3,1},... | collective-permute-start | bytes 786440 | tf_op jit(solution)/shard_map/ppermute | solution.py:28
  73.5 13.4 %collective-permute-start.11 = (bf16[256,512]{1,0:T(8,128)(2,1)S(1)}, bf16[256,512]{1,0:T(8,128)(2,1)S(1)}, u32[]{:S(2)}, u32[]{:S(2)}) collective-permute-start(bf16[256,512]{1,0:T(8,128)(2,1)S(1)} %get-tuple-element.56), channel_id=1, source_target_pairs={{0,2},{2,0},{4,6},{6,4},{8,10},{10,8},{12,14},{14,12},{1,3},{3,1},... | collective-permute-start | bytes 786440 | tf_op jit(solution)/shard_map/ppermute | solution.py:28
  74.0 7.4 %collective-permute-start.9 = (bf16[16,7168]{1,0:T(8,128)(2,1)S(1)}, bf16[16,7168]{1,0:T(8,128)(2,1)S(1)}, u32[]{:S(2)}, u32[]{:S(2)}) collective-permute-start(bf16[16,7168]{1,0:T(8,128)(2,1)S(1)} %stack_rows.5.mine_ref), channel_id=1, source_target_pairs={{0,1},{1,0},{2,3},{3,2},{4,5},{5,4},{6,7},{7,6},{8,9},{9,8},{10,11... | collective-permute-start | bytes 688136 | tf_op jit(solution)/shard_map/ppermute | solution.py:28
  74.0 12.9 %copy-start.2 = (bf16[1,7168,128]{2,1,0:T(8,128)(2,1)S(1)}, bf16[1,7168,128]{2,1,0:T(8,128)(2,1)}, u32[]{:S(2)}) copy-start(bf16[1,7168,128]{2,1,0:T(8,128)(2,1)} %gate_hbm.1) | copy-start | bytes 5505028
  74.0 12.9 %copy-start.3 = (bf16[1,7168,128]{2,1,0:T(8,128)(2,1)S(1)}, bf16[1,7168,128]{2,1,0:T(8,128)(2,1)}, u32[]{:S(2)}) copy-start(bf16[1,7168,128]{2,1,0:T(8,128)(2,1)} %up_hbm.1) | copy-start | bytes 5505028
  74.0 12.9 %copy-start.4 = (bf16[1,128,7168]{2,1,0:T(8,128)(2,1)S(1)}, bf16[1,128,7168]{2,1,0:T(8,128)(2,1)}, u32[]{:S(2)}) copy-start(bf16[1,128,7168]{2,1,0:T(8,128)(2,1)} %down_hbm.1) | copy-start | bytes 5505028
  79.8 23.4 %collective-permute-start.15 = (bf16[256,512]{1,0:T(8,128)(2,1)S(1)}, bf16[256,512]{1,0:T(8,128)(2,1)S(1)}, u32[]{:S(2)}, u32[]{:S(2)}) collective-permute-start(bf16[256,512]{1,0:T(8,128)(2,1)S(1)} %get-tuple-element.68), channel_id=1, source_target_pairs={{0,2},{2,0},{4,6},{6,4},{8,10},{10,8},{12,14},{14,12},{1,3},{3,1},... | collective-permute-start | bytes 786440 | tf_op jit(solution)/shard_map/ppermute | solution.py:28
  88.5 1.6 %collective-permute-start.16 = (bf16[16,7168]{1,0:T(8,128)(2,1)S(1)}, bf16[16,7168]{1,0:T(8,128)(2,1)S(1)}, u32[]{:S(2)}, u32[]{:S(2)}) collective-permute-start(bf16[16,7168]{1,0:T(8,128)(2,1)S(1)} %get-tuple-element.72), channel_id=1, source_target_pairs={{0,1},{1,0},{2,3},{3,2},{4,5},{5,4},{6,7},{7,6},{8,9},{9,8},{10,11... | collective-permute-start | bytes 688136 | tf_op jit(solution)/shard_map/ppermute | solution.py:28
  103.3 5.0 %collective-permute-start.17 = (bf16[8,7168]{1,0:T(8,128)(2,1)S(1)}, bf16[8,7168]{1,0:T(8,128)(2,1)S(1)}, u32[]{:S(2)}, u32[]{:S(2)}) collective-permute-start(bf16[8,7168]{1,0:T(8,128)(2,1)S(1)} %get-tuple-element.77), channel_id=1, source_target_pairs={{0,2},{2,0},{4,6},{6,4},{8,10},{10,8},{12,14},{14,12},{1,3},{3,1},... | collective-permute-start | bytes 344072 | tf_op jit(solution)/shard_map/ppermute | solution.py:28
  104.9 4.1 %collective-permute-start.18 = (bf16[1152,512]{1,0:T(8,128)(2,1)S(1)}, bf16[1152,512]{1,0:T(8,128)(2,1)S(1)}, u32[]{:S(2)}, u32[]{:S(2)}) collective-permute-start(bf16[1152,512]{1,0:T(8,128)(2,1)S(1)} %broadcast_select_fusion.refs_0_), channel_id=1, source_target_pairs={{0,1},{1,0},{2,3},{3,2},{4,5},{5,4},{6,7},{7,6},{8,9},{9,8},{10,11... | collective-permute-start | bytes 3538952 | tf_op jit(solution)/shard_map/ppermute | solution.py:28
  114.7 0.7 copy-start.8
  115.4 6.0 %collective-permute-start.20 = (bf16[2,7168]{1,0:T(2,128)(2,1)}, bf16[2,7168]{1,0:T(2,128)(2,1)S(1)}, u32[]{:S(2)}, u32[]{:S(2)}) collective-permute-start(bf16[2,7168]{1,0:T(2,128)(2,1)} %get-tuple-element.87), channel_id=1, source_target_pairs={{0,4},{2,6},{4,0},{6,2},{8,12},{10,14},{12,8},{14,10},{1,5},{3,7},... | collective-permute-start | bytes 86024 | tf_op jit(solution)/shard_map/ppermute | solution.py:553
  115.5 11.5 %collective-permute-start.19 = (bf16[256,512]{1,0:T(8,128)(2,1)}, bf16[256,512]{1,0:T(8,128)(2,1)S(1)}, u32[]{:S(2)}, u32[]{:S(2)}) collective-permute-start(bf16[256,512]{1,0:T(8,128)(2,1)} %copy-done.8), channel_id=1, source_target_pairs={{0,2},{2,0},{4,6},{6,4},{8,10},{10,8},{12,14},{14,12},{1,3},{3,1},... | collective-permute-start | bytes 786440 | tf_op jit(solution)/shard_map/ppermute | solution.py:28
  117.0 5.1 %collective-permute-start.21 = (bf16[2,7168]{1,0:T(2,128)(2,1)S(1)}, bf16[2,7168]{1,0:T(2,128)(2,1)S(1)}, u32[]{:S(2)}, u32[]{:S(2)}) collective-permute-start(bf16[2,7168]{1,0:T(2,128)(2,1)S(1)} %get-tuple-element.89), channel_id=1, source_target_pairs={{0,8},{2,10},{4,12},{6,14},{8,0},{10,2},{12,4},{14,6},{1,9},{3,11}... | collective-permute-start | bytes 86024 | tf_op jit(solution)/shard_map/ppermute | solution.py:553
  120.2 5.7 %collective-permute-start.22 = (bf16[2,7168]{1,0:T(2,128)(2,1)S(1)}, bf16[2,7168]{1,0:T(2,128)(2,1)S(1)}, u32[]{:S(2)}, u32[]{:S(2)}) collective-permute-start(bf16[2,7168]{1,0:T(2,128)(2,1)S(1)} %get-tuple-element.91), channel_id=1, source_target_pairs={{0,12},{2,14},{4,8},{6,10},{8,4},{10,6},{12,0},{14,2},{1,13},{3,15... | collective-permute-start | bytes 86024 | tf_op jit(solution)/shard_map/ppermute | solution.py:553

commit v9 on v8

--- a/solution.py
+++ b/solution.py
@@ -410,8 +410,10 @@
     )(*arrays)
 
 
-def experts_kernel(mine_ref, theirs_ref, gate_hbm, up_hbm, down_hbm, keep_ref, send_ref, *scratch):
-    gate_ref, up_ref, down_ref, sems = scratch
+def experts_kernel(count, *refs):
+    row_refs, (gate_hbm, up_hbm, down_hbm) = refs[:count], refs[count : count + 3]
+    out_refs = refs[count + 3 : 2 * count + 3]
+    gate_ref, up_ref, down_ref, sems = refs[2 * count + 3 :]
     copies = [
         pltpu.make_async_copy(source.at[0], there, sems.at[i])
         for i, (source, there) in enumerate(
@@ -420,7 +422,8 @@
     ]
     for copy in copies:
         copy.start()
-    rows = jnp.concatenate([mine_ref[...], theirs_ref[...]], axis=0)
+    rows = jnp.concatenate([ref[...].astype(jnp.float32) for ref in row_refs], axis=0)
+    rows = rows.astype(jnp.bfloat16)
     copies[0].wait()
     gate = jnp.dot(rows, gate_ref[...], preferred_element_type=jnp.float32)
     copies[1].wait()
@@ -428,21 +431,22 @@
     hidden = (gate / (1.0 + jnp.exp(-gate)) * lifted).astype(jnp.bfloat16)
     copies[2].wait()
     parts = jnp.dot(hidden, down_ref[...], preferred_element_type=jnp.float32)
-    count = mine_ref.shape[0]
-    keep_ref[...] = parts[:count]
-    send_ref[...] = parts[count:].astype(jnp.bfloat16)
-
-
-def run_experts(mine, theirs, w_gate, w_up, w_down):
+    for i, (row_ref, out_ref) in enumerate(zip(row_refs, out_refs)):
+        size = row_ref.shape[0]
+        out_ref[...] = parts[i * size : (i + 1) * size].astype(out_ref.dtype)
+
+
+def run_experts(groups, w_gate, w_up, w_down):
+    count = len(groups)
+    vmem = pl.BlockSpec(memory_space=pltpu.VMEM)
     return pl.pallas_call(
-        experts_kernel,
-        out_shape=(
-            jax.ShapeDtypeStruct(mine.shape, jnp.float32),
-            jax.ShapeDtypeStruct(mine.shape, jnp.bfloat16),
+        functools.partial(experts_kernel, count),
+        out_shape=tuple(
+            jax.ShapeDtypeStruct(x.shape, jnp.bfloat16 if i else jnp.float32)
+            for i, x in enumerate(groups)
         ),
-        in_specs=[pl.BlockSpec(memory_space=pltpu.VMEM)] * 2
-        + [pl.BlockSpec(memory_space=pltpu.HBM)] * 3,
-        out_specs=(pl.BlockSpec(memory_space=pltpu.VMEM),) * 2,
+        in_specs=[vmem] * count + [pl.BlockSpec(memory_space=pltpu.HBM)] * 3,
+        out_specs=(vmem,) * count,
         scratch_shapes=[
             pltpu.VMEM(w_gate.shape[1:], w_gate.dtype),
             pltpu.VMEM(w_up.shape[1:], w_up.dtype),
@@ -452,28 +456,7 @@
         cost_estimate=SMALL,
         compiler_params=pltpu.CompilerParams(vmem_limit_bytes=16 * 1024 * 1024),
         name="experts",
-    )(mine, theirs, w_gate, w_up, w_down)
-
-
-def halve_kernel(sum_ref, arrived_ref, keep_ref, send_ref):
-    count = keep_ref.shape[0]
-    total = sum_ref[...] + arrived_ref[...].astype(jnp.float32)
-    keep_ref[...] = total[:count]
-    send_ref[...] = total[count:].astype(jnp.bfloat16)
-
-
-def halve(kept, arrived):
-    shape = (kept.shape[0] // 2, kept.shape[1])
-    return pl.pallas_call(
-        halve_kernel,
-        out_shape=(
-            jax.ShapeDtypeStruct(shape, jnp.float32),
-            jax.ShapeDtypeStruct(shape, jnp.bfloat16),
-        ),
-        cost_estimate=SMALL,
-        compiler_params=pltpu.CompilerParams(vmem_limit_bytes=8 * 1024 * 1024),
-        name="halve",
-    )(kept, arrived)
+    )(*groups, w_gate, w_up, w_down)
 
 
 def on_device(
@@ -554,7 +537,9 @@
 
     ways = [(k, m) for m in range(around) for k in range(experts)]
     pieces = outgoing[:1] + [along(outgoing[k], k, 0) for k in range(1, experts)]
-    cache_a, first_b, *pieces = lax.optimization_barrier((cache_a, first_b, *pieces))
+    cache_a, first_b, stay, *pieces = lax.optimization_barrier(
+        (cache_a, first_b, stay, *pieces)
+    )
     second_b = line_hop(first_b, tok_rows, outward)
     first_c = line_hop(cache_a, tok_rows, inner)
 
@@ -562,44 +547,58 @@
         return cache, swapped(cache, "expert", 0)
 
     guest = after(guest, cache_a, first_b)
-    rows = stack_rows(*pieces)
-    rows = stack_rows(rows, *(along(rows, 0, m) for m in range(1, around)))
     given_0, placed = attend(scalars, 0, guest, stay, both_halves(own_cache), None)
     back_0 = swapped(given_0, "branch", 0)
+    rows = stack_rows(*lax.optimization_barrier((given_0, *pieces))[1:])
+    rows = [rows] + [along(rows, 0, m) for m in range(1, around)]
     given_1, placed = attend(scalars, 1, guest, stay, both_halves(cache_a), placed)
     back_1 = swapped(given_1, "branch", 0)
-    rows = after(rows, given_0)
-    rows = stack_rows(rows, swapped(rows, "branch", 0))
-
-    second_b, given_1, rows = lax.optimization_barrier((second_b, given_1, rows))
+
+    second_b, given_1, back_0, *rows = lax.optimization_barrier(
+        (second_b, given_1, back_0, *rows)
+    )
     first_c, second_b = lax.optimization_barrier((first_c, second_b))
     second_c = line_hop(first_c, tok_rows, outward)
     cache_b = jnp.where(middle, first_b, second_b)
     given_2, placed = attend(scalars, 2, guest, stay, both_halves(cache_b), placed)
     back_2 = swapped(given_2, "branch", 0)
-    theirs = swapped(rows, "expert", 0)
-    rows, theirs, back_0, back_1 = lax.optimization_barrier((rows, theirs, back_0, back_1))
-    kept, sent = run_experts(rows, theirs, w_gate, w_up, w_down)
-    kept, sent = halve(kept, swapped(sent, "expert", 0))
-
-    second_c, back_2, kept, sent = lax.optimization_barrier((second_c, back_2, kept, sent))
+    rows = stack_rows(*rows)
+
+    def around_chip(x, i):
+        pairs = []
+        for there in range(lax.axis_size("branch") * cores):
+            row, core = there // cores, there % cores
+            pairs.append((there, (row ^ (i & 1)) * cores + (core ^ (i >> 1))))
+        return lax.ppermute(x, ("branch", "expert"), pairs)
+
+    groups = [rows] + [around_chip(rows, i) for i in range(1, 2 * cores)]
+    groups = lax.optimization_barrier((given_2, *groups))[1:]
+    parts, *others = run_experts(groups, w_gate, w_up, w_down)
+    others = [around_chip(x, i + 1) for i, x in enumerate(others)]
+
+    second_c, back_1, parts, *others = lax.optimization_barrier(
+        (second_c, back_1, parts, *others)
+    )
+    for other in others:
+        parts = parts + other.astype(jnp.float32)
     cache_c = both_halves(jnp.where(middle, first_c, second_c))
-    parts = kept + swapped(sent, "branch", 0).astype(jnp.float32)
     homeward = [
         parts[w * CAP : (w + 1) * CAP].astype(jnp.float32 if way == (0, 0) else jnp.bfloat16)
         for w, way in enumerate(ways)
     ]
-    guest, *homeward = lax.optimization_barrier((guest, *homeward))
+    homeward = [
+        piece if (k, m) == (0, 0) else along(piece, -k, m)
+        for (k, m), piece in zip(ways, homeward)
+    ]
+    guest, back_2 = lax.optimization_barrier((guest, back_2))
     given_3, placed = attend(scalars, 3, guest, stay, cache_c, placed)
     back_3 = swapped(given_3, "branch", 0)
-    homeward = [after(x, given_3) for x in homeward]
+    homeward = [after(x, given_3).astype(jnp.float32) for x in homeward]
     placed = place(scalars, (back_0, back_1, back_2, back_3), placed)
     attended = placed.reshape(tok_rows, step_count, head_count, width)
 
     sums = [0.0] * experts
-    for (k, m), piece in zip(ways, homeward):
-        if (k, m) != (0, 0):
-            piece = along(piece, -k, m).astype(jnp.float32)
+    for (k, _), piece in zip(ways, homeward):
         sums[k] = sums[k] + piece
     sums = jnp.concatenate(sums, axis=0)
     combined = jnp.sum(share[:, :, None] * sums[None, :, :], axis=1)

time: 129 us -> 129 us (level)
  waiting for transfers between devices: 57 us -> 46.3 us
  starting transfers between devices: 27 us -> 33 us
  other arithmetic: 1.88 us -> 4.4 us
  Pallas kernels: 35.9 us -> 37.4 us
    ppermute x13 -> x9, waiting for transfers between devices: 13.5 us -> 6.36 us  [swapped(): lax.ppermute(x, axis, [(i, i ^ 1 << bit) for i in range(lax.axis_size(axi...]
    ppermute x0 -> x6, starting transfers between devices: none -> 4.41 us  [around_chip(): return lax.ppermute(x, ('branch', 'expert'), pairs)]
    ppermute x5, waiting for transfers between devices: 15.6 us -> 11.6 us  [line_hop(): return lax.ppermute(x, 'branch', pairs)]
    ppermute x5, starting transfers between devices: 7.73 us -> 11.4 us  [along(): return lax.ppermute(x, 'branch', list(enumerate(there)))]
    ppermute x0 -> x6, waiting for transfers between devices: none -> 2.74 us  [around_chip(): return lax.ppermute(x, ('branch', 'expert'), pairs)]
    ppermute x5, waiting for transfers between devices: 27.9 us -> 25.5 us  [along(): return lax.ppermute(x, 'branch', list(enumerate(there)))]
    ppermute x13 -> x9, starting transfers between devices: 10.1 us -> 7.93 us  [swapped(): lax.ppermute(x, axis, [(i, i ^ 1 << bit) for i in range(lax.axis_size(axi...]
    pallas_call x4, Pallas kernels: 26 us -> 27.8 us  [call(): pl.pallas_call(functools.partial(kernel, slot, placed is not None), out_s...]
  transfers between devices with their start and end apart: 23 -> 25, of which waited for: 10 -> 7; matrix products, arithmetic and copies ran while one was open for 2% -> 4% of each run, Pallas kernels for 20% -> 26%
where the time goes in v9:
time: 129 us; the launch traced here: 128 us
  waiting for transfers between devices  46.3 us (36%)
  Pallas kernels  37.4 us (29%)
  starting transfers between devices  33 us (26%)
  local copies, waits for them, and re-layouts  5.96 us (5%)
  other arithmetic  4.4 us (3%)
    pallas_call x4, Pallas kernels, call(): pl.pallas_call(functools.partial(kernel, slot, placed is not None), out_s...  27.8 us
    ppermute x5, waiting for transfers between devices, along(): return lax.ppermute(x, 'branch', list(enumerate(there)))  25.5 us
    ppermute x5, waiting for transfers between devices, line_hop(): return lax.ppermute(x, 'branch', pairs)  11.6 us
    ppermute x5, starting transfers between devices, along(): return lax.ppermute(x, 'branch', list(enumerate(there)))  11.4 us
    ppermute x5, starting transfers between devices, line_hop(): return lax.ppermute(x, 'branch', pairs)  9.23 us
    ppermute x9, starting transfers between devices, swapped(): lax.ppermute(x, axis, [(i, i ^ 1 << bit) for i in range(lax.axis_size(axi...  7.93 us
    ppermute x9, waiting for transfers between devices, swapped(): lax.ppermute(x, axis, [(i, i ^ 1 << bit) for i in range(lax.axis_size(axi...  6.36 us
    ppermute x6, starting transfers between devices, around_chip(): return lax.ppermute(x, ('branch', 'expert'), pairs)  4.41 us
  transfers between devices with their start and end apart: 25, of which 7 were waited for; matrix products, arithmetic and copies ran while one was open for 4% of the time, Pallas kernels for 26%

profile of v9, /device:TPU:0, one launch (start us, length us, event | category | flops | bytes accessed | tf_op | source)
XLA Modules:
  0.0 128.1 jit_solution(4988649220009359951)
XLA Ops:
  0.7 2.3 %pack_cache.1.refs_0_ = bf16[1152,512]{1,0:T(8,128)(2,1)} custom-call(bf16[1024,512]{1,0:T(8,128)(2,1)} %bitcast.13, bf16[128,512]{1,0:T(8,128)(2,1)} %bitcast.14), custom_call_target="tpu_custom_call" | custom-call | bytes 1024 | tf_op jit(solution)/shard_map/pack_cache/pallas_call | solution.py:52
  3.0 3.1 %collective-permute-start = (bf16[1152,512]{1,0:T(8,128)(2,1)}, bf16[1152,512]{1,0:T(8,128)(2,1)}, u32[]{:S(2)}, u32[]{:S(2)}) collective-permute-start(bf16[1152,512]{1,0:T(8,128)(2,1)} %pack_cache.1.refs_0_), channel_id=1, source_target_pairs={{0,4},{4,0},{8,12},{12,8},{2,6},{6,2},{10,14},{14,10},{1,5},{5,1},... | collective-permute-start | bytes 3538952 | tf_op jit(solution)/shard_map/ppermute | solution.py:36
  6.1 1.7 %collective-permute-start.1 = (bf16[1152,512]{1,0:T(8,128)(2,1)}, bf16[1152,512]{1,0:T(8,128)(2,1)}, u32[]{:S(2)}, u32[]{:S(2)}) collective-permute-start(bf16[1152,512]{1,0:T(8,128)(2,1)} %pack_cache.1.refs_0_), channel_id=1, source_target_pairs={{4,8},{8,4},{6,10},{10,6},{5,9},{9,5},{7,11},{11,7},{20,24},{24,20... | collective-permute-start | bytes 3538952 | tf_op jit(solution)/shard_map/ppermute | solution.py:36
  8.0 1.6 %copy-done = bf16[8,2,128,512]{3,2,1,0:T(8,128)(2,1)S(1)} copy-done((bf16[8,2,128,512]{3,2,1,0:T(8,128)(2,1)S(1)}, bf16[8,2,128,512]{3,2,1,0:T(8,128)(2,1)}, u32[]{:S(2)}) %copy-start) | copy-done | bytes 2097176
  9.6 2.2 %pack_tokens.2 = bf16[4,320,512]{2,1,0:T(8,128)(2,1)} custom-call(s32[8]{0:T(128)S(1)} %copy-done.5, s32[1]{0:T(128)} %bitcast.own_ref, bf16[8,256,512]{2,1,0:T(8,128)(2,1)S(1)} %bitcast.8, bf16[8,32,512]{2,1,0:T(8,128)(2,1)S(1)} %reshape.28.rope_ref, bf16[8,32,512]{2,1,0:T(8,128)(2,1)S(1)} %fusion.2.new_ref), custom_call_target="tpu_custom_call" | custom-call | bytes 1024 | tf_op jit(solution)/shard_map/pack_tokens/pallas_call | solution.py:106
  11.8 1.6 %collective-permute-start.4 = (bf16[4,320,512]{2,1,0:T(8,128)(2,1)}, bf16[4,320,512]{2,1,0:T(8,128)(2,1)S(1)}, u32[]{:S(2)}, u32[]{:S(2)}) collective-permute-start(bf16[4,320,512]{2,1,0:T(8,128)(2,1)} %pack_tokens.2), channel_id=1, source_target_pairs={{0,2},{2,0},{4,6},{6,4},{8,10},{10,8},{12,14},{14,12},{1,3},{3,1},... | collective-permute-start | bytes 3932168 | tf_op jit(solution)/shard_map/ppermute | solution.py:28
  13.5 0.3 dispatch.1
  13.8 2.9 %collective-permute-start.2 = (bf16[2,7168]{1,0:T(2,128)(2,1)S(1)}, bf16[2,7168]{1,0:T(2,128)(2,1)S(1)}, u32[]{:S(2)}, u32[]{:S(2)}) collective-permute-start(bf16[2,7168]{1,0:T(2,128)(2,1)S(1)} %get-tuple-element.54), channel_id=1, source_target_pairs={{0,8},{2,10},{4,12},{6,14},{8,0},{10,2},{12,4},{14,6},{1,9},{3,11}... | collective-permute-start | bytes 86024 | tf_op jit(solution)/shard_map/ppermute | solution.py:536
  16.8 1.6 %copy-done.1 = bf16[8,2,128,512]{3,2,1,0:T(8,128)(2,1)S(1)} copy-done((bf16[8,2,128,512]{3,2,1,0:T(8,128)(2,1)S(1)}, bf16[8,2,128,512]{3,2,1,0:T(8,128)(2,1)}, u32[]{:S(2)}) %copy-start.1) | copy-done | bytes 2097176
  18.4 1.1 pack_tokens.3.stay
  19.5 18.2 %collective-permute-done.2.refs_1_ = bf16[2,7168]{1,0:T(2,128)(2,1)S(1)} collective-permute-done((bf16[2,7168]{1,0:T(2,128)(2,1)S(1)}, bf16[2,7168]{1,0:T(2,128)(2,1)S(1)}, u32[]{:S(2)}, u32[]{:S(2)}) %collective-permute-start.2) | collective-permute-done | bytes 28704 | tf_op jit(solution)/shard_map/ppermute | solution.py:536
  37.7 1.3 %collective-permute-start.3 = (bf16[1152,512]{1,0:T(8,128)(2,1)}, bf16[1152,512]{1,0:T(8,128)(2,1)}, u32[]{:S(2)}, u32[]{:S(2)}) collective-permute-start(bf16[1152,512]{1,0:T(8,128)(2,1)} %collective-permute-done.1), channel_id=1, source_target_pairs={{4,0},{8,12},{6,2},{10,14},{5,1},{9,13},{7,3},{11,15},{20,16},{24,... | collective-permute-start | bytes 3538952 | tf_op jit(solution)/shard_map/ppermute | solution.py:36
  39.0 1.7 %collective-permute-start.9 = (bf16[1152,512]{1,0:T(8,128)(2,1)}, bf16[1152,512]{1,0:T(8,128)(2,1)}, u32[]{:S(2)}, u32[]{:S(2)}) collective-permute-start(bf16[1152,512]{1,0:T(8,128)(2,1)} %collective-permute-done.refs_0_), channel_id=1, source_target_pairs={{4,8},{8,4},{6,10},{10,6},{5,9},{9,5},{7,11},{11,7},{20,24},{24,20... | collective-permute-start | bytes 3538952 | tf_op jit(solution)/shard_map/ppermute | solution.py:36
  40.7 1.6 %collective-permute-done.4.guest = bf16[4,320,512]{2,1,0:T(8,128)(2,1)S(1)} collective-permute-done((bf16[4,320,512]{2,1,0:T(8,128)(2,1)}, bf16[4,320,512]{2,1,0:T(8,128)(2,1)S(1)}, u32[]{:S(2)}, u32[]{:S(2)}) %collective-permute-start.4) | collective-permute-done | bytes 1310752 | tf_op jit(solution)/shard_map/ppermute | solution.py:28
  42.3 6.9 %attend.4 = (bf16[256,512]{1,0:T(8,128)(2,1)S(1)}, bf16[8,256,512]{2,1,0:T(8,128)(2,1)}) custom-call(s32[8]{0:T(128)S(1)} %copy-done.5, s32[1]{0:T(128)} %bitcast.own_ref, bf16[4,320,512]{2,1,0:T(8,128)(2,1)S(1)} %collective-permute-done.4.guest, bf16[4,320,512]{2,1,0:T(8,128)(2,1)S(1)} %pack_tokens.3.stay, bf16[1152,512]{1,0:T(8,128)(2,1)} %pack_cache.1.refs_0_, ...), custom_call_target="tpu_custom_call" | custom-call | bytes 1024 | tf_op jit(solution)/shard_map/attend/pallas_call | solution.py:270
  49.2 1.6 %collective-permute-start.7 = (bf16[256,512]{1,0:T(8,128)(2,1)S(1)}, bf16[256,512]{1,0:T(8,128)(2,1)S(1)}, u32[]{:S(2)}, u32[]{:S(2)}) collective-permute-start(bf16[256,512]{1,0:T(8,128)(2,1)S(1)} %get-tuple-element.61), channel_id=1, source_target_pairs={{0,2},{2,0},{4,6},{6,4},{8,10},{10,8},{12,14},{14,12},{1,3},{3,1},... | collective-permute-start | bytes 786440 | tf_op jit(solution)/shard_map/ppermute | solution.py:28
  50.8 0.3 stack_rows.2.refs_0_
  51.0 4.1 %collective-permute-start.8 = (bf16[4,7168]{1,0:T(4,128)(2,1)S(1)}, bf16[4,7168]{1,0:T(4,128)(2,1)S(1)}, u32[]{:S(2)}, u32[]{:S(2)}) collective-permute-start(bf16[4,7168]{1,0:T(4,128)(2,1)S(1)} %stack_rows.2.refs_0_), channel_id=1, source_target_pairs={{0,4},{2,6},{4,0},{6,2},{8,12},{10,14},{12,8},{14,10},{1,5},{3,7},... | collective-permute-start | bytes 172040 | tf_op jit(solution)/shard_map/ppermute | solution.py:536
  55.1 6.9 %attend.5 = (bf16[256,512]{1,0:T(8,128)(2,1)S(1)}, bf16[8,256,512]{2,1,0:T(8,128)(2,1)}) custom-call(s32[8]{0:T(128)S(1)} %copy-done.5, s32[1]{0:T(128)} %bitcast.own_ref, bf16[4,320,512]{2,1,0:T(8,128)(2,1)S(1)} %collective-permute-done.4.guest, bf16[4,320,512]{2,1,0:T(8,128)(2,1)S(1)} %pack_tokens.3.stay, ...), custom_call_target="tpu_custom_call", output_to_operand_aliasing={{1}: (6, {})} | custom-call | bytes 1024 | tf_op jit(solution)/shard_map/attend/pallas_call | solution.py:270
  62.0 7.4 %collective-permute-done.8.refs_1_ = bf16[4,7168]{1,0:T(4,128)(2,1)S(1)} collective-permute-done((bf16[4,7168]{1,0:T(4,128)(2,1)S(1)}, bf16[4,7168]{1,0:T(4,128)(2,1)S(1)}, u32[]{:S(2)}, u32[]{:S(2)}) %collective-permute-start.8) | collective-permute-done | bytes 57376 | tf_op jit(solution)/shard_map/ppermute | solution.py:536
  69.4 1.4 %broadcast_select_fusion.1.refs_0_ = bf16[1152,512]{1,0:T(8,128)(2,1)S(1)} fusion(bf16[1152,512]{1,0:T(8,128)(2,1)} %collective-permute-done.1, bf16[1152,512]{1,0:T(8,128)(2,1)} %collective-permute-done.3, pred[]{:T(512)S(6)} %and.22), kind=kLoop, calls=%fused_computation.2 | loop fusion | flops 589824 | bytes 3538945 | tf_op jit(solution)/shard_map/jit(_where)/select_n | solution.py:562
  70.9 1.5 %collective-permute-start.10 = (bf16[1152,512]{1,0:T(8,128)(2,1)}, bf16[1152,512]{1,0:T(8,128)(2,1)S(1)}, u32[]{:S(2)}, u32[]{:S(2)}) collective-permute-start(bf16[1152,512]{1,0:T(8,128)(2,1)} %collective-permute-done.9), channel_id=1, source_target_pairs={{4,0},{8,12},{6,2},{10,14},{5,1},{9,13},{7,3},{11,15},{20,16},{24,... | collective-permute-start | bytes 3538952 | tf_op jit(solution)/shard_map/ppermute | solution.py:36
  72.4 1.6 %collective-permute-start.11 = (bf16[256,512]{1,0:T(8,128)(2,1)S(1)}, bf16[256,512]{1,0:T(8,128)(2,1)S(1)}, u32[]{:S(2)}, u32[]{:S(2)}) collective-permute-start(bf16[256,512]{1,0:T(8,128)(2,1)S(1)} %get-tuple-element.60), channel_id=1, source_target_pairs={{0,2},{2,0},{4,6},{6,4},{8,10},{10,8},{12,14},{14,12},{1,3},{3,1},... | collective-permute-start | bytes 786440 | tf_op jit(solution)/shard_map/ppermute | solution.py:28
  73.9 0.2 stack_rows.3.refs_0_
  74.2 0.6 collective-permute-start.13
  74.8 1.6 %collective-permute-start.15 = (bf16[8,7168]{1,0:T(8,128)(2,1)S(1)}, bf16[8,7168]{1,0:T(8,128)(2,1)S(1)}, u32[]{:S(2)}, u32[]{:S(2)}) collective-permute-start(bf16[8,7168]{1,0:T(8,128)(2,1)S(1)} %stack_rows.3.refs_0_), channel_id=1, source_target_pairs={{0,3},{1,2},{2,1},{3,0},{4,7},{5,6},{6,5},{7,4},{8,11},{9,10},{10,... | collective-permute-start | bytes 344072 | tf_op jit(solution)/shard_map/ppermute | solution.py:572
  76.4 6.5 %attend.6 = (bf16[256,512]{1,0:T(8,128)(2,1)}, bf16[8,256,512]{2,1,0:T(8,128)(2,1)}) custom-call(s32[8]{0:T(128)S(1)} %copy-done.5, s32[1]{0:T(128)} %bitcast.own_ref, bf16[4,320,512]{2,1,0:T(8,128)(2,1)S(1)} %collective-permute-done.4.guest, bf16[4,320,512]{2,1,0:T(8,128)(2,1)S(1)} %pack_tokens.3.stay, ...), custom_call_target="tpu_custom_call", output_to_operand_aliasing={{1}: (6, {})} | custom-call | bytes 1024 | tf_op jit(solution)/shard_map/attend/pallas_call | solution.py:270
  82.9 1.1 collective-permute-done.13.refs_1_
  84.0 1.6 %collective-permute-done.15.refs_3_ = bf16[8,7168]{1,0:T(8,128)(2,1)S(1)} collective-permute-done((bf16[8,7168]{1,0:T(8,128)(2,1)S(1)}, bf16[8,7168]{1,0:T(8,128)(2,1)S(1)}, u32[]{:S(2)}, u32[]{:S(2)}) %collective-permute-start.15) | collective-permute-done | bytes 114720 | tf_op jit(solution)/shard_map/ppermute | solution.py:572
  85.6 1.6 %experts.1 = (f32[8,7168]{1,0:T(8,128)S(1)}, bf16[8,7168]{1,0:T(8,128)(2,1)S(1)}, bf16[8,7168]{1,0:T(8,128)(2,1)S(1)}, bf16[8,7168]{1,0:T(8,128)(2,1)S(1)}) custom-call(bf16[8,7168]{1,0:T(8,128)(2,1)S(1)} %stack_rows.3.refs_0_, bf16[8,7168]{1,0:T(8,128)(2,1)S(1)} %collective-permute-done.13.refs_1_, bf16[8,7168]{1,0:T(8,128)(2,1)S(1)} %collective-permute-done.14.refs_2_, ...), custom_call_target="tpu_custom_call" | custom-call | bytes 1024 | tf_op jit(solution)/shard_map/experts/pallas_call | solution.py:442
  87.2 1.6 %collective-permute-start.16 = (bf16[8,7168]{1,0:T(8,128)(2,1)S(1)}, bf16[8,7168]{1,0:T(8,128)(2,1)S(1)}, u32[]{:S(2)}, u32[]{:S(2)}) collective-permute-start(bf16[8,7168]{1,0:T(8,128)(2,1)S(1)} %get-tuple-element.79), channel_id=1, source_target_pairs={{0,2},{1,3},{2,0},{3,1},{4,6},{5,7},{6,4},{7,5},{8,10},{9,11},{10,... | collective-permute-start | bytes 344072 | tf_op jit(solution)/shard_map/ppermute | solution.py:572
  88.8 0.2 collective-permute-start.17
  89.0 0.4 collective-permute-start.18
  89.4 1.5 %collective-permute-start.19 = (bf16[256,512]{1,0:T(8,128)(2,1)}, bf16[256,512]{1,0:T(8,128)(2,1)S(1)}, u32[]{:S(2)}, u32[]{:S(2)}) collective-permute-start(bf16[256,512]{1,0:T(8,128)(2,1)} %get-tuple-element.71), channel_id=1, source_target_pairs={{0,2},{2,0},{4,6},{6,4},{8,10},{10,8},{12,14},{14,12},{1,3},{3,1},... | collective-permute-start | bytes 786440 | tf_op jit(solution)/shard_map/ppermute | solution.py:28
  90.9 11.6 %collective-permute-done.10 = bf16[1152,512]{1,0:T(8,128)(2,1)S(1)} collective-permute-done((bf16[1152,512]{1,0:T(8,128)(2,1)}, bf16[1152,512]{1,0:T(8,128)(2,1)S(1)}, u32[]{:S(2)}, u32[]{:S(2)}) %collective-permute-start.10) | collective-permute-done | bytes 1179680 | tf_op jit(solution)/shard_map/ppermute | solution.py:36
  102.6 1.2 broadcast_select_fusion.refs_0_
  103.7 0.7 fusion.3
  104.5 0.7 fusion.4
  105.1 0.9 collective-permute-start.22
  106.1 2.3 %collective-permute-start.23 = (bf16[2,7168]{1,0:T(2,128)(2,1)S(1)}, bf16[2,7168]{1,0:T(2,128)(2,1)S(1)}, u32[]{:S(2)}, u32[]{:S(2)}) collective-permute-start(bf16[2,7168]{1,0:T(2,128)(2,1)S(1)} %get-tuple-element.102), channel_id=1, source_target_pairs={{0,8},{2,10},{4,12},{6,14},{8,0},{10,2},{12,4},{14,6},{1,9},{3,11}... | collective-permute-start | bytes 86024 | tf_op jit(solution)/shard_map/ppermute | solution.py:536
  108.3 1.2 collective-permute-start.24
  109.6 1.0 slice.19
  110.6 7.6 %attend.7 = (bf16[256,512]{1,0:T(8,128)(2,1)}, bf16[8,256,512]{2,1,0:T(8,128)(2,1)}) custom-call(s32[8]{0:T(128)S(1)} %copy-done.5, s32[1]{0:T(128)} %bitcast.own_ref, bf16[4,320,512]{2,1,0:T(8,128)(2,1)S(1)} %collective-permute-done.4.guest, bf16[4,320,512]{2,1,0:T(8,128)(2,1)S(1)} %pack_tokens.3.stay, ...), custom_call_target="tpu_custom_call", output_to_operand_aliasing={{1}: (6, {})} | custom-call | bytes 1024 | tf_op jit(solution)/shard_map/attend/pallas_call | solution.py:270
  118.2 1.6 %collective-permute-start.21 = (bf16[256,512]{1,0:T(8,128)(2,1)}, bf16[256,512]{1,0:T(8,128)(2,1)S(1)}, u32[]{:S(2)}, u32[]{:S(2)}) collective-permute-start(bf16[256,512]{1,0:T(8,128)(2,1)} %get-tuple-element.87), channel_id=1, source_target_pairs={{0,2},{2,0},{4,6},{6,4},{8,10},{10,8},{12,14},{14,12},{1,3},{3,1},... | collective-permute-start | bytes 786440 | tf_op jit(solution)/shard_map/ppermute | solution.py:28
  119.8 0.8 convert_add_fusion.1
  120.8 0.8 convert_element_type.39
  121.6 4.7 %collective-permute-done.21.refs_3_ = bf16[256,512]{1,0:T(8,128)(2,1)S(1)} collective-permute-done((bf16[256,512]{1,0:T(8,128)(2,1)}, bf16[256,512]{1,0:T(8,128)(2,1)S(1)}, u32[]{:S(2)}, u32[]{:S(2)}) %collective-permute-start.21) | collective-permute-done | bytes 262176 | tf_op jit(solution)/shard_map/ppermute | solution.py:28
  126.3 1.5 %place.1 = bf16[8,256,512]{2,1,0:T(8,128)(2,1)} custom-call(s32[8]{0:T(128)S(1)} %copy-done.5, s32[1]{0:T(128)} %bitcast.own_ref, bf16[256,512]{1,0:T(8,128)(2,1)S(1)} %collective-permute-done.7.refs_0_, bf16[256,512]{1,0:T(8,128)(2,1)S(1)} %collective-permute-done.11.refs_1_, ...), custom_call_target="tpu_custom_call", output_to_operand_aliasing={{}: (6, {})} | custom-call | bytes 1024 | tf_op jit(solution)/shard_map/place/pallas_call | solution.py:309
  (51 shorter events, 0.8 us)
Async XLA Ops:
  0.6 7.1 %copy-start.8 = (bf16[8,2,8192]{2,1,0:T(2,128)(2,1)S(1)}, bf16[8,2,8192]{2,1,0:T(2,128)(2,1)}, u32[]{:S(2)}) copy-start(bf16[8,2,8192]{2,1,0:T(2,128)(2,1)} %param.16) | copy-start | bytes 786436
  0.6 7.3 %copy-start.10 = (bf16[8,2,512]{2,1,0:T(2,128)(2,1)S(1)}, bf16[8,2,512]{2,1,0:T(2,128)(2,1)}, u32[]{:S(2)}) copy-start(bf16[8,2,512]{2,1,0:T(2,128)(2,1)} %param.17) | copy-start | bytes 49156
  0.7 7.3 %copy-start.11 = (bf16[8,2,64]{2,1,0:T(2,128)(2,1)S(1)}, bf16[8,2,64]{2,1,0:T(2,128)(2,1)}, u32[]{:S(2)}) copy-start(bf16[8,2,64]{2,1,0:T(2,128)(2,1)} %param.18) | copy-start | bytes 6148
  0.7 7.3 %copy-start.5 = (s32[8]{0:T(128)S(1)}, s32[8]{0:T(128)}, u32[]{:S(2)}) copy-start(s32[8]{0:T(128)} %slot_ref.13) | copy-start | bytes 100
  3.0 34.7 %collective-permute-start = (bf16[1152,512]{1,0:T(8,128)(2,1)}, bf16[1152,512]{1,0:T(8,128)(2,1)}, u32[]{:S(2)}, u32[]{:S(2)}) collective-permute-start(bf16[1152,512]{1,0:T(8,128)(2,1)} %pack_cache.1.refs_0_), channel_id=1, source_target_pairs={{0,4},{4,0},{8,12},{12,8},{2,6},{6,2},{10,14},{14,10},{1,5},{5,1},... | collective-permute-start | bytes 3538952 | tf_op jit(solution)/shard_map/ppermute | solution.py:36
  6.1 31.6 %collective-permute-start.1 = (bf16[1152,512]{1,0:T(8,128)(2,1)}, bf16[1152,512]{1,0:T(8,128)(2,1)}, u32[]{:S(2)}, u32[]{:S(2)}) collective-permute-start(bf16[1152,512]{1,0:T(8,128)(2,1)} %pack_cache.1.refs_0_), channel_id=1, source_target_pairs={{4,8},{8,4},{6,10},{10,6},{5,9},{9,5},{7,11},{11,7},{20,24},{24,20... | collective-permute-start | bytes 3538952 | tf_op jit(solution)/shard_map/ppermute | solution.py:36
  8.0 1.6 %copy-start = (bf16[8,2,128,512]{3,2,1,0:T(8,128)(2,1)S(1)}, bf16[8,2,128,512]{3,2,1,0:T(8,128)(2,1)}, u32[]{:S(2)}) copy-start(bf16[8,2,128,512]{3,2,1,0:T(8,128)(2,1)} %param.15) | copy-start | bytes 6291460
  9.6 3.8 %copy-start.9 = (bf16[8,2,7168]{2,1,0:T(2,128)(2,1)S(1)}, bf16[8,2,7168]{2,1,0:T(2,128)(2,1)}, u32[]{:S(2)}) copy-start(bf16[8,2,7168]{2,1,0:T(2,128)(2,1)} %param.20) | copy-start | bytes 688132
  9.6 3.9 %copy-start.6 = (s32[8,2,8]{2,1,0:T(2,128)S(1)}, s32[8,2,8]{2,1,0:T(2,128)}, u32[]{:S(2)}) copy-start(s32[8,2,8]{2,1,0:T(2,128)} %param.21) | copy-start | bytes 1540
  9.6 3.9 %copy-start.7 = (f32[8,2,8]{2,1,0:T(2,128)S(1)}, f32[8,2,8]{2,1,0:T(2,128)}, u32[]{:S(2)}) copy-start(f32[8,2,8]{2,1,0:T(2,128)} %param.22) | copy-start | bytes 1540
  11.8 30.5 %collective-permute-start.4 = (bf16[4,320,512]{2,1,0:T(8,128)(2,1)}, bf16[4,320,512]{2,1,0:T(8,128)(2,1)S(1)}, u32[]{:S(2)}, u32[]{:S(2)}) collective-permute-start(bf16[4,320,512]{2,1,0:T(8,128)(2,1)} %pack_tokens.2), channel_id=1, source_target_pairs={{0,2},{2,0},{4,6},{6,4},{8,10},{10,8},{12,14},{14,12},{1,3},{3,1},... | collective-permute-start | bytes 3932168 | tf_op jit(solution)/shard_map/ppermute | solution.py:28
  13.4 28.9 %collective-permute-start.6 = (bf16[1152,512]{1,0:T(8,128)(2,1)}, bf16[1152,512]{1,0:T(8,128)(2,1)}, u32[]{:S(2)}, u32[]{:S(2)}) collective-permute-start(bf16[1152,512]{1,0:T(8,128)(2,1)} %pack_cache.1.refs_0_), channel_id=1, source_target_pairs={{0,1},{1,0},{2,3},{3,2},{4,5},{5,4},{6,7},{7,6},{8,9},{9,8},{10,11... | collective-permute-start | bytes 3538952 | tf_op jit(solution)/shard_map/ppermute | solution.py:28
  13.8 23.8 %collective-permute-start.2 = (bf16[2,7168]{1,0:T(2,128)(2,1)S(1)}, bf16[2,7168]{1,0:T(2,128)(2,1)S(1)}, u32[]{:S(2)}, u32[]{:S(2)}) collective-permute-start(bf16[2,7168]{1,0:T(2,128)(2,1)S(1)} %get-tuple-element.54), channel_id=1, source_target_pairs={{0,8},{2,10},{4,12},{6,14},{8,0},{10,2},{12,4},{14,6},{1,9},{3,11}... | collective-permute-start | bytes 86024 | tf_op jit(solution)/shard_map/ppermute | solution.py:536
  16.8 1.6 %copy-start.1 = (bf16[8,2,128,512]{3,2,1,0:T(8,128)(2,1)S(1)}, bf16[8,2,128,512]{3,2,1,0:T(8,128)(2,1)}, u32[]{:S(2)}) copy-start(bf16[8,2,128,512]{3,2,1,0:T(8,128)(2,1)} %param.15) | copy-start | bytes 6291460
  37.7 17.5 %collective-permute-start.5 = (bf16[1152,512]{1,0:T(8,128)(2,1)}, bf16[1152,512]{1,0:T(8,128)(2,1)}, u32[]{:S(2)}, u32[]{:S(2)}) collective-permute-start(bf16[1152,512]{1,0:T(8,128)(2,1)} %collective-permute-done.refs_0_), channel_id=1, source_target_pairs={{0,1},{1,0},{2,3},{3,2},{4,5},{5,4},{6,7},{7,6},{8,9},{9,8},{10,11... | collective-permute-start | bytes 3538952 | tf_op jit(solution)/shard_map/ppermute | solution.py:28
  37.7 31.7 %collective-permute-start.3 = (bf16[1152,512]{1,0:T(8,128)(2,1)}, bf16[1152,512]{1,0:T(8,128)(2,1)}, u32[]{:S(2)}, u32[]{:S(2)}) collective-permute-start(bf16[1152,512]{1,0:T(8,128)(2,1)} %collective-permute-done.1), channel_id=1, source_target_pairs={{4,0},{8,12},{6,2},{10,14},{5,1},{9,13},{7,3},{11,15},{20,16},{24,... | collective-permute-start | bytes 3538952 | tf_op jit(solution)/shard_map/ppermute | solution.py:36
  39.0 30.4 %collective-permute-start.9 = (bf16[1152,512]{1,0:T(8,128)(2,1)}, bf16[1152,512]{1,0:T(8,128)(2,1)}, u32[]{:S(2)}, u32[]{:S(2)}) collective-permute-start(bf16[1152,512]{1,0:T(8,128)(2,1)} %collective-permute-done.refs_0_), channel_id=1, source_target_pairs={{4,8},{8,4},{6,10},{10,6},{5,9},{9,5},{7,11},{11,7},{20,24},{24,20... | collective-permute-start | bytes 3538952 | tf_op jit(solution)/shard_map/ppermute | solution.py:36
  49.2 20.2 %collective-permute-start.7 = (bf16[256,512]{1,0:T(8,128)(2,1)S(1)}, bf16[256,512]{1,0:T(8,128)(2,1)S(1)}, u32[]{:S(2)}, u32[]{:S(2)}) collective-permute-start(bf16[256,512]{1,0:T(8,128)(2,1)S(1)} %get-tuple-element.61), channel_id=1, source_target_pairs={{0,2},{2,0},{4,6},{6,4},{8,10},{10,8},{12,14},{14,12},{1,3},{3,1},... | collective-permute-start | bytes 786440 | tf_op jit(solution)/shard_map/ppermute | solution.py:28
  51.0 18.3 %collective-permute-start.8 = (bf16[4,7168]{1,0:T(4,128)(2,1)S(1)}, bf16[4,7168]{1,0:T(4,128)(2,1)S(1)}, u32[]{:S(2)}, u32[]{:S(2)}) collective-permute-start(bf16[4,7168]{1,0:T(4,128)(2,1)S(1)} %stack_rows.2.refs_0_), channel_id=1, source_target_pairs={{0,4},{2,6},{4,0},{6,2},{8,12},{10,14},{12,8},{14,10},{1,5},{3,7},... | collective-permute-start | bytes 172040 | tf_op jit(solution)/shard_map/ppermute | solution.py:536
  70.8 4.0 %collective-permute-start.12 = (bf16[1152,512]{1,0:T(8,128)(2,1)S(1)}, bf16[1152,512]{1,0:T(8,128)(2,1)S(1)}, u32[]{:S(2)}, u32[]{:S(2)}) collective-permute-start(bf16[1152,512]{1,0:T(8,128)(2,1)S(1)} %broadcast_select_fusion.1.refs_0_), channel_id=1, source_target_pairs={{0,1},{1,0},{2,3},{3,2},{4,5},{5,4},{6,7},{7,6},{8,9},{9,8},{10,11... | collective-permute-start | bytes 3538952 | tf_op jit(solution)/shard_map/ppermute | solution.py:28
  70.9 31.7 %collective-permute-start.10 = (bf16[1152,512]{1,0:T(8,128)(2,1)}, bf16[1152,512]{1,0:T(8,128)(2,1)S(1)}, u32[]{:S(2)}, u32[]{:S(2)}) collective-permute-start(bf16[1152,512]{1,0:T(8,128)(2,1)} %collective-permute-done.9), channel_id=1, source_target_pairs={{4,0},{8,12},{6,2},{10,14},{5,1},{9,13},{7,3},{11,15},{20,16},{24,... | collective-permute-start | bytes 3538952 | tf_op jit(solution)/shard_map/ppermute | solution.py:36
  72.4 17.1 %collective-permute-start.11 = (bf16[256,512]{1,0:T(8,128)(2,1)S(1)}, bf16[256,512]{1,0:T(8,128)(2,1)S(1)}, u32[]{:S(2)}, u32[]{:S(2)}) collective-permute-start(bf16[256,512]{1,0:T(8,128)(2,1)S(1)} %get-tuple-element.60), channel_id=1, source_target_pairs={{0,2},{2,0},{4,6},{6,4},{8,10},{10,8},{12,14},{14,12},{1,3},{3,1},... | collective-permute-start | bytes 786440 | tf_op jit(solution)/shard_map/ppermute | solution.py:28
  74.2 9.8 %collective-permute-start.13 = (bf16[8,7168]{1,0:T(8,128)(2,1)S(1)}, bf16[8,7168]{1,0:T(8,128)(2,1)S(1)}, u32[]{:S(2)}, u32[]{:S(2)}) collective-permute-start(bf16[8,7168]{1,0:T(8,128)(2,1)S(1)} %stack_rows.3.refs_0_), channel_id=1, source_target_pairs={{0,2},{1,3},{2,0},{3,1},{4,6},{5,7},{6,4},{7,5},{8,10},{9,11},{10,... | collective-permute-start | bytes 344072 | tf_op jit(solution)/shard_map/ppermute | solution.py:572
  74.8 9.2 %collective-permute-start.14 = (bf16[8,7168]{1,0:T(8,128)(2,1)S(1)}, bf16[8,7168]{1,0:T(8,128)(2,1)S(1)}, u32[]{:S(2)}, u32[]{:S(2)}) collective-permute-start(bf16[8,7168]{1,0:T(8,128)(2,1)S(1)} %stack_rows.3.refs_0_), channel_id=1, source_target_pairs={{0,1},{1,0},{2,3},{3,2},{4,5},{5,4},{6,7},{7,6},{8,9},{9,8},{10,11... | collective-permute-start | bytes 344072 | tf_op jit(solution)/shard_map/ppermute | solution.py:572
  74.8 10.9 %collective-permute-start.15 = (bf16[8,7168]{1,0:T(8,128)(2,1)S(1)}, bf16[8,7168]{1,0:T(8,128)(2,1)S(1)}, u32[]{:S(2)}, u32[]{:S(2)}) collective-permute-start(bf16[8,7168]{1,0:T(8,128)(2,1)S(1)} %stack_rows.3.refs_0_), channel_id=1, source_target_pairs={{0,3},{1,2},{2,1},{3,0},{4,7},{5,6},{6,5},{7,4},{8,11},{9,10},{10,... | collective-permute-start | bytes 344072 | tf_op jit(solution)/shard_map/ppermute | solution.py:572
  76.4 9.2 %copy-start.2 = (bf16[1,7168,128]{2,1,0:T(8,128)(2,1)S(1)}, bf16[1,7168,128]{2,1,0:T(8,128)(2,1)}, u32[]{:S(2)}) copy-start(bf16[1,7168,128]{2,1,0:T(8,128)(2,1)} %refs_4_.1) | copy-start | bytes 5505028
  76.4 9.2 %copy-start.3 = (bf16[1,7168,128]{2,1,0:T(8,128)(2,1)S(1)}, bf16[1,7168,128]{2,1,0:T(8,128)(2,1)}, u32[]{:S(2)}) copy-start(bf16[1,7168,128]{2,1,0:T(8,128)(2,1)} %refs_5_.1) | copy-start | bytes 5505028
  76.4 9.2 %copy-start.4 = (bf16[1,128,7168]{2,1,0:T(8,128)(2,1)S(1)}, bf16[1,128,7168]{2,1,0:T(8,128)(2,1)}, u32[]{:S(2)}) copy-start(bf16[1,128,7168]{2,1,0:T(8,128)(2,1)} %refs_6_.1) | copy-start | bytes 5505028
  87.2 15.3 %collective-permute-start.16 = (bf16[8,7168]{1,0:T(8,128)(2,1)S(1)}, bf16[8,7168]{1,0:T(8,128)(2,1)S(1)}, u32[]{:S(2)}, u32[]{:S(2)}) collective-permute-start(bf16[8,7168]{1,0:T(8,128)(2,1)S(1)} %get-tuple-element.79), channel_id=1, source_target_pairs={{0,2},{1,3},{2,0},{3,1},{4,6},{5,7},{6,4},{7,5},{8,10},{9,11},{10,... | collective-permute-start | bytes 344072 | tf_op jit(solution)/shard_map/ppermute | solution.py:572
  88.8 13.8 %collective-permute-start.17 = (bf16[8,7168]{1,0:T(8,128)(2,1)S(1)}, bf16[8,7168]{1,0:T(8,128)(2,1)S(1)}, u32[]{:S(2)}, u32[]{:S(2)}) collective-permute-start(bf16[8,7168]{1,0:T(8,128)(2,1)S(1)} %get-tuple-element.80), channel_id=1, source_target_pairs={{0,1},{1,0},{2,3},{3,2},{4,5},{5,4},{6,7},{7,6},{8,9},{9,8},{10,11... | collective-permute-start | bytes 344072 | tf_op jit(solution)/shard_map/ppermute | solution.py:572
  89.0 13.5 %collective-permute-start.18 = (bf16[8,7168]{1,0:T(8,128)(2,1)S(1)}, bf16[8,7168]{1,0:T(8,128)(2,1)S(1)}, u32[]{:S(2)}, u32[]{:S(2)}) collective-permute-start(bf16[8,7168]{1,0:T(8,128)(2,1)S(1)} %get-tuple-element.81), channel_id=1, source_target_pairs={{0,3},{1,2},{2,1},{3,0},{4,7},{5,6},{6,5},{7,4},{8,11},{9,10},{10,... | collective-permute-start | bytes 344072 | tf_op jit(solution)/shard_map/ppermute | solution.py:572
  89.4 21.2 %collective-permute-start.19 = (bf16[256,512]{1,0:T(8,128)(2,1)}, bf16[256,512]{1,0:T(8,128)(2,1)S(1)}, u32[]{:S(2)}, u32[]{:S(2)}) collective-permute-start(bf16[256,512]{1,0:T(8,128)(2,1)} %get-tuple-element.71), channel_id=1, source_target_pairs={{0,2},{2,0},{4,6},{6,4},{8,10},{10,8},{12,14},{14,12},{1,3},{3,1},... | collective-permute-start | bytes 786440 | tf_op jit(solution)/shard_map/ppermute | solution.py:28
  103.7 6.9 %collective-permute-start.20 = (bf16[1152,512]{1,0:T(8,128)(2,1)}, bf16[1152,512]{1,0:T(8,128)(2,1)}, u32[]{:S(2)}, u32[]{:S(2)}) collective-permute-start(bf16[1152,512]{1,0:T(8,128)(2,1)} %broadcast_select_fusion.refs_0_), channel_id=1, source_target_pairs={{0,1},{1,0},{2,3},{3,2},{4,5},{5,4},{6,7},{7,6},{8,9},{9,8},{10,11... | collective-permute-start | bytes 3538952 | tf_op jit(solution)/shard_map/ppermute | solution.py:28
  105.1 14.6 %collective-permute-start.22 = (bf16[2,7168]{1,0:T(2,128)(2,1)}, bf16[2,7168]{1,0:T(2,128)(2,1)S(1)}, u32[]{:S(2)}, u32[]{:S(2)}) collective-permute-start(bf16[2,7168]{1,0:T(2,128)(2,1)} %get-tuple-element.100), channel_id=1, source_target_pairs={{0,4},{2,6},{4,0},{6,2},{8,12},{10,14},{12,8},{14,10},{1,5},{3,7},... | collective-permute-start | bytes 86024 | tf_op jit(solution)/shard_map/ppermute | solution.py:536
  106.1 13.7 %collective-permute-start.23 = (bf16[2,7168]{1,0:T(2,128)(2,1)S(1)}, bf16[2,7168]{1,0:T(2,128)(2,1)S(1)}, u32[]{:S(2)}, u32[]{:S(2)}) collective-permute-start(bf16[2,7168]{1,0:T(2,128)(2,1)S(1)} %get-tuple-element.102), channel_id=1, source_target_pairs={{0,8},{2,10},{4,12},{6,14},{8,0},{10,2},{12,4},{14,6},{1,9},{3,11}... | collective-permute-start | bytes 86024 | tf_op jit(solution)/shard_map/ppermute | solution.py:536
  108.3 11.4 %collective-permute-start.24 = (bf16[2,7168]{1,0:T(2,128)(2,1)S(1)}, bf16[2,7168]{1,0:T(2,128)(2,1)}, u32[]{:S(2)}, u32[]{:S(2)}) collective-permute-start(bf16[2,7168]{1,0:T(2,128)(2,1)S(1)} %get-tuple-element.101), channel_id=1, source_target_pairs={{0,12},{2,14},{4,8},{6,10},{8,4},{10,6},{12,0},{14,2},{1,13},{3,15... | collective-permute-start | bytes 86024 | tf_op jit(solution)/shard_map/ppermute | solution.py:536
  118.2 8.2 %collective-permute-start.21 = (bf16[256,512]{1,0:T(8,128)(2,1)}, bf16[256,512]{1,0:T(8,128)(2,1)S(1)}, u32[]{:S(2)}, u32[]{:S(2)}) collective-permute-start(bf16[256,512]{1,0:T(8,128)(2,1)} %get-tuple-element.87), channel_id=1, source_target_pairs={{0,2},{2,0},{4,6},{6,4},{8,10},{10,8},{12,14},{14,12},{1,3},{3,1},... | collective-permute-start | bytes 786440 | tf_op jit(solution)/shard_map/ppermute | solution.py:28

commit v10 on v9

--- a/solution.py
+++ b/solution.py
@@ -188,11 +188,15 @@
             row = first + i * grown
             rope_keys[row : row + grown, :] = part.astype(jnp.bfloat16)
 
-    def kernel(slot, has_placed, slot_ref, own_ref, guest, stay, *refs):
-        own_half, other_half = refs[:2]
-        refs = refs[3:] if has_placed else refs[2:]
-        give, placed, rope_keys, query_rope, scores, summed, result, sem = refs
-        tokens = (guest.at[slot], stay.at[slot])
+    def kernel(slot, gives, keeps, has_placed, slot_ref, own_ref, *refs):
+        refs = list(refs)
+        tokens = [refs.pop(0).at[slot] for _ in range(gives + keeps)]
+        own_half, other_half = refs.pop(0), refs.pop(0)
+        if has_placed:
+            refs.pop(0)
+        give = refs.pop(0) if gives else None
+        placed = refs.pop(0) if keeps else None
+        rope_keys, query_rope, scores, summed, result, sem = refs
         matrix = spread_matrix(raw_group, width)
         middle = q_rows + token_rope
         for number, token in enumerate(tokens):
@@ -218,7 +222,7 @@
                     )
                     scores[rows, i * half + first : i * half + first + chunk] = part
                     highs.append(jnp.max(part, axis=1, keepdims=True))
-                high = jnp.concatenate(highs, axis=0)
+                high = jnp.concatenate(highs, axis=0) if len(highs) > 1 else highs[0]
                 peak = high if peak is None else jnp.maximum(peak, high)
         scaled = peak * factor
         total = None
@@ -247,39 +251,47 @@
                 total[rows],
                 summed[rows, :],
             )
-            if number == 0:
+            if number < gives:
                 give[...] = value
             else:
                 result[...] = value
-        row = row_for(slot, 0, slot_ref, own_ref)
-        copy = pltpu.make_async_copy(result, placed.at[row], sem)
-        copy.start()
-        copy.wait()
+        if keeps:
+            row = row_for(slot, 0, slot_ref, own_ref)
+            copy = pltpu.make_async_copy(result, placed.at[row], sem)
+            copy.start()
+            copy.wait()
 
     def call(scalars, slot, guest, stay, caches, placed):
         count = scalars[0].shape[0]
         vmem = pl.BlockSpec(memory_space=pltpu.VMEM)
         anywhere = pl.BlockSpec(memory_space=pl.ANY)
-        operands = [*scalars, guest, stay, *caches]
-        in_specs = [pl.BlockSpec(memory_space=pltpu.SMEM)] * 2 + [vmem] * 4
-        alias = {}
-        if placed is not None:
-            alias = {len(operands): 1}
+        gives, keeps = int(guest is not None), int(stay is not None)
+        n_tok = gives + keeps
+        operands = [x for x in (guest, stay) if x is not None] + [*caches]
+        in_specs = [pl.BlockSpec(memory_space=pltpu.SMEM)] * 2 + [vmem] * len(operands)
+        operands = [*scalars, *operands]
+        out_shape, out_specs, alias = [], [], {}
+        if gives:
+            out_shape.append(jax.ShapeDtypeStruct((q_rows, width), jnp.bfloat16))
+            out_specs.append(vmem)
+        if keeps:
+            out_shape.append(jax.ShapeDtypeStruct((count, q_rows, width), jnp.bfloat16))
+            out_specs.append(anywhere)
+        has_placed = bool(keeps and placed is not None)
+        if has_placed:
+            alias = {len(operands): gives}
             in_specs.append(anywhere)
             operands.append(placed)
         return pl.pallas_call(
-            functools.partial(kernel, slot, placed is not None),
-            out_shape=(
-                jax.ShapeDtypeStruct((q_rows, width), jnp.bfloat16),
-                jax.ShapeDtypeStruct((count, q_rows, width), jnp.bfloat16),
-            ),
+            functools.partial(kernel, slot, gives, keeps, has_placed),
+            out_shape=tuple(out_shape),
             in_specs=in_specs,
-            out_specs=(vmem, anywhere),
+            out_specs=tuple(out_specs),
             scratch_shapes=[
                 pltpu.VMEM((half, LANES), jnp.bfloat16),
-                pltpu.VMEM((2 * q_rows, LANES), jnp.bfloat16),
-                pltpu.VMEM((2 * q_rows, 2 * half), jnp.float32),
-                pltpu.VMEM((2 * q_rows, width), jnp.float32),
+                pltpu.VMEM((n_tok * q_rows, LANES), jnp.bfloat16),
+                pltpu.VMEM((n_tok * q_rows, 2 * half), jnp.float32),
+                pltpu.VMEM((n_tok * q_rows, width), jnp.float32),
                 pltpu.VMEM((q_rows, width), jnp.bfloat16),
                 pltpu.SemaphoreType.DMA,
             ],
@@ -554,10 +566,9 @@
     given_1, placed = attend(scalars, 1, guest, stay, both_halves(cache_a), placed)
     back_1 = swapped(given_1, "branch", 0)
 
-    second_b, given_1, back_0, *rows = lax.optimization_barrier(
-        (second_b, given_1, back_0, *rows)
+    first_c, given_1, back_0, first_b, *rows = lax.optimization_barrier(
+        (first_c, given_1, back_0, first_b, *rows)
     )
-    first_c, second_b = lax.optimization_barrier((first_c, second_b))
     second_c = line_hop(first_c, tok_rows, outward)
     cache_b = jnp.where(middle, first_b, second_b)
     given_2, placed = attend(scalars, 2, guest, stay, both_halves(cache_b), placed)
@@ -591,8 +602,9 @@
         for (k, m), piece in zip(ways, homeward)
     ]
     guest, back_2 = lax.optimization_barrier((guest, back_2))
-    given_3, placed = attend(scalars, 3, guest, stay, cache_c, placed)
+    (given_3,) = attend(scalars, 3, guest, None, cache_c, None)
     back_3 = swapped(given_3, "branch", 0)
+    (placed,) = attend(scalars, 3, None, after(stay, given_3), cache_c, placed)
     homeward = [after(x, given_3).astype(jnp.float32) for x in homeward]
     placed = place(scalars, (back_0, back_1, back_2, back_3), placed)
     attended = placed.reshape(tok_rows, step_count, head_count, width)

time: 129 us -> 127 us (0.984)
  waiting for transfers between devices: 46.3 us -> 42.9 us
  Pallas kernels: 37.4 us -> 40.1 us
    ppermute x9, waiting for transfers between devices: 6.36 us -> 1.64 us  [swapped(): lax.ppermute(x, axis, [(i, i ^ 1 << bit) for i in range(lax.axis_size(axi...]
    pallas_call x4 -> x5, Pallas kernels: 27.8 us -> 30.5 us  [call(): pl.pallas_call(functools.partial(kernel, slot, gives, keeps, has_placed),...]
    ppermute x5, waiting for transfers between devices: 25.5 us -> 28.1 us  [along(): return lax.ppermute(x, 'branch', list(enumerate(there)))]
  transfers between devices with their start and end apart: 25 -> 25, of which waited for: 7 -> 6; matrix products, arithmetic and copies ran while one was open for 4% -> 5% of each run, Pallas kernels for 26% -> 29%
where the time goes in v10:
time: 127 us
  waiting for transfers between devices  42.9 us (34%)
  Pallas kernels  40.1 us (32%)
  starting transfers between devices  32.1 us (25%)
  local copies, waits for them, and re-layouts  5.97 us (5%)
  other arithmetic  4.41 us (3%)
    pallas_call x5, Pallas kernels, call(): pl.pallas_call(functools.partial(kernel, slot, gives, keeps, has_placed),...  30.5 us
    ppermute x5, waiting for transfers between devices, along(): return lax.ppermute(x, 'branch', list(enumerate(there)))  28.1 us
    ppermute x5, starting transfers between devices, along(): return lax.ppermute(x, 'branch', list(enumerate(there)))  10.5 us
    ppermute x5, waiting for transfers between devices, line_hop(): return lax.ppermute(x, 'branch', pairs)  10.4 us
    ppermute x5, starting transfers between devices, line_hop(): return lax.ppermute(x, 'branch', pairs)  9.21 us
    ppermute x9, starting transfers between devices, swapped(): lax.ppermute(x, axis, [(i, i ^ 1 << bit) for i in range(lax.axis_size(axi...  7.94 us
    ppermute x6, starting transfers between devices, around_chip(): return lax.ppermute(x, ('branch', 'expert'), pairs)  4.41 us
    pallas_call x2, Pallas kernels, pack_tokens(): pl.pallas_call(functools.partial(pack_tokens_kernel, parity), out_shape=j...  3.35 us
  transfers between devices with their start and end apart: 25, of which 6 were waited for; matrix products, arithmetic and copies ran while one was open for 5% of the time, Pallas kernels for 29%

profile of v10, /device:TPU:0, one launch (start us, length us, event | category | flops | bytes accessed | tf_op | source)
XLA Modules:
  0.0 126.6 jit_solution(6930084053487098538)
XLA Ops:
  0.7 2.3 %pack_cache.1.refs_2_ = bf16[1152,512]{1,0:T(8,128)(2,1)} custom-call(bf16[1024,512]{1,0:T(8,128)(2,1)} %bitcast.13, bf16[128,512]{1,0:T(8,128)(2,1)} %bitcast.14), custom_call_target="tpu_custom_call" | custom-call | bytes 1024 | tf_op jit(solution)/shard_map/pack_cache/pallas_call | solution.py:52
  3.0 3.1 %collective-permute-start = (bf16[1152,512]{1,0:T(8,128)(2,1)}, bf16[1152,512]{1,0:T(8,128)(2,1)}, u32[]{:S(2)}, u32[]{:S(2)}) collective-permute-start(bf16[1152,512]{1,0:T(8,128)(2,1)} %pack_cache.1.refs_2_), channel_id=1, source_target_pairs={{0,4},{4,0},{8,12},{12,8},{2,6},{6,2},{10,14},{14,10},{1,5},{5,1},... | collective-permute-start | bytes 3538952 | tf_op jit(solution)/shard_map/ppermute | solution.py:36
  6.1 1.7 %collective-permute-start.1 = (bf16[1152,512]{1,0:T(8,128)(2,1)}, bf16[1152,512]{1,0:T(8,128)(2,1)}, u32[]{:S(2)}, u32[]{:S(2)}) collective-permute-start(bf16[1152,512]{1,0:T(8,128)(2,1)} %pack_cache.1.refs_2_), channel_id=1, source_target_pairs={{4,8},{8,4},{6,10},{10,6},{5,9},{9,5},{7,11},{11,7},{20,24},{24,20... | collective-permute-start | bytes 3538952 | tf_op jit(solution)/shard_map/ppermute | solution.py:36
  8.0 1.6 %copy-done = bf16[8,2,128,512]{3,2,1,0:T(8,128)(2,1)S(1)} copy-done((bf16[8,2,128,512]{3,2,1,0:T(8,128)(2,1)S(1)}, bf16[8,2,128,512]{3,2,1,0:T(8,128)(2,1)}, u32[]{:S(2)}) %copy-start) | copy-done | bytes 2097176
  9.6 2.2 %pack_tokens.2 = bf16[4,320,512]{2,1,0:T(8,128)(2,1)} custom-call(s32[8]{0:T(128)S(1)} %copy-done.5, s32[1]{0:T(128)} %bitcast.own_ref, bf16[8,256,512]{2,1,0:T(8,128)(2,1)S(1)} %bitcast.8, bf16[8,32,512]{2,1,0:T(8,128)(2,1)S(1)} %reshape.28.rope_ref, bf16[8,32,512]{2,1,0:T(8,128)(2,1)S(1)} %fusion.2.new_ref), custom_call_target="tpu_custom_call" | custom-call | bytes 1024 | tf_op jit(solution)/shard_map/pack_tokens/pallas_call | solution.py:106
  11.8 1.6 %collective-permute-start.4 = (bf16[4,320,512]{2,1,0:T(8,128)(2,1)}, bf16[4,320,512]{2,1,0:T(8,128)(2,1)S(1)}, u32[]{:S(2)}, u32[]{:S(2)}) collective-permute-start(bf16[4,320,512]{2,1,0:T(8,128)(2,1)} %pack_tokens.2), channel_id=1, source_target_pairs={{0,2},{2,0},{4,6},{6,4},{8,10},{10,8},{12,14},{14,12},{1,3},{3,1},... | collective-permute-start | bytes 3932168 | tf_op jit(solution)/shard_map/ppermute | solution.py:28
  13.5 0.3 dispatch.1
  13.8 2.9 %collective-permute-start.2 = (bf16[2,7168]{1,0:T(2,128)(2,1)S(1)}, bf16[2,7168]{1,0:T(2,128)(2,1)S(1)}, u32[]{:S(2)}, u32[]{:S(2)}) collective-permute-start(bf16[2,7168]{1,0:T(2,128)(2,1)S(1)} %get-tuple-element.52), channel_id=1, source_target_pairs={{0,8},{2,10},{4,12},{6,14},{8,0},{10,2},{12,4},{14,6},{1,9},{3,11}... | collective-permute-start | bytes 86024 | tf_op jit(solution)/shard_map/ppermute | solution.py:548
  16.8 1.6 %copy-done.1 = bf16[8,2,128,512]{3,2,1,0:T(8,128)(2,1)S(1)} copy-done((bf16[8,2,128,512]{3,2,1,0:T(8,128)(2,1)S(1)}, bf16[8,2,128,512]{3,2,1,0:T(8,128)(2,1)}, u32[]{:S(2)}) %copy-start.1) | copy-done | bytes 2097176
  18.4 1.1 pack_tokens.3.refs_1_.refs_0_
  19.5 18.2 %collective-permute-done.2.refs_1_ = bf16[2,7168]{1,0:T(2,128)(2,1)S(1)} collective-permute-done((bf16[2,7168]{1,0:T(2,128)(2,1)S(1)}, bf16[2,7168]{1,0:T(2,128)(2,1)S(1)}, u32[]{:S(2)}, u32[]{:S(2)}) %collective-permute-start.2) | collective-permute-done | bytes 28704 | tf_op jit(solution)/shard_map/ppermute | solution.py:548
  37.7 1.7 %collective-permute-start.3 = (bf16[1152,512]{1,0:T(8,128)(2,1)}, bf16[1152,512]{1,0:T(8,128)(2,1)}, u32[]{:S(2)}, u32[]{:S(2)}) collective-permute-start(bf16[1152,512]{1,0:T(8,128)(2,1)} %collective-permute-done.refs_2_), channel_id=1, source_target_pairs={{4,8},{8,4},{6,10},{10,6},{5,9},{9,5},{7,11},{11,7},{20,24},{24,20... | collective-permute-start | bytes 3538952 | tf_op jit(solution)/shard_map/ppermute | solution.py:36
  39.4 1.3 %collective-permute-start.11 = (bf16[1152,512]{1,0:T(8,128)(2,1)}, bf16[1152,512]{1,0:T(8,128)(2,1)}, u32[]{:S(2)}, u32[]{:S(2)}) collective-permute-start(bf16[1152,512]{1,0:T(8,128)(2,1)} %collective-permute-done.1), channel_id=1, source_target_pairs={{4,0},{8,12},{6,2},{10,14},{5,1},{9,13},{7,3},{11,15},{20,16},{24,... | collective-permute-start | bytes 3538952 | tf_op jit(solution)/shard_map/ppermute | solution.py:36
  40.7 1.6 %collective-permute-done.4.refs_0_ = bf16[4,320,512]{2,1,0:T(8,128)(2,1)S(1)} collective-permute-done((bf16[4,320,512]{2,1,0:T(8,128)(2,1)}, bf16[4,320,512]{2,1,0:T(8,128)(2,1)S(1)}, u32[]{:S(2)}, u32[]{:S(2)}) %collective-permute-start.4) | collective-permute-done | bytes 1310752 | tf_op jit(solution)/shard_map/ppermute | solution.py:28
  42.3 6.9 %attend.5 = (bf16[256,512]{1,0:T(8,128)(2,1)S(1)}, bf16[8,256,512]{2,1,0:T(8,128)(2,1)}) custom-call(s32[8]{0:T(128)S(1)} %copy-done.5, s32[1]{0:T(128)} %bitcast.own_ref, bf16[4,320,512]{2,1,0:T(8,128)(2,1)S(1)} %collective-permute-done.4.refs_0_, bf16[4,320,512]{2,1,0:T(8,128)(2,1)S(1)} %pack_tokens.3.refs_1_.refs_0_, ...), custom_call_target="tpu_custom_call" | custom-call | bytes 1024 | tf_op jit(solution)/shard_map/attend/pallas_call | solution.py:285
  49.2 1.6 %collective-permute-start.7 = (bf16[256,512]{1,0:T(8,128)(2,1)S(1)}, bf16[256,512]{1,0:T(8,128)(2,1)S(1)}, u32[]{:S(2)}, u32[]{:S(2)}) collective-permute-start(bf16[256,512]{1,0:T(8,128)(2,1)S(1)} %get-tuple-element.59), channel_id=1, source_target_pairs={{0,2},{2,0},{4,6},{6,4},{8,10},{10,8},{12,14},{14,12},{1,3},{3,1},... | collective-permute-start | bytes 786440 | tf_op jit(solution)/shard_map/ppermute | solution.py:28
  50.7 0.3 stack_rows.2.refs_0_
  51.0 3.2 %collective-permute-start.8 = (bf16[4,7168]{1,0:T(4,128)(2,1)S(1)}, bf16[4,7168]{1,0:T(4,128)(2,1)S(1)}, u32[]{:S(2)}, u32[]{:S(2)}) collective-permute-start(bf16[4,7168]{1,0:T(4,128)(2,1)S(1)} %stack_rows.2.refs_0_), channel_id=1, source_target_pairs={{0,4},{2,6},{4,0},{6,2},{8,12},{10,14},{12,8},{14,10},{1,5},{3,7},... | collective-permute-start | bytes 172040 | tf_op jit(solution)/shard_map/ppermute | solution.py:548
  54.2 6.9 %attend.6 = (bf16[256,512]{1,0:T(8,128)(2,1)S(1)}, bf16[8,256,512]{2,1,0:T(8,128)(2,1)}) custom-call(s32[8]{0:T(128)S(1)} %copy-done.5, s32[1]{0:T(128)} %bitcast.own_ref, bf16[4,320,512]{2,1,0:T(8,128)(2,1)S(1)} %collective-permute-done.4.refs_0_, bf16[4,320,512]{2,1,0:T(8,128)(2,1)S(1)} %pack_tokens.3.refs_1_.refs_0_, ...), custom_call_target="tpu_custom_call", output_to_operand_aliasing={{1}: (6, {})} | custom-call | bytes 1024 | tf_op jit(solution)/shard_map/attend/pallas_call | solution.py:285
  61.1 10.0 %collective-permute-done.8.refs_1_ = bf16[4,7168]{1,0:T(4,128)(2,1)S(1)} collective-permute-done((bf16[4,7168]{1,0:T(4,128)(2,1)S(1)}, bf16[4,7168]{1,0:T(4,128)(2,1)S(1)}, u32[]{:S(2)}, u32[]{:S(2)}) %collective-permute-start.8) | collective-permute-done | bytes 57376 | tf_op jit(solution)/shard_map/ppermute | solution.py:548
  71.1 1.4 %broadcast_select_fusion.1.refs_2_ = bf16[1152,512]{1,0:T(8,128)(2,1)S(1)} fusion(bf16[1152,512]{1,0:T(8,128)(2,1)} %collective-permute-done.1, bf16[1152,512]{1,0:T(8,128)(2,1)} %collective-permute-done.11, pred[]{:T(512)S(6)} %and.22), kind=kLoop, calls=%fused_computation.2 | loop fusion | flops 589824 | bytes 3538945 | tf_op jit(solution)/shard_map/jit(_where)/select_n | solution.py:573
  72.6 1.5 %collective-permute-start.9 = (bf16[1152,512]{1,0:T(8,128)(2,1)}, bf16[1152,512]{1,0:T(8,128)(2,1)S(1)}, u32[]{:S(2)}, u32[]{:S(2)}) collective-permute-start(bf16[1152,512]{1,0:T(8,128)(2,1)} %collective-permute-done.3), channel_id=1, source_target_pairs={{4,0},{8,12},{6,2},{10,14},{5,1},{9,13},{7,3},{11,15},{20,16},{24,... | collective-permute-start | bytes 3538952 | tf_op jit(solution)/shard_map/ppermute | solution.py:36
  74.1 1.6 %collective-permute-start.10 = (bf16[256,512]{1,0:T(8,128)(2,1)S(1)}, bf16[256,512]{1,0:T(8,128)(2,1)S(1)}, u32[]{:S(2)}, u32[]{:S(2)}) collective-permute-start(bf16[256,512]{1,0:T(8,128)(2,1)S(1)} %get-tuple-element.58), channel_id=1, source_target_pairs={{0,2},{2,0},{4,6},{6,4},{8,10},{10,8},{12,14},{14,12},{1,3},{3,1},... | collective-permute-start | bytes 786440 | tf_op jit(solution)/shard_map/ppermute | solution.py:28
  75.6 0.2 stack_rows.3.refs_0_
  75.9 0.6 collective-permute-start.13
  76.5 1.6 %collective-permute-start.15 = (bf16[8,7168]{1,0:T(8,128)(2,1)S(1)}, bf16[8,7168]{1,0:T(8,128)(2,1)S(1)}, u32[]{:S(2)}, u32[]{:S(2)}) collective-permute-start(bf16[8,7168]{1,0:T(8,128)(2,1)S(1)} %stack_rows.3.refs_0_), channel_id=1, source_target_pairs={{0,3},{1,2},{2,1},{3,0},{4,7},{5,6},{6,5},{7,4},{8,11},{9,10},{10,... | collective-permute-start | bytes 344072 | tf_op jit(solution)/shard_map/ppermute | solution.py:583
  78.1 6.5 %attend.7 = (bf16[256,512]{1,0:T(8,128)(2,1)}, bf16[8,256,512]{2,1,0:T(8,128)(2,1)}) custom-call(s32[8]{0:T(128)S(1)} %copy-done.5, s32[1]{0:T(128)} %bitcast.own_ref, bf16[4,320,512]{2,1,0:T(8,128)(2,1)S(1)} %collective-permute-done.4.refs_0_, bf16[4,320,512]{2,1,0:T(8,128)(2,1)S(1)} %pack_tokens.3.refs_1_.refs_0_, ...), custom_call_target="tpu_custom_call", output_to_operand_aliasing={{1}: (6, {})} | custom-call | bytes 1024 | tf_op jit(solution)/shard_map/attend/pallas_call | solution.py:285
  84.6 1.1 collective-permute-done.13.refs_1_
  85.7 1.6 %collective-permute-done.15.refs_3_ = bf16[8,7168]{1,0:T(8,128)(2,1)S(1)} collective-permute-done((bf16[8,7168]{1,0:T(8,128)(2,1)S(1)}, bf16[8,7168]{1,0:T(8,128)(2,1)S(1)}, u32[]{:S(2)}, u32[]{:S(2)}) %collective-permute-start.15) | collective-permute-done | bytes 114720 | tf_op jit(solution)/shard_map/ppermute | solution.py:583
  87.3 1.6 %experts.1 = (f32[8,7168]{1,0:T(8,128)S(1)}, bf16[8,7168]{1,0:T(8,128)(2,1)S(1)}, bf16[8,7168]{1,0:T(8,128)(2,1)S(1)}, bf16[8,7168]{1,0:T(8,128)(2,1)S(1)}) custom-call(bf16[8,7168]{1,0:T(8,128)(2,1)S(1)} %stack_rows.3.refs_0_, bf16[8,7168]{1,0:T(8,128)(2,1)S(1)} %collective-permute-done.13.refs_1_, bf16[8,7168]{1,0:T(8,128)(2,1)S(1)} %collective-permute-done.14.refs_2_, ...), custom_call_target="tpu_custom_call" | custom-call | bytes 1024 | tf_op jit(solution)/shard_map/experts/pallas_call | solution.py:454
  88.9 1.6 %collective-permute-start.16 = (bf16[8,7168]{1,0:T(8,128)(2,1)S(1)}, bf16[8,7168]{1,0:T(8,128)(2,1)S(1)}, u32[]{:S(2)}, u32[]{:S(2)}) collective-permute-start(bf16[8,7168]{1,0:T(8,128)(2,1)S(1)} %get-tuple-element.76), channel_id=1, source_target_pairs={{0,2},{1,3},{2,0},{3,1},{4,6},{5,7},{6,4},{7,5},{8,10},{9,11},{10,... | collective-permute-start | bytes 344072 | tf_op jit(solution)/shard_map/ppermute | solution.py:583
  90.5 0.2 collective-permute-start.17
  90.7 0.4 collective-permute-start.18
  91.1 1.5 %collective-permute-start.19 = (bf16[256,512]{1,0:T(8,128)(2,1)}, bf16[256,512]{1,0:T(8,128)(2,1)S(1)}, u32[]{:S(2)}, u32[]{:S(2)}) collective-permute-start(bf16[256,512]{1,0:T(8,128)(2,1)} %get-tuple-element.68), channel_id=1, source_target_pairs={{0,2},{2,0},{4,6},{6,4},{8,10},{10,8},{12,14},{14,12},{1,3},{3,1},... | collective-permute-start | bytes 786440 | tf_op jit(solution)/shard_map/ppermute | solution.py:28
  92.6 10.4 %collective-permute-done.9 = bf16[1152,512]{1,0:T(8,128)(2,1)S(1)} collective-permute-done((bf16[1152,512]{1,0:T(8,128)(2,1)}, bf16[1152,512]{1,0:T(8,128)(2,1)S(1)}, u32[]{:S(2)}, u32[]{:S(2)}) %collective-permute-start.9) | collective-permute-done | bytes 1179680 | tf_op jit(solution)/shard_map/ppermute | solution.py:36
  103.0 1.2 broadcast_select_fusion.refs_1_
  104.2 0.7 fusion.3
  105.0 0.7 fusion.4
  105.7 0.9 collective-permute-start.22
  106.6 2.3 %collective-permute-start.23 = (bf16[2,7168]{1,0:T(2,128)(2,1)S(1)}, bf16[2,7168]{1,0:T(2,128)(2,1)S(1)}, u32[]{:S(2)}, u32[]{:S(2)}) collective-permute-start(bf16[2,7168]{1,0:T(2,128)(2,1)S(1)} %get-tuple-element.98), channel_id=1, source_target_pairs={{0,8},{2,10},{4,12},{6,14},{8,0},{10,2},{12,4},{14,6},{1,9},{3,11}... | collective-permute-start | bytes 86024 | tf_op jit(solution)/shard_map/ppermute | solution.py:548
  108.9 1.2 collective-permute-start.24
  110.1 1.0 slice.19
  111.1 5.2 %attend.8 = bf16[256,512]{1,0:T(8,128)(2,1)} custom-call(s32[8]{0:T(128)S(1)} %copy-done.5, s32[1]{0:T(128)} %bitcast.own_ref, bf16[4,320,512]{2,1,0:T(8,128)(2,1)S(1)} %collective-permute-done.4.refs_0_, bf16[1152,512]{1,0:T(8,128)(2,1)} %broadcast_select_fusion.refs_1_, bf16[1152,512]{1,0:T(8,128)(2,1)} %collective-permute-done.20.refs_2_), custom_call_target="tpu_custom_call" | custom-call | bytes 1024 | tf_op jit(solution)/shard_map/attend/pallas_call | solution.py:285
  116.3 1.6 %collective-permute-start.21 = (bf16[256,512]{1,0:T(8,128)(2,1)}, bf16[256,512]{1,0:T(8,128)(2,1)S(1)}, u32[]{:S(2)}, u32[]{:S(2)}) collective-permute-start(bf16[256,512]{1,0:T(8,128)(2,1)} %attend.8), channel_id=1, source_target_pairs={{0,2},{2,0},{4,6},{6,4},{8,10},{10,8},{12,14},{14,12},{1,3},{3,1},... | collective-permute-start | bytes 786440 | tf_op jit(solution)/shard_map/ppermute | solution.py:28
  117.9 0.8 convert_add_fusion.1
  118.9 0.8 convert_element_type.39
  119.7 5.2 %attend.9.refs_4_ = bf16[8,256,512]{2,1,0:T(8,128)(2,1)} custom-call(s32[8]{0:T(128)S(1)} %copy-done.5, s32[1]{0:T(128)} %bitcast.own_ref, bf16[4,320,512]{2,1,0:T(8,128)(2,1)S(1)} %pack_tokens.3.refs_1_.refs_0_, bf16[1152,512]{1,0:T(8,128)(2,1)} %broadcast_select_fusion.refs_1_, ...), custom_call_target="tpu_custom_call", output_to_operand_aliasing={{}: (5, {})} | custom-call | bytes 1024 | tf_op jit(solution)/shard_map/attend/pallas_call | solution.py:285
  124.9 1.6 %place.1 = bf16[8,256,512]{2,1,0:T(8,128)(2,1)} custom-call(s32[8]{0:T(128)S(1)} %copy-done.5, s32[1]{0:T(128)} %bitcast.own_ref, bf16[256,512]{1,0:T(8,128)(2,1)S(1)} %collective-permute-done.7.refs_0_, bf16[256,512]{1,0:T(8,128)(2,1)S(1)} %collective-permute-done.10.refs_1_, ...), custom_call_target="tpu_custom_call", output_to_operand_aliasing={{}: (6, {})} | custom-call | bytes 1024 | tf_op jit(solution)/shard_map/place/pallas_call | solution.py:321
  (52 shorter events, 0.8 us)
Async XLA Ops:
  0.6 7.1 %copy-start.8 = (bf16[8,2,8192]{2,1,0:T(2,128)(2,1)S(1)}, bf16[8,2,8192]{2,1,0:T(2,128)(2,1)}, u32[]{:S(2)}) copy-start(bf16[8,2,8192]{2,1,0:T(2,128)(2,1)} %param.16) | copy-start | bytes 786436
  0.6 7.3 %copy-start.10 = (bf16[8,2,512]{2,1,0:T(2,128)(2,1)S(1)}, bf16[8,2,512]{2,1,0:T(2,128)(2,1)}, u32[]{:S(2)}) copy-start(bf16[8,2,512]{2,1,0:T(2,128)(2,1)} %param.17) | copy-start | bytes 49156
  0.7 7.3 %copy-start.11 = (bf16[8,2,64]{2,1,0:T(2,128)(2,1)S(1)}, bf16[8,2,64]{2,1,0:T(2,128)(2,1)}, u32[]{:S(2)}) copy-start(bf16[8,2,64]{2,1,0:T(2,128)(2,1)} %param.18) | copy-start | bytes 6148
  0.7 7.3 %copy-start.5 = (s32[8]{0:T(128)S(1)}, s32[8]{0:T(128)}, u32[]{:S(2)}) copy-start(s32[8]{0:T(128)} %slot_ref.15) | copy-start | bytes 100
  3.0 34.7 %collective-permute-start = (bf16[1152,512]{1,0:T(8,128)(2,1)}, bf16[1152,512]{1,0:T(8,128)(2,1)}, u32[]{:S(2)}, u32[]{:S(2)}) collective-permute-start(bf16[1152,512]{1,0:T(8,128)(2,1)} %pack_cache.1.refs_2_), channel_id=1, source_target_pairs={{0,4},{4,0},{8,12},{12,8},{2,6},{6,2},{10,14},{14,10},{1,5},{5,1},... | collective-permute-start | bytes 3538952 | tf_op jit(solution)/shard_map/ppermute | solution.py:36
  6.1 31.6 %collective-permute-start.1 = (bf16[1152,512]{1,0:T(8,128)(2,1)}, bf16[1152,512]{1,0:T(8,128)(2,1)}, u32[]{:S(2)}, u32[]{:S(2)}) collective-permute-start(bf16[1152,512]{1,0:T(8,128)(2,1)} %pack_cache.1.refs_2_), channel_id=1, source_target_pairs={{4,8},{8,4},{6,10},{10,6},{5,9},{9,5},{7,11},{11,7},{20,24},{24,20... | collective-permute-start | bytes 3538952 | tf_op jit(solution)/shard_map/ppermute | solution.py:36
  8.0 1.6 %copy-start = (bf16[8,2,128,512]{3,2,1,0:T(8,128)(2,1)S(1)}, bf16[8,2,128,512]{3,2,1,0:T(8,128)(2,1)}, u32[]{:S(2)}) copy-start(bf16[8,2,128,512]{3,2,1,0:T(8,128)(2,1)} %param.15) | copy-start | bytes 6291460
  9.6 3.8 %copy-start.9 = (bf16[8,2,7168]{2,1,0:T(2,128)(2,1)S(1)}, bf16[8,2,7168]{2,1,0:T(2,128)(2,1)}, u32[]{:S(2)}) copy-start(bf16[8,2,7168]{2,1,0:T(2,128)(2,1)} %param.20) | copy-start | bytes 688132
  9.6 3.9 %copy-start.6 = (s32[8,2,8]{2,1,0:T(2,128)S(1)}, s32[8,2,8]{2,1,0:T(2,128)}, u32[]{:S(2)}) copy-start(s32[8,2,8]{2,1,0:T(2,128)} %param.21) | copy-start | bytes 1540
  9.6 3.9 %copy-start.7 = (f32[8,2,8]{2,1,0:T(2,128)S(1)}, f32[8,2,8]{2,1,0:T(2,128)}, u32[]{:S(2)}) copy-start(f32[8,2,8]{2,1,0:T(2,128)} %param.22) | copy-start | bytes 1540
  11.8 30.5 %collective-permute-start.4 = (bf16[4,320,512]{2,1,0:T(8,128)(2,1)}, bf16[4,320,512]{2,1,0:T(8,128)(2,1)S(1)}, u32[]{:S(2)}, u32[]{:S(2)}) collective-permute-start(bf16[4,320,512]{2,1,0:T(8,128)(2,1)} %pack_tokens.2), channel_id=1, source_target_pairs={{0,2},{2,0},{4,6},{6,4},{8,10},{10,8},{12,14},{14,12},{1,3},{3,1},... | collective-permute-start | bytes 3932168 | tf_op jit(solution)/shard_map/ppermute | solution.py:28
  13.4 28.9 %collective-permute-start.6 = (bf16[1152,512]{1,0:T(8,128)(2,1)}, bf16[1152,512]{1,0:T(8,128)(2,1)}, u32[]{:S(2)}, u32[]{:S(2)}) collective-permute-start(bf16[1152,512]{1,0:T(8,128)(2,1)} %pack_cache.1.refs_2_), channel_id=1, source_target_pairs={{0,1},{1,0},{2,3},{3,2},{4,5},{5,4},{6,7},{7,6},{8,9},{9,8},{10,11... | collective-permute-start | bytes 3538952 | tf_op jit(solution)/shard_map/ppermute | solution.py:28
  13.8 23.8 %collective-permute-start.2 = (bf16[2,7168]{1,0:T(2,128)(2,1)S(1)}, bf16[2,7168]{1,0:T(2,128)(2,1)S(1)}, u32[]{:S(2)}, u32[]{:S(2)}) collective-permute-start(bf16[2,7168]{1,0:T(2,128)(2,1)S(1)} %get-tuple-element.52), channel_id=1, source_target_pairs={{0,8},{2,10},{4,12},{6,14},{8,0},{10,2},{12,4},{14,6},{1,9},{3,11}... | collective-permute-start | bytes 86024 | tf_op jit(solution)/shard_map/ppermute | solution.py:548
  16.8 1.6 %copy-start.1 = (bf16[8,2,128,512]{3,2,1,0:T(8,128)(2,1)S(1)}, bf16[8,2,128,512]{3,2,1,0:T(8,128)(2,1)}, u32[]{:S(2)}) copy-start(bf16[8,2,128,512]{3,2,1,0:T(8,128)(2,1)} %param.15) | copy-start | bytes 6291460
  37.7 16.5 %collective-permute-start.5 = (bf16[1152,512]{1,0:T(8,128)(2,1)}, bf16[1152,512]{1,0:T(8,128)(2,1)}, u32[]{:S(2)}, u32[]{:S(2)}) collective-permute-start(bf16[1152,512]{1,0:T(8,128)(2,1)} %collective-permute-done.refs_2_), channel_id=1, source_target_pairs={{0,1},{1,0},{2,3},{3,2},{4,5},{5,4},{6,7},{7,6},{8,9},{9,8},{10,11... | collective-permute-start | bytes 3538952 | tf_op jit(solution)/shard_map/ppermute | solution.py:28
  37.7 33.4 %collective-permute-start.3 = (bf16[1152,512]{1,0:T(8,128)(2,1)}, bf16[1152,512]{1,0:T(8,128)(2,1)}, u32[]{:S(2)}, u32[]{:S(2)}) collective-permute-start(bf16[1152,512]{1,0:T(8,128)(2,1)} %collective-permute-done.refs_2_), channel_id=1, source_target_pairs={{4,8},{8,4},{6,10},{10,6},{5,9},{9,5},{7,11},{11,7},{20,24},{24,20... | collective-permute-start | bytes 3538952 | tf_op jit(solution)/shard_map/ppermute | solution.py:36
  39.4 31.7 %collective-permute-start.11 = (bf16[1152,512]{1,0:T(8,128)(2,1)}, bf16[1152,512]{1,0:T(8,128)(2,1)}, u32[]{:S(2)}, u32[]{:S(2)}) collective-permute-start(bf16[1152,512]{1,0:T(8,128)(2,1)} %collective-permute-done.1), channel_id=1, source_target_pairs={{4,0},{8,12},{6,2},{10,14},{5,1},{9,13},{7,3},{11,15},{20,16},{24,... | collective-permute-start | bytes 3538952 | tf_op jit(solution)/shard_map/ppermute | solution.py:36
  49.2 21.9 %collective-permute-start.7 = (bf16[256,512]{1,0:T(8,128)(2,1)S(1)}, bf16[256,512]{1,0:T(8,128)(2,1)S(1)}, u32[]{:S(2)}, u32[]{:S(2)}) collective-permute-start(bf16[256,512]{1,0:T(8,128)(2,1)S(1)} %get-tuple-element.59), channel_id=1, source_target_pairs={{0,2},{2,0},{4,6},{6,4},{8,10},{10,8},{12,14},{14,12},{1,3},{3,1},... | collective-permute-start | bytes 786440 | tf_op jit(solution)/shard_map/ppermute | solution.py:28
  51.0 20.1 %collective-permute-start.8 = (bf16[4,7168]{1,0:T(4,128)(2,1)S(1)}, bf16[4,7168]{1,0:T(4,128)(2,1)S(1)}, u32[]{:S(2)}, u32[]{:S(2)}) collective-permute-start(bf16[4,7168]{1,0:T(4,128)(2,1)S(1)} %stack_rows.2.refs_0_), channel_id=1, source_target_pairs={{0,4},{2,6},{4,0},{6,2},{8,12},{10,14},{12,8},{14,10},{1,5},{3,7},... | collective-permute-start | bytes 172040 | tf_op jit(solution)/shard_map/ppermute | solution.py:548
  72.5 4.0 %collective-permute-start.12 = (bf16[1152,512]{1,0:T(8,128)(2,1)S(1)}, bf16[1152,512]{1,0:T(8,128)(2,1)S(1)}, u32[]{:S(2)}, u32[]{:S(2)}) collective-permute-start(bf16[1152,512]{1,0:T(8,128)(2,1)S(1)} %broadcast_select_fusion.1.refs_2_), channel_id=1, source_target_pairs={{0,1},{1,0},{2,3},{3,2},{4,5},{5,4},{6,7},{7,6},{8,9},{9,8},{10,11... | collective-permute-start | bytes 3538952 | tf_op jit(solution)/shard_map/ppermute | solution.py:28
  72.6 30.5 %collective-permute-start.9 = (bf16[1152,512]{1,0:T(8,128)(2,1)}, bf16[1152,512]{1,0:T(8,128)(2,1)S(1)}, u32[]{:S(2)}, u32[]{:S(2)}) collective-permute-start(bf16[1152,512]{1,0:T(8,128)(2,1)} %collective-permute-done.3), channel_id=1, source_target_pairs={{4,0},{8,12},{6,2},{10,14},{5,1},{9,13},{7,3},{11,15},{20,16},{24,... | collective-permute-start | bytes 3538952 | tf_op jit(solution)/shard_map/ppermute | solution.py:36
  74.1 17.1 %collective-permute-start.10 = (bf16[256,512]{1,0:T(8,128)(2,1)S(1)}, bf16[256,512]{1,0:T(8,128)(2,1)S(1)}, u32[]{:S(2)}, u32[]{:S(2)}) collective-permute-start(bf16[256,512]{1,0:T(8,128)(2,1)S(1)} %get-tuple-element.58), channel_id=1, source_target_pairs={{0,2},{2,0},{4,6},{6,4},{8,10},{10,8},{12,14},{14,12},{1,3},{3,1},... | collective-permute-start | bytes 786440 | tf_op jit(solution)/shard_map/ppermute | solution.py:28
  75.9 9.8 %collective-permute-start.13 = (bf16[8,7168]{1,0:T(8,128)(2,1)S(1)}, bf16[8,7168]{1,0:T(8,128)(2,1)S(1)}, u32[]{:S(2)}, u32[]{:S(2)}) collective-permute-start(bf16[8,7168]{1,0:T(8,128)(2,1)S(1)} %stack_rows.3.refs_0_), channel_id=1, source_target_pairs={{0,2},{1,3},{2,0},{3,1},{4,6},{5,7},{6,4},{7,5},{8,10},{9,11},{10,... | collective-permute-start | bytes 344072 | tf_op jit(solution)/shard_map/ppermute | solution.py:583
  76.5 9.2 %collective-permute-start.14 = (bf16[8,7168]{1,0:T(8,128)(2,1)S(1)}, bf16[8,7168]{1,0:T(8,128)(2,1)S(1)}, u32[]{:S(2)}, u32[]{:S(2)}) collective-permute-start(bf16[8,7168]{1,0:T(8,128)(2,1)S(1)} %stack_rows.3.refs_0_), channel_id=1, source_target_pairs={{0,1},{1,0},{2,3},{3,2},{4,5},{5,4},{6,7},{7,6},{8,9},{9,8},{10,11... | collective-permute-start | bytes 344072 | tf_op jit(solution)/shard_map/ppermute | solution.py:583
  76.5 10.8 %collective-permute-start.15 = (bf16[8,7168]{1,0:T(8,128)(2,1)S(1)}, bf16[8,7168]{1,0:T(8,128)(2,1)S(1)}, u32[]{:S(2)}, u32[]{:S(2)}) collective-permute-start(bf16[8,7168]{1,0:T(8,128)(2,1)S(1)} %stack_rows.3.refs_0_), channel_id=1, source_target_pairs={{0,3},{1,2},{2,1},{3,0},{4,7},{5,6},{6,5},{7,4},{8,11},{9,10},{10,... | collective-permute-start | bytes 344072 | tf_op jit(solution)/shard_map/ppermute | solution.py:583
  78.1 9.2 %copy-start.2 = (bf16[1,7168,128]{2,1,0:T(8,128)(2,1)S(1)}, bf16[1,7168,128]{2,1,0:T(8,128)(2,1)}, u32[]{:S(2)}) copy-start(bf16[1,7168,128]{2,1,0:T(8,128)(2,1)} %refs_4_.1) | copy-start | bytes 5505028
  78.1 9.2 %copy-start.3 = (bf16[1,7168,128]{2,1,0:T(8,128)(2,1)S(1)}, bf16[1,7168,128]{2,1,0:T(8,128)(2,1)}, u32[]{:S(2)}) copy-start(bf16[1,7168,128]{2,1,0:T(8,128)(2,1)} %refs_5_.1) | copy-start | bytes 5505028
  78.1 9.2 %copy-start.4 = (bf16[1,128,7168]{2,1,0:T(8,128)(2,1)S(1)}, bf16[1,128,7168]{2,1,0:T(8,128)(2,1)}, u32[]{:S(2)}) copy-start(bf16[1,128,7168]{2,1,0:T(8,128)(2,1)} %refs_6_.1) | copy-start | bytes 5505028
  88.9 14.1 %collective-permute-start.16 = (bf16[8,7168]{1,0:T(8,128)(2,1)S(1)}, bf16[8,7168]{1,0:T(8,128)(2,1)S(1)}, u32[]{:S(2)}, u32[]{:S(2)}) collective-permute-start(bf16[8,7168]{1,0:T(8,128)(2,1)S(1)} %get-tuple-element.76), channel_id=1, source_target_pairs={{0,2},{1,3},{2,0},{3,1},{4,6},{5,7},{6,4},{7,5},{8,10},{9,11},{10,... | collective-permute-start | bytes 344072 | tf_op jit(solution)/shard_map/ppermute | solution.py:583
  90.5 12.6 %collective-permute-start.17 = (bf16[8,7168]{1,0:T(8,128)(2,1)S(1)}, bf16[8,7168]{1,0:T(8,128)(2,1)S(1)}, u32[]{:S(2)}, u32[]{:S(2)}) collective-permute-start(bf16[8,7168]{1,0:T(8,128)(2,1)S(1)} %get-tuple-element.77), channel_id=1, source_target_pairs={{0,1},{1,0},{2,3},{3,2},{4,5},{5,4},{6,7},{7,6},{8,9},{9,8},{10,11... | collective-permute-start | bytes 344072 | tf_op jit(solution)/shard_map/ppermute | solution.py:583
  90.7 12.3 %collective-permute-start.18 = (bf16[8,7168]{1,0:T(8,128)(2,1)S(1)}, bf16[8,7168]{1,0:T(8,128)(2,1)S(1)}, u32[]{:S(2)}, u32[]{:S(2)}) collective-permute-start(bf16[8,7168]{1,0:T(8,128)(2,1)S(1)} %get-tuple-element.78), channel_id=1, source_target_pairs={{0,3},{1,2},{2,1},{3,0},{4,7},{5,6},{6,5},{7,4},{8,11},{9,10},{10,... | collective-permute-start | bytes 344072 | tf_op jit(solution)/shard_map/ppermute | solution.py:583
  91.1 20.0 %collective-permute-start.19 = (bf16[256,512]{1,0:T(8,128)(2,1)}, bf16[256,512]{1,0:T(8,128)(2,1)S(1)}, u32[]{:S(2)}, u32[]{:S(2)}) collective-permute-start(bf16[256,512]{1,0:T(8,128)(2,1)} %get-tuple-element.68), channel_id=1, source_target_pairs={{0,2},{2,0},{4,6},{6,4},{8,10},{10,8},{12,14},{14,12},{1,3},{3,1},... | collective-permute-start | bytes 786440 | tf_op jit(solution)/shard_map/ppermute | solution.py:28
  104.2 6.9 %collective-permute-start.20 = (bf16[1152,512]{1,0:T(8,128)(2,1)}, bf16[1152,512]{1,0:T(8,128)(2,1)}, u32[]{:S(2)}, u32[]{:S(2)}) collective-permute-start(bf16[1152,512]{1,0:T(8,128)(2,1)} %broadcast_select_fusion.refs_1_), channel_id=1, source_target_pairs={{0,1},{1,0},{2,3},{3,2},{4,5},{5,4},{6,7},{7,6},{8,9},{9,8},{10,11... | collective-permute-start | bytes 3538952 | tf_op jit(solution)/shard_map/ppermute | solution.py:28
  105.7 12.2 %collective-permute-start.22 = (bf16[2,7168]{1,0:T(2,128)(2,1)}, bf16[2,7168]{1,0:T(2,128)(2,1)S(1)}, u32[]{:S(2)}, u32[]{:S(2)}) collective-permute-start(bf16[2,7168]{1,0:T(2,128)(2,1)} %get-tuple-element.96), channel_id=1, source_target_pairs={{0,4},{2,6},{4,0},{6,2},{8,12},{10,14},{12,8},{14,10},{1,5},{3,7},... | collective-permute-start | bytes 86024 | tf_op jit(solution)/shard_map/ppermute | solution.py:548
  106.6 11.3 %collective-permute-start.23 = (bf16[2,7168]{1,0:T(2,128)(2,1)S(1)}, bf16[2,7168]{1,0:T(2,128)(2,1)S(1)}, u32[]{:S(2)}, u32[]{:S(2)}) collective-permute-start(bf16[2,7168]{1,0:T(2,128)(2,1)S(1)} %get-tuple-element.98), channel_id=1, source_target_pairs={{0,8},{2,10},{4,12},{6,14},{8,0},{10,2},{12,4},{14,6},{1,9},{3,11}... | collective-permute-start | bytes 86024 | tf_op jit(solution)/shard_map/ppermute | solution.py:548
  108.9 9.0 %collective-permute-start.24 = (bf16[2,7168]{1,0:T(2,128)(2,1)S(1)}, bf16[2,7168]{1,0:T(2,128)(2,1)}, u32[]{:S(2)}, u32[]{:S(2)}) collective-permute-start(bf16[2,7168]{1,0:T(2,128)(2,1)S(1)} %get-tuple-element.97), channel_id=1, source_target_pairs={{0,12},{2,14},{4,8},{6,10},{8,4},{10,6},{12,0},{14,2},{1,13},{3,15... | collective-permute-start | bytes 86024 | tf_op jit(solution)/shard_map/ppermute | solution.py:548
  116.3 8.6 %collective-permute-start.21 = (bf16[256,512]{1,0:T(8,128)(2,1)}, bf16[256,512]{1,0:T(8,128)(2,1)S(1)}, u32[]{:S(2)}, u32[]{:S(2)}) collective-permute-start(bf16[256,512]{1,0:T(8,128)(2,1)} %attend.8), channel_id=1, source_target_pairs={{0,2},{2,0},{4,6},{6,4},{8,10},{10,8},{12,14},{14,12},{1,3},{3,1},... | collective-permute-start | bytes 786440 | tf_op jit(solution)/shard_map/ppermute | solution.py:28

commit v11 on v10

--- a/solution.py
+++ b/solution.py
@@ -548,9 +548,8 @@
         return lax.ppermute(x, "branch", list(enumerate(there)))
 
     ways = [(k, m) for m in range(around) for k in range(experts)]
-    pieces = outgoing[:1] + [along(outgoing[k], k, 0) for k in range(1, experts)]
-    cache_a, first_b, stay, *pieces = lax.optimization_barrier(
-        (cache_a, first_b, stay, *pieces)
+    cache_a, first_b, stay, *outgoing = lax.optimization_barrier(
+        (cache_a, first_b, stay, *outgoing)
     )
     second_b = line_hop(first_b, tok_rows, outward)
     first_c = line_hop(cache_a, tok_rows, inner)
@@ -561,20 +560,14 @@
     guest = after(guest, cache_a, first_b)
     given_0, placed = attend(scalars, 0, guest, stay, both_halves(own_cache), None)
     back_0 = swapped(given_0, "branch", 0)
-    rows = stack_rows(*lax.optimization_barrier((given_0, *pieces))[1:])
-    rows = [rows] + [along(rows, 0, m) for m in range(1, around)]
     given_1, placed = attend(scalars, 1, guest, stay, both_halves(cache_a), placed)
     back_1 = swapped(given_1, "branch", 0)
 
-    first_c, given_1, back_0, first_b, *rows = lax.optimization_barrier(
-        (first_c, given_1, back_0, first_b, *rows)
-    )
+    first_c, given_1, first_b = lax.optimization_barrier((first_c, given_1, first_b))
     second_c = line_hop(first_c, tok_rows, outward)
     cache_b = jnp.where(middle, first_b, second_b)
     given_2, placed = attend(scalars, 2, guest, stay, both_halves(cache_b), placed)
     back_2 = swapped(given_2, "branch", 0)
-    rows = stack_rows(*rows)
-
     def around_chip(x, i):
         pairs = []
         for there in range(lax.axis_size("branch") * cores):
@@ -582,17 +575,25 @@
             pairs.append((there, (row ^ (i & 1)) * cores + (core ^ (i >> 1))))
         return lax.ppermute(x, ("branch", "expert"), pairs)
 
+    outgoing = lax.optimization_barrier((given_2, back_0, back_1, *outgoing))[3:]
+    pieces = [
+        outgoing[k] if (k, m) == (0, 0) else along(outgoing[k], k, m) for k, m in ways
+    ]
+
+    second_c, back_1, back_2, *pieces = lax.optimization_barrier(
+        (second_c, back_1, back_2, *pieces)
+    )
+    cache_c = both_halves(jnp.where(middle, first_c, second_c))
+    rows = stack_rows(*pieces)
     groups = [rows] + [around_chip(rows, i) for i in range(1, 2 * cores)]
-    groups = lax.optimization_barrier((given_2, *groups))[1:]
     parts, *others = run_experts(groups, w_gate, w_up, w_down)
     others = [around_chip(x, i + 1) for i, x in enumerate(others)]
-
-    second_c, back_1, parts, *others = lax.optimization_barrier(
-        (second_c, back_1, parts, *others)
-    )
+    guest, parts = lax.optimization_barrier((guest, parts))
+    given_3, placed = attend(scalars, 3, guest, stay, cache_c, placed)
+    back_3 = swapped(given_3, "branch", 0)
+    others = [after(other, given_3) for other in others]
     for other in others:
         parts = parts + other.astype(jnp.float32)
-    cache_c = both_halves(jnp.where(middle, first_c, second_c))
     homeward = [
         parts[w * CAP : (w + 1) * CAP].astype(jnp.float32 if way == (0, 0) else jnp.bfloat16)
         for w, way in enumerate(ways)
@@ -601,11 +602,7 @@
         piece if (k, m) == (0, 0) else along(piece, -k, m)
         for (k, m), piece in zip(ways, homeward)
     ]
-    guest, back_2 = lax.optimization_barrier((guest, back_2))
-    (given_3,) = attend(scalars, 3, guest, None, cache_c, None)
-    back_3 = swapped(given_3, "branch", 0)
-    (placed,) = attend(scalars, 3, None, after(stay, given_3), cache_c, placed)
-    homeward = [after(x, given_3).astype(jnp.float32) for x in homeward]
+    homeward = [x.astype(jnp.float32) for x in homeward]
     placed = place(scalars, (back_0, back_1, back_2, back_3), placed)
     attended = placed.reshape(tok_rows, step_count, head_count, width)
 

time: 127 us -> 133 us (1.047)
  waiting for transfers between devices: 42.9 us -> 60 us
  Pallas kernels: 40.1 us -> 34.8 us
  other arithmetic: 4.41 us -> 1.91 us
  starting transfers between devices: 32.1 us -> 30.1 us
    ppermute x5, waiting for transfers between devices: 10.4 us -> 39 us  [line_hop(): return lax.ppermute(x, 'branch', pairs)]
    ppermute x5 -> x6, waiting for transfers between devices: 28.1 us -> 3.31 us  [along(): return lax.ppermute(x, 'branch', list(enumerate(there)))]
    ppermute x9, waiting for transfers between devices: 1.64 us -> 12.3 us  [swapped(): lax.ppermute(x, axis, [(i, i ^ 1 << bit) for i in range(lax.axis_size(axi...]
    pallas_call x5 -> x4, Pallas kernels: 30.5 us -> 25.3 us  [call(): pl.pallas_call(functools.partial(kernel, slot, gives, keeps, has_placed),...]
    ppermute x6, waiting for transfers between devices: 2.75 us -> 5.47 us  [around_chip(): return lax.ppermute(x, ('branch', 'expert'), pairs)]
    slice x2 -> x1, local copies, waits for them, and re-layouts: 1.64 us -> 0.08 us  [on_device(): parts[w * CAP:(w + 1) * CAP]]
    ppermute x5 -> x6, starting transfers between devices: 10.5 us -> 9.56 us  [along(): return lax.ppermute(x, 'branch', list(enumerate(there)))]
    unnamed x24 -> x26, local copies, waits for them, and re-layouts: 3.22 us -> 3.81 us
  transfers between devices with their start and end apart: 25 -> 26, of which waited for: 6 -> 10; matrix products, arithmetic and copies ran while one was open for 5% -> 1% of each run, Pallas kernels for 29% -> 23%
where the time goes in v11:
time: 133 us
  waiting for transfers between devices  60 us (45%)
  Pallas kernels  34.8 us (26%)
  starting transfers between devices  30.1 us (23%)
  local copies, waits for them, and re-layouts  5 us (4%)
  other arithmetic  1.91 us (1%)
    ppermute x5, waiting for transfers between devices, line_hop(): return lax.ppermute(x, 'branch', pairs)  39 us
    pallas_call x4, Pallas kernels, call(): pl.pallas_call(functools.partial(kernel, slot, gives, keeps, has_placed),...  25.3 us
    ppermute x9, waiting for transfers between devices, swapped(): lax.ppermute(x, axis, [(i, i ^ 1 << bit) for i in range(lax.axis_size(axi...  12.3 us
    ppermute x6, starting transfers between devices, along(): return lax.ppermute(x, 'branch', list(enumerate(there)))  9.56 us
    ppermute x5, starting transfers between devices, line_hop(): return lax.ppermute(x, 'branch', pairs)  9.18 us
    ppermute x9, starting transfers between devices, swapped(): lax.ppermute(x, axis, [(i, i ^ 1 << bit) for i in range(lax.axis_size(axi...  6.93 us
    ppermute x6, waiting for transfers between devices, around_chip(): return lax.ppermute(x, ('branch', 'expert'), pairs)  5.47 us
    ppermute x6, starting transfers between devices, around_chip(): return lax.ppermute(x, ('branch', 'expert'), pairs)  4.41 us
  transfers between devices with their start and end apart: 26, of which 10 were waited for; matrix products, arithmetic and copies ran while one was open for 1% of the time, Pallas kernels for 23%

profile of v11, /device:TPU:0, one launch (start us, length us, event | category | flops | bytes accessed | tf_op | source)
XLA Modules:
  0.0 133.0 jit_solution(6418684247411870816)
XLA Ops:
  0.7 2.3 %pack_cache.1.refs_2_ = bf16[1152,512]{1,0:T(8,128)(2,1)} custom-call(bf16[1024,512]{1,0:T(8,128)(2,1)} %bitcast.13, bf16[128,512]{1,0:T(8,128)(2,1)} %bitcast.14), custom_call_target="tpu_custom_call" | custom-call | bytes 1024 | tf_op jit(solution)/shard_map/pack_cache/pallas_call | solution.py:52
  3.0 3.1 %collective-permute-start.1 = (bf16[1152,512]{1,0:T(8,128)(2,1)}, bf16[1152,512]{1,0:T(8,128)(2,1)}, u32[]{:S(2)}, u32[]{:S(2)}) collective-permute-start(bf16[1152,512]{1,0:T(8,128)(2,1)} %pack_cache.1.refs_2_), channel_id=1, source_target_pairs={{0,4},{4,0},{8,12},{12,8},{2,6},{6,2},{10,14},{14,10},{1,5},{5,1},... | collective-permute-start | bytes 3538952 | tf_op jit(solution)/shard_map/ppermute | solution.py:36
  6.1 1.7 %collective-permute-start.2 = (bf16[1152,512]{1,0:T(8,128)(2,1)}, bf16[1152,512]{1,0:T(8,128)(2,1)}, u32[]{:S(2)}, u32[]{:S(2)}) collective-permute-start(bf16[1152,512]{1,0:T(8,128)(2,1)} %pack_cache.1.refs_2_), channel_id=1, source_target_pairs={{4,8},{8,4},{6,10},{10,6},{5,9},{9,5},{7,11},{11,7},{20,24},{24,20... | collective-permute-start | bytes 3538952 | tf_op jit(solution)/shard_map/ppermute | solution.py:36
  8.0 1.6 %copy-done = bf16[8,2,128,512]{3,2,1,0:T(8,128)(2,1)S(1)} copy-done((bf16[8,2,128,512]{3,2,1,0:T(8,128)(2,1)S(1)}, bf16[8,2,128,512]{3,2,1,0:T(8,128)(2,1)}, u32[]{:S(2)}) %copy-start) | copy-done | bytes 2097176
  9.6 2.2 %pack_tokens.2 = bf16[4,320,512]{2,1,0:T(8,128)(2,1)} custom-call(s32[8]{0:T(128)S(1)} %copy-done.5, s32[1]{0:T(128)} %bitcast.own_ref, bf16[8,256,512]{2,1,0:T(8,128)(2,1)S(1)} %bitcast.8, bf16[8,32,512]{2,1,0:T(8,128)(2,1)S(1)} %reshape.28.rope_ref, bf16[8,32,512]{2,1,0:T(8,128)(2,1)S(1)} %fusion.2.new_ref), custom_call_target="tpu_custom_call" | custom-call | bytes 1024 | tf_op jit(solution)/shard_map/pack_tokens/pallas_call | solution.py:106
  11.8 1.6 %collective-permute-start = (bf16[4,320,512]{2,1,0:T(8,128)(2,1)}, bf16[4,320,512]{2,1,0:T(8,128)(2,1)S(1)}, u32[]{:S(2)}, u32[]{:S(2)}) collective-permute-start(bf16[4,320,512]{2,1,0:T(8,128)(2,1)} %pack_tokens.2), channel_id=1, source_target_pairs={{0,2},{2,0},{4,6},{6,4},{8,10},{10,8},{12,14},{14,12},{1,3},{3,1},... | collective-permute-start | bytes 3932168 | tf_op jit(solution)/shard_map/ppermute | solution.py:28
  13.4 1.6 %copy-done.1 = bf16[8,2,128,512]{3,2,1,0:T(8,128)(2,1)S(1)} copy-done((bf16[8,2,128,512]{3,2,1,0:T(8,128)(2,1)S(1)}, bf16[8,2,128,512]{3,2,1,0:T(8,128)(2,1)}, u32[]{:S(2)}) %copy-start.1) | copy-done | bytes 2097176
  15.0 1.1 pack_tokens.3.refs_1_
  16.3 0.4 dispatch.1
  16.6 15.7 %collective-permute-done.1.refs_2_ = bf16[1152,512]{1,0:T(8,128)(2,1)} collective-permute-done((bf16[1152,512]{1,0:T(8,128)(2,1)}, bf16[1152,512]{1,0:T(8,128)(2,1)}, u32[]{:S(2)}, u32[]{:S(2)}) %collective-permute-start.1) | collective-permute-done | bytes 1179680 | tf_op jit(solution)/shard_map/ppermute | solution.py:36
  32.4 1.7 %collective-permute-start.5 = (bf16[1152,512]{1,0:T(8,128)(2,1)}, bf16[1152,512]{1,0:T(8,128)(2,1)}, u32[]{:S(2)}, u32[]{:S(2)}) collective-permute-start(bf16[1152,512]{1,0:T(8,128)(2,1)} %collective-permute-done.1.refs_2_), channel_id=1, source_target_pairs={{4,8},{8,4},{6,10},{10,6},{5,9},{9,5},{7,11},{11,7},{20,24},{24,20... | collective-permute-start | bytes 3538952 | tf_op jit(solution)/shard_map/ppermute | solution.py:36
  34.0 1.3 collective-permute-start.9
  35.3 7.0 %collective-permute-done.refs_0_ = bf16[4,320,512]{2,1,0:T(8,128)(2,1)S(1)} collective-permute-done((bf16[4,320,512]{2,1,0:T(8,128)(2,1)}, bf16[4,320,512]{2,1,0:T(8,128)(2,1)S(1)}, u32[]{:S(2)}, u32[]{:S(2)}) %collective-permute-start) | collective-permute-done | bytes 1310752 | tf_op jit(solution)/shard_map/ppermute | solution.py:28
  42.3 6.9 %attend.4 = (bf16[256,512]{1,0:T(8,128)(2,1)S(1)}, bf16[8,256,512]{2,1,0:T(8,128)(2,1)}) custom-call(s32[8]{0:T(128)S(1)} %copy-done.5, s32[1]{0:T(128)} %bitcast.own_ref, bf16[4,320,512]{2,1,0:T(8,128)(2,1)S(1)} %collective-permute-done.refs_0_, bf16[4,320,512]{2,1,0:T(8,128)(2,1)S(1)} %pack_tokens.3.refs_1_, bf16[1152,512]{1,0:T(8,128)(2,1)} %pack_cache.1.refs_2_, ...), custom_call_target="tpu_custom_call" | custom-call | bytes 1024 | tf_op jit(solution)/shard_map/attend/pallas_call | solution.py:285
  49.2 6.9 %attend.5 = (bf16[256,512]{1,0:T(8,128)(2,1)S(1)}, bf16[8,256,512]{2,1,0:T(8,128)(2,1)}) custom-call(s32[8]{0:T(128)S(1)} %copy-done.5, s32[1]{0:T(128)} %bitcast.own_ref, bf16[4,320,512]{2,1,0:T(8,128)(2,1)S(1)} %collective-permute-done.refs_0_, bf16[4,320,512]{2,1,0:T(8,128)(2,1)S(1)} %pack_tokens.3.refs_1_, ...), custom_call_target="tpu_custom_call", output_to_operand_aliasing={{1}: (6, {})} | custom-call | bytes 1024 | tf_op jit(solution)/shard_map/attend/pallas_call | solution.py:285
  56.1 12.6 %collective-permute-done.9 = bf16[1152,512]{1,0:T(8,128)(2,1)} collective-permute-done((bf16[1152,512]{1,0:T(8,128)(2,1)}, bf16[1152,512]{1,0:T(8,128)(2,1)}, u32[]{:S(2)}, u32[]{:S(2)}) %collective-permute-start.9) | collective-permute-done | bytes 1179680 | tf_op jit(solution)/shard_map/ppermute | solution.py:36
  68.7 1.4 %broadcast_select_fusion.1.refs_2_ = bf16[1152,512]{1,0:T(8,128)(2,1)S(1)} fusion(bf16[1152,512]{1,0:T(8,128)(2,1)} %collective-permute-done.2, bf16[1152,512]{1,0:T(8,128)(2,1)} %collective-permute-done.9, pred[]{:T(512)S(6)} %and.22), kind=kLoop, calls=%fused_computation.2 | loop fusion | flops 589824 | bytes 3538945 | tf_op jit(solution)/shard_map/jit(_where)/select_n | solution.py:568
  70.2 1.5 %collective-permute-start.7 = (bf16[1152,512]{1,0:T(8,128)(2,1)}, bf16[1152,512]{1,0:T(8,128)(2,1)S(1)}, u32[]{:S(2)}, u32[]{:S(2)}) collective-permute-start(bf16[1152,512]{1,0:T(8,128)(2,1)} %collective-permute-done.5), channel_id=1, source_target_pairs={{4,0},{8,12},{6,2},{10,14},{5,1},{9,13},{7,3},{11,15},{20,16},{24,... | collective-permute-start | bytes 3538952 | tf_op jit(solution)/shard_map/ppermute | solution.py:36
  71.7 1.6 %collective-permute-start.4 = (bf16[256,512]{1,0:T(8,128)(2,1)S(1)}, bf16[256,512]{1,0:T(8,128)(2,1)S(1)}, u32[]{:S(2)}, u32[]{:S(2)}) collective-permute-start(bf16[256,512]{1,0:T(8,128)(2,1)S(1)} %get-tuple-element.51), channel_id=1, source_target_pairs={{0,2},{2,0},{4,6},{6,4},{8,10},{10,8},{12,14},{14,12},{1,3},{3,1},... | collective-permute-start | bytes 786440 | tf_op jit(solution)/shard_map/ppermute | solution.py:28
  73.3 0.5 collective-permute-start.8
  73.8 5.8 %attend.6 = (bf16[256,512]{1,0:T(8,128)(2,1)S(1)}, bf16[8,256,512]{2,1,0:T(8,128)(2,1)}) custom-call(s32[8]{0:T(128)S(1)} %copy-done.5, s32[1]{0:T(128)} %bitcast.own_ref, bf16[4,320,512]{2,1,0:T(8,128)(2,1)S(1)} %collective-permute-done.refs_0_, bf16[4,320,512]{2,1,0:T(8,128)(2,1)S(1)} %pack_tokens.3.refs_1_, ...), custom_call_target="tpu_custom_call", output_to_operand_aliasing={{1}: (6, {})} | custom-call | bytes 1024 | tf_op jit(solution)/shard_map/attend/pallas_call | solution.py:285
  79.6 1.6 %collective-permute-start.11 = (bf16[256,512]{1,0:T(8,128)(2,1)S(1)}, bf16[256,512]{1,0:T(8,128)(2,1)S(1)}, u32[]{:S(2)}, u32[]{:S(2)}) collective-permute-start(bf16[256,512]{1,0:T(8,128)(2,1)S(1)} %get-tuple-element.57), channel_id=1, source_target_pairs={{0,2},{2,0},{4,6},{6,4},{8,10},{10,8},{12,14},{14,12},{1,3},{3,1},... | collective-permute-start | bytes 786440 | tf_op jit(solution)/shard_map/ppermute | solution.py:28
  81.2 5.3 %collective-permute-done.8.refs_1_ = bf16[256,512]{1,0:T(8,128)(2,1)S(1)} collective-permute-done((bf16[256,512]{1,0:T(8,128)(2,1)S(1)}, bf16[256,512]{1,0:T(8,128)(2,1)S(1)}, u32[]{:S(2)}, u32[]{:S(2)}) %collective-permute-start.8) | collective-permute-done | bytes 262176 | tf_op jit(solution)/shard_map/ppermute | solution.py:28
  86.5 2.5 %collective-permute-start.12 = (bf16[2,7168]{1,0:T(2,128)(2,1)S(1)}, bf16[2,7168]{1,0:T(2,128)(2,1)S(1)}, u32[]{:S(2)}, u32[]{:S(2)}) collective-permute-start(bf16[2,7168]{1,0:T(2,128)(2,1)S(1)} %get-tuple-element.61), channel_id=1, source_target_pairs={{0,8},{2,10},{4,12},{6,14},{8,0},{10,2},{12,4},{14,6},{1,9},{3,11}... | collective-permute-start | bytes 86024 | tf_op jit(solution)/shard_map/ppermute | solution.py:548
  88.9 0.3 collective-permute-start.13
  89.2 2.4 %collective-permute-start.14 = (bf16[2,7168]{1,0:T(2,128)(2,1)S(1)}, bf16[2,7168]{1,0:T(2,128)(2,1)S(1)}, u32[]{:S(2)}, u32[]{:S(2)}) collective-permute-start(bf16[2,7168]{1,0:T(2,128)(2,1)S(1)} %get-tuple-element.61), channel_id=1, source_target_pairs={{0,12},{2,14},{4,8},{6,10},{8,4},{10,6},{12,0},{14,2},{1,13},{3,15... | collective-permute-start | bytes 86024 | tf_op jit(solution)/shard_map/ppermute | solution.py:548
  91.6 10.6 %collective-permute-done.7 = bf16[1152,512]{1,0:T(8,128)(2,1)S(1)} collective-permute-done((bf16[1152,512]{1,0:T(8,128)(2,1)}, bf16[1152,512]{1,0:T(8,128)(2,1)S(1)}, u32[]{:S(2)}, u32[]{:S(2)}) %collective-permute-start.7) | collective-permute-done | bytes 1179680 | tf_op jit(solution)/shard_map/ppermute | solution.py:36
  102.2 0.3 collective-permute-done.13.refs_2_
  102.7 0.4 stack_rows.1.refs_0_
  103.1 1.6 %collective-permute-start.15 = (bf16[8,7168]{1,0:T(8,128)(2,1)S(1)}, bf16[8,7168]{1,0:T(8,128)(2,1)S(1)}, u32[]{:S(2)}, u32[]{:S(2)}) collective-permute-start(bf16[8,7168]{1,0:T(8,128)(2,1)S(1)} %stack_rows.1.refs_0_), channel_id=1, source_target_pairs={{0,2},{1,3},{2,0},{3,1},{4,6},{5,7},{6,4},{7,5},{8,10},{9,11},{10,... | collective-permute-start | bytes 344072 | tf_op jit(solution)/shard_map/ppermute | solution.py:576
  104.7 0.2 collective-permute-start.16
  104.9 0.4 collective-permute-start.17
  105.3 3.8 %collective-permute-done.15.refs_1_ = bf16[8,7168]{1,0:T(8,128)(2,1)S(1)} collective-permute-done((bf16[8,7168]{1,0:T(8,128)(2,1)S(1)}, bf16[8,7168]{1,0:T(8,128)(2,1)S(1)}, u32[]{:S(2)}, u32[]{:S(2)}) %collective-permute-start.15) | collective-permute-done | bytes 114720 | tf_op jit(solution)/shard_map/ppermute | solution.py:576
  109.1 1.7 %collective-permute-done.17.refs_3_ = bf16[8,7168]{1,0:T(8,128)(2,1)S(1)} collective-permute-done((bf16[8,7168]{1,0:T(8,128)(2,1)S(1)}, bf16[8,7168]{1,0:T(8,128)(2,1)S(1)}, u32[]{:S(2)}, u32[]{:S(2)}) %collective-permute-start.17) | collective-permute-done | bytes 114720 | tf_op jit(solution)/shard_map/ppermute | solution.py:576
  110.8 1.6 %experts.1 = (f32[8,7168]{1,0:T(8,128)S(1)}, bf16[8,7168]{1,0:T(8,128)(2,1)S(1)}, bf16[8,7168]{1,0:T(8,128)(2,1)S(1)}, bf16[8,7168]{1,0:T(8,128)(2,1)S(1)}) custom-call(bf16[8,7168]{1,0:T(8,128)(2,1)S(1)} %stack_rows.1.refs_0_, bf16[8,7168]{1,0:T(8,128)(2,1)S(1)} %collective-permute-done.15.refs_1_, bf16[8,7168]{1,0:T(8,128)(2,1)S(1)} %collective-permute-done.16.refs_2_, ...), custom_call_target="tpu_custom_call" | custom-call | bytes 1024 | tf_op jit(solution)/shard_map/experts/pallas_call | solution.py:454
  112.4 1.6 %collective-permute-start.20 = (bf16[8,7168]{1,0:T(8,128)(2,1)S(1)}, bf16[8,7168]{1,0:T(8,128)(2,1)S(1)}, u32[]{:S(2)}, u32[]{:S(2)}) collective-permute-start(bf16[8,7168]{1,0:T(8,128)(2,1)S(1)} %get-tuple-element.76), channel_id=1, source_target_pairs={{0,2},{1,3},{2,0},{3,1},{4,6},{5,7},{6,4},{7,5},{8,10},{9,11},{10,... | collective-permute-start | bytes 344072 | tf_op jit(solution)/shard_map/ppermute | solution.py:576
  113.9 0.6 collective-permute-start.22
  114.6 5.8 %attend.7 = (bf16[256,512]{1,0:T(8,128)(2,1)S(1)}, bf16[8,256,512]{2,1,0:T(8,128)(2,1)}) custom-call(s32[8]{0:T(128)S(1)} %copy-done.5, s32[1]{0:T(128)} %bitcast.own_ref, bf16[4,320,512]{2,1,0:T(8,128)(2,1)S(1)} %collective-permute-done.refs_0_, bf16[4,320,512]{2,1,0:T(8,128)(2,1)S(1)} %pack_tokens.3.refs_1_, ...), custom_call_target="tpu_custom_call", output_to_operand_aliasing={{1}: (6, {})} | custom-call | bytes 1024 | tf_op jit(solution)/shard_map/attend/pallas_call | solution.py:285
  120.4 0.6 copy-done.8
  121.1 0.9 collective-permute-start.23
  122.1 1.5 %collective-permute-start.19 = (bf16[256,512]{1,0:T(8,128)(2,1)}, bf16[256,512]{1,0:T(8,128)(2,1)S(1)}, u32[]{:S(2)}, u32[]{:S(2)}) collective-permute-start(bf16[256,512]{1,0:T(8,128)(2,1)} %copy-done.8), channel_id=1, source_target_pairs={{0,2},{2,0},{4,6},{6,4},{8,10},{10,8},{12,14},{14,12},{1,3},{3,1},... | collective-permute-start | bytes 786440 | tf_op jit(solution)/shard_map/ppermute | solution.py:28
  123.6 0.9 collective-permute-start.24
  124.5 2.6 %collective-permute-start.25 = (bf16[2,7168]{1,0:T(2,128)(2,1)S(1)}, bf16[2,7168]{1,0:T(2,128)(2,1)S(1)}, u32[]{:S(2)}, u32[]{:S(2)}) collective-permute-start(bf16[2,7168]{1,0:T(2,128)(2,1)S(1)} %get-tuple-element.85), channel_id=1, source_target_pairs={{0,12},{2,14},{4,8},{6,10},{8,4},{10,6},{12,0},{14,2},{1,13},{3,15... | collective-permute-start | bytes 86024 | tf_op jit(solution)/shard_map/ppermute | solution.py:548
  127.2 1.5 %collective-permute-done.24 = bf16[2,7168]{1,0:T(2,128)(2,1)S(1)} collective-permute-done((bf16[2,7168]{1,0:T(2,128)(2,1)S(1)}, bf16[2,7168]{1,0:T(2,128)(2,1)S(1)}, u32[]{:S(2)}, u32[]{:S(2)}) %collective-permute-start.24) | collective-permute-done | bytes 28704 | tf_op jit(solution)/shard_map/ppermute | solution.py:548
  128.7 1.5 %collective-permute-done.25 = bf16[2,7168]{1,0:T(2,128)(2,1)S(1)} collective-permute-done((bf16[2,7168]{1,0:T(2,128)(2,1)S(1)}, bf16[2,7168]{1,0:T(2,128)(2,1)S(1)}, u32[]{:S(2)}, u32[]{:S(2)}) %collective-permute-start.25) | collective-permute-done | bytes 28704 | tf_op jit(solution)/shard_map/ppermute | solution.py:548
  130.3 0.2 multiply_reduce_fusion
  130.5 0.8 convert_element_type.39
  131.3 1.5 %place.1 = bf16[8,256,512]{2,1,0:T(8,128)(2,1)} custom-call(s32[8]{0:T(128)S(1)} %copy-done.5, s32[1]{0:T(128)} %bitcast.own_ref, bf16[256,512]{1,0:T(8,128)(2,1)S(1)} %collective-permute-done.4.refs_0_, bf16[256,512]{1,0:T(8,128)(2,1)S(1)} %collective-permute-done.8.refs_1_, ...), custom_call_target="tpu_custom_call", output_to_operand_aliasing={{}: (6, {})} | custom-call | bytes 1024 | tf_op jit(solution)/shard_map/place/pallas_call | solution.py:321
  (54 shorter events, 1.0 us)
Async XLA Ops:
  0.6 7.1 %copy-start.9 = (bf16[8,2,8192]{2,1,0:T(2,128)(2,1)S(1)}, bf16[8,2,8192]{2,1,0:T(2,128)(2,1)}, u32[]{:S(2)}) copy-start(bf16[8,2,8192]{2,1,0:T(2,128)(2,1)} %param.16) | copy-start | bytes 786436
  0.6 7.3 %copy-start.11 = (bf16[8,2,512]{2,1,0:T(2,128)(2,1)S(1)}, bf16[8,2,512]{2,1,0:T(2,128)(2,1)}, u32[]{:S(2)}) copy-start(bf16[8,2,512]{2,1,0:T(2,128)(2,1)} %param.17) | copy-start | bytes 49156
  0.7 7.3 %copy-start.12 = (bf16[8,2,64]{2,1,0:T(2,128)(2,1)S(1)}, bf16[8,2,64]{2,1,0:T(2,128)(2,1)}, u32[]{:S(2)}) copy-start(bf16[8,2,64]{2,1,0:T(2,128)(2,1)} %param.18) | copy-start | bytes 6148
  0.7 7.3 %copy-start.5 = (s32[8]{0:T(128)S(1)}, s32[8]{0:T(128)}, u32[]{:S(2)}) copy-start(s32[8]{0:T(128)} %slot_ref.13) | copy-start | bytes 100
  3.0 29.4 %collective-permute-start.1 = (bf16[1152,512]{1,0:T(8,128)(2,1)}, bf16[1152,512]{1,0:T(8,128)(2,1)}, u32[]{:S(2)}, u32[]{:S(2)}) collective-permute-start(bf16[1152,512]{1,0:T(8,128)(2,1)} %pack_cache.1.refs_2_), channel_id=1, source_target_pairs={{0,4},{4,0},{8,12},{12,8},{2,6},{6,2},{10,14},{14,10},{1,5},{5,1},... | collective-permute-start | bytes 3538952 | tf_op jit(solution)/shard_map/ppermute | solution.py:36
  6.1 26.3 %collective-permute-start.2 = (bf16[1152,512]{1,0:T(8,128)(2,1)}, bf16[1152,512]{1,0:T(8,128)(2,1)}, u32[]{:S(2)}, u32[]{:S(2)}) collective-permute-start(bf16[1152,512]{1,0:T(8,128)(2,1)} %pack_cache.1.refs_2_), channel_id=1, source_target_pairs={{4,8},{8,4},{6,10},{10,6},{5,9},{9,5},{7,11},{11,7},{20,24},{24,20... | collective-permute-start | bytes 3538952 | tf_op jit(solution)/shard_map/ppermute | solution.py:36
  8.0 1.6 %copy-start = (bf16[8,2,128,512]{3,2,1,0:T(8,128)(2,1)S(1)}, bf16[8,2,128,512]{3,2,1,0:T(8,128)(2,1)}, u32[]{:S(2)}) copy-start(bf16[8,2,128,512]{3,2,1,0:T(8,128)(2,1)} %param.15) | copy-start | bytes 6291460
  11.8 30.5 %collective-permute-start = (bf16[4,320,512]{2,1,0:T(8,128)(2,1)}, bf16[4,320,512]{2,1,0:T(8,128)(2,1)S(1)}, u32[]{:S(2)}, u32[]{:S(2)}) collective-permute-start(bf16[4,320,512]{2,1,0:T(8,128)(2,1)} %pack_tokens.2), channel_id=1, source_target_pairs={{0,2},{2,0},{4,6},{6,4},{8,10},{10,8},{12,14},{14,12},{1,3},{3,1},... | collective-permute-start | bytes 3932168 | tf_op jit(solution)/shard_map/ppermute | solution.py:28
  13.4 28.9 %collective-permute-start.3 = (bf16[1152,512]{1,0:T(8,128)(2,1)}, bf16[1152,512]{1,0:T(8,128)(2,1)}, u32[]{:S(2)}, u32[]{:S(2)}) collective-permute-start(bf16[1152,512]{1,0:T(8,128)(2,1)} %pack_cache.1.refs_2_), channel_id=1, source_target_pairs={{0,1},{1,0},{2,3},{3,2},{4,5},{5,4},{6,7},{7,6},{8,9},{9,8},{10,11... | collective-permute-start | bytes 3538952 | tf_op jit(solution)/shard_map/ppermute | solution.py:28
  13.4 1.6 %copy-start.1 = (bf16[8,2,128,512]{3,2,1,0:T(8,128)(2,1)S(1)}, bf16[8,2,128,512]{3,2,1,0:T(8,128)(2,1)}, u32[]{:S(2)}) copy-start(bf16[8,2,128,512]{3,2,1,0:T(8,128)(2,1)} %param.15) | copy-start | bytes 6291460
  15.0 1.2 copy-start.10
  15.0 1.3 copy-start.6
  15.0 1.3 copy-start.7
  32.4 16.8 %collective-permute-start.6 = (bf16[1152,512]{1,0:T(8,128)(2,1)}, bf16[1152,512]{1,0:T(8,128)(2,1)}, u32[]{:S(2)}, u32[]{:S(2)}) collective-permute-start(bf16[1152,512]{1,0:T(8,128)(2,1)} %collective-permute-done.1.refs_2_), channel_id=1, source_target_pairs={{0,1},{1,0},{2,3},{3,2},{4,5},{5,4},{6,7},{7,6},{8,9},{9,8},{10,11... | collective-permute-start | bytes 3538952 | tf_op jit(solution)/shard_map/ppermute | solution.py:28
  32.4 23.7 %collective-permute-start.5 = (bf16[1152,512]{1,0:T(8,128)(2,1)}, bf16[1152,512]{1,0:T(8,128)(2,1)}, u32[]{:S(2)}, u32[]{:S(2)}) collective-permute-start(bf16[1152,512]{1,0:T(8,128)(2,1)} %collective-permute-done.1.refs_2_), channel_id=1, source_target_pairs={{4,8},{8,4},{6,10},{10,6},{5,9},{9,5},{7,11},{11,7},{20,24},{24,20... | collective-permute-start | bytes 3538952 | tf_op jit(solution)/shard_map/ppermute | solution.py:36
  34.0 34.7 %collective-permute-start.9 = (bf16[1152,512]{1,0:T(8,128)(2,1)}, bf16[1152,512]{1,0:T(8,128)(2,1)}, u32[]{:S(2)}, u32[]{:S(2)}) collective-permute-start(bf16[1152,512]{1,0:T(8,128)(2,1)} %collective-permute-done.2), channel_id=1, source_target_pairs={{4,0},{8,12},{6,2},{10,14},{5,1},{9,13},{7,3},{11,15},{20,16},{24,... | collective-permute-start | bytes 3538952 | tf_op jit(solution)/shard_map/ppermute | solution.py:36
  70.1 3.7 %collective-permute-start.10 = (bf16[1152,512]{1,0:T(8,128)(2,1)S(1)}, bf16[1152,512]{1,0:T(8,128)(2,1)S(1)}, u32[]{:S(2)}, u32[]{:S(2)}) collective-permute-start(bf16[1152,512]{1,0:T(8,128)(2,1)S(1)} %broadcast_select_fusion.1.refs_2_), channel_id=1, source_target_pairs={{0,1},{1,0},{2,3},{3,2},{4,5},{5,4},{6,7},{7,6},{8,9},{9,8},{10,11... | collective-permute-start | bytes 3538952 | tf_op jit(solution)/shard_map/ppermute | solution.py:28
  70.2 32.0 %collective-permute-start.7 = (bf16[1152,512]{1,0:T(8,128)(2,1)}, bf16[1152,512]{1,0:T(8,128)(2,1)S(1)}, u32[]{:S(2)}, u32[]{:S(2)}) collective-permute-start(bf16[1152,512]{1,0:T(8,128)(2,1)} %collective-permute-done.5), channel_id=1, source_target_pairs={{4,0},{8,12},{6,2},{10,14},{5,1},{9,13},{7,3},{11,15},{20,16},{24,... | collective-permute-start | bytes 3538952 | tf_op jit(solution)/shard_map/ppermute | solution.py:36
  71.7 9.5 %collective-permute-start.4 = (bf16[256,512]{1,0:T(8,128)(2,1)S(1)}, bf16[256,512]{1,0:T(8,128)(2,1)S(1)}, u32[]{:S(2)}, u32[]{:S(2)}) collective-permute-start(bf16[256,512]{1,0:T(8,128)(2,1)S(1)} %get-tuple-element.51), channel_id=1, source_target_pairs={{0,2},{2,0},{4,6},{6,4},{8,10},{10,8},{12,14},{14,12},{1,3},{3,1},... | collective-permute-start | bytes 786440 | tf_op jit(solution)/shard_map/ppermute | solution.py:28
  73.3 13.2 %collective-permute-start.8 = (bf16[256,512]{1,0:T(8,128)(2,1)S(1)}, bf16[256,512]{1,0:T(8,128)(2,1)S(1)}, u32[]{:S(2)}, u32[]{:S(2)}) collective-permute-start(bf16[256,512]{1,0:T(8,128)(2,1)S(1)} %get-tuple-element.53), channel_id=1, source_target_pairs={{0,2},{2,0},{4,6},{6,4},{8,10},{10,8},{12,14},{14,12},{1,3},{3,1},... | collective-permute-start | bytes 786440 | tf_op jit(solution)/shard_map/ppermute | solution.py:28
  73.8 37.0 %copy-start.4 = (bf16[1,128,7168]{2,1,0:T(8,128)(2,1)S(1)}, bf16[1,128,7168]{2,1,0:T(8,128)(2,1)}, u32[]{:S(2)}) copy-start(bf16[1,128,7168]{2,1,0:T(8,128)(2,1)} %refs_6_.1) | copy-start | bytes 5505028
  79.6 31.2 %copy-start.2 = (bf16[1,7168,128]{2,1,0:T(8,128)(2,1)S(1)}, bf16[1,7168,128]{2,1,0:T(8,128)(2,1)}, u32[]{:S(2)}) copy-start(bf16[1,7168,128]{2,1,0:T(8,128)(2,1)} %refs_4_.1) | copy-start | bytes 5505028
  79.6 31.2 %copy-start.3 = (bf16[1,7168,128]{2,1,0:T(8,128)(2,1)S(1)}, bf16[1,7168,128]{2,1,0:T(8,128)(2,1)}, u32[]{:S(2)}) copy-start(bf16[1,7168,128]{2,1,0:T(8,128)(2,1)} %refs_5_.1) | copy-start | bytes 5505028
  79.6 22.9 %collective-permute-start.11 = (bf16[256,512]{1,0:T(8,128)(2,1)S(1)}, bf16[256,512]{1,0:T(8,128)(2,1)S(1)}, u32[]{:S(2)}, u32[]{:S(2)}) collective-permute-start(bf16[256,512]{1,0:T(8,128)(2,1)S(1)} %get-tuple-element.57), channel_id=1, source_target_pairs={{0,2},{2,0},{4,6},{6,4},{8,10},{10,8},{12,14},{14,12},{1,3},{3,1},... | collective-permute-start | bytes 786440 | tf_op jit(solution)/shard_map/ppermute | solution.py:28
  86.5 15.7 %collective-permute-start.12 = (bf16[2,7168]{1,0:T(2,128)(2,1)S(1)}, bf16[2,7168]{1,0:T(2,128)(2,1)S(1)}, u32[]{:S(2)}, u32[]{:S(2)}) collective-permute-start(bf16[2,7168]{1,0:T(2,128)(2,1)S(1)} %get-tuple-element.61), channel_id=1, source_target_pairs={{0,8},{2,10},{4,12},{6,14},{8,0},{10,2},{12,4},{14,6},{1,9},{3,11}... | collective-permute-start | bytes 86024 | tf_op jit(solution)/shard_map/ppermute | solution.py:548
  88.9 13.6 %collective-permute-start.13 = (bf16[2,7168]{1,0:T(2,128)(2,1)S(1)}, bf16[2,7168]{1,0:T(2,128)(2,1)S(1)}, u32[]{:S(2)}, u32[]{:S(2)}) collective-permute-start(bf16[2,7168]{1,0:T(2,128)(2,1)S(1)} %get-tuple-element.64.refs_0_), channel_id=1, source_target_pairs={{0,4},{2,6},{4,0},{6,2},{8,12},{10,14},{12,8},{14,10},{1,5},{3,7},... | collective-permute-start | bytes 86024 | tf_op jit(solution)/shard_map/ppermute | solution.py:548
  89.2 13.3 %collective-permute-start.14 = (bf16[2,7168]{1,0:T(2,128)(2,1)S(1)}, bf16[2,7168]{1,0:T(2,128)(2,1)S(1)}, u32[]{:S(2)}, u32[]{:S(2)}) collective-permute-start(bf16[2,7168]{1,0:T(2,128)(2,1)S(1)} %get-tuple-element.61), channel_id=1, source_target_pairs={{0,12},{2,14},{4,8},{6,10},{8,4},{10,6},{12,0},{14,2},{1,13},{3,15... | collective-permute-start | bytes 86024 | tf_op jit(solution)/shard_map/ppermute | solution.py:548
  102.6 11.9 %collective-permute-start.18 = (bf16[1152,512]{1,0:T(8,128)(2,1)S(1)}, bf16[1152,512]{1,0:T(8,128)(2,1)S(1)}, u32[]{:S(2)}, u32[]{:S(2)}) collective-permute-start(bf16[1152,512]{1,0:T(8,128)(2,1)S(1)} %broadcast_select_fusion.refs_2_), channel_id=1, source_target_pairs={{0,1},{1,0},{2,3},{3,2},{4,5},{5,4},{6,7},{7,6},{8,9},{9,8},{10,11... | collective-permute-start | bytes 3538952 | tf_op jit(solution)/shard_map/ppermute | solution.py:28
  103.1 6.0 %collective-permute-start.15 = (bf16[8,7168]{1,0:T(8,128)(2,1)S(1)}, bf16[8,7168]{1,0:T(8,128)(2,1)S(1)}, u32[]{:S(2)}, u32[]{:S(2)}) collective-permute-start(bf16[8,7168]{1,0:T(8,128)(2,1)S(1)} %stack_rows.1.refs_0_), channel_id=1, source_target_pairs={{0,2},{1,3},{2,0},{3,1},{4,6},{5,7},{6,4},{7,5},{8,10},{9,11},{10,... | collective-permute-start | bytes 344072 | tf_op jit(solution)/shard_map/ppermute | solution.py:576
  104.7 4.4 %collective-permute-start.16 = (bf16[8,7168]{1,0:T(8,128)(2,1)S(1)}, bf16[8,7168]{1,0:T(8,128)(2,1)S(1)}, u32[]{:S(2)}, u32[]{:S(2)}) collective-permute-start(bf16[8,7168]{1,0:T(8,128)(2,1)S(1)} %stack_rows.1.refs_0_), channel_id=1, source_target_pairs={{0,1},{1,0},{2,3},{3,2},{4,5},{5,4},{6,7},{7,6},{8,9},{9,8},{10,11... | collective-permute-start | bytes 344072 | tf_op jit(solution)/shard_map/ppermute | solution.py:576
  104.9 5.9 %collective-permute-start.17 = (bf16[8,7168]{1,0:T(8,128)(2,1)S(1)}, bf16[8,7168]{1,0:T(8,128)(2,1)S(1)}, u32[]{:S(2)}, u32[]{:S(2)}) collective-permute-start(bf16[8,7168]{1,0:T(8,128)(2,1)S(1)} %stack_rows.1.refs_0_), channel_id=1, source_target_pairs={{0,3},{1,2},{2,1},{3,0},{4,7},{5,6},{6,5},{7,4},{8,11},{9,10},{10,... | collective-permute-start | bytes 344072 | tf_op jit(solution)/shard_map/ppermute | solution.py:576
  112.4 8.0 %collective-permute-start.20 = (bf16[8,7168]{1,0:T(8,128)(2,1)S(1)}, bf16[8,7168]{1,0:T(8,128)(2,1)S(1)}, u32[]{:S(2)}, u32[]{:S(2)}) collective-permute-start(bf16[8,7168]{1,0:T(8,128)(2,1)S(1)} %get-tuple-element.76), channel_id=1, source_target_pairs={{0,2},{1,3},{2,0},{3,1},{4,6},{5,7},{6,4},{7,5},{8,10},{9,11},{10,... | collective-permute-start | bytes 344072 | tf_op jit(solution)/shard_map/ppermute | solution.py:576
  113.9 6.4 %collective-permute-start.21 = (bf16[8,7168]{1,0:T(8,128)(2,1)S(1)}, bf16[8,7168]{1,0:T(8,128)(2,1)S(1)}, u32[]{:S(2)}, u32[]{:S(2)}) collective-permute-start(bf16[8,7168]{1,0:T(8,128)(2,1)S(1)} %get-tuple-element.78), channel_id=1, source_target_pairs={{0,1},{1,0},{2,3},{3,2},{4,5},{5,4},{6,7},{7,6},{8,9},{9,8},{10,11... | collective-permute-start | bytes 344072 | tf_op jit(solution)/shard_map/ppermute | solution.py:576
  113.9 6.4 %collective-permute-start.22 = (bf16[8,7168]{1,0:T(8,128)(2,1)S(1)}, bf16[8,7168]{1,0:T(8,128)(2,1)S(1)}, u32[]{:S(2)}, u32[]{:S(2)}) collective-permute-start(bf16[8,7168]{1,0:T(8,128)(2,1)S(1)} %get-tuple-element.80), channel_id=1, source_target_pairs={{0,3},{1,2},{2,1},{3,0},{4,7},{5,6},{6,5},{7,4},{8,11},{9,10},{10,... | collective-permute-start | bytes 344072 | tf_op jit(solution)/shard_map/ppermute | solution.py:576
  120.3 0.7 copy-start.8
  121.1 6.0 %collective-permute-start.23 = (bf16[2,7168]{1,0:T(2,128)(2,1)S(1)}, bf16[2,7168]{1,0:T(2,128)(2,1)S(1)}, u32[]{:S(2)}, u32[]{:S(2)}) collective-permute-start(bf16[2,7168]{1,0:T(2,128)(2,1)S(1)} %get-tuple-element.84), channel_id=1, source_target_pairs={{0,4},{2,6},{4,0},{6,2},{8,12},{10,14},{12,8},{14,10},{1,5},{3,7},... | collective-permute-start | bytes 86024 | tf_op jit(solution)/shard_map/ppermute | solution.py:548
  122.1 9.2 %collective-permute-start.19 = (bf16[256,512]{1,0:T(8,128)(2,1)}, bf16[256,512]{1,0:T(8,128)(2,1)S(1)}, u32[]{:S(2)}, u32[]{:S(2)}) collective-permute-start(bf16[256,512]{1,0:T(8,128)(2,1)} %copy-done.8), channel_id=1, source_target_pairs={{0,2},{2,0},{4,6},{6,4},{8,10},{10,8},{12,14},{14,12},{1,3},{3,1},... | collective-permute-start | bytes 786440 | tf_op jit(solution)/shard_map/ppermute | solution.py:28
  123.6 5.1 %collective-permute-start.24 = (bf16[2,7168]{1,0:T(2,128)(2,1)S(1)}, bf16[2,7168]{1,0:T(2,128)(2,1)S(1)}, u32[]{:S(2)}, u32[]{:S(2)}) collective-permute-start(bf16[2,7168]{1,0:T(2,128)(2,1)S(1)} %get-tuple-element.86), channel_id=1, source_target_pairs={{0,8},{2,10},{4,12},{6,14},{8,0},{10,2},{12,4},{14,6},{1,9},{3,11}... | collective-permute-start | bytes 86024 | tf_op jit(solution)/shard_map/ppermute | solution.py:548
  124.5 5.7 %collective-permute-start.25 = (bf16[2,7168]{1,0:T(2,128)(2,1)S(1)}, bf16[2,7168]{1,0:T(2,128)(2,1)S(1)}, u32[]{:S(2)}, u32[]{:S(2)}) collective-permute-start(bf16[2,7168]{1,0:T(2,128)(2,1)S(1)} %get-tuple-element.85), channel_id=1, source_target_pairs={{0,12},{2,14},{4,8},{6,10},{8,4},{10,6},{12,0},{14,2},{1,13},{3,15... | collective-permute-start | bytes 86024 | tf_op jit(solution)/shard_map/ppermute | solution.py:548

commit v12 on v10

--- a/solution.py
+++ b/solution.py
@@ -297,7 +297,7 @@
             ],
             input_output_aliases=alias,
             cost_estimate=SMALL,
-            compiler_params=pltpu.CompilerParams(vmem_limit_bytes=16 * 1024 * 1024),
+            compiler_params=pltpu.CompilerParams(vmem_limit_bytes=(4 + 4 * n_tok) * 1024 * 1024),
             name="attend",
         )(*operands)
 
@@ -505,6 +505,7 @@
     own_cache = pack_cache(latent_cache[0], rope_cache[0])
     cache_a = line_hop(own_cache, tok_rows, outer)
     first_b = line_hop(own_cache, tok_rows, inner)
+    first_c = line_hop(own_cache, tok_rows, [(i ^ 1, j) for i, j in inner])
 
     q_lat = q_latent.reshape(tok_rows, q_rows, width)
     rope_raw = q_rope.reshape(tok_rows, q_rows * rope_width // width, width)
@@ -549,11 +550,8 @@
 
     ways = [(k, m) for m in range(around) for k in range(experts)]
     pieces = outgoing[:1] + [along(outgoing[k], k, 0) for k in range(1, experts)]
-    cache_a, first_b, stay, *pieces = lax.optimization_barrier(
-        (cache_a, first_b, stay, *pieces)
-    )
     second_b = line_hop(first_b, tok_rows, outward)
-    first_c = line_hop(cache_a, tok_rows, inner)
+    cache_a, stay, *pieces = lax.optimization_barrier((cache_a, stay, *pieces))
 
     def both_halves(cache):
         return cache, swapped(cache, "expert", 0)

time: 127 us -> 128 us (level)
    ppermute x5, waiting for transfers between devices: 10.4 us -> 15.1 us  [line_hop(): return lax.ppermute(x, 'branch', pairs)]
    ppermute x5, waiting for transfers between devices: 28.1 us -> 24.1 us  [along(): return lax.ppermute(x, 'branch', list(enumerate(there)))]
  transfers between devices with their start and end apart: 25 -> 25, of which waited for: 6 -> 7; matrix products, arithmetic and copies ran while one was open for 5% -> 5% of each run, Pallas kernels for 29% -> 29%
where the time goes in v12:
time: 128 us; the launch traced here: 127 us
  waiting for transfers between devices  42.8 us (33%)
  Pallas kernels  40.2 us (31%)
  starting transfers between devices  32.8 us (26%)
  local copies, waits for them, and re-layouts  5.97 us (5%)
  other arithmetic  4.4 us (3%)
    pallas_call x5, Pallas kernels, call(): pl.pallas_call(functools.partial(kernel, slot, gives, keeps, has_placed),...  30.6 us
    ppermute x5, waiting for transfers between devices, along(): return lax.ppermute(x, 'branch', list(enumerate(there)))  24.1 us
    ppermute x5, waiting for transfers between devices, line_hop(): return lax.ppermute(x, 'branch', pairs)  15.1 us
    ppermute x5, starting transfers between devices, along(): return lax.ppermute(x, 'branch', list(enumerate(there)))  10.5 us
    ppermute x5, starting transfers between devices, line_hop(): return lax.ppermute(x, 'branch', pairs)  9.99 us
    ppermute x9, starting transfers between devices, swapped(): lax.ppermute(x, axis, [(i, i ^ 1 << bit) for i in range(lax.axis_size(axi...  7.93 us
    ppermute x6, starting transfers between devices, around_chip(): return lax.ppermute(x, ('branch', 'expert'), pairs)  4.41 us
    pallas_call x2, Pallas kernels, pack_tokens(): pl.pallas_call(functools.partial(pack_tokens_kernel, parity), out_shape=j...  3.35 us
  transfers between devices with their start and end apart: 25, of which 7 were waited for; matrix products, arithmetic and copies ran while one was open for 5% of the time, Pallas kernels for 29%

profile of v12, /device:TPU:0, one launch (start us, length us, event | category | flops | bytes accessed | tf_op | source)
XLA Modules:
  0.0 127.3 jit_solution(4954857403977742558)
XLA Ops:
  0.7 2.3 %pack_cache.1.refs_2_ = bf16[1152,512]{1,0:T(8,128)(2,1)} custom-call(bf16[1024,512]{1,0:T(8,128)(2,1)} %bitcast.13, bf16[128,512]{1,0:T(8,128)(2,1)} %bitcast.14), custom_call_target="tpu_custom_call" | custom-call | bytes 1024 | tf_op jit(solution)/shard_map/pack_cache/pallas_call | solution.py:52
  3.0 3.1 %collective-permute-start.2 = (bf16[1152,512]{1,0:T(8,128)(2,1)}, bf16[1152,512]{1,0:T(8,128)(2,1)}, u32[]{:S(2)}, u32[]{:S(2)}) collective-permute-start(bf16[1152,512]{1,0:T(8,128)(2,1)} %pack_cache.1.refs_2_), channel_id=1, source_target_pairs={{0,4},{4,0},{8,12},{12,8},{2,6},{6,2},{10,14},{14,10},{1,5},{5,1},... | collective-permute-start | bytes 3538952 | tf_op jit(solution)/shard_map/ppermute | solution.py:36
  6.1 1.7 %collective-permute-start.4 = (bf16[1152,512]{1,0:T(8,128)(2,1)}, bf16[1152,512]{1,0:T(8,128)(2,1)}, u32[]{:S(2)}, u32[]{:S(2)}) collective-permute-start(bf16[1152,512]{1,0:T(8,128)(2,1)} %pack_cache.1.refs_2_), channel_id=1, source_target_pairs={{4,8},{8,4},{6,10},{10,6},{5,9},{9,5},{7,11},{11,7},{20,24},{24,20... | collective-permute-start | bytes 3538952 | tf_op jit(solution)/shard_map/ppermute | solution.py:36
  8.0 1.6 %copy-done = bf16[8,2,128,512]{3,2,1,0:T(8,128)(2,1)S(1)} copy-done((bf16[8,2,128,512]{3,2,1,0:T(8,128)(2,1)S(1)}, bf16[8,2,128,512]{3,2,1,0:T(8,128)(2,1)}, u32[]{:S(2)}) %copy-start) | copy-done | bytes 2097176
  9.6 2.2 %pack_tokens.2 = bf16[4,320,512]{2,1,0:T(8,128)(2,1)} custom-call(s32[8]{0:T(128)S(1)} %copy-done.5, s32[1]{0:T(128)} %bitcast.own_ref, bf16[8,256,512]{2,1,0:T(8,128)(2,1)S(1)} %bitcast.8, bf16[8,32,512]{2,1,0:T(8,128)(2,1)S(1)} %reshape.28.rope_ref, bf16[8,32,512]{2,1,0:T(8,128)(2,1)S(1)} %fusion.2.new_ref), custom_call_target="tpu_custom_call" | custom-call | bytes 1024 | tf_op jit(solution)/shard_map/pack_tokens/pallas_call | solution.py:106
  11.8 1.6 %collective-permute-start.1 = (bf16[4,320,512]{2,1,0:T(8,128)(2,1)}, bf16[4,320,512]{2,1,0:T(8,128)(2,1)S(1)}, u32[]{:S(2)}, u32[]{:S(2)}) collective-permute-start(bf16[4,320,512]{2,1,0:T(8,128)(2,1)} %pack_tokens.2), channel_id=1, source_target_pairs={{0,2},{2,0},{4,6},{6,4},{8,10},{10,8},{12,14},{14,12},{1,3},{3,1},... | collective-permute-start | bytes 3932168 | tf_op jit(solution)/shard_map/ppermute | solution.py:28
  13.5 0.3 dispatch.1
  13.9 2.9 %collective-permute-start.3 = (bf16[2,7168]{1,0:T(2,128)(2,1)S(1)}, bf16[2,7168]{1,0:T(2,128)(2,1)S(1)}, u32[]{:S(2)}, u32[]{:S(2)}) collective-permute-start(bf16[2,7168]{1,0:T(2,128)(2,1)S(1)} %get-tuple-element.51), channel_id=1, source_target_pairs={{0,8},{2,10},{4,12},{6,14},{8,0},{10,2},{12,4},{14,6},{1,9},{3,11}... | collective-permute-start | bytes 86024 | tf_op jit(solution)/shard_map/ppermute | solution.py:549
  16.8 1.6 %copy-done.1 = bf16[8,2,128,512]{3,2,1,0:T(8,128)(2,1)S(1)} copy-done((bf16[8,2,128,512]{3,2,1,0:T(8,128)(2,1)S(1)}, bf16[8,2,128,512]{3,2,1,0:T(8,128)(2,1)}, u32[]{:S(2)}) %copy-start.1) | copy-done | bytes 2097176
  18.4 1.1 pack_tokens.3.refs_1_.refs_0_
  19.5 18.2 %collective-permute-done.3.refs_1_ = bf16[2,7168]{1,0:T(2,128)(2,1)S(1)} collective-permute-done((bf16[2,7168]{1,0:T(2,128)(2,1)S(1)}, bf16[2,7168]{1,0:T(2,128)(2,1)S(1)}, u32[]{:S(2)}, u32[]{:S(2)}) %collective-permute-start.3) | collective-permute-done | bytes 28704 | tf_op jit(solution)/shard_map/ppermute | solution.py:549
  37.7 2.5 %collective-permute-start = (bf16[1152,512]{1,0:T(8,128)(2,1)}, bf16[1152,512]{1,0:T(8,128)(2,1)}, u32[]{:S(2)}, u32[]{:S(2)}) collective-permute-start(bf16[1152,512]{1,0:T(8,128)(2,1)} %pack_cache.1.refs_2_), channel_id=1, source_target_pairs={{0,8},{12,4},{2,10},{14,6},{1,9},{13,5},{3,11},{15,7},{16,24},{28,... | collective-permute-start | bytes 3538952 | tf_op jit(solution)/shard_map/ppermute | solution.py:36
  40.2 1.3 %collective-permute-start.11 = (bf16[1152,512]{1,0:T(8,128)(2,1)}, bf16[1152,512]{1,0:T(8,128)(2,1)}, u32[]{:S(2)}, u32[]{:S(2)}) collective-permute-start(bf16[1152,512]{1,0:T(8,128)(2,1)} %collective-permute-done.4), channel_id=1, source_target_pairs={{4,0},{8,12},{6,2},{10,14},{5,1},{9,13},{7,3},{11,15},{20,16},{24,... | collective-permute-start | bytes 3538952 | tf_op jit(solution)/shard_map/ppermute | solution.py:36
  41.5 0.8 collective-permute-done.1.refs_0_
  42.3 6.9 %attend.5 = (bf16[256,512]{1,0:T(8,128)(2,1)S(1)}, bf16[8,256,512]{2,1,0:T(8,128)(2,1)}) custom-call(s32[8]{0:T(128)S(1)} %copy-done.5, s32[1]{0:T(128)} %bitcast.own_ref, bf16[4,320,512]{2,1,0:T(8,128)(2,1)S(1)} %collective-permute-done.1.refs_0_, bf16[4,320,512]{2,1,0:T(8,128)(2,1)S(1)} %pack_tokens.3.refs_1_.refs_0_, ...), custom_call_target="tpu_custom_call" | custom-call | bytes 1024 | tf_op jit(solution)/shard_map/attend/pallas_call | solution.py:285
  49.2 1.6 %collective-permute-start.7 = (bf16[256,512]{1,0:T(8,128)(2,1)S(1)}, bf16[256,512]{1,0:T(8,128)(2,1)S(1)}, u32[]{:S(2)}, u32[]{:S(2)}) collective-permute-start(bf16[256,512]{1,0:T(8,128)(2,1)S(1)} %get-tuple-element.57), channel_id=1, source_target_pairs={{0,2},{2,0},{4,6},{6,4},{8,10},{10,8},{12,14},{14,12},{1,3},{3,1},... | collective-permute-start | bytes 786440 | tf_op jit(solution)/shard_map/ppermute | solution.py:28
  50.8 0.3 stack_rows.2.refs_0_
  51.1 3.2 %collective-permute-start.8 = (bf16[4,7168]{1,0:T(4,128)(2,1)S(1)}, bf16[4,7168]{1,0:T(4,128)(2,1)S(1)}, u32[]{:S(2)}, u32[]{:S(2)}) collective-permute-start(bf16[4,7168]{1,0:T(4,128)(2,1)S(1)} %stack_rows.2.refs_0_), channel_id=1, source_target_pairs={{0,4},{2,6},{4,0},{6,2},{8,12},{10,14},{12,8},{14,10},{1,5},{3,7},... | collective-permute-start | bytes 172040 | tf_op jit(solution)/shard_map/ppermute | solution.py:549
  54.2 6.9 %attend.6 = (bf16[256,512]{1,0:T(8,128)(2,1)S(1)}, bf16[8,256,512]{2,1,0:T(8,128)(2,1)}) custom-call(s32[8]{0:T(128)S(1)} %copy-done.5, s32[1]{0:T(128)} %bitcast.own_ref, bf16[4,320,512]{2,1,0:T(8,128)(2,1)S(1)} %collective-permute-done.1.refs_0_, bf16[4,320,512]{2,1,0:T(8,128)(2,1)S(1)} %pack_tokens.3.refs_1_.refs_0_, ...), custom_call_target="tpu_custom_call", output_to_operand_aliasing={{1}: (6, {})} | custom-call | bytes 1024 | tf_op jit(solution)/shard_map/attend/pallas_call | solution.py:285
  61.1 4.7 %collective-permute-done = bf16[1152,512]{1,0:T(8,128)(2,1)} collective-permute-done((bf16[1152,512]{1,0:T(8,128)(2,1)}, bf16[1152,512]{1,0:T(8,128)(2,1)}, u32[]{:S(2)}, u32[]{:S(2)}) %collective-permute-start) | collective-permute-done | bytes 1179680 | tf_op jit(solution)/shard_map/ppermute | solution.py:36
  65.8 5.9 %collective-permute-done.8.refs_1_ = bf16[4,7168]{1,0:T(4,128)(2,1)S(1)} collective-permute-done((bf16[4,7168]{1,0:T(4,128)(2,1)S(1)}, bf16[4,7168]{1,0:T(4,128)(2,1)S(1)}, u32[]{:S(2)}, u32[]{:S(2)}) %collective-permute-start.8) | collective-permute-done | bytes 57376 | tf_op jit(solution)/shard_map/ppermute | solution.py:549
  71.7 1.4 %broadcast_select_fusion.1.refs_2_ = bf16[1152,512]{1,0:T(8,128)(2,1)S(1)} fusion(bf16[1152,512]{1,0:T(8,128)(2,1)} %collective-permute-done.4, bf16[1152,512]{1,0:T(8,128)(2,1)} %collective-permute-done.11, pred[]{:T(512)S(6)} %and.22), kind=kLoop, calls=%fused_computation.2 | loop fusion | flops 589824 | bytes 3538945 | tf_op jit(solution)/shard_map/jit(_where)/select_n | solution.py:571
  73.2 1.5 %collective-permute-start.9 = (bf16[1152,512]{1,0:T(8,128)(2,1)}, bf16[1152,512]{1,0:T(8,128)(2,1)S(1)}, u32[]{:S(2)}, u32[]{:S(2)}) collective-permute-start(bf16[1152,512]{1,0:T(8,128)(2,1)} %collective-permute-done), channel_id=1, source_target_pairs={{4,0},{8,12},{6,2},{10,14},{5,1},{9,13},{7,3},{11,15},{20,16},{24,... | collective-permute-start | bytes 3538952 | tf_op jit(solution)/shard_map/ppermute | solution.py:36
  74.7 1.6 %collective-permute-start.10 = (bf16[256,512]{1,0:T(8,128)(2,1)S(1)}, bf16[256,512]{1,0:T(8,128)(2,1)S(1)}, u32[]{:S(2)}, u32[]{:S(2)}) collective-permute-start(bf16[256,512]{1,0:T(8,128)(2,1)S(1)} %get-tuple-element.56), channel_id=1, source_target_pairs={{0,2},{2,0},{4,6},{6,4},{8,10},{10,8},{12,14},{14,12},{1,3},{3,1},... | collective-permute-start | bytes 786440 | tf_op jit(solution)/shard_map/ppermute | solution.py:28
  76.5 0.6 collective-permute-start.13
  77.1 1.6 %collective-permute-start.15 = (bf16[8,7168]{1,0:T(8,128)(2,1)S(1)}, bf16[8,7168]{1,0:T(8,128)(2,1)S(1)}, u32[]{:S(2)}, u32[]{:S(2)}) collective-permute-start(bf16[8,7168]{1,0:T(8,128)(2,1)S(1)} %stack_rows.3.refs_0_), channel_id=1, source_target_pairs={{0,3},{1,2},{2,1},{3,0},{4,7},{5,6},{6,5},{7,4},{8,11},{9,10},{10,... | collective-permute-start | bytes 344072 | tf_op jit(solution)/shard_map/ppermute | solution.py:581
  78.8 6.5 %attend.7 = (bf16[256,512]{1,0:T(8,128)(2,1)}, bf16[8,256,512]{2,1,0:T(8,128)(2,1)}) custom-call(s32[8]{0:T(128)S(1)} %copy-done.5, s32[1]{0:T(128)} %bitcast.own_ref, bf16[4,320,512]{2,1,0:T(8,128)(2,1)S(1)} %collective-permute-done.1.refs_0_, bf16[4,320,512]{2,1,0:T(8,128)(2,1)S(1)} %pack_tokens.3.refs_1_.refs_0_, ...), custom_call_target="tpu_custom_call", output_to_operand_aliasing={{1}: (6, {})} | custom-call | bytes 1024 | tf_op jit(solution)/shard_map/attend/pallas_call | solution.py:285
  85.3 1.0 collective-permute-done.13.refs_1_
  86.3 1.6 %collective-permute-done.15.refs_3_ = bf16[8,7168]{1,0:T(8,128)(2,1)S(1)} collective-permute-done((bf16[8,7168]{1,0:T(8,128)(2,1)S(1)}, bf16[8,7168]{1,0:T(8,128)(2,1)S(1)}, u32[]{:S(2)}, u32[]{:S(2)}) %collective-permute-start.15) | collective-permute-done | bytes 114720 | tf_op jit(solution)/shard_map/ppermute | solution.py:581
  88.0 1.6 %experts.1 = (f32[8,7168]{1,0:T(8,128)S(1)}, bf16[8,7168]{1,0:T(8,128)(2,1)S(1)}, bf16[8,7168]{1,0:T(8,128)(2,1)S(1)}, bf16[8,7168]{1,0:T(8,128)(2,1)S(1)}) custom-call(bf16[8,7168]{1,0:T(8,128)(2,1)S(1)} %stack_rows.3.refs_0_, bf16[8,7168]{1,0:T(8,128)(2,1)S(1)} %collective-permute-done.13.refs_1_, bf16[8,7168]{1,0:T(8,128)(2,1)S(1)} %collective-permute-done.14.refs_2_, ...), custom_call_target="tpu_custom_call" | custom-call | bytes 1024 | tf_op jit(solution)/shard_map/experts/pallas_call | solution.py:454
  89.5 1.6 %collective-permute-start.16 = (bf16[8,7168]{1,0:T(8,128)(2,1)S(1)}, bf16[8,7168]{1,0:T(8,128)(2,1)S(1)}, u32[]{:S(2)}, u32[]{:S(2)}) collective-permute-start(bf16[8,7168]{1,0:T(8,128)(2,1)S(1)} %get-tuple-element.74), channel_id=1, source_target_pairs={{0,2},{1,3},{2,0},{3,1},{4,6},{5,7},{6,4},{7,5},{8,10},{9,11},{10,... | collective-permute-start | bytes 344072 | tf_op jit(solution)/shard_map/ppermute | solution.py:581
  91.1 0.2 collective-permute-start.17
  91.4 0.4 collective-permute-start.18
  91.8 1.5 %collective-permute-start.19 = (bf16[256,512]{1,0:T(8,128)(2,1)}, bf16[256,512]{1,0:T(8,128)(2,1)S(1)}, u32[]{:S(2)}, u32[]{:S(2)}) collective-permute-start(bf16[256,512]{1,0:T(8,128)(2,1)} %get-tuple-element.66), channel_id=1, source_target_pairs={{0,2},{2,0},{4,6},{6,4},{8,10},{10,8},{12,14},{14,12},{1,3},{3,1},... | collective-permute-start | bytes 786440 | tf_op jit(solution)/shard_map/ppermute | solution.py:28
  93.3 10.4 %collective-permute-done.9 = bf16[1152,512]{1,0:T(8,128)(2,1)S(1)} collective-permute-done((bf16[1152,512]{1,0:T(8,128)(2,1)}, bf16[1152,512]{1,0:T(8,128)(2,1)S(1)}, u32[]{:S(2)}, u32[]{:S(2)}) %collective-permute-start.9) | collective-permute-done | bytes 1179680 | tf_op jit(solution)/shard_map/ppermute | solution.py:36
  103.7 1.2 broadcast_select_fusion.refs_1_
  104.9 0.7 fusion.3
  105.6 0.7 fusion.4
  106.3 0.9 collective-permute-start.22
  107.2 2.3 %collective-permute-start.23 = (bf16[2,7168]{1,0:T(2,128)(2,1)S(1)}, bf16[2,7168]{1,0:T(2,128)(2,1)S(1)}, u32[]{:S(2)}, u32[]{:S(2)}) collective-permute-start(bf16[2,7168]{1,0:T(2,128)(2,1)S(1)} %get-tuple-element.96), channel_id=1, source_target_pairs={{0,8},{2,10},{4,12},{6,14},{8,0},{10,2},{12,4},{14,6},{1,9},{3,11}... | collective-permute-start | bytes 86024 | tf_op jit(solution)/shard_map/ppermute | solution.py:549
  109.5 1.2 collective-permute-start.24
  110.8 1.0 slice.19
  111.8 5.2 %attend.8 = bf16[256,512]{1,0:T(8,128)(2,1)} custom-call(s32[8]{0:T(128)S(1)} %copy-done.5, s32[1]{0:T(128)} %bitcast.own_ref, bf16[4,320,512]{2,1,0:T(8,128)(2,1)S(1)} %collective-permute-done.1.refs_0_, bf16[1152,512]{1,0:T(8,128)(2,1)} %broadcast_select_fusion.refs_1_, bf16[1152,512]{1,0:T(8,128)(2,1)} %collective-permute-done.20.refs_2_), custom_call_target="tpu_custom_call" | custom-call | bytes 1024 | tf_op jit(solution)/shard_map/attend/pallas_call | solution.py:285
  116.9 1.6 %collective-permute-start.21 = (bf16[256,512]{1,0:T(8,128)(2,1)}, bf16[256,512]{1,0:T(8,128)(2,1)S(1)}, u32[]{:S(2)}, u32[]{:S(2)}) collective-permute-start(bf16[256,512]{1,0:T(8,128)(2,1)} %attend.8), channel_id=1, source_target_pairs={{0,2},{2,0},{4,6},{6,4},{8,10},{10,8},{12,14},{14,12},{1,3},{3,1},... | collective-permute-start | bytes 786440 | tf_op jit(solution)/shard_map/ppermute | solution.py:28
  118.5 0.8 convert_add_fusion.1
  119.6 0.8 convert_element_type.39
  120.4 5.2 %attend.9.refs_4_ = bf16[8,256,512]{2,1,0:T(8,128)(2,1)} custom-call(s32[8]{0:T(128)S(1)} %copy-done.5, s32[1]{0:T(128)} %bitcast.own_ref, bf16[4,320,512]{2,1,0:T(8,128)(2,1)S(1)} %pack_tokens.3.refs_1_.refs_0_, bf16[1152,512]{1,0:T(8,128)(2,1)} %broadcast_select_fusion.refs_1_, ...), custom_call_target="tpu_custom_call", output_to_operand_aliasing={{}: (5, {})} | custom-call | bytes 1024 | tf_op jit(solution)/shard_map/attend/pallas_call | solution.py:285
  125.5 1.6 %place.1 = bf16[8,256,512]{2,1,0:T(8,128)(2,1)} custom-call(s32[8]{0:T(128)S(1)} %copy-done.5, s32[1]{0:T(128)} %bitcast.own_ref, bf16[256,512]{1,0:T(8,128)(2,1)S(1)} %collective-permute-done.7.refs_0_, bf16[256,512]{1,0:T(8,128)(2,1)S(1)} %collective-permute-done.10.refs_1_, ...), custom_call_target="tpu_custom_call", output_to_operand_aliasing={{}: (6, {})} | custom-call | bytes 1024 | tf_op jit(solution)/shard_map/place/pallas_call | solution.py:321
  (52 shorter events, 1.0 us)
Async XLA Ops:
  0.6 7.1 %copy-start.8 = (bf16[8,2,8192]{2,1,0:T(2,128)(2,1)S(1)}, bf16[8,2,8192]{2,1,0:T(2,128)(2,1)}, u32[]{:S(2)}) copy-start(bf16[8,2,8192]{2,1,0:T(2,128)(2,1)} %param.16) | copy-start | bytes 786436
  0.6 7.3 %copy-start.10 = (bf16[8,2,512]{2,1,0:T(2,128)(2,1)S(1)}, bf16[8,2,512]{2,1,0:T(2,128)(2,1)}, u32[]{:S(2)}) copy-start(bf16[8,2,512]{2,1,0:T(2,128)(2,1)} %param.17) | copy-start | bytes 49156
  0.7 7.3 %copy-start.11 = (bf16[8,2,64]{2,1,0:T(2,128)(2,1)S(1)}, bf16[8,2,64]{2,1,0:T(2,128)(2,1)}, u32[]{:S(2)}) copy-start(bf16[8,2,64]{2,1,0:T(2,128)(2,1)} %param.18) | copy-start | bytes 6148
  0.7 7.3 %copy-start.5 = (s32[8]{0:T(128)S(1)}, s32[8]{0:T(128)}, u32[]{:S(2)}) copy-start(s32[8]{0:T(128)} %slot_ref.15) | copy-start | bytes 100
  3.0 34.7 %collective-permute-start.2 = (bf16[1152,512]{1,0:T(8,128)(2,1)}, bf16[1152,512]{1,0:T(8,128)(2,1)}, u32[]{:S(2)}, u32[]{:S(2)}) collective-permute-start(bf16[1152,512]{1,0:T(8,128)(2,1)} %pack_cache.1.refs_2_), channel_id=1, source_target_pairs={{0,4},{4,0},{8,12},{12,8},{2,6},{6,2},{10,14},{14,10},{1,5},{5,1},... | collective-permute-start | bytes 3538952 | tf_op jit(solution)/shard_map/ppermute | solution.py:36
  6.1 34.1 %collective-permute-start.4 = (bf16[1152,512]{1,0:T(8,128)(2,1)}, bf16[1152,512]{1,0:T(8,128)(2,1)}, u32[]{:S(2)}, u32[]{:S(2)}) collective-permute-start(bf16[1152,512]{1,0:T(8,128)(2,1)} %pack_cache.1.refs_2_), channel_id=1, source_target_pairs={{4,8},{8,4},{6,10},{10,6},{5,9},{9,5},{7,11},{11,7},{20,24},{24,20... | collective-permute-start | bytes 3538952 | tf_op jit(solution)/shard_map/ppermute | solution.py:36
  8.0 1.6 %copy-start = (bf16[8,2,128,512]{3,2,1,0:T(8,128)(2,1)S(1)}, bf16[8,2,128,512]{3,2,1,0:T(8,128)(2,1)}, u32[]{:S(2)}) copy-start(bf16[8,2,128,512]{3,2,1,0:T(8,128)(2,1)} %param.15) | copy-start | bytes 6291460
  9.6 3.8 %copy-start.9 = (bf16[8,2,7168]{2,1,0:T(2,128)(2,1)S(1)}, bf16[8,2,7168]{2,1,0:T(2,128)(2,1)}, u32[]{:S(2)}) copy-start(bf16[8,2,7168]{2,1,0:T(2,128)(2,1)} %param.20) | copy-start | bytes 688132
  9.6 3.9 %copy-start.6 = (s32[8,2,8]{2,1,0:T(2,128)S(1)}, s32[8,2,8]{2,1,0:T(2,128)}, u32[]{:S(2)}) copy-start(s32[8,2,8]{2,1,0:T(2,128)} %param.21) | copy-start | bytes 1540
  9.6 3.9 %copy-start.7 = (f32[8,2,8]{2,1,0:T(2,128)S(1)}, f32[8,2,8]{2,1,0:T(2,128)}, u32[]{:S(2)}) copy-start(f32[8,2,8]{2,1,0:T(2,128)} %param.22) | copy-start | bytes 1540
  11.8 30.5 %collective-permute-start.1 = (bf16[4,320,512]{2,1,0:T(8,128)(2,1)}, bf16[4,320,512]{2,1,0:T(8,128)(2,1)S(1)}, u32[]{:S(2)}, u32[]{:S(2)}) collective-permute-start(bf16[4,320,512]{2,1,0:T(8,128)(2,1)} %pack_tokens.2), channel_id=1, source_target_pairs={{0,2},{2,0},{4,6},{6,4},{8,10},{10,8},{12,14},{14,12},{1,3},{3,1},... | collective-permute-start | bytes 3932168 | tf_op jit(solution)/shard_map/ppermute | solution.py:28
  13.4 28.9 %collective-permute-start.6 = (bf16[1152,512]{1,0:T(8,128)(2,1)}, bf16[1152,512]{1,0:T(8,128)(2,1)}, u32[]{:S(2)}, u32[]{:S(2)}) collective-permute-start(bf16[1152,512]{1,0:T(8,128)(2,1)} %pack_cache.1.refs_2_), channel_id=1, source_target_pairs={{0,1},{1,0},{2,3},{3,2},{4,5},{5,4},{6,7},{7,6},{8,9},{9,8},{10,11... | collective-permute-start | bytes 3538952 | tf_op jit(solution)/shard_map/ppermute | solution.py:28
  13.9 23.8 %collective-permute-start.3 = (bf16[2,7168]{1,0:T(2,128)(2,1)S(1)}, bf16[2,7168]{1,0:T(2,128)(2,1)S(1)}, u32[]{:S(2)}, u32[]{:S(2)}) collective-permute-start(bf16[2,7168]{1,0:T(2,128)(2,1)S(1)} %get-tuple-element.51), channel_id=1, source_target_pairs={{0,8},{2,10},{4,12},{6,14},{8,0},{10,2},{12,4},{14,6},{1,9},{3,11}... | collective-permute-start | bytes 86024 | tf_op jit(solution)/shard_map/ppermute | solution.py:549
  16.8 1.6 %copy-start.1 = (bf16[8,2,128,512]{3,2,1,0:T(8,128)(2,1)S(1)}, bf16[8,2,128,512]{3,2,1,0:T(8,128)(2,1)}, u32[]{:S(2)}) copy-start(bf16[8,2,128,512]{3,2,1,0:T(8,128)(2,1)} %param.15) | copy-start | bytes 6291460
  37.7 16.5 %collective-permute-start.5 = (bf16[1152,512]{1,0:T(8,128)(2,1)}, bf16[1152,512]{1,0:T(8,128)(2,1)}, u32[]{:S(2)}, u32[]{:S(2)}) collective-permute-start(bf16[1152,512]{1,0:T(8,128)(2,1)} %collective-permute-done.2.refs_2_), channel_id=1, source_target_pairs={{0,1},{1,0},{2,3},{3,2},{4,5},{5,4},{6,7},{7,6},{8,9},{9,8},{10,11... | collective-permute-start | bytes 3538952 | tf_op jit(solution)/shard_map/ppermute | solution.py:28
  37.7 28.1 %collective-permute-start = (bf16[1152,512]{1,0:T(8,128)(2,1)}, bf16[1152,512]{1,0:T(8,128)(2,1)}, u32[]{:S(2)}, u32[]{:S(2)}) collective-permute-start(bf16[1152,512]{1,0:T(8,128)(2,1)} %pack_cache.1.refs_2_), channel_id=1, source_target_pairs={{0,8},{12,4},{2,10},{14,6},{1,9},{13,5},{3,11},{15,7},{16,24},{28,... | collective-permute-start | bytes 3538952 | tf_op jit(solution)/shard_map/ppermute | solution.py:36
  40.2 31.6 %collective-permute-start.11 = (bf16[1152,512]{1,0:T(8,128)(2,1)}, bf16[1152,512]{1,0:T(8,128)(2,1)}, u32[]{:S(2)}, u32[]{:S(2)}) collective-permute-start(bf16[1152,512]{1,0:T(8,128)(2,1)} %collective-permute-done.4), channel_id=1, source_target_pairs={{4,0},{8,12},{6,2},{10,14},{5,1},{9,13},{7,3},{11,15},{20,16},{24,... | collective-permute-start | bytes 3538952 | tf_op jit(solution)/shard_map/ppermute | solution.py:36
  49.2 22.5 %collective-permute-start.7 = (bf16[256,512]{1,0:T(8,128)(2,1)S(1)}, bf16[256,512]{1,0:T(8,128)(2,1)S(1)}, u32[]{:S(2)}, u32[]{:S(2)}) collective-permute-start(bf16[256,512]{1,0:T(8,128)(2,1)S(1)} %get-tuple-element.57), channel_id=1, source_target_pairs={{0,2},{2,0},{4,6},{6,4},{8,10},{10,8},{12,14},{14,12},{1,3},{3,1},... | collective-permute-start | bytes 786440 | tf_op jit(solution)/shard_map/ppermute | solution.py:28
  51.1 20.7 %collective-permute-start.8 = (bf16[4,7168]{1,0:T(4,128)(2,1)S(1)}, bf16[4,7168]{1,0:T(4,128)(2,1)S(1)}, u32[]{:S(2)}, u32[]{:S(2)}) collective-permute-start(bf16[4,7168]{1,0:T(4,128)(2,1)S(1)} %stack_rows.2.refs_0_), channel_id=1, source_target_pairs={{0,4},{2,6},{4,0},{6,2},{8,12},{10,14},{12,8},{14,10},{1,5},{3,7},... | collective-permute-start | bytes 172040 | tf_op jit(solution)/shard_map/ppermute | solution.py:549
  73.1 4.0 %collective-permute-start.12 = (bf16[1152,512]{1,0:T(8,128)(2,1)S(1)}, bf16[1152,512]{1,0:T(8,128)(2,1)S(1)}, u32[]{:S(2)}, u32[]{:S(2)}) collective-permute-start(bf16[1152,512]{1,0:T(8,128)(2,1)S(1)} %broadcast_select_fusion.1.refs_2_), channel_id=1, source_target_pairs={{0,1},{1,0},{2,3},{3,2},{4,5},{5,4},{6,7},{7,6},{8,9},{9,8},{10,11... | collective-permute-start | bytes 3538952 | tf_op jit(solution)/shard_map/ppermute | solution.py:28
  73.2 30.5 %collective-permute-start.9 = (bf16[1152,512]{1,0:T(8,128)(2,1)}, bf16[1152,512]{1,0:T(8,128)(2,1)S(1)}, u32[]{:S(2)}, u32[]{:S(2)}) collective-permute-start(bf16[1152,512]{1,0:T(8,128)(2,1)} %collective-permute-done), channel_id=1, source_target_pairs={{4,0},{8,12},{6,2},{10,14},{5,1},{9,13},{7,3},{11,15},{20,16},{24,... | collective-permute-start | bytes 3538952 | tf_op jit(solution)/shard_map/ppermute | solution.py:36
  74.7 17.1 %collective-permute-start.10 = (bf16[256,512]{1,0:T(8,128)(2,1)S(1)}, bf16[256,512]{1,0:T(8,128)(2,1)S(1)}, u32[]{:S(2)}, u32[]{:S(2)}) collective-permute-start(bf16[256,512]{1,0:T(8,128)(2,1)S(1)} %get-tuple-element.56), channel_id=1, source_target_pairs={{0,2},{2,0},{4,6},{6,4},{8,10},{10,8},{12,14},{14,12},{1,3},{3,1},... | collective-permute-start | bytes 786440 | tf_op jit(solution)/shard_map/ppermute | solution.py:28
  76.5 9.8 %collective-permute-start.13 = (bf16[8,7168]{1,0:T(8,128)(2,1)S(1)}, bf16[8,7168]{1,0:T(8,128)(2,1)S(1)}, u32[]{:S(2)}, u32[]{:S(2)}) collective-permute-start(bf16[8,7168]{1,0:T(8,128)(2,1)S(1)} %stack_rows.3.refs_0_), channel_id=1, source_target_pairs={{0,2},{1,3},{2,0},{3,1},{4,6},{5,7},{6,4},{7,5},{8,10},{9,11},{10,... | collective-permute-start | bytes 344072 | tf_op jit(solution)/shard_map/ppermute | solution.py:581
  77.1 9.2 %collective-permute-start.14 = (bf16[8,7168]{1,0:T(8,128)(2,1)S(1)}, bf16[8,7168]{1,0:T(8,128)(2,1)S(1)}, u32[]{:S(2)}, u32[]{:S(2)}) collective-permute-start(bf16[8,7168]{1,0:T(8,128)(2,1)S(1)} %stack_rows.3.refs_0_), channel_id=1, source_target_pairs={{0,1},{1,0},{2,3},{3,2},{4,5},{5,4},{6,7},{7,6},{8,9},{9,8},{10,11... | collective-permute-start | bytes 344072 | tf_op jit(solution)/shard_map/ppermute | solution.py:581
  77.1 10.8 %collective-permute-start.15 = (bf16[8,7168]{1,0:T(8,128)(2,1)S(1)}, bf16[8,7168]{1,0:T(8,128)(2,1)S(1)}, u32[]{:S(2)}, u32[]{:S(2)}) collective-permute-start(bf16[8,7168]{1,0:T(8,128)(2,1)S(1)} %stack_rows.3.refs_0_), channel_id=1, source_target_pairs={{0,3},{1,2},{2,1},{3,0},{4,7},{5,6},{6,5},{7,4},{8,11},{9,10},{10,... | collective-permute-start | bytes 344072 | tf_op jit(solution)/shard_map/ppermute | solution.py:581
  78.7 9.2 %copy-start.2 = (bf16[1,7168,128]{2,1,0:T(8,128)(2,1)S(1)}, bf16[1,7168,128]{2,1,0:T(8,128)(2,1)}, u32[]{:S(2)}) copy-start(bf16[1,7168,128]{2,1,0:T(8,128)(2,1)} %refs_4_.1) | copy-start | bytes 5505028
  78.8 9.2 %copy-start.3 = (bf16[1,7168,128]{2,1,0:T(8,128)(2,1)S(1)}, bf16[1,7168,128]{2,1,0:T(8,128)(2,1)}, u32[]{:S(2)}) copy-start(bf16[1,7168,128]{2,1,0:T(8,128)(2,1)} %refs_5_.1) | copy-start | bytes 5505028
  78.8 9.2 %copy-start.4 = (bf16[1,128,7168]{2,1,0:T(8,128)(2,1)S(1)}, bf16[1,128,7168]{2,1,0:T(8,128)(2,1)}, u32[]{:S(2)}) copy-start(bf16[1,128,7168]{2,1,0:T(8,128)(2,1)} %refs_6_.1) | copy-start | bytes 5505028
  89.5 14.1 %collective-permute-start.16 = (bf16[8,7168]{1,0:T(8,128)(2,1)S(1)}, bf16[8,7168]{1,0:T(8,128)(2,1)S(1)}, u32[]{:S(2)}, u32[]{:S(2)}) collective-permute-start(bf16[8,7168]{1,0:T(8,128)(2,1)S(1)} %get-tuple-element.74), channel_id=1, source_target_pairs={{0,2},{1,3},{2,0},{3,1},{4,6},{5,7},{6,4},{7,5},{8,10},{9,11},{10,... | collective-permute-start | bytes 344072 | tf_op jit(solution)/shard_map/ppermute | solution.py:581
  91.1 12.6 %collective-permute-start.17 = (bf16[8,7168]{1,0:T(8,128)(2,1)S(1)}, bf16[8,7168]{1,0:T(8,128)(2,1)S(1)}, u32[]{:S(2)}, u32[]{:S(2)}) collective-permute-start(bf16[8,7168]{1,0:T(8,128)(2,1)S(1)} %get-tuple-element.75), channel_id=1, source_target_pairs={{0,1},{1,0},{2,3},{3,2},{4,5},{5,4},{6,7},{7,6},{8,9},{9,8},{10,11... | collective-permute-start | bytes 344072 | tf_op jit(solution)/shard_map/ppermute | solution.py:581
  91.4 12.3 %collective-permute-start.18 = (bf16[8,7168]{1,0:T(8,128)(2,1)S(1)}, bf16[8,7168]{1,0:T(8,128)(2,1)S(1)}, u32[]{:S(2)}, u32[]{:S(2)}) collective-permute-start(bf16[8,7168]{1,0:T(8,128)(2,1)S(1)} %get-tuple-element.76), channel_id=1, source_target_pairs={{0,3},{1,2},{2,1},{3,0},{4,7},{5,6},{6,5},{7,4},{8,11},{9,10},{10,... | collective-permute-start | bytes 344072 | tf_op jit(solution)/shard_map/ppermute | solution.py:581
  91.8 20.0 %collective-permute-start.19 = (bf16[256,512]{1,0:T(8,128)(2,1)}, bf16[256,512]{1,0:T(8,128)(2,1)S(1)}, u32[]{:S(2)}, u32[]{:S(2)}) collective-permute-start(bf16[256,512]{1,0:T(8,128)(2,1)} %get-tuple-element.66), channel_id=1, source_target_pairs={{0,2},{2,0},{4,6},{6,4},{8,10},{10,8},{12,14},{14,12},{1,3},{3,1},... | collective-permute-start | bytes 786440 | tf_op jit(solution)/shard_map/ppermute | solution.py:28
  104.9 6.9 %collective-permute-start.20 = (bf16[1152,512]{1,0:T(8,128)(2,1)}, bf16[1152,512]{1,0:T(8,128)(2,1)}, u32[]{:S(2)}, u32[]{:S(2)}) collective-permute-start(bf16[1152,512]{1,0:T(8,128)(2,1)} %broadcast_select_fusion.refs_1_), channel_id=1, source_target_pairs={{0,1},{1,0},{2,3},{3,2},{4,5},{5,4},{6,7},{7,6},{8,9},{9,8},{10,11... | collective-permute-start | bytes 3538952 | tf_op jit(solution)/shard_map/ppermute | solution.py:28
  106.3 12.2 %collective-permute-start.22 = (bf16[2,7168]{1,0:T(2,128)(2,1)}, bf16[2,7168]{1,0:T(2,128)(2,1)S(1)}, u32[]{:S(2)}, u32[]{:S(2)}) collective-permute-start(bf16[2,7168]{1,0:T(2,128)(2,1)} %get-tuple-element.94), channel_id=1, source_target_pairs={{0,4},{2,6},{4,0},{6,2},{8,12},{10,14},{12,8},{14,10},{1,5},{3,7},... | collective-permute-start | bytes 86024 | tf_op jit(solution)/shard_map/ppermute | solution.py:549
  107.2 11.3 %collective-permute-start.23 = (bf16[2,7168]{1,0:T(2,128)(2,1)S(1)}, bf16[2,7168]{1,0:T(2,128)(2,1)S(1)}, u32[]{:S(2)}, u32[]{:S(2)}) collective-permute-start(bf16[2,7168]{1,0:T(2,128)(2,1)S(1)} %get-tuple-element.96), channel_id=1, source_target_pairs={{0,8},{2,10},{4,12},{6,14},{8,0},{10,2},{12,4},{14,6},{1,9},{3,11}... | collective-permute-start | bytes 86024 | tf_op jit(solution)/shard_map/ppermute | solution.py:549
  109.5 9.0 %collective-permute-start.24 = (bf16[2,7168]{1,0:T(2,128)(2,1)S(1)}, bf16[2,7168]{1,0:T(2,128)(2,1)}, u32[]{:S(2)}, u32[]{:S(2)}) collective-permute-start(bf16[2,7168]{1,0:T(2,128)(2,1)S(1)} %get-tuple-element.95), channel_id=1, source_target_pairs={{0,12},{2,14},{4,8},{6,10},{8,4},{10,6},{12,0},{14,2},{1,13},{3,15... | collective-permute-start | bytes 86024 | tf_op jit(solution)/shard_map/ppermute | solution.py:549
  116.9 8.6 %collective-permute-start.21 = (bf16[256,512]{1,0:T(8,128)(2,1)}, bf16[256,512]{1,0:T(8,128)(2,1)S(1)}, u32[]{:S(2)}, u32[]{:S(2)}) collective-permute-start(bf16[256,512]{1,0:T(8,128)(2,1)} %attend.8), channel_id=1, source_target_pairs={{0,2},{2,0},{4,6},{6,4},{8,10},{10,8},{12,14},{14,12},{1,3},{3,1},... | collective-permute-start | bytes 786440 | tf_op jit(solution)/shard_map/ppermute | solution.py:28

commit v13 on v10

--- a/solution.py
+++ b/solution.py
@@ -267,6 +267,7 @@
         anywhere = pl.BlockSpec(memory_space=pl.ANY)
         gives, keeps = int(guest is not None), int(stay is not None)
         n_tok = gives + keeps
+        caches = [pltpu.with_memory_space_constraint(x, pltpu.VMEM) for x in caches]
         operands = [x for x in (guest, stay) if x is not None] + [*caches]
         in_specs = [pl.BlockSpec(memory_space=pltpu.SMEM)] * 2 + [vmem] * len(operands)
         operands = [*scalars, *operands]
@@ -304,22 +305,22 @@
     return call
 
 
-def place_kernel(slot_ref, own_ref, *refs):
+def place_kernel(slots, slot_ref, own_ref, *refs):
     sources, (before, placed_ref, sems) = refs[:-3], refs[-3:]
     copies = []
-    for slot, source in enumerate(sources):
+    for i, (slot, source) in enumerate(zip(slots, sources)):
         row = row_for(slot, 1, slot_ref, own_ref)
-        copies.append(pltpu.make_async_copy(source, placed_ref.at[row], sems.at[slot]))
+        copies.append(pltpu.make_async_copy(source, placed_ref.at[row], sems.at[i]))
     for copy in copies:
         copy.start()
     for copy in copies:
         copy.wait()
 
 
-def place(scalars, sources, placed):
+def place(scalars, slots, sources, placed):
     vmem = pl.BlockSpec(memory_space=pltpu.VMEM)
     return pl.pallas_call(
-        place_kernel,
+        functools.partial(place_kernel, slots),
         out_shape=jax.ShapeDtypeStruct(placed.shape, placed.dtype),
         in_specs=[pl.BlockSpec(memory_space=pltpu.SMEM)] * 2
         + [vmem] * len(sources)
@@ -602,11 +603,12 @@
         for (k, m), piece in zip(ways, homeward)
     ]
     guest, back_2 = lax.optimization_barrier((guest, back_2))
+    placed = place(scalars, (0, 1, 2), (back_0, back_1, back_2), placed)
     (given_3,) = attend(scalars, 3, guest, None, cache_c, None)
     back_3 = swapped(given_3, "branch", 0)
     (placed,) = attend(scalars, 3, None, after(stay, given_3), cache_c, placed)
     homeward = [after(x, given_3).astype(jnp.float32) for x in homeward]
-    placed = place(scalars, (back_0, back_1, back_2, back_3), placed)
+    placed = place(scalars, (3,), (back_3,), placed)
     attended = placed.reshape(tok_rows, step_count, head_count, width)
 
     sums = [0.0] * experts

time: 127 us -> 128 us (level)
    pallas_call x1 -> x2, Pallas kernels: 1.55 us -> 2.73 us  [place(): pl.pallas_call(functools.partial(place_kernel, slots), out_shape=jax.Shap...]
where the time goes in v13:
time: 128 us; the launch traced here: 127 us
  waiting for transfers between devices  42.9 us (34%)
  Pallas kernels  40.6 us (32%)
  starting transfers between devices  32.1 us (25%)
  local copies, waits for them, and re-layouts  5.97 us (5%)
  other arithmetic  4.41 us (3%)
    pallas_call x5, Pallas kernels, call(): pl.pallas_call(functools.partial(kernel, slot, gives, keeps, has_placed),...  29.8 us
    ppermute x5, waiting for transfers between devices, along(): return lax.ppermute(x, 'branch', list(enumerate(there)))  28.1 us
    ppermute x5, starting transfers between devices, along(): return lax.ppermute(x, 'branch', list(enumerate(there)))  10.5 us
    ppermute x5, waiting for transfers between devices, line_hop(): return lax.ppermute(x, 'branch', pairs)  10.4 us
    ppermute x5, starting transfers between devices, line_hop(): return lax.ppermute(x, 'branch', pairs)  9.21 us
    ppermute x9, starting transfers between devices, swapped(): lax.ppermute(x, axis, [(i, i ^ 1 << bit) for i in range(lax.axis_size(axi...  7.96 us
    ppermute x6, starting transfers between devices, around_chip(): return lax.ppermute(x, ('branch', 'expert'), pairs)  4.41 us
    pallas_call x2, Pallas kernels, pack_tokens(): pl.pallas_call(functools.partial(pack_tokens_kernel, parity), out_shape=j...  3.35 us
  transfers between devices with their start and end apart: 25, of which 6 were waited for; matrix products, arithmetic and copies ran while one was open for 5% of the time, Pallas kernels for 29%

profile of v13, /device:TPU:0, one launch (start us, length us, event | category | flops | bytes accessed | tf_op | source)
XLA Modules:
  0.0 127.1 jit_solution(8917659596368375382)
XLA Ops:
  0.7 2.3 %pack_cache.1.refs_2_ = bf16[1152,512]{1,0:T(8,128)(2,1)} custom-call(bf16[1024,512]{1,0:T(8,128)(2,1)} %bitcast.13, bf16[128,512]{1,0:T(8,128)(2,1)} %bitcast.14), custom_call_target="tpu_custom_call" | custom-call | bytes 1024 | tf_op jit(solution)/shard_map/pack_cache/pallas_call | solution.py:52
  3.0 3.1 %collective-permute-start.1 = (bf16[1152,512]{1,0:T(8,128)(2,1)}, bf16[1152,512]{1,0:T(8,128)(2,1)}, u32[]{:S(2)}, u32[]{:S(2)}) collective-permute-start(bf16[1152,512]{1,0:T(8,128)(2,1)} %pack_cache.1.refs_2_), channel_id=1, source_target_pairs={{0,4},{4,0},{8,12},{12,8},{2,6},{6,2},{10,14},{14,10},{1,5},{5,1},... | collective-permute-start | bytes 3538952 | tf_op jit(solution)/shard_map/ppermute | solution.py:36
  6.1 1.7 %collective-permute-start.2 = (bf16[1152,512]{1,0:T(8,128)(2,1)}, bf16[1152,512]{1,0:T(8,128)(2,1)}, u32[]{:S(2)}, u32[]{:S(2)}) collective-permute-start(bf16[1152,512]{1,0:T(8,128)(2,1)} %pack_cache.1.refs_2_), channel_id=1, source_target_pairs={{4,8},{8,4},{6,10},{10,6},{5,9},{9,5},{7,11},{11,7},{20,24},{24,20... | collective-permute-start | bytes 3538952 | tf_op jit(solution)/shard_map/ppermute | solution.py:36
  8.0 1.6 %copy-done = bf16[8,2,128,512]{3,2,1,0:T(8,128)(2,1)S(1)} copy-done((bf16[8,2,128,512]{3,2,1,0:T(8,128)(2,1)S(1)}, bf16[8,2,128,512]{3,2,1,0:T(8,128)(2,1)}, u32[]{:S(2)}) %copy-start) | copy-done | bytes 2097176
  9.6 2.2 %pack_tokens.2 = bf16[4,320,512]{2,1,0:T(8,128)(2,1)} custom-call(s32[8]{0:T(128)S(1)} %copy-done.5, s32[1]{0:T(128)} %bitcast.own_ref, bf16[8,256,512]{2,1,0:T(8,128)(2,1)S(1)} %bitcast.8, bf16[8,32,512]{2,1,0:T(8,128)(2,1)S(1)} %reshape.28.rope_ref, bf16[8,32,512]{2,1,0:T(8,128)(2,1)S(1)} %fusion.2.new_ref), custom_call_target="tpu_custom_call" | custom-call | bytes 1024 | tf_op jit(solution)/shard_map/pack_tokens/pallas_call | solution.py:106
  11.8 1.6 %collective-permute-start = (bf16[4,320,512]{2,1,0:T(8,128)(2,1)}, bf16[4,320,512]{2,1,0:T(8,128)(2,1)S(1)}, u32[]{:S(2)}, u32[]{:S(2)}) collective-permute-start(bf16[4,320,512]{2,1,0:T(8,128)(2,1)} %pack_tokens.2), channel_id=1, source_target_pairs={{0,2},{2,0},{4,6},{6,4},{8,10},{10,8},{12,14},{14,12},{1,3},{3,1},... | collective-permute-start | bytes 3932168 | tf_op jit(solution)/shard_map/ppermute | solution.py:28
  13.5 0.3 dispatch.1
  13.9 2.9 %collective-permute-start.3 = (bf16[2,7168]{1,0:T(2,128)(2,1)S(1)}, bf16[2,7168]{1,0:T(2,128)(2,1)S(1)}, u32[]{:S(2)}, u32[]{:S(2)}) collective-permute-start(bf16[2,7168]{1,0:T(2,128)(2,1)S(1)} %get-tuple-element.52), channel_id=1, source_target_pairs={{0,8},{2,10},{4,12},{6,14},{8,0},{10,2},{12,4},{14,6},{1,9},{3,11}... | collective-permute-start | bytes 86024 | tf_op jit(solution)/shard_map/ppermute | solution.py:549
  16.8 1.6 %copy-done.1 = bf16[8,2,128,512]{3,2,1,0:T(8,128)(2,1)S(1)} copy-done((bf16[8,2,128,512]{3,2,1,0:T(8,128)(2,1)S(1)}, bf16[8,2,128,512]{3,2,1,0:T(8,128)(2,1)}, u32[]{:S(2)}) %copy-start.1) | copy-done | bytes 2097176
  18.4 1.1 pack_tokens.3.refs_1_.refs_0_
  19.5 18.2 %collective-permute-done.3.refs_1_ = bf16[2,7168]{1,0:T(2,128)(2,1)S(1)} collective-permute-done((bf16[2,7168]{1,0:T(2,128)(2,1)S(1)}, bf16[2,7168]{1,0:T(2,128)(2,1)S(1)}, u32[]{:S(2)}, u32[]{:S(2)}) %collective-permute-start.3) | collective-permute-done | bytes 28704 | tf_op jit(solution)/shard_map/ppermute | solution.py:549
  37.7 1.7 %collective-permute-start.4 = (bf16[1152,512]{1,0:T(8,128)(2,1)}, bf16[1152,512]{1,0:T(8,128)(2,1)}, u32[]{:S(2)}, u32[]{:S(2)}) collective-permute-start(bf16[1152,512]{1,0:T(8,128)(2,1)} %collective-permute-done.1.refs_2_), channel_id=1, source_target_pairs={{4,8},{8,4},{6,10},{10,6},{5,9},{9,5},{7,11},{11,7},{20,24},{24,20... | collective-permute-start | bytes 3538952 | tf_op jit(solution)/shard_map/ppermute | solution.py:36
  39.4 1.3 %collective-permute-start.9 = (bf16[1152,512]{1,0:T(8,128)(2,1)}, bf16[1152,512]{1,0:T(8,128)(2,1)}, u32[]{:S(2)}, u32[]{:S(2)}) collective-permute-start(bf16[1152,512]{1,0:T(8,128)(2,1)} %collective-permute-done.2), channel_id=1, source_target_pairs={{4,0},{8,12},{6,2},{10,14},{5,1},{9,13},{7,3},{11,15},{20,16},{24,... | collective-permute-start | bytes 3538952 | tf_op jit(solution)/shard_map/ppermute | solution.py:36
  40.6 1.7 %collective-permute-done.refs_0_ = bf16[4,320,512]{2,1,0:T(8,128)(2,1)S(1)} collective-permute-done((bf16[4,320,512]{2,1,0:T(8,128)(2,1)}, bf16[4,320,512]{2,1,0:T(8,128)(2,1)S(1)}, u32[]{:S(2)}, u32[]{:S(2)}) %collective-permute-start) | collective-permute-done | bytes 1310752 | tf_op jit(solution)/shard_map/ppermute | solution.py:28
  42.3 6.8 %attend.5 = (bf16[256,512]{1,0:T(8,128)(2,1)S(1)}, bf16[8,256,512]{2,1,0:T(8,128)(2,1)}) custom-call(s32[8]{0:T(128)S(1)} %copy-done.5, s32[1]{0:T(128)} %bitcast.own_ref, bf16[4,320,512]{2,1,0:T(8,128)(2,1)S(1)} %collective-permute-done.refs_0_, bf16[4,320,512]{2,1,0:T(8,128)(2,1)S(1)} %pack_tokens.3.refs_1_.refs_0_, bf16[1152,512]{1,0:T(8,128)(2,1)} %pack_cache.1.refs_2_, ...), custom_call_target="tpu_custom_call" | custom-call | bytes 1024 | tf_op jit(solution)/shard_map/attend/pallas_call | solution.py:286
  49.2 1.6 %collective-permute-start.7 = (bf16[256,512]{1,0:T(8,128)(2,1)S(1)}, bf16[256,512]{1,0:T(8,128)(2,1)S(1)}, u32[]{:S(2)}, u32[]{:S(2)}) collective-permute-start(bf16[256,512]{1,0:T(8,128)(2,1)S(1)} %get-tuple-element.59), channel_id=1, source_target_pairs={{0,2},{2,0},{4,6},{6,4},{8,10},{10,8},{12,14},{14,12},{1,3},{3,1},... | collective-permute-start | bytes 786440 | tf_op jit(solution)/shard_map/ppermute | solution.py:28
  50.8 0.3 stack_rows.2.refs_0_
  51.0 3.2 %collective-permute-start.8 = (bf16[4,7168]{1,0:T(4,128)(2,1)S(1)}, bf16[4,7168]{1,0:T(4,128)(2,1)S(1)}, u32[]{:S(2)}, u32[]{:S(2)}) collective-permute-start(bf16[4,7168]{1,0:T(4,128)(2,1)S(1)} %stack_rows.2.refs_0_), channel_id=1, source_target_pairs={{0,4},{2,6},{4,0},{6,2},{8,12},{10,14},{12,8},{14,10},{1,5},{3,7},... | collective-permute-start | bytes 172040 | tf_op jit(solution)/shard_map/ppermute | solution.py:549
  54.2 6.9 %attend.6 = (bf16[256,512]{1,0:T(8,128)(2,1)S(1)}, bf16[8,256,512]{2,1,0:T(8,128)(2,1)}) custom-call(s32[8]{0:T(128)S(1)} %copy-done.5, s32[1]{0:T(128)} %bitcast.own_ref, bf16[4,320,512]{2,1,0:T(8,128)(2,1)S(1)} %collective-permute-done.refs_0_, bf16[4,320,512]{2,1,0:T(8,128)(2,1)S(1)} %pack_tokens.3.refs_1_.refs_0_, ...), custom_call_target="tpu_custom_call", output_to_operand_aliasing={{1}: (6, {})} | custom-call | bytes 1024 | tf_op jit(solution)/shard_map/attend/pallas_call | solution.py:286
  61.1 10.0 %collective-permute-done.8.refs_1_ = bf16[4,7168]{1,0:T(4,128)(2,1)S(1)} collective-permute-done((bf16[4,7168]{1,0:T(4,128)(2,1)S(1)}, bf16[4,7168]{1,0:T(4,128)(2,1)S(1)}, u32[]{:S(2)}, u32[]{:S(2)}) %collective-permute-start.8) | collective-permute-done | bytes 57376 | tf_op jit(solution)/shard_map/ppermute | solution.py:549
  71.1 1.4 %broadcast_select_fusion.1.refs_2_ = bf16[1152,512]{1,0:T(8,128)(2,1)S(1)} fusion(bf16[1152,512]{1,0:T(8,128)(2,1)} %collective-permute-done.2, bf16[1152,512]{1,0:T(8,128)(2,1)} %collective-permute-done.9, pred[]{:T(512)S(6)} %and.22), kind=kLoop, calls=%fused_computation.2 | loop fusion | flops 589824 | bytes 3538945 | tf_op jit(solution)/shard_map/jit(_where)/select_n | solution.py:574
  72.5 1.5 %collective-permute-start.12 = (bf16[1152,512]{1,0:T(8,128)(2,1)}, bf16[1152,512]{1,0:T(8,128)(2,1)S(1)}, u32[]{:S(2)}, u32[]{:S(2)}) collective-permute-start(bf16[1152,512]{1,0:T(8,128)(2,1)} %collective-permute-done.4), channel_id=1, source_target_pairs={{4,0},{8,12},{6,2},{10,14},{5,1},{9,13},{7,3},{11,15},{20,16},{24,... | collective-permute-start | bytes 3538952 | tf_op jit(solution)/shard_map/ppermute | solution.py:36
  74.0 1.6 %collective-permute-start.13 = (bf16[256,512]{1,0:T(8,128)(2,1)S(1)}, bf16[256,512]{1,0:T(8,128)(2,1)S(1)}, u32[]{:S(2)}, u32[]{:S(2)}) collective-permute-start(bf16[256,512]{1,0:T(8,128)(2,1)S(1)} %get-tuple-element.58), channel_id=1, source_target_pairs={{0,2},{2,0},{4,6},{6,4},{8,10},{10,8},{12,14},{14,12},{1,3},{3,1},... | collective-permute-start | bytes 786440 | tf_op jit(solution)/shard_map/ppermute | solution.py:28
  75.9 0.6 collective-permute-start.14
  76.4 1.6 %collective-permute-start.16 = (bf16[8,7168]{1,0:T(8,128)(2,1)S(1)}, bf16[8,7168]{1,0:T(8,128)(2,1)S(1)}, u32[]{:S(2)}, u32[]{:S(2)}) collective-permute-start(bf16[8,7168]{1,0:T(8,128)(2,1)S(1)} %stack_rows.3.refs_0_), channel_id=1, source_target_pairs={{0,3},{1,2},{2,1},{3,0},{4,7},{5,6},{6,5},{7,4},{8,11},{9,10},{10,... | collective-permute-start | bytes 344072 | tf_op jit(solution)/shard_map/ppermute | solution.py:584
  78.1 6.5 %attend.7 = (bf16[256,512]{1,0:T(8,128)(2,1)}, bf16[8,256,512]{2,1,0:T(8,128)(2,1)}) custom-call(s32[8]{0:T(128)S(1)} %copy-done.5, s32[1]{0:T(128)} %bitcast.own_ref, bf16[4,320,512]{2,1,0:T(8,128)(2,1)S(1)} %collective-permute-done.refs_0_, bf16[4,320,512]{2,1,0:T(8,128)(2,1)S(1)} %pack_tokens.3.refs_1_.refs_0_, ...), custom_call_target="tpu_custom_call", output_to_operand_aliasing={{1}: (6, {})} | custom-call | bytes 1024 | tf_op jit(solution)/shard_map/attend/pallas_call | solution.py:286
  84.6 1.1 collective-permute-done.14.refs_1_
  85.7 1.6 %collective-permute-done.16.refs_3_ = bf16[8,7168]{1,0:T(8,128)(2,1)S(1)} collective-permute-done((bf16[8,7168]{1,0:T(8,128)(2,1)S(1)}, bf16[8,7168]{1,0:T(8,128)(2,1)S(1)}, u32[]{:S(2)}, u32[]{:S(2)}) %collective-permute-start.16) | collective-permute-done | bytes 114720 | tf_op jit(solution)/shard_map/ppermute | solution.py:584
  87.3 1.6 %experts.1 = (f32[8,7168]{1,0:T(8,128)S(1)}, bf16[8,7168]{1,0:T(8,128)(2,1)S(1)}, bf16[8,7168]{1,0:T(8,128)(2,1)S(1)}, bf16[8,7168]{1,0:T(8,128)(2,1)S(1)}) custom-call(bf16[8,7168]{1,0:T(8,128)(2,1)S(1)} %stack_rows.3.refs_0_, bf16[8,7168]{1,0:T(8,128)(2,1)S(1)} %collective-permute-done.14.refs_1_, bf16[8,7168]{1,0:T(8,128)(2,1)S(1)} %collective-permute-done.15.refs_2_, ...), custom_call_target="tpu_custom_call" | custom-call | bytes 1024 | tf_op jit(solution)/shard_map/experts/pallas_call | solution.py:455
  88.9 1.6 %collective-permute-start.17 = (bf16[8,7168]{1,0:T(8,128)(2,1)S(1)}, bf16[8,7168]{1,0:T(8,128)(2,1)S(1)}, u32[]{:S(2)}, u32[]{:S(2)}) collective-permute-start(bf16[8,7168]{1,0:T(8,128)(2,1)S(1)} %get-tuple-element.76), channel_id=1, source_target_pairs={{0,2},{1,3},{2,0},{3,1},{4,6},{5,7},{6,4},{7,5},{8,10},{9,11},{10,... | collective-permute-start | bytes 344072 | tf_op jit(solution)/shard_map/ppermute | solution.py:584
  90.5 0.2 collective-permute-start.18
  90.7 0.4 collective-permute-start.19
  91.1 1.5 %collective-permute-start.11 = (bf16[256,512]{1,0:T(8,128)(2,1)}, bf16[256,512]{1,0:T(8,128)(2,1)S(1)}, u32[]{:S(2)}, u32[]{:S(2)}) collective-permute-start(bf16[256,512]{1,0:T(8,128)(2,1)} %get-tuple-element.66), channel_id=1, source_target_pairs={{0,2},{2,0},{4,6},{6,4},{8,10},{10,8},{12,14},{14,12},{1,3},{3,1},... | collective-permute-start | bytes 786440 | tf_op jit(solution)/shard_map/ppermute | solution.py:28
  92.6 10.4 %collective-permute-done.12 = bf16[1152,512]{1,0:T(8,128)(2,1)S(1)} collective-permute-done((bf16[1152,512]{1,0:T(8,128)(2,1)}, bf16[1152,512]{1,0:T(8,128)(2,1)S(1)}, u32[]{:S(2)}, u32[]{:S(2)}) %collective-permute-start.12) | collective-permute-done | bytes 1179680 | tf_op jit(solution)/shard_map/ppermute | solution.py:36
  103.0 1.2 broadcast_select_fusion.refs_1_
  104.2 0.7 fusion.3
  104.9 0.7 fusion.4
  105.6 0.9 collective-permute-start.22
  106.6 2.3 %collective-permute-start.23 = (bf16[2,7168]{1,0:T(2,128)(2,1)S(1)}, bf16[2,7168]{1,0:T(2,128)(2,1)S(1)}, u32[]{:S(2)}, u32[]{:S(2)}) collective-permute-start(bf16[2,7168]{1,0:T(2,128)(2,1)S(1)} %get-tuple-element.98), channel_id=1, source_target_pairs={{0,8},{2,10},{4,12},{6,14},{8,0},{10,2},{12,4},{14,6},{1,9},{3,11}... | collective-permute-start | bytes 86024 | tf_op jit(solution)/shard_map/ppermute | solution.py:549
  108.8 1.2 collective-permute-start.24
  110.1 1.0 slice.19
  111.1 1.5 %place.2.refs_3_ = bf16[8,256,512]{2,1,0:T(8,128)(2,1)} custom-call(s32[8]{0:T(128)S(1)} %copy-done.5, s32[1]{0:T(128)} %bitcast.own_ref, bf16[256,512]{1,0:T(8,128)(2,1)S(1)} %collective-permute-done.7.refs_0_, bf16[256,512]{1,0:T(8,128)(2,1)S(1)} %collective-permute-done.13.refs_1_, ...), custom_call_target="tpu_custom_call", output_to_operand_aliasing={{}: (5, {})} | custom-call | bytes 1024 | tf_op jit(solution)/shard_map/place/pallas_call | solution.py:322
  112.5 4.5 %attend.8 = bf16[256,512]{1,0:T(8,128)(2,1)S(1)} custom-call(s32[8]{0:T(128)S(1)} %copy-done.5, s32[1]{0:T(128)} %bitcast.own_ref, bf16[4,320,512]{2,1,0:T(8,128)(2,1)S(1)} %collective-permute-done.refs_0_, bf16[1152,512]{1,0:T(8,128)(2,1)} %broadcast_select_fusion.refs_1_, bf16[1152,512]{1,0:T(8,128)(2,1)} %collective-permute-done.20.refs_2_), custom_call_target="tpu_custom_call" | custom-call | bytes 1024 | tf_op jit(solution)/shard_map/attend/pallas_call | solution.py:286
  117.0 1.6 %collective-permute-start.21 = (bf16[256,512]{1,0:T(8,128)(2,1)S(1)}, bf16[256,512]{1,0:T(8,128)(2,1)S(1)}, u32[]{:S(2)}, u32[]{:S(2)}) collective-permute-start(bf16[256,512]{1,0:T(8,128)(2,1)S(1)} %attend.8), channel_id=1, source_target_pairs={{0,2},{2,0},{4,6},{6,4},{8,10},{10,8},{12,14},{14,12},{1,3},{3,1},... | collective-permute-start | bytes 786440 | tf_op jit(solution)/shard_map/ppermute | solution.py:28
  118.6 0.8 convert_add_fusion.1
  119.7 0.8 convert_element_type.39
  120.5 5.2 %attend.9.refs_1_ = bf16[8,256,512]{2,1,0:T(8,128)(2,1)} custom-call(s32[8]{0:T(128)S(1)} %copy-done.5, s32[1]{0:T(128)} %bitcast.own_ref, bf16[4,320,512]{2,1,0:T(8,128)(2,1)S(1)} %pack_tokens.3.refs_1_.refs_0_, bf16[1152,512]{1,0:T(8,128)(2,1)} %broadcast_select_fusion.refs_1_, ...), custom_call_target="tpu_custom_call", output_to_operand_aliasing={{}: (5, {})} | custom-call | bytes 1024 | tf_op jit(solution)/shard_map/attend/pallas_call | solution.py:286
  125.6 1.3 place.3
  (53 shorter events, 1.0 us)
Async XLA Ops:
  0.6 7.1 %copy-start.8 = (bf16[8,2,8192]{2,1,0:T(2,128)(2,1)S(1)}, bf16[8,2,8192]{2,1,0:T(2,128)(2,1)}, u32[]{:S(2)}) copy-start(bf16[8,2,8192]{2,1,0:T(2,128)(2,1)} %param.16) | copy-start | bytes 786436
  0.6 7.3 %copy-start.10 = (bf16[8,2,512]{2,1,0:T(2,128)(2,1)S(1)}, bf16[8,2,512]{2,1,0:T(2,128)(2,1)}, u32[]{:S(2)}) copy-start(bf16[8,2,512]{2,1,0:T(2,128)(2,1)} %param.17) | copy-start | bytes 49156
  0.7 7.3 %copy-start.11 = (bf16[8,2,64]{2,1,0:T(2,128)(2,1)S(1)}, bf16[8,2,64]{2,1,0:T(2,128)(2,1)}, u32[]{:S(2)}) copy-start(bf16[8,2,64]{2,1,0:T(2,128)(2,1)} %param.18) | copy-start | bytes 6148
  0.7 7.3 %copy-start.5 = (s32[8]{0:T(128)S(1)}, s32[8]{0:T(128)}, u32[]{:S(2)}) copy-start(s32[8]{0:T(128)} %slot_ref.17) | copy-start | bytes 100
  3.0 34.7 %collective-permute-start.1 = (bf16[1152,512]{1,0:T(8,128)(2,1)}, bf16[1152,512]{1,0:T(8,128)(2,1)}, u32[]{:S(2)}, u32[]{:S(2)}) collective-permute-start(bf16[1152,512]{1,0:T(8,128)(2,1)} %pack_cache.1.refs_2_), channel_id=1, source_target_pairs={{0,4},{4,0},{8,12},{12,8},{2,6},{6,2},{10,14},{14,10},{1,5},{5,1},... | collective-permute-start | bytes 3538952 | tf_op jit(solution)/shard_map/ppermute | solution.py:36
  6.1 31.6 %collective-permute-start.2 = (bf16[1152,512]{1,0:T(8,128)(2,1)}, bf16[1152,512]{1,0:T(8,128)(2,1)}, u32[]{:S(2)}, u32[]{:S(2)}) collective-permute-start(bf16[1152,512]{1,0:T(8,128)(2,1)} %pack_cache.1.refs_2_), channel_id=1, source_target_pairs={{4,8},{8,4},{6,10},{10,6},{5,9},{9,5},{7,11},{11,7},{20,24},{24,20... | collective-permute-start | bytes 3538952 | tf_op jit(solution)/shard_map/ppermute | solution.py:36
  8.0 1.6 %copy-start = (bf16[8,2,128,512]{3,2,1,0:T(8,128)(2,1)S(1)}, bf16[8,2,128,512]{3,2,1,0:T(8,128)(2,1)}, u32[]{:S(2)}) copy-start(bf16[8,2,128,512]{3,2,1,0:T(8,128)(2,1)} %param.15) | copy-start | bytes 6291460
  9.6 3.8 %copy-start.9 = (bf16[8,2,7168]{2,1,0:T(2,128)(2,1)S(1)}, bf16[8,2,7168]{2,1,0:T(2,128)(2,1)}, u32[]{:S(2)}) copy-start(bf16[8,2,7168]{2,1,0:T(2,128)(2,1)} %param.20) | copy-start | bytes 688132
  9.6 3.9 %copy-start.6 = (s32[8,2,8]{2,1,0:T(2,128)S(1)}, s32[8,2,8]{2,1,0:T(2,128)}, u32[]{:S(2)}) copy-start(s32[8,2,8]{2,1,0:T(2,128)} %param.21) | copy-start | bytes 1540
  9.6 3.9 %copy-start.7 = (f32[8,2,8]{2,1,0:T(2,128)S(1)}, f32[8,2,8]{2,1,0:T(2,128)}, u32[]{:S(2)}) copy-start(f32[8,2,8]{2,1,0:T(2,128)} %param.22) | copy-start | bytes 1540
  11.8 30.5 %collective-permute-start = (bf16[4,320,512]{2,1,0:T(8,128)(2,1)}, bf16[4,320,512]{2,1,0:T(8,128)(2,1)S(1)}, u32[]{:S(2)}, u32[]{:S(2)}) collective-permute-start(bf16[4,320,512]{2,1,0:T(8,128)(2,1)} %pack_tokens.2), channel_id=1, source_target_pairs={{0,2},{2,0},{4,6},{6,4},{8,10},{10,8},{12,14},{14,12},{1,3},{3,1},... | collective-permute-start | bytes 3932168 | tf_op jit(solution)/shard_map/ppermute | solution.py:28
  13.4 28.9 %collective-permute-start.6 = (bf16[1152,512]{1,0:T(8,128)(2,1)}, bf16[1152,512]{1,0:T(8,128)(2,1)}, u32[]{:S(2)}, u32[]{:S(2)}) collective-permute-start(bf16[1152,512]{1,0:T(8,128)(2,1)} %pack_cache.1.refs_2_), channel_id=1, source_target_pairs={{0,1},{1,0},{2,3},{3,2},{4,5},{5,4},{6,7},{7,6},{8,9},{9,8},{10,11... | collective-permute-start | bytes 3538952 | tf_op jit(solution)/shard_map/ppermute | solution.py:28
  13.9 23.8 %collective-permute-start.3 = (bf16[2,7168]{1,0:T(2,128)(2,1)S(1)}, bf16[2,7168]{1,0:T(2,128)(2,1)S(1)}, u32[]{:S(2)}, u32[]{:S(2)}) collective-permute-start(bf16[2,7168]{1,0:T(2,128)(2,1)S(1)} %get-tuple-element.52), channel_id=1, source_target_pairs={{0,8},{2,10},{4,12},{6,14},{8,0},{10,2},{12,4},{14,6},{1,9},{3,11}... | collective-permute-start | bytes 86024 | tf_op jit(solution)/shard_map/ppermute | solution.py:549
  16.8 1.6 %copy-start.1 = (bf16[8,2,128,512]{3,2,1,0:T(8,128)(2,1)S(1)}, bf16[8,2,128,512]{3,2,1,0:T(8,128)(2,1)}, u32[]{:S(2)}) copy-start(bf16[8,2,128,512]{3,2,1,0:T(8,128)(2,1)} %param.15) | copy-start | bytes 6291460
  37.7 16.5 %collective-permute-start.5 = (bf16[1152,512]{1,0:T(8,128)(2,1)}, bf16[1152,512]{1,0:T(8,128)(2,1)}, u32[]{:S(2)}, u32[]{:S(2)}) collective-permute-start(bf16[1152,512]{1,0:T(8,128)(2,1)} %collective-permute-done.1.refs_2_), channel_id=1, source_target_pairs={{0,1},{1,0},{2,3},{3,2},{4,5},{5,4},{6,7},{7,6},{8,9},{9,8},{10,11... | collective-permute-start | bytes 3538952 | tf_op jit(solution)/shard_map/ppermute | solution.py:28
  37.7 33.4 %collective-permute-start.4 = (bf16[1152,512]{1,0:T(8,128)(2,1)}, bf16[1152,512]{1,0:T(8,128)(2,1)}, u32[]{:S(2)}, u32[]{:S(2)}) collective-permute-start(bf16[1152,512]{1,0:T(8,128)(2,1)} %collective-permute-done.1.refs_2_), channel_id=1, source_target_pairs={{4,8},{8,4},{6,10},{10,6},{5,9},{9,5},{7,11},{11,7},{20,24},{24,20... | collective-permute-start | bytes 3538952 | tf_op jit(solution)/shard_map/ppermute | solution.py:36
  39.4 31.7 %collective-permute-start.9 = (bf16[1152,512]{1,0:T(8,128)(2,1)}, bf16[1152,512]{1,0:T(8,128)(2,1)}, u32[]{:S(2)}, u32[]{:S(2)}) collective-permute-start(bf16[1152,512]{1,0:T(8,128)(2,1)} %collective-permute-done.2), channel_id=1, source_target_pairs={{4,0},{8,12},{6,2},{10,14},{5,1},{9,13},{7,3},{11,15},{20,16},{24,... | collective-permute-start | bytes 3538952 | tf_op jit(solution)/shard_map/ppermute | solution.py:36
  49.2 21.9 %collective-permute-start.7 = (bf16[256,512]{1,0:T(8,128)(2,1)S(1)}, bf16[256,512]{1,0:T(8,128)(2,1)S(1)}, u32[]{:S(2)}, u32[]{:S(2)}) collective-permute-start(bf16[256,512]{1,0:T(8,128)(2,1)S(1)} %get-tuple-element.59), channel_id=1, source_target_pairs={{0,2},{2,0},{4,6},{6,4},{8,10},{10,8},{12,14},{14,12},{1,3},{3,1},... | collective-permute-start | bytes 786440 | tf_op jit(solution)/shard_map/ppermute | solution.py:28
  51.0 20.0 %collective-permute-start.8 = (bf16[4,7168]{1,0:T(4,128)(2,1)S(1)}, bf16[4,7168]{1,0:T(4,128)(2,1)S(1)}, u32[]{:S(2)}, u32[]{:S(2)}) collective-permute-start(bf16[4,7168]{1,0:T(4,128)(2,1)S(1)} %stack_rows.2.refs_0_), channel_id=1, source_target_pairs={{0,4},{2,6},{4,0},{6,2},{8,12},{10,14},{12,8},{14,10},{1,5},{3,7},... | collective-permute-start | bytes 172040 | tf_op jit(solution)/shard_map/ppermute | solution.py:549
  72.5 4.0 %collective-permute-start.10 = (bf16[1152,512]{1,0:T(8,128)(2,1)S(1)}, bf16[1152,512]{1,0:T(8,128)(2,1)S(1)}, u32[]{:S(2)}, u32[]{:S(2)}) collective-permute-start(bf16[1152,512]{1,0:T(8,128)(2,1)S(1)} %broadcast_select_fusion.1.refs_2_), channel_id=1, source_target_pairs={{0,1},{1,0},{2,3},{3,2},{4,5},{5,4},{6,7},{7,6},{8,9},{9,8},{10,11... | collective-permute-start | bytes 3538952 | tf_op jit(solution)/shard_map/ppermute | solution.py:28
  72.5 30.5 %collective-permute-start.12 = (bf16[1152,512]{1,0:T(8,128)(2,1)}, bf16[1152,512]{1,0:T(8,128)(2,1)S(1)}, u32[]{:S(2)}, u32[]{:S(2)}) collective-permute-start(bf16[1152,512]{1,0:T(8,128)(2,1)} %collective-permute-done.4), channel_id=1, source_target_pairs={{4,0},{8,12},{6,2},{10,14},{5,1},{9,13},{7,3},{11,15},{20,16},{24,... | collective-permute-start | bytes 3538952 | tf_op jit(solution)/shard_map/ppermute | solution.py:36
  74.0 17.1 %collective-permute-start.13 = (bf16[256,512]{1,0:T(8,128)(2,1)S(1)}, bf16[256,512]{1,0:T(8,128)(2,1)S(1)}, u32[]{:S(2)}, u32[]{:S(2)}) collective-permute-start(bf16[256,512]{1,0:T(8,128)(2,1)S(1)} %get-tuple-element.58), channel_id=1, source_target_pairs={{0,2},{2,0},{4,6},{6,4},{8,10},{10,8},{12,14},{14,12},{1,3},{3,1},... | collective-permute-start | bytes 786440 | tf_op jit(solution)/shard_map/ppermute | solution.py:28
  75.9 9.8 %collective-permute-start.14 = (bf16[8,7168]{1,0:T(8,128)(2,1)S(1)}, bf16[8,7168]{1,0:T(8,128)(2,1)S(1)}, u32[]{:S(2)}, u32[]{:S(2)}) collective-permute-start(bf16[8,7168]{1,0:T(8,128)(2,1)S(1)} %stack_rows.3.refs_0_), channel_id=1, source_target_pairs={{0,2},{1,3},{2,0},{3,1},{4,6},{5,7},{6,4},{7,5},{8,10},{9,11},{10,... | collective-permute-start | bytes 344072 | tf_op jit(solution)/shard_map/ppermute | solution.py:584
  76.4 9.2 %collective-permute-start.15 = (bf16[8,7168]{1,0:T(8,128)(2,1)S(1)}, bf16[8,7168]{1,0:T(8,128)(2,1)S(1)}, u32[]{:S(2)}, u32[]{:S(2)}) collective-permute-start(bf16[8,7168]{1,0:T(8,128)(2,1)S(1)} %stack_rows.3.refs_0_), channel_id=1, source_target_pairs={{0,1},{1,0},{2,3},{3,2},{4,5},{5,4},{6,7},{7,6},{8,9},{9,8},{10,11... | collective-permute-start | bytes 344072 | tf_op jit(solution)/shard_map/ppermute | solution.py:584
  76.4 10.9 %collective-permute-start.16 = (bf16[8,7168]{1,0:T(8,128)(2,1)S(1)}, bf16[8,7168]{1,0:T(8,128)(2,1)S(1)}, u32[]{:S(2)}, u32[]{:S(2)}) collective-permute-start(bf16[8,7168]{1,0:T(8,128)(2,1)S(1)} %stack_rows.3.refs_0_), channel_id=1, source_target_pairs={{0,3},{1,2},{2,1},{3,0},{4,7},{5,6},{6,5},{7,4},{8,11},{9,10},{10,... | collective-permute-start | bytes 344072 | tf_op jit(solution)/shard_map/ppermute | solution.py:584
  78.1 9.2 %copy-start.2 = (bf16[1,7168,128]{2,1,0:T(8,128)(2,1)S(1)}, bf16[1,7168,128]{2,1,0:T(8,128)(2,1)}, u32[]{:S(2)}) copy-start(bf16[1,7168,128]{2,1,0:T(8,128)(2,1)} %refs_4_.1) | copy-start | bytes 5505028
  78.1 9.2 %copy-start.3 = (bf16[1,7168,128]{2,1,0:T(8,128)(2,1)S(1)}, bf16[1,7168,128]{2,1,0:T(8,128)(2,1)}, u32[]{:S(2)}) copy-start(bf16[1,7168,128]{2,1,0:T(8,128)(2,1)} %refs_5_.1) | copy-start | bytes 5505028
  78.1 9.2 %copy-start.4 = (bf16[1,128,7168]{2,1,0:T(8,128)(2,1)S(1)}, bf16[1,128,7168]{2,1,0:T(8,128)(2,1)}, u32[]{:S(2)}) copy-start(bf16[1,128,7168]{2,1,0:T(8,128)(2,1)} %refs_6_.1) | copy-start | bytes 5505028
  88.9 14.1 %collective-permute-start.17 = (bf16[8,7168]{1,0:T(8,128)(2,1)S(1)}, bf16[8,7168]{1,0:T(8,128)(2,1)S(1)}, u32[]{:S(2)}, u32[]{:S(2)}) collective-permute-start(bf16[8,7168]{1,0:T(8,128)(2,1)S(1)} %get-tuple-element.76), channel_id=1, source_target_pairs={{0,2},{1,3},{2,0},{3,1},{4,6},{5,7},{6,4},{7,5},{8,10},{9,11},{10,... | collective-permute-start | bytes 344072 | tf_op jit(solution)/shard_map/ppermute | solution.py:584
  90.5 12.5 %collective-permute-start.18 = (bf16[8,7168]{1,0:T(8,128)(2,1)S(1)}, bf16[8,7168]{1,0:T(8,128)(2,1)S(1)}, u32[]{:S(2)}, u32[]{:S(2)}) collective-permute-start(bf16[8,7168]{1,0:T(8,128)(2,1)S(1)} %get-tuple-element.77), channel_id=1, source_target_pairs={{0,1},{1,0},{2,3},{3,2},{4,5},{5,4},{6,7},{7,6},{8,9},{9,8},{10,11... | collective-permute-start | bytes 344072 | tf_op jit(solution)/shard_map/ppermute | solution.py:584
  90.7 12.3 %collective-permute-start.19 = (bf16[8,7168]{1,0:T(8,128)(2,1)S(1)}, bf16[8,7168]{1,0:T(8,128)(2,1)S(1)}, u32[]{:S(2)}, u32[]{:S(2)}) collective-permute-start(bf16[8,7168]{1,0:T(8,128)(2,1)S(1)} %get-tuple-element.78), channel_id=1, source_target_pairs={{0,3},{1,2},{2,1},{3,0},{4,7},{5,6},{6,5},{7,4},{8,11},{9,10},{10,... | collective-permute-start | bytes 344072 | tf_op jit(solution)/shard_map/ppermute | solution.py:584
  91.1 20.0 %collective-permute-start.11 = (bf16[256,512]{1,0:T(8,128)(2,1)}, bf16[256,512]{1,0:T(8,128)(2,1)S(1)}, u32[]{:S(2)}, u32[]{:S(2)}) collective-permute-start(bf16[256,512]{1,0:T(8,128)(2,1)} %get-tuple-element.66), channel_id=1, source_target_pairs={{0,2},{2,0},{4,6},{6,4},{8,10},{10,8},{12,14},{14,12},{1,3},{3,1},... | collective-permute-start | bytes 786440 | tf_op jit(solution)/shard_map/ppermute | solution.py:28
  104.2 8.3 %collective-permute-start.20 = (bf16[1152,512]{1,0:T(8,128)(2,1)}, bf16[1152,512]{1,0:T(8,128)(2,1)}, u32[]{:S(2)}, u32[]{:S(2)}) collective-permute-start(bf16[1152,512]{1,0:T(8,128)(2,1)} %broadcast_select_fusion.refs_1_), channel_id=1, source_target_pairs={{0,1},{1,0},{2,3},{3,2},{4,5},{5,4},{6,7},{7,6},{8,9},{9,8},{10,11... | collective-permute-start | bytes 3538952 | tf_op jit(solution)/shard_map/ppermute | solution.py:28
  105.6 13.0 %collective-permute-start.22 = (bf16[2,7168]{1,0:T(2,128)(2,1)}, bf16[2,7168]{1,0:T(2,128)(2,1)S(1)}, u32[]{:S(2)}, u32[]{:S(2)}) collective-permute-start(bf16[2,7168]{1,0:T(2,128)(2,1)} %get-tuple-element.96), channel_id=1, source_target_pairs={{0,4},{2,6},{4,0},{6,2},{8,12},{10,14},{12,8},{14,10},{1,5},{3,7},... | collective-permute-start | bytes 86024 | tf_op jit(solution)/shard_map/ppermute | solution.py:549
  106.6 12.1 %collective-permute-start.23 = (bf16[2,7168]{1,0:T(2,128)(2,1)S(1)}, bf16[2,7168]{1,0:T(2,128)(2,1)S(1)}, u32[]{:S(2)}, u32[]{:S(2)}) collective-permute-start(bf16[2,7168]{1,0:T(2,128)(2,1)S(1)} %get-tuple-element.98), channel_id=1, source_target_pairs={{0,8},{2,10},{4,12},{6,14},{8,0},{10,2},{12,4},{14,6},{1,9},{3,11}... | collective-permute-start | bytes 86024 | tf_op jit(solution)/shard_map/ppermute | solution.py:549
  108.8 9.8 %collective-permute-start.24 = (bf16[2,7168]{1,0:T(2,128)(2,1)S(1)}, bf16[2,7168]{1,0:T(2,128)(2,1)}, u32[]{:S(2)}, u32[]{:S(2)}) collective-permute-start(bf16[2,7168]{1,0:T(2,128)(2,1)S(1)} %get-tuple-element.97), channel_id=1, source_target_pairs={{0,12},{2,14},{4,8},{6,10},{8,4},{10,6},{12,0},{14,2},{1,13},{3,15... | collective-permute-start | bytes 86024 | tf_op jit(solution)/shard_map/ppermute | solution.py:549
  117.0 8.6 %collective-permute-start.21 = (bf16[256,512]{1,0:T(8,128)(2,1)S(1)}, bf16[256,512]{1,0:T(8,128)(2,1)S(1)}, u32[]{:S(2)}, u32[]{:S(2)}) collective-permute-start(bf16[256,512]{1,0:T(8,128)(2,1)S(1)} %attend.8), channel_id=1, source_target_pairs={{0,2},{2,0},{4,6},{6,4},{8,10},{10,8},{12,14},{14,12},{1,3},{3,1},... | collective-permute-start | bytes 786440 | tf_op jit(solution)/shard_map/ppermute | solution.py:28

commit v14 on v10

--- a/solution.py
+++ b/solution.py
@@ -471,6 +471,34 @@
     )(*groups, w_gate, w_up, w_down)
 
 
+def combine_kernel(ways, share_ref, *refs):
+    pieces, out_ref = refs[:-1], refs[-1]
+    sums = {}
+    for (k, _), piece in zip(ways, pieces):
+        rows = piece[...].astype(jnp.float32)
+        sums[k] = sums[k] + rows if k in sums else rows
+    total = None
+    for k, rows in sums.items():
+        for c in range(CAP):
+            slot = k * CAP + c
+            part = share_ref[:, slot : slot + 1] * rows[c : c + 1, :]
+            total = part if total is None else total + part
+    out_ref[...] = total.astype(jnp.bfloat16)
+
+
+def combine(ways, share, pieces):
+    vmem = pl.BlockSpec(memory_space=pltpu.VMEM)
+    return pl.pallas_call(
+        functools.partial(combine_kernel, tuple(ways)),
+        out_shape=jax.ShapeDtypeStruct((share.shape[0], pieces[0].shape[1]), jnp.bfloat16),
+        in_specs=[vmem] * (1 + len(pieces)),
+        out_specs=vmem,
+        cost_estimate=SMALL,
+        compiler_params=pltpu.CompilerParams(vmem_limit_bytes=8 * 1024 * 1024),
+        name="combine",
+    )(share, *pieces)
+
+
 def on_device(
     latent_cache,
     rope_cache,
@@ -605,16 +633,12 @@
     (given_3,) = attend(scalars, 3, guest, None, cache_c, None)
     back_3 = swapped(given_3, "branch", 0)
     (placed,) = attend(scalars, 3, None, after(stay, given_3), cache_c, placed)
-    homeward = [after(x, given_3).astype(jnp.float32) for x in homeward]
+    placed, *homeward = lax.optimization_barrier((placed, *homeward))
     placed = place(scalars, (back_0, back_1, back_2, back_3), placed)
     attended = placed.reshape(tok_rows, step_count, head_count, width)
 
-    sums = [0.0] * experts
-    for (k, _), piece in zip(ways, homeward):
-        sums[k] = sums[k] + piece
-    sums = jnp.concatenate(sums, axis=0)
-    combined = jnp.sum(share[:, :, None] * sums[None, :, :], axis=1)
-    moe_out = combined.astype(jnp.bfloat16).reshape(tok_rows, step_count, model_width)
+    combined = combine(ways, share, homeward)
+    moe_out = combined.reshape(tok_rows, step_count, model_width)
     return (attended, moe_out)
 
 

time: 127 us -> 124 us (0.976)
  waiting for transfers between devices: 42.9 us -> 46.8 us
  other arithmetic: 4.41 us -> 1.63 us
  Pallas kernels: 40.1 us -> 37.6 us
  local copies, waits for them, and re-layouts: 5.97 us -> 4.34 us
    pallas_call x5, Pallas kernels: 30.5 us -> 27.6 us  [call(): pl.pallas_call(functools.partial(kernel, slot, gives, keeps, has_placed),...]
    ppermute x9, waiting for transfers between devices: 1.64 us -> 4.43 us  [swapped(): lax.ppermute(x, axis, [(i, i ^ 1 << bit) for i in range(lax.axis_size(axi...]
    slice x2, local copies, waits for them, and re-layouts: 1.64 us -> 0.09 us  [on_device(): parts[w * CAP:(w + 1) * CAP]]
  transfers between devices with their start and end apart: 25 -> 25, of which waited for: 6 -> 8; matrix products, arithmetic and copies ran while one was open for 5% -> 1% of each run, Pallas kernels for 29% -> 24%
where the time goes in v14:
time: 124 us
  waiting for transfers between devices  46.8 us (38%)
  Pallas kernels  37.6 us (30%)
  starting transfers between devices  32.2 us (26%)
  local copies, waits for them, and re-layouts  4.34 us (4%)
  other arithmetic  1.63 us (1%)
    ppermute x5, waiting for transfers between devices, along(): return lax.ppermute(x, 'branch', list(enumerate(there)))  28.5 us
    pallas_call x5, Pallas kernels, call(): pl.pallas_call(functools.partial(kernel, slot, gives, keeps, has_placed),...  27.6 us
    ppermute x5, starting transfers between devices, along(): return lax.ppermute(x, 'branch', list(enumerate(there)))  10.5 us
    ppermute x5, waiting for transfers between devices, line_hop(): return lax.ppermute(x, 'branch', pairs)  10.4 us
    ppermute x5, starting transfers between devices, line_hop(): return lax.ppermute(x, 'branch', pairs)  9.2 us
    ppermute x9, starting transfers between devices, swapped(): lax.ppermute(x, axis, [(i, i ^ 1 << bit) for i in range(lax.axis_size(axi...  8.01 us
    ppermute x9, waiting for transfers between devices, swapped(): lax.ppermute(x, axis, [(i, i ^ 1 << bit) for i in range(lax.axis_size(axi...  4.43 us
    ppermute x6, starting transfers between devices, around_chip(): return lax.ppermute(x, ('branch', 'expert'), pairs)  4.41 us
  transfers between devices with their start and end apart: 25, of which 8 were waited for; matrix products, arithmetic and copies ran while one was open for 1% of the time, Pallas kernels for 24%

profile of v14, /device:TPU:0, one launch (start us, length us, event | category | flops | bytes accessed | tf_op | source)
XLA Modules:
  0.0 123.6 jit_solution(17822184481833158518)
XLA Ops:
  0.7 2.3 %pack_cache.1.refs_2_ = bf16[1152,512]{1,0:T(8,128)(2,1)} custom-call(bf16[1024,512]{1,0:T(8,128)(2,1)} %bitcast.13, bf16[128,512]{1,0:T(8,128)(2,1)} %bitcast.14), custom_call_target="tpu_custom_call" | custom-call | bytes 1024 | tf_op jit(solution)/shard_map/pack_cache/pallas_call | solution.py:52
  3.0 3.1 %collective-permute-start = (bf16[1152,512]{1,0:T(8,128)(2,1)}, bf16[1152,512]{1,0:T(8,128)(2,1)}, u32[]{:S(2)}, u32[]{:S(2)}) collective-permute-start(bf16[1152,512]{1,0:T(8,128)(2,1)} %pack_cache.1.refs_2_), channel_id=1, source_target_pairs={{0,4},{4,0},{8,12},{12,8},{2,6},{6,2},{10,14},{14,10},{1,5},{5,1},... | collective-permute-start | bytes 3538952 | tf_op jit(solution)/shard_map/ppermute | solution.py:36
  6.1 1.7 %collective-permute-start.1 = (bf16[1152,512]{1,0:T(8,128)(2,1)}, bf16[1152,512]{1,0:T(8,128)(2,1)}, u32[]{:S(2)}, u32[]{:S(2)}) collective-permute-start(bf16[1152,512]{1,0:T(8,128)(2,1)} %pack_cache.1.refs_2_), channel_id=1, source_target_pairs={{4,8},{8,4},{6,10},{10,6},{5,9},{9,5},{7,11},{11,7},{20,24},{24,20... | collective-permute-start | bytes 3538952 | tf_op jit(solution)/shard_map/ppermute | solution.py:36
  7.8 0.2 reshape.26.rope_ref
  8.0 1.6 %copy-done = bf16[8,2,128,512]{3,2,1,0:T(8,128)(2,1)S(1)} copy-done((bf16[8,2,128,512]{3,2,1,0:T(8,128)(2,1)S(1)}, bf16[8,2,128,512]{3,2,1,0:T(8,128)(2,1)}, u32[]{:S(2)}) %copy-start) | copy-done | bytes 2097176
  9.6 2.2 %pack_tokens.2 = bf16[4,320,512]{2,1,0:T(8,128)(2,1)} custom-call(s32[8]{0:T(128)S(1)} %copy-done.5, s32[1]{0:T(128)} %bitcast.own_ref, bf16[8,256,512]{2,1,0:T(8,128)(2,1)S(1)} %bitcast.8, bf16[8,32,512]{2,1,0:T(8,128)(2,1)S(1)} %reshape.26.rope_ref, bf16[8,32,512]{2,1,0:T(8,128)(2,1)S(1)} %fusion.2.new_ref), custom_call_target="tpu_custom_call" | custom-call | bytes 1024 | tf_op jit(solution)/shard_map/pack_tokens/pallas_call | solution.py:106
  11.8 1.6 %collective-permute-start.4 = (bf16[4,320,512]{2,1,0:T(8,128)(2,1)}, bf16[4,320,512]{2,1,0:T(8,128)(2,1)S(1)}, u32[]{:S(2)}, u32[]{:S(2)}) collective-permute-start(bf16[4,320,512]{2,1,0:T(8,128)(2,1)} %pack_tokens.2), channel_id=1, source_target_pairs={{0,2},{2,0},{4,6},{6,4},{8,10},{10,8},{12,14},{14,12},{1,3},{3,1},... | collective-permute-start | bytes 3932168 | tf_op jit(solution)/shard_map/ppermute | solution.py:28
  13.5 0.3 dispatch.1
  13.9 2.9 %collective-permute-start.2 = (bf16[2,7168]{1,0:T(2,128)(2,1)S(1)}, bf16[2,7168]{1,0:T(2,128)(2,1)S(1)}, u32[]{:S(2)}, u32[]{:S(2)}) collective-permute-start(bf16[2,7168]{1,0:T(2,128)(2,1)S(1)} %get-tuple-element.53), channel_id=1, source_target_pairs={{0,8},{2,10},{4,12},{6,14},{8,0},{10,2},{12,4},{14,6},{1,9},{3,11}... | collective-permute-start | bytes 86024 | tf_op jit(solution)/shard_map/ppermute | solution.py:576
  16.8 1.6 %copy-done.1 = bf16[8,2,128,512]{3,2,1,0:T(8,128)(2,1)S(1)} copy-done((bf16[8,2,128,512]{3,2,1,0:T(8,128)(2,1)S(1)}, bf16[8,2,128,512]{3,2,1,0:T(8,128)(2,1)}, u32[]{:S(2)}) %copy-start.1) | copy-done | bytes 2097176
  18.4 1.1 pack_tokens.3.refs_1_.refs_0_
  19.5 18.2 %collective-permute-done.2.refs_1_ = bf16[2,7168]{1,0:T(2,128)(2,1)S(1)} collective-permute-done((bf16[2,7168]{1,0:T(2,128)(2,1)S(1)}, bf16[2,7168]{1,0:T(2,128)(2,1)S(1)}, u32[]{:S(2)}, u32[]{:S(2)}) %collective-permute-start.2) | collective-permute-done | bytes 28704 | tf_op jit(solution)/shard_map/ppermute | solution.py:576
  37.7 1.7 %collective-permute-start.3 = (bf16[1152,512]{1,0:T(8,128)(2,1)}, bf16[1152,512]{1,0:T(8,128)(2,1)}, u32[]{:S(2)}, u32[]{:S(2)}) collective-permute-start(bf16[1152,512]{1,0:T(8,128)(2,1)} %collective-permute-done.refs_2_), channel_id=1, source_target_pairs={{4,8},{8,4},{6,10},{10,6},{5,9},{9,5},{7,11},{11,7},{20,24},{24,20... | collective-permute-start | bytes 3538952 | tf_op jit(solution)/shard_map/ppermute | solution.py:36
  39.4 1.3 %collective-permute-start.11 = (bf16[1152,512]{1,0:T(8,128)(2,1)}, bf16[1152,512]{1,0:T(8,128)(2,1)}, u32[]{:S(2)}, u32[]{:S(2)}) collective-permute-start(bf16[1152,512]{1,0:T(8,128)(2,1)} %collective-permute-done.1), channel_id=1, source_target_pairs={{4,0},{8,12},{6,2},{10,14},{5,1},{9,13},{7,3},{11,15},{20,16},{24,... | collective-permute-start | bytes 3538952 | tf_op jit(solution)/shard_map/ppermute | solution.py:36
  40.7 1.7 %collective-permute-done.4.refs_0_ = bf16[4,320,512]{2,1,0:T(8,128)(2,1)S(1)} collective-permute-done((bf16[4,320,512]{2,1,0:T(8,128)(2,1)}, bf16[4,320,512]{2,1,0:T(8,128)(2,1)S(1)}, u32[]{:S(2)}, u32[]{:S(2)}) %collective-permute-start.4) | collective-permute-done | bytes 1310752 | tf_op jit(solution)/shard_map/ppermute | solution.py:28
  42.3 6.9 %attend.5 = (bf16[256,512]{1,0:T(8,128)(2,1)S(1)}, bf16[8,256,512]{2,1,0:T(8,128)(2,1)}) custom-call(s32[8]{0:T(128)S(1)} %copy-done.5, s32[1]{0:T(128)} %bitcast.own_ref, bf16[4,320,512]{2,1,0:T(8,128)(2,1)S(1)} %collective-permute-done.4.refs_0_, bf16[4,320,512]{2,1,0:T(8,128)(2,1)S(1)} %pack_tokens.3.refs_1_.refs_0_, ...), custom_call_target="tpu_custom_call" | custom-call | bytes 1024 | tf_op jit(solution)/shard_map/attend/pallas_call | solution.py:285
  49.2 1.6 %collective-permute-start.7 = (bf16[256,512]{1,0:T(8,128)(2,1)S(1)}, bf16[256,512]{1,0:T(8,128)(2,1)S(1)}, u32[]{:S(2)}, u32[]{:S(2)}) collective-permute-start(bf16[256,512]{1,0:T(8,128)(2,1)S(1)} %get-tuple-element.60), channel_id=1, source_target_pairs={{0,2},{2,0},{4,6},{6,4},{8,10},{10,8},{12,14},{14,12},{1,3},{3,1},... | collective-permute-start | bytes 786440 | tf_op jit(solution)/shard_map/ppermute | solution.py:28
  50.8 0.3 stack_rows.2.refs_0_
  51.1 3.2 %collective-permute-start.8 = (bf16[4,7168]{1,0:T(4,128)(2,1)S(1)}, bf16[4,7168]{1,0:T(4,128)(2,1)S(1)}, u32[]{:S(2)}, u32[]{:S(2)}) collective-permute-start(bf16[4,7168]{1,0:T(4,128)(2,1)S(1)} %stack_rows.2.refs_0_), channel_id=1, source_target_pairs={{0,4},{2,6},{4,0},{6,2},{8,12},{10,14},{12,8},{14,10},{1,5},{3,7},... | collective-permute-start | bytes 172040 | tf_op jit(solution)/shard_map/ppermute | solution.py:576
  54.2 6.9 %attend.6 = (bf16[256,512]{1,0:T(8,128)(2,1)S(1)}, bf16[8,256,512]{2,1,0:T(8,128)(2,1)}) custom-call(s32[8]{0:T(128)S(1)} %copy-done.5, s32[1]{0:T(128)} %bitcast.own_ref, bf16[4,320,512]{2,1,0:T(8,128)(2,1)S(1)} %collective-permute-done.4.refs_0_, bf16[4,320,512]{2,1,0:T(8,128)(2,1)S(1)} %pack_tokens.3.refs_1_.refs_0_, ...), custom_call_target="tpu_custom_call", output_to_operand_aliasing={{1}: (6, {})} | custom-call | bytes 1024 | tf_op jit(solution)/shard_map/attend/pallas_call | solution.py:285
  61.1 10.0 %collective-permute-done.8.refs_1_ = bf16[4,7168]{1,0:T(4,128)(2,1)S(1)} collective-permute-done((bf16[4,7168]{1,0:T(4,128)(2,1)S(1)}, bf16[4,7168]{1,0:T(4,128)(2,1)S(1)}, u32[]{:S(2)}, u32[]{:S(2)}) %collective-permute-start.8) | collective-permute-done | bytes 57376 | tf_op jit(solution)/shard_map/ppermute | solution.py:576
  71.1 1.4 %broadcast_select_fusion.1.refs_2_ = bf16[1152,512]{1,0:T(8,128)(2,1)S(1)} fusion(bf16[1152,512]{1,0:T(8,128)(2,1)} %collective-permute-done.1, bf16[1152,512]{1,0:T(8,128)(2,1)} %collective-permute-done.11, pred[]{:T(512)S(6)} %and.22), kind=kLoop, calls=%fused_computation.1 | loop fusion | flops 589824 | bytes 3538945 | tf_op jit(solution)/shard_map/jit(_where)/select_n | solution.py:601
  72.6 1.5 %collective-permute-start.9 = (bf16[1152,512]{1,0:T(8,128)(2,1)}, bf16[1152,512]{1,0:T(8,128)(2,1)S(1)}, u32[]{:S(2)}, u32[]{:S(2)}) collective-permute-start(bf16[1152,512]{1,0:T(8,128)(2,1)} %collective-permute-done.3), channel_id=1, source_target_pairs={{4,0},{8,12},{6,2},{10,14},{5,1},{9,13},{7,3},{11,15},{20,16},{24,... | collective-permute-start | bytes 3538952 | tf_op jit(solution)/shard_map/ppermute | solution.py:36
  74.0 1.6 %collective-permute-start.10 = (bf16[256,512]{1,0:T(8,128)(2,1)S(1)}, bf16[256,512]{1,0:T(8,128)(2,1)S(1)}, u32[]{:S(2)}, u32[]{:S(2)}) collective-permute-start(bf16[256,512]{1,0:T(8,128)(2,1)S(1)} %get-tuple-element.59), channel_id=1, source_target_pairs={{0,2},{2,0},{4,6},{6,4},{8,10},{10,8},{12,14},{14,12},{1,3},{3,1},... | collective-permute-start | bytes 786440 | tf_op jit(solution)/shard_map/ppermute | solution.py:28
  75.6 0.2 stack_rows.3.refs_0_
  75.9 0.6 collective-permute-start.13
  76.5 1.6 %collective-permute-start.15 = (bf16[8,7168]{1,0:T(8,128)(2,1)S(1)}, bf16[8,7168]{1,0:T(8,128)(2,1)S(1)}, u32[]{:S(2)}, u32[]{:S(2)}) collective-permute-start(bf16[8,7168]{1,0:T(8,128)(2,1)S(1)} %stack_rows.3.refs_0_), channel_id=1, source_target_pairs={{0,3},{1,2},{2,1},{3,0},{4,7},{5,6},{6,5},{7,4},{8,11},{9,10},{10,... | collective-permute-start | bytes 344072 | tf_op jit(solution)/shard_map/ppermute | solution.py:611
  78.1 5.8 %attend.7 = (bf16[256,512]{1,0:T(8,128)(2,1)S(1)}, bf16[8,256,512]{2,1,0:T(8,128)(2,1)}) custom-call(s32[8]{0:T(128)S(1)} %copy-done.5, s32[1]{0:T(128)} %bitcast.own_ref, bf16[4,320,512]{2,1,0:T(8,128)(2,1)S(1)} %collective-permute-done.4.refs_0_, bf16[4,320,512]{2,1,0:T(8,128)(2,1)S(1)} %pack_tokens.3.refs_1_.refs_0_, ...), custom_call_target="tpu_custom_call", output_to_operand_aliasing={{1}: (6, {})} | custom-call | bytes 1024 | tf_op jit(solution)/shard_map/attend/pallas_call | solution.py:285
  83.9 1.8 %collective-permute-done.13.refs_1_ = bf16[8,7168]{1,0:T(8,128)(2,1)S(1)} collective-permute-done((bf16[8,7168]{1,0:T(8,128)(2,1)S(1)}, bf16[8,7168]{1,0:T(8,128)(2,1)S(1)}, u32[]{:S(2)}, u32[]{:S(2)}) %collective-permute-start.13) | collective-permute-done | bytes 114720 | tf_op jit(solution)/shard_map/ppermute | solution.py:611
  85.7 1.6 %collective-permute-done.15.refs_3_ = bf16[8,7168]{1,0:T(8,128)(2,1)S(1)} collective-permute-done((bf16[8,7168]{1,0:T(8,128)(2,1)S(1)}, bf16[8,7168]{1,0:T(8,128)(2,1)S(1)}, u32[]{:S(2)}, u32[]{:S(2)}) %collective-permute-start.15) | collective-permute-done | bytes 114720 | tf_op jit(solution)/shard_map/ppermute | solution.py:611
  87.3 1.6 %experts.1 = (f32[8,7168]{1,0:T(8,128)S(1)}, bf16[8,7168]{1,0:T(8,128)(2,1)S(1)}, bf16[8,7168]{1,0:T(8,128)(2,1)S(1)}, bf16[8,7168]{1,0:T(8,128)(2,1)S(1)}) custom-call(bf16[8,7168]{1,0:T(8,128)(2,1)S(1)} %stack_rows.3.refs_0_, bf16[8,7168]{1,0:T(8,128)(2,1)S(1)} %collective-permute-done.13.refs_1_, bf16[8,7168]{1,0:T(8,128)(2,1)S(1)} %collective-permute-done.14.refs_2_, ...), custom_call_target="tpu_custom_call" | custom-call | bytes 1024 | tf_op jit(solution)/shard_map/experts/pallas_call | solution.py:454
  88.9 1.6 %collective-permute-start.16 = (bf16[8,7168]{1,0:T(8,128)(2,1)S(1)}, bf16[8,7168]{1,0:T(8,128)(2,1)S(1)}, u32[]{:S(2)}, u32[]{:S(2)}) collective-permute-start(bf16[8,7168]{1,0:T(8,128)(2,1)S(1)} %get-tuple-element.77), channel_id=1, source_target_pairs={{0,2},{1,3},{2,0},{3,1},{4,6},{5,7},{6,4},{7,5},{8,10},{9,11},{10,... | collective-permute-start | bytes 344072 | tf_op jit(solution)/shard_map/ppermute | solution.py:611
  90.5 0.2 collective-permute-start.17
  90.7 0.4 collective-permute-start.18
  91.1 1.5 %collective-permute-start.19 = (bf16[256,512]{1,0:T(8,128)(2,1)S(1)}, bf16[256,512]{1,0:T(8,128)(2,1)S(1)}, u32[]{:S(2)}, u32[]{:S(2)}) collective-permute-start(bf16[256,512]{1,0:T(8,128)(2,1)S(1)} %get-tuple-element.69), channel_id=1, source_target_pairs={{0,2},{2,0},{4,6},{6,4},{8,10},{10,8},{12,14},{14,12},{1,3},{3,1},... | collective-permute-start | bytes 786440 | tf_op jit(solution)/shard_map/ppermute | solution.py:28
  92.6 10.4 %collective-permute-done.9 = bf16[1152,512]{1,0:T(8,128)(2,1)S(1)} collective-permute-done((bf16[1152,512]{1,0:T(8,128)(2,1)}, bf16[1152,512]{1,0:T(8,128)(2,1)S(1)}, u32[]{:S(2)}, u32[]{:S(2)}) %collective-permute-start.9) | collective-permute-done | bytes 1179680 | tf_op jit(solution)/shard_map/ppermute | solution.py:36
  103.0 0.1 broadcast_select_fusion.refs_1_
  103.3 2.8 %collective-permute-done.20.refs_2_ = bf16[1152,512]{1,0:T(8,128)(2,1)S(1)} collective-permute-done((bf16[1152,512]{1,0:T(8,128)(2,1)S(1)}, bf16[1152,512]{1,0:T(8,128)(2,1)S(1)}, u32[]{:S(2)}, u32[]{:S(2)}) %collective-permute-start.20) | collective-permute-done | bytes 1179680 | tf_op jit(solution)/shard_map/ppermute | solution.py:28
  106.1 4.1 %attend.8 = bf16[256,512]{1,0:T(8,128)(2,1)} custom-call(s32[8]{0:T(128)S(1)} %copy-done.5, s32[1]{0:T(128)} %bitcast.own_ref, bf16[4,320,512]{2,1,0:T(8,128)(2,1)S(1)} %collective-permute-done.4.refs_0_, bf16[1152,512]{1,0:T(8,128)(2,1)S(1)} %broadcast_select_fusion.refs_1_, bf16[1152,512]{1,0:T(8,128)(2,1)S(1)} %collective-permute-done.20.refs_2_), custom_call_target="tpu_custom_call" | custom-call | bytes 1024 | tf_op jit(solution)/shard_map/attend/pallas_call | solution.py:285
  110.2 1.6 %collective-permute-start.21 = (bf16[256,512]{1,0:T(8,128)(2,1)}, bf16[256,512]{1,0:T(8,128)(2,1)S(1)}, u32[]{:S(2)}, u32[]{:S(2)}) collective-permute-start(bf16[256,512]{1,0:T(8,128)(2,1)} %attend.8), channel_id=1, source_target_pairs={{0,2},{2,0},{4,6},{6,4},{8,10},{10,8},{12,14},{14,12},{1,3},{3,1},... | collective-permute-start | bytes 786440 | tf_op jit(solution)/shard_map/ppermute | solution.py:28
  111.8 2.1 %collective-permute-start.22 = (bf16[2,7168]{1,0:T(2,128)(2,1)S(1)}, bf16[2,7168]{1,0:T(2,128)(2,1)S(1)}, u32[]{:S(2)}, u32[]{:S(2)}) collective-permute-start(bf16[2,7168]{1,0:T(2,128)(2,1)S(1)} %get-tuple-element.100), channel_id=1, source_target_pairs={{0,8},{2,10},{4,12},{6,14},{8,0},{10,2},{12,4},{14,6},{1,9},{3,11}... | collective-permute-start | bytes 86024 | tf_op jit(solution)/shard_map/ppermute | solution.py:576
  114.0 1.1 collective-permute-start.23
  115.1 1.2 collective-permute-start.24
  116.3 4.1 %attend.9.refs_4_ = bf16[8,256,512]{2,1,0:T(8,128)(2,1)} custom-call(s32[8]{0:T(128)S(1)} %copy-done.5, s32[1]{0:T(128)} %bitcast.own_ref, bf16[4,320,512]{2,1,0:T(8,128)(2,1)S(1)} %pack_tokens.3.refs_1_.refs_0_, bf16[1152,512]{1,0:T(8,128)(2,1)S(1)} %broadcast_select_fusion.refs_1_, ...), custom_call_target="tpu_custom_call", output_to_operand_aliasing={{}: (5, {})} | custom-call | bytes 1024 | tf_op jit(solution)/shard_map/attend/pallas_call | solution.py:285
  120.4 0.4 collective-permute-done.24.refs_3_
  120.8 0.3 combine.1
  121.1 0.8 reshape.31
  121.9 1.5 %place.1 = bf16[8,256,512]{2,1,0:T(8,128)(2,1)} custom-call(s32[8]{0:T(128)S(1)} %copy-done.5, s32[1]{0:T(128)} %bitcast.own_ref, bf16[256,512]{1,0:T(8,128)(2,1)S(1)} %collective-permute-done.7.refs_0_, bf16[256,512]{1,0:T(8,128)(2,1)S(1)} %collective-permute-done.10.refs_1_, ...), custom_call_target="tpu_custom_call", output_to_operand_aliasing={{}: (6, {})} | custom-call | bytes 1024 | tf_op jit(solution)/shard_map/place/pallas_call | solution.py:321
  (49 shorter events, 0.5 us)
Async XLA Ops:
  0.6 7.1 %copy-start.8 = (bf16[8,2,8192]{2,1,0:T(2,128)(2,1)S(1)}, bf16[8,2,8192]{2,1,0:T(2,128)(2,1)}, u32[]{:S(2)}) copy-start(bf16[8,2,8192]{2,1,0:T(2,128)(2,1)} %param.16) | copy-start | bytes 786436
  0.6 7.3 %copy-start.10 = (bf16[8,2,512]{2,1,0:T(2,128)(2,1)S(1)}, bf16[8,2,512]{2,1,0:T(2,128)(2,1)}, u32[]{:S(2)}) copy-start(bf16[8,2,512]{2,1,0:T(2,128)(2,1)} %param.17) | copy-start | bytes 49156
  0.7 7.3 %copy-start.11 = (bf16[8,2,64]{2,1,0:T(2,128)(2,1)S(1)}, bf16[8,2,64]{2,1,0:T(2,128)(2,1)}, u32[]{:S(2)}) copy-start(bf16[8,2,64]{2,1,0:T(2,128)(2,1)} %param.18) | copy-start | bytes 6148
  0.7 7.3 %copy-start.5 = (s32[8]{0:T(128)S(1)}, s32[8]{0:T(128)}, u32[]{:S(2)}) copy-start(s32[8]{0:T(128)} %slot_ref.15) | copy-start | bytes 100
  3.0 34.7 %collective-permute-start = (bf16[1152,512]{1,0:T(8,128)(2,1)}, bf16[1152,512]{1,0:T(8,128)(2,1)}, u32[]{:S(2)}, u32[]{:S(2)}) collective-permute-start(bf16[1152,512]{1,0:T(8,128)(2,1)} %pack_cache.1.refs_2_), channel_id=1, source_target_pairs={{0,4},{4,0},{8,12},{12,8},{2,6},{6,2},{10,14},{14,10},{1,5},{5,1},... | collective-permute-start | bytes 3538952 | tf_op jit(solution)/shard_map/ppermute | solution.py:36
  6.1 31.6 %collective-permute-start.1 = (bf16[1152,512]{1,0:T(8,128)(2,1)}, bf16[1152,512]{1,0:T(8,128)(2,1)}, u32[]{:S(2)}, u32[]{:S(2)}) collective-permute-start(bf16[1152,512]{1,0:T(8,128)(2,1)} %pack_cache.1.refs_2_), channel_id=1, source_target_pairs={{4,8},{8,4},{6,10},{10,6},{5,9},{9,5},{7,11},{11,7},{20,24},{24,20... | collective-permute-start | bytes 3538952 | tf_op jit(solution)/shard_map/ppermute | solution.py:36
  8.0 1.6 %copy-start = (bf16[8,2,128,512]{3,2,1,0:T(8,128)(2,1)S(1)}, bf16[8,2,128,512]{3,2,1,0:T(8,128)(2,1)}, u32[]{:S(2)}) copy-start(bf16[8,2,128,512]{3,2,1,0:T(8,128)(2,1)} %param.15) | copy-start | bytes 6291460
  9.6 3.8 %copy-start.9 = (bf16[8,2,7168]{2,1,0:T(2,128)(2,1)S(1)}, bf16[8,2,7168]{2,1,0:T(2,128)(2,1)}, u32[]{:S(2)}) copy-start(bf16[8,2,7168]{2,1,0:T(2,128)(2,1)} %param.20) | copy-start | bytes 688132
  9.6 3.9 %copy-start.6 = (s32[8,2,8]{2,1,0:T(2,128)S(1)}, s32[8,2,8]{2,1,0:T(2,128)}, u32[]{:S(2)}) copy-start(s32[8,2,8]{2,1,0:T(2,128)} %param.21) | copy-start | bytes 1540
  9.6 3.9 %copy-start.7 = (f32[8,2,8]{2,1,0:T(2,128)S(1)}, f32[8,2,8]{2,1,0:T(2,128)}, u32[]{:S(2)}) copy-start(f32[8,2,8]{2,1,0:T(2,128)} %param.22) | copy-start | bytes 1540
  11.8 30.5 %collective-permute-start.4 = (bf16[4,320,512]{2,1,0:T(8,128)(2,1)}, bf16[4,320,512]{2,1,0:T(8,128)(2,1)S(1)}, u32[]{:S(2)}, u32[]{:S(2)}) collective-permute-start(bf16[4,320,512]{2,1,0:T(8,128)(2,1)} %pack_tokens.2), channel_id=1, source_target_pairs={{0,2},{2,0},{4,6},{6,4},{8,10},{10,8},{12,14},{14,12},{1,3},{3,1},... | collective-permute-start | bytes 3932168 | tf_op jit(solution)/shard_map/ppermute | solution.py:28
  13.4 28.9 %collective-permute-start.6 = (bf16[1152,512]{1,0:T(8,128)(2,1)}, bf16[1152,512]{1,0:T(8,128)(2,1)}, u32[]{:S(2)}, u32[]{:S(2)}) collective-permute-start(bf16[1152,512]{1,0:T(8,128)(2,1)} %pack_cache.1.refs_2_), channel_id=1, source_target_pairs={{0,1},{1,0},{2,3},{3,2},{4,5},{5,4},{6,7},{7,6},{8,9},{9,8},{10,11... | collective-permute-start | bytes 3538952 | tf_op jit(solution)/shard_map/ppermute | solution.py:28
  13.9 23.8 %collective-permute-start.2 = (bf16[2,7168]{1,0:T(2,128)(2,1)S(1)}, bf16[2,7168]{1,0:T(2,128)(2,1)S(1)}, u32[]{:S(2)}, u32[]{:S(2)}) collective-permute-start(bf16[2,7168]{1,0:T(2,128)(2,1)S(1)} %get-tuple-element.53), channel_id=1, source_target_pairs={{0,8},{2,10},{4,12},{6,14},{8,0},{10,2},{12,4},{14,6},{1,9},{3,11}... | collective-permute-start | bytes 86024 | tf_op jit(solution)/shard_map/ppermute | solution.py:576
  16.8 1.6 %copy-start.1 = (bf16[8,2,128,512]{3,2,1,0:T(8,128)(2,1)S(1)}, bf16[8,2,128,512]{3,2,1,0:T(8,128)(2,1)}, u32[]{:S(2)}) copy-start(bf16[8,2,128,512]{3,2,1,0:T(8,128)(2,1)} %param.15) | copy-start | bytes 6291460
  37.7 16.6 %collective-permute-start.5 = (bf16[1152,512]{1,0:T(8,128)(2,1)}, bf16[1152,512]{1,0:T(8,128)(2,1)}, u32[]{:S(2)}, u32[]{:S(2)}) collective-permute-start(bf16[1152,512]{1,0:T(8,128)(2,1)} %collective-permute-done.refs_2_), channel_id=1, source_target_pairs={{0,1},{1,0},{2,3},{3,2},{4,5},{5,4},{6,7},{7,6},{8,9},{9,8},{10,11... | collective-permute-start | bytes 3538952 | tf_op jit(solution)/shard_map/ppermute | solution.py:28
  37.7 33.4 %collective-permute-start.3 = (bf16[1152,512]{1,0:T(8,128)(2,1)}, bf16[1152,512]{1,0:T(8,128)(2,1)}, u32[]{:S(2)}, u32[]{:S(2)}) collective-permute-start(bf16[1152,512]{1,0:T(8,128)(2,1)} %collective-permute-done.refs_2_), channel_id=1, source_target_pairs={{4,8},{8,4},{6,10},{10,6},{5,9},{9,5},{7,11},{11,7},{20,24},{24,20... | collective-permute-start | bytes 3538952 | tf_op jit(solution)/shard_map/ppermute | solution.py:36
  39.4 31.7 %collective-permute-start.11 = (bf16[1152,512]{1,0:T(8,128)(2,1)}, bf16[1152,512]{1,0:T(8,128)(2,1)}, u32[]{:S(2)}, u32[]{:S(2)}) collective-permute-start(bf16[1152,512]{1,0:T(8,128)(2,1)} %collective-permute-done.1), channel_id=1, source_target_pairs={{4,0},{8,12},{6,2},{10,14},{5,1},{9,13},{7,3},{11,15},{20,16},{24,... | collective-permute-start | bytes 3538952 | tf_op jit(solution)/shard_map/ppermute | solution.py:36
  49.2 21.9 %collective-permute-start.7 = (bf16[256,512]{1,0:T(8,128)(2,1)S(1)}, bf16[256,512]{1,0:T(8,128)(2,1)S(1)}, u32[]{:S(2)}, u32[]{:S(2)}) collective-permute-start(bf16[256,512]{1,0:T(8,128)(2,1)S(1)} %get-tuple-element.60), channel_id=1, source_target_pairs={{0,2},{2,0},{4,6},{6,4},{8,10},{10,8},{12,14},{14,12},{1,3},{3,1},... | collective-permute-start | bytes 786440 | tf_op jit(solution)/shard_map/ppermute | solution.py:28
  51.1 20.0 %collective-permute-start.8 = (bf16[4,7168]{1,0:T(4,128)(2,1)S(1)}, bf16[4,7168]{1,0:T(4,128)(2,1)S(1)}, u32[]{:S(2)}, u32[]{:S(2)}) collective-permute-start(bf16[4,7168]{1,0:T(4,128)(2,1)S(1)} %stack_rows.2.refs_0_), channel_id=1, source_target_pairs={{0,4},{2,6},{4,0},{6,2},{8,12},{10,14},{12,8},{14,10},{1,5},{3,7},... | collective-permute-start | bytes 172040 | tf_op jit(solution)/shard_map/ppermute | solution.py:576
  72.5 4.0 %collective-permute-start.12 = (bf16[1152,512]{1,0:T(8,128)(2,1)S(1)}, bf16[1152,512]{1,0:T(8,128)(2,1)S(1)}, u32[]{:S(2)}, u32[]{:S(2)}) collective-permute-start(bf16[1152,512]{1,0:T(8,128)(2,1)S(1)} %broadcast_select_fusion.1.refs_2_), channel_id=1, source_target_pairs={{0,1},{1,0},{2,3},{3,2},{4,5},{5,4},{6,7},{7,6},{8,9},{9,8},{10,11... | collective-permute-start | bytes 3538952 | tf_op jit(solution)/shard_map/ppermute | solution.py:28
  72.6 30.5 %collective-permute-start.9 = (bf16[1152,512]{1,0:T(8,128)(2,1)}, bf16[1152,512]{1,0:T(8,128)(2,1)S(1)}, u32[]{:S(2)}, u32[]{:S(2)}) collective-permute-start(bf16[1152,512]{1,0:T(8,128)(2,1)} %collective-permute-done.3), channel_id=1, source_target_pairs={{4,0},{8,12},{6,2},{10,14},{5,1},{9,13},{7,3},{11,15},{20,16},{24,... | collective-permute-start | bytes 3538952 | tf_op jit(solution)/shard_map/ppermute | solution.py:36
  74.0 17.1 %collective-permute-start.10 = (bf16[256,512]{1,0:T(8,128)(2,1)S(1)}, bf16[256,512]{1,0:T(8,128)(2,1)S(1)}, u32[]{:S(2)}, u32[]{:S(2)}) collective-permute-start(bf16[256,512]{1,0:T(8,128)(2,1)S(1)} %get-tuple-element.59), channel_id=1, source_target_pairs={{0,2},{2,0},{4,6},{6,4},{8,10},{10,8},{12,14},{14,12},{1,3},{3,1},... | collective-permute-start | bytes 786440 | tf_op jit(solution)/shard_map/ppermute | solution.py:28
  75.9 9.8 %collective-permute-start.13 = (bf16[8,7168]{1,0:T(8,128)(2,1)S(1)}, bf16[8,7168]{1,0:T(8,128)(2,1)S(1)}, u32[]{:S(2)}, u32[]{:S(2)}) collective-permute-start(bf16[8,7168]{1,0:T(8,128)(2,1)S(1)} %stack_rows.3.refs_0_), channel_id=1, source_target_pairs={{0,2},{1,3},{2,0},{3,1},{4,6},{5,7},{6,4},{7,5},{8,10},{9,11},{10,... | collective-permute-start | bytes 344072 | tf_op jit(solution)/shard_map/ppermute | solution.py:611
  76.5 9.2 %collective-permute-start.14 = (bf16[8,7168]{1,0:T(8,128)(2,1)S(1)}, bf16[8,7168]{1,0:T(8,128)(2,1)S(1)}, u32[]{:S(2)}, u32[]{:S(2)}) collective-permute-start(bf16[8,7168]{1,0:T(8,128)(2,1)S(1)} %stack_rows.3.refs_0_), channel_id=1, source_target_pairs={{0,1},{1,0},{2,3},{3,2},{4,5},{5,4},{6,7},{7,6},{8,9},{9,8},{10,11... | collective-permute-start | bytes 344072 | tf_op jit(solution)/shard_map/ppermute | solution.py:611
  76.5 10.9 %collective-permute-start.15 = (bf16[8,7168]{1,0:T(8,128)(2,1)S(1)}, bf16[8,7168]{1,0:T(8,128)(2,1)S(1)}, u32[]{:S(2)}, u32[]{:S(2)}) collective-permute-start(bf16[8,7168]{1,0:T(8,128)(2,1)S(1)} %stack_rows.3.refs_0_), channel_id=1, source_target_pairs={{0,3},{1,2},{2,1},{3,0},{4,7},{5,6},{6,5},{7,4},{8,11},{9,10},{10,... | collective-permute-start | bytes 344072 | tf_op jit(solution)/shard_map/ppermute | solution.py:611
  78.1 9.2 %copy-start.2 = (bf16[1,7168,128]{2,1,0:T(8,128)(2,1)S(1)}, bf16[1,7168,128]{2,1,0:T(8,128)(2,1)}, u32[]{:S(2)}) copy-start(bf16[1,7168,128]{2,1,0:T(8,128)(2,1)} %refs_4_.1) | copy-start | bytes 5505028
  78.1 9.2 %copy-start.3 = (bf16[1,7168,128]{2,1,0:T(8,128)(2,1)S(1)}, bf16[1,7168,128]{2,1,0:T(8,128)(2,1)}, u32[]{:S(2)}) copy-start(bf16[1,7168,128]{2,1,0:T(8,128)(2,1)} %refs_5_.1) | copy-start | bytes 5505028
  78.1 9.2 %copy-start.4 = (bf16[1,128,7168]{2,1,0:T(8,128)(2,1)S(1)}, bf16[1,128,7168]{2,1,0:T(8,128)(2,1)}, u32[]{:S(2)}) copy-start(bf16[1,128,7168]{2,1,0:T(8,128)(2,1)} %refs_6_.1) | copy-start | bytes 5505028
  88.9 14.1 %collective-permute-start.16 = (bf16[8,7168]{1,0:T(8,128)(2,1)S(1)}, bf16[8,7168]{1,0:T(8,128)(2,1)S(1)}, u32[]{:S(2)}, u32[]{:S(2)}) collective-permute-start(bf16[8,7168]{1,0:T(8,128)(2,1)S(1)} %get-tuple-element.77), channel_id=1, source_target_pairs={{0,2},{1,3},{2,0},{3,1},{4,6},{5,7},{6,4},{7,5},{8,10},{9,11},{10,... | collective-permute-start | bytes 344072 | tf_op jit(solution)/shard_map/ppermute | solution.py:611
  90.5 12.5 %collective-permute-start.17 = (bf16[8,7168]{1,0:T(8,128)(2,1)S(1)}, bf16[8,7168]{1,0:T(8,128)(2,1)S(1)}, u32[]{:S(2)}, u32[]{:S(2)}) collective-permute-start(bf16[8,7168]{1,0:T(8,128)(2,1)S(1)} %get-tuple-element.78), channel_id=1, source_target_pairs={{0,1},{1,0},{2,3},{3,2},{4,5},{5,4},{6,7},{7,6},{8,9},{9,8},{10,11... | collective-permute-start | bytes 344072 | tf_op jit(solution)/shard_map/ppermute | solution.py:611
  90.7 12.3 %collective-permute-start.18 = (bf16[8,7168]{1,0:T(8,128)(2,1)S(1)}, bf16[8,7168]{1,0:T(8,128)(2,1)S(1)}, u32[]{:S(2)}, u32[]{:S(2)}) collective-permute-start(bf16[8,7168]{1,0:T(8,128)(2,1)S(1)} %get-tuple-element.79), channel_id=1, source_target_pairs={{0,3},{1,2},{2,1},{3,0},{4,7},{5,6},{6,5},{7,4},{8,11},{9,10},{10,... | collective-permute-start | bytes 344072 | tf_op jit(solution)/shard_map/ppermute | solution.py:611
  91.1 12.2 %collective-permute-start.19 = (bf16[256,512]{1,0:T(8,128)(2,1)S(1)}, bf16[256,512]{1,0:T(8,128)(2,1)S(1)}, u32[]{:S(2)}, u32[]{:S(2)}) collective-permute-start(bf16[256,512]{1,0:T(8,128)(2,1)S(1)} %get-tuple-element.69), channel_id=1, source_target_pairs={{0,2},{2,0},{4,6},{6,4},{8,10},{10,8},{12,14},{14,12},{1,3},{3,1},... | collective-permute-start | bytes 786440 | tf_op jit(solution)/shard_map/ppermute | solution.py:28
  103.2 2.9 %collective-permute-start.20 = (bf16[1152,512]{1,0:T(8,128)(2,1)S(1)}, bf16[1152,512]{1,0:T(8,128)(2,1)S(1)}, u32[]{:S(2)}, u32[]{:S(2)}) collective-permute-start(bf16[1152,512]{1,0:T(8,128)(2,1)S(1)} %broadcast_select_fusion.refs_1_), channel_id=1, source_target_pairs={{0,1},{1,0},{2,3},{3,2},{4,5},{5,4},{6,7},{7,6},{8,9},{9,8},{10,11... | collective-permute-start | bytes 3538952 | tf_op jit(solution)/shard_map/ppermute | solution.py:28
  110.2 11.7 %collective-permute-start.21 = (bf16[256,512]{1,0:T(8,128)(2,1)}, bf16[256,512]{1,0:T(8,128)(2,1)S(1)}, u32[]{:S(2)}, u32[]{:S(2)}) collective-permute-start(bf16[256,512]{1,0:T(8,128)(2,1)} %attend.8), channel_id=1, source_target_pairs={{0,2},{2,0},{4,6},{6,4},{8,10},{10,8},{12,14},{14,12},{1,3},{3,1},... | collective-permute-start | bytes 786440 | tf_op jit(solution)/shard_map/ppermute | solution.py:28
  111.8 8.5 %collective-permute-start.22 = (bf16[2,7168]{1,0:T(2,128)(2,1)S(1)}, bf16[2,7168]{1,0:T(2,128)(2,1)S(1)}, u32[]{:S(2)}, u32[]{:S(2)}) collective-permute-start(bf16[2,7168]{1,0:T(2,128)(2,1)S(1)} %get-tuple-element.100), channel_id=1, source_target_pairs={{0,8},{2,10},{4,12},{6,14},{8,0},{10,2},{12,4},{14,6},{1,9},{3,11}... | collective-permute-start | bytes 86024 | tf_op jit(solution)/shard_map/ppermute | solution.py:576
  114.0 6.4 %collective-permute-start.23 = (bf16[2,7168]{1,0:T(2,128)(2,1)S(1)}, bf16[2,7168]{1,0:T(2,128)(2,1)S(1)}, u32[]{:S(2)}, u32[]{:S(2)}) collective-permute-start(bf16[2,7168]{1,0:T(2,128)(2,1)S(1)} %get-tuple-element.99), channel_id=1, source_target_pairs={{0,4},{2,6},{4,0},{6,2},{8,12},{10,14},{12,8},{14,10},{1,5},{3,7},... | collective-permute-start | bytes 86024 | tf_op jit(solution)/shard_map/ppermute | solution.py:576
  115.1 5.7 %collective-permute-start.24 = (bf16[2,7168]{1,0:T(2,128)(2,1)S(1)}, bf16[2,7168]{1,0:T(2,128)(2,1)S(1)}, u32[]{:S(2)}, u32[]{:S(2)}) collective-permute-start(bf16[2,7168]{1,0:T(2,128)(2,1)S(1)} %get-tuple-element.98), channel_id=1, source_target_pairs={{0,12},{2,14},{4,8},{6,10},{8,4},{10,6},{12,0},{14,2},{1,13},{3,15... | collective-permute-start | bytes 86024 | tf_op jit(solution)/shard_map/ppermute | solution.py:576
